TPU v7x, 256 devices: a whole 4x4x8 slice. The times are simulated.
256 devices in a mesh: dp: 4 (over y_hi, core), ctx: 64 (over x, z, y_lo).
Axes of the slice: x: 4, y: 4 (y_hi: 2, y_lo: 2; y = y_hi * 2 + y_lo), z: 8, core: 2. Of those that a mesh axis runs over, the one named last changes fastest.
Arguments:
- q_mid: bfloat16 [4, 8192, 1024], P('dp', 'ctx'), may hold values from -160 to 160
- k_mid: bfloat16 [4, 8192, 1024], P('dp', 'ctx'), may hold values from -8 to 8
- v_mid: bfloat16 [4, 8192, 1024], P('dp', 'ctx'), may hold values from -6 to 6
- doc_ids: int32 [4, 8192], P('dp', 'ctx'), may hold values from 0 to 63, never falling along the last dimension, each value on 1 to 512 neighbouring positions
- q_full: bfloat16 [4, 24576, 1024], P('dp', 'ctx'), may hold values from -160 to 160
- k_full: bfloat16 [4, 24576, 1024], P('dp', 'ctx'), may hold values from -8 to 8
- v_base: bfloat16 [4, 24576, 1024], P('dp', 'ctx'), may hold values from -6 to 6
- w_link: bfloat16 [1024, 1024], replicated, may hold values from -0.1875 to 0.1875
- cotangent: bfloat16 [4, 24576, 1024], P('dp', 'ctx'), may hold values from -6 to 6
Outputs:
- grad_q_mid: bfloat16 [4, 8192, 1024], P('dp', 'ctx')
- grad_k_mid: bfloat16 [4, 8192, 1024], P('dp', 'ctx')
- grad_v_mid: bfloat16 [4, 8192, 1024], P('dp', 'ctx')
- grad_q_full: bfloat16 [4, 24576, 1024], P('dp', 'ctx')
- grad_k_full: bfloat16 [4, 24576, 1024], P('dp', 'ctx')
- grad_v_full: bfloat16 [4, 24576, 1024], P('dp', 'ctx')
- grad_link: float32 [1024, 1024], P('ctx')
Inputs may be any that keep to these rules, and one draw needn't show every extreme that they name: `doc_ids`: ids never fall along a sequence; every document holds 1 to 512 positions, and one holds exactly 512.
All inputs are finite; a program needn't handle non-finite values.
Results may differ from a plain program's by a relative error of at most 0.012.
Values may be sent and summed in bfloat16 or wider, within the bound.
No kernel may reach another device: no remote copies, remote signals or barrier semaphores. Data moves between devices by JAX's collectives and lax.ppermute only.
A program may use at most 192 MiB of HBM per device.

v0:
```python
import jax
import jax.numpy as jnp
from jax import lax
from jax.sharding import PartitionSpec as P

H = 8
E = 128
SPAN = 4
FULL_REACH = 2


def shifted(value, axis, steps):
    count = lax.axis_size(axis)
    initial, last = (max(0, -steps), min(count, count - steps))
    return lax.ppermute(value, axis, [(source, source + steps) for source in range(initial, last)])


def split_heads(rows):
    return rows.reshape(rows.shape[0], H, E)


def joined_heads(rows):
    return rows.reshape(rows.shape[0], H * E)


def attend(queries, keys, values, allowed):
    scores = jnp.einsum(
        "qhe,khe->hqk", split_heads(queries), split_heads(keys), preferred_element_type=jnp.float32
    ) * E ** (-0.5)
    scores = jnp.where(allowed[None], scores, -jnp.inf)
    peak = jnp.max(scores, axis=2, keepdims=True)
    expo = jnp.exp(scores - peak)
    total = jnp.sum(expo, axis=2, keepdims=True)
    probs = expo / total
    weights = probs.astype(jnp.bfloat16)
    attended = jnp.einsum(
        "hqk,khe->qhe", weights, split_heads(values), preferred_element_type=jnp.float32
    )
    return (joined_heads(attended), probs, weights, peak, total)


def query_side(probs, cot, attended, keys, values):
    cot_heads = split_heads(cot)
    dots = jnp.einsum(
        "qhe,khe->hqk", cot_heads, split_heads(values), preferred_element_type=jnp.float32
    )
    delta = jnp.transpose(jnp.sum(cot_heads * split_heads(attended), axis=2))[:, :, None]
    grads = (probs * (dots - delta)).astype(jnp.bfloat16)
    grad_q = jnp.einsum(
        "hqk,khe->qhe", grads, split_heads(keys), preferred_element_type=jnp.float32
    ) * E ** (-0.5)
    return (joined_heads(grad_q), grads, delta)


def key_side(grads, weights, cot, queries):
    grad_k = jnp.einsum(
        "hqk,qhe->khe", grads, split_heads(queries), preferred_element_type=jnp.float32
    ) * E ** (-0.5)
    grad_v = jnp.einsum(
        "hqk,qhe->khe", weights, split_heads(cot), preferred_element_type=jnp.float32
    )
    return (joined_heads(grad_k), joined_heads(grad_v))


def shards(q_mid, k_mid, v_mid, doc_ids, q_full, k_full, v_base, w_link, cotangent):
    place = lax.axis_index("ctx")
    cycle = lax.axis_size("ctx")
    rows = q_mid.shape[1]
    frows = q_full.shape[1]
    width = q_mid.shape[2]
    q_m = q_mid[0]
    k_m = k_mid[0]
    v_m = v_mid[0]
    docs = doc_ids[0]
    q_f = q_full[0]
    k_f = k_full[0]
    cot = cotangent[0]
    far_keys = [k_f]
    for dist in range(1, FULL_REACH + 1):
        far_keys.append(shifted(k_f, "ctx", dist))
    near_keys, near_values, near_docs = ([k_m], [v_m], [docs])
    for dist in range(1, SPAN + 1):
        moved = shifted((k_m, v_m, docs), "ctx", dist)
        near_keys.append(moved[0])
        near_values.append(moved[1])
        near_docs.append(moved[2])
    keys_m = jnp.concatenate(near_keys[::-1], axis=0)
    values_m = jnp.concatenate(near_values[::-1], axis=0)
    kdocs_m = jnp.concatenate(near_docs[::-1], axis=0)
    q_pos = place * rows + jnp.arange(rows, dtype=jnp.int32)
    k_pos = (place - SPAN) * rows + jnp.arange((SPAN + 1) * rows, dtype=jnp.int32)
    gap_m = q_pos[:, None] - k_pos[None, :]
    allowed_m = (k_pos[None, :] >= 0) & (gap_m >= 0) & (kdocs_m[None, :] == docs[:, None])
    out_m, probs_m, weights_m, peak_m, total_m = attend(q_m, keys_m, values_m, allowed_m)
    mid_out = out_m.astype(jnp.bfloat16)
    edge = shifted(mid_out[rows - 1 :], "ctx", 1)
    upsampled = jnp.repeat(jnp.concatenate([edge, mid_out], axis=0), 3, axis=0)[1 : frows + 1]
    values_f = (v_base[0] + jnp.dot(upsampled, w_link, preferred_element_type=jnp.float32)).astype(
        jnp.bfloat16
    )
    far_values = [values_f]
    for dist in range(1, FULL_REACH + 1):
        far_values.append(shifted(values_f, "ctx", dist))
    keys_f = jnp.concatenate(far_keys[::-1], axis=0)
    values_all_f = jnp.concatenate(far_values[::-1], axis=0)
    fdocs = jnp.repeat(docs, 3)
    kdocs_f = jnp.concatenate(
        [jnp.repeat(near_docs[dist], 3) for dist in range(FULL_REACH, -1, -1)], axis=0
    )
    fq_pos = place * frows + jnp.arange(frows, dtype=jnp.int32)
    fk_pos = (place - FULL_REACH) * frows + jnp.arange((FULL_REACH + 1) * frows, dtype=jnp.int32)
    gap_f = fq_pos[:, None] - fk_pos[None, :]
    window = FULL_REACH * frows
    allowed_f = (
        (fk_pos[None, :] >= 0)
        & (gap_f >= 0)
        & (gap_f < window)
        & (kdocs_f[None, :] == fdocs[:, None])
    )
    out_f, probs_f, weights_f, peak_f, total_f = attend(q_f, keys_f, values_all_f, allowed_f)
    grad_q_f, grads_f, delta_f = query_side(probs_f, cot, out_f, keys_f, values_all_f)
    lead_f = FULL_REACH * frows
    dk_f, dv_f = key_side(grads_f, weights_f, cot, q_f)
    own_k_f = dk_f[lead_f:]
    own_v_f = dv_f[lead_f:]
    for dist in range(1, FULL_REACH + 1):
        low = (FULL_REACH - dist) * frows
        back = shifted(
            (
                dk_f[low : low + frows].astype(jnp.bfloat16),
                dv_f[low : low + frows].astype(jnp.bfloat16),
            ),
            "ctx",
            -dist,
        )
        own_k_f = own_k_f + back[0].astype(jnp.float32)
        own_v_f = own_v_f + back[1].astype(jnp.float32)
    grad_k_full = own_k_f.astype(jnp.bfloat16)
    grad_v_full = own_v_f.astype(jnp.bfloat16)
    share = width // cycle
    factor = float(lax.axis_size("dp") * cycle * frows) ** (-0.5)
    link_term = jnp.einsum("pa,pb->ab", upsampled, grad_v_full, preferred_element_type=jnp.float32)
    link_all = lax.psum(link_term, ("dp", "ctx"))
    grad_link = lax.dynamic_slice_in_dim(link_all, place * share, share, 0) * factor
    up_grads = jnp.einsum("pb,ab->pa", grad_v_full, w_link, preferred_element_type=jnp.float32)
    tail = shifted(up_grads[:2], "ctx", -1)
    stacked = jnp.concatenate([up_grads[2:], tail], axis=0)
    mid_out_grads = jnp.sum(stacked.reshape(rows, 3, width), axis=1).astype(jnp.bfloat16)
    grad_q_m, grads_m, delta_m = query_side(probs_m, mid_out_grads, out_m, keys_m, values_m)
    lead_m = SPAN * rows
    dk_m, dv_m = key_side(grads_m, weights_m, mid_out_grads, q_m)
    own_k_m = dk_m[lead_m:]
    own_v_m = dv_m[lead_m:]
    for dist in range(1, SPAN + 1):
        low = (SPAN - dist) * rows
        back = shifted(
            (
                dk_m[low : low + rows].astype(jnp.bfloat16),
                dv_m[low : low + rows].astype(jnp.bfloat16),
            ),
            "ctx",
            -dist,
        )
        own_k_m = own_k_m + back[0].astype(jnp.float32)
        own_v_m = own_v_m + back[1].astype(jnp.float32)
    return (
        grad_q_m.astype(jnp.bfloat16)[None],
        own_k_m.astype(jnp.bfloat16)[None],
        own_v_m.astype(jnp.bfloat16)[None],
        grad_q_f.astype(jnp.bfloat16)[None],
        grad_k_full[None],
        grad_v_full[None],
        grad_link,
    )


def solution(mesh):
    in_specs = (
        P("dp", "ctx", None),
        P("dp", "ctx", None),
        P("dp", "ctx", None),
        P("dp", "ctx"),
        P("dp", "ctx", None),
        P("dp", "ctx", None),
        P("dp", "ctx", None),
        P(),
        P("dp", "ctx", None),
    )
    out_specs = (
        P("dp", "ctx", None),
        P("dp", "ctx", None),
        P("dp", "ctx", None),
        P("dp", "ctx", None),
        P("dp", "ctx", None),
        P("dp", "ctx", None),
        P("ctx", None),
    )
    return jax.shard_map(shards, mesh=mesh, in_specs=in_specs, out_specs=out_specs, check_vma=False)
```

profile of v0, /device:TPU:1, one launch (start us, length us, event | category | flops | bytes accessed | tf_op | source)
XLA Modules:
  0.0 598.4 jit_solution(15659019628454274050)
XLA Ops:
  8.5 6.4 %collective-permute-start = (bf16[128,1024]{0,1:T(8,128)(2,1)S(1)}, bf16[128,1024]{0,1:T(8,128)(2,1)}, u32[]{:S(2)}, u32[]{:S(2)}) collective-permute-start(bf16[128,1024]{0,1:T(8,128)(2,1)S(1)} %bitcast.168), channel_id=1, source_target_pairs={{0,4},{1,5},{2,6},{3,7},{4,8},{5,9},{6,10},{7,11},{8,12},{9,13},{1... | collective-permute-start | bytes 786440 | tf_op jit(solution)/shard_map/ppermute | solution.py:15
  15.0 5.3 collective-permute-start.1
  20.2 4.8 collective-permute-start.2
  39.9 6.4 %collective-permute-start.3 = (bf16[128,1024]{0,1:T(8,128)(2,1)S(1)}, bf16[128,1024]{0,1:T(8,128)(2,1)}, u32[]{:S(2)}, u32[]{:S(2)}) collective-permute-start(bf16[128,1024]{0,1:T(8,128)(2,1)S(1)} %bitcast.172), channel_id=1, source_target_pairs={{0,1},{1,2},{2,3},{3,4},{4,5},{5,6},{6,7},{7,8},{8,9},{9,10},{10,1... | collective-permute-start | bytes 786440 | tf_op jit(solution)/shard_map/ppermute | solution.py:15
  46.5 5.4 collective-permute-start.4
  54.3 6.2 %collective-permute-start.5 = (s32[128]{0:T(128)S(1)}, s32[128]{0:T(128)S(1)}, u32[]{:S(2)}, u32[]{:S(2)}) collective-permute-start(s32[128]{0:T(128)S(1)} %bitcast.195), channel_id=1, source_target_pairs={{0,3},{1,4},{2,5},{3,6},{4,7},{5,8},{6,9},{7,10},{8,11},{9,12},{10... | collective-permute-start | bytes 1544 | tf_op jit(solution)/shard_map/ppermute | solution.py:15
  61.2 4.2 collective-permute-start.13
  71.7 5.2 collective-permute-start.14
  90.6 7.1 %collective-permute-done.14 = bf16[128,1024]{0,1:T(8,128)(2,1)} collective-permute-done((bf16[128,1024]{0,1:T(8,128)(2,1)S(1)}, bf16[128,1024]{0,1:T(8,128)(2,1)}, u32[]{:S(2)}, u32[]{:S(2)}) %collective-permute-start.14) | collective-permute-done | bytes 262176 | tf_op jit(solution)/shard_map/ppermute | solution.py:15
  115.0 9.3 %fusion.46 = (f32[8,384]{1,0:T(8,128)S(1)}, f32[8,384,1152]{1,2,0:T(8,128)}) fusion(pred[384,1152]{0,1:T(8,128)(4,1)} %fusion.14, bf16[384,8,128]{0,2,1:T(8,128)(2,1)} %bitcast.151, bf16[384,8,128]{2,0,1:T(8,128)(2,1)} %copy.127, bf16[384,8,128]{2,0,1:T(8,128)(2,1)} %copy.126, bf16[384,8,128]{2,0,1:T(8,128)(2,1)} %copy.125), kind=kOutput, calls=%fused_computation.96 | convolution fusion | flops 927204480 | bytes 17756160 | tf_op jit(solution)/shard_map/sub | solution.py:32
  124.3 9.1 %fusion.7 = bf16[8,384,1152]{1,2,0:T(8,128)(2,1)} fusion(f32[8,384,1152]{1,2,0:T(8,128)} %get-tuple-element.43, f32[8,384]{1,0:T(8,128)S(1)} %get-tuple-element.42), kind=kLoop, calls=%fused_computation.11 | loop fusion | flops 7077888 | bytes 21245952 | tf_op jit(solution)/shard_map/convert_element_type | solution.py:35
  133.4 7.6 %fusion.47 = (bf16[1152,8,128]{0,2,1:T(8,128)(2,1)S(1)}, f32[1152,8,128]{0,2,1:T(8,128)}) fusion(bf16[8,384,1152]{1,2,0:T(8,128)(2,1)} %fusion.7, bf16[384,8,128]{0,2,1:T(8,128)(2,1)S(1)} %bitcast.146), kind=kOutput, calls=%fused_computation.97 | convolution fusion | flops 907149312 | bytes 14942208 | tf_op jit(solution)/shard_map/hqk,qhe->khe/dot_general | solution.py:59
  164.3 24.8 %collective-permute-done.11 = bf16[384,1024]{1,0:T(8,128)(2,1)} collective-permute-done((bf16[384,1024]{1,0:T(8,128)(2,1)}, bf16[384,1024]{1,0:T(8,128)(2,1)}, u32[]{:S(2)}, u32[]{:S(2)}) %collective-permute-start.11) | collective-permute-done | bytes 786464 | tf_op jit(solution)/shard_map/ppermute | solution.py:15
  203.1 11.5 %collective-permute-done.12 = f32[2,1024]{1,0:T(2,128)S(1)} collective-permute-done((f32[2,1024]{1,0:T(2,128)S(1)}, f32[2,1024]{1,0:T(2,128)S(1)}, u32[]{:S(2)}, u32[]{:S(2)}) %collective-permute-start.12) | collective-permute-done | bytes 8224 | tf_op jit(solution)/shard_map/ppermute | solution.py:15
  232.8 4.7 fusion.50
  237.8 6.3 %collective-permute-start.25 = (bf16[1,1024]{1,0:T(2,128)(2,1)S(1)}, bf16[1,1024]{1,0:T(2,128)(2,1)S(1)}, u32[]{:S(2)}, u32[]{:S(2)}) collective-permute-start(bf16[1,1024]{1,0:T(2,128)(2,1)S(1)} %bitcast.190), channel_id=1, source_target_pairs={{0,1},{1,2},{2,3},{3,4},{4,5},{5,6},{6,7},{7,8},{8,9},{9,10},{10,1... | collective-permute-start | bytes 6152 | tf_op jit(solution)/shard_map/ppermute | solution.py:15
  272.3 5.2 collective-permute-start.27
  277.5 5.5 collective-permute-start.26
  307.9 4.3 copy.195
  312.3 5.4 fusion.16
  317.8 8.2 %fusion.2 = bf16[8,384,1152]{1,2,0:T(8,128)(2,1)} fusion(bf16[1152,8,128]{0,2,1:T(8,128)(2,1)S(1)} %bitcast.145, bf16[384,8,128]{0,2,1:T(8,128)(2,1)S(1)} %bitcast.148, f32[8,384]{1,0:T(8,128)S(1)} %bitcast.188, f32[8,384,1152]{1,2,0:T(8,128)} %get-tuple-element.43, f32[8,384]{1,0:T(8,128)S(1)} %get-tuple-element.42), kind=kOutput, calls=%fused_computation.3 | convolution fusion | flops 920125440 | bytes 24403968 | tf_op jit(solution)/shard_map/qhe,khe->hqk/dot_general | solution.py:44
  325.9 7.6 %fusion.51 = (bf16[1152,8,128]{0,2,1:T(8,128)(2,1)S(1)}, f32[1152,8,128]{0,2,1:T(8,128)}) fusion(bf16[8,384,1152]{1,2,0:T(8,128)(2,1)} %fusion.2, bf16[384,8,128]{0,2,1:T(8,128)(2,1)S(1)} %bitcast.152), kind=kOutput, calls=%fused_computation.101 | convolution fusion | flops 908328960 | bytes 14942208 | tf_op jit(solution)/shard_map/hqk,qhe->khe/dot_general | solution.py:56
  344.7 5.5 multiply_convert_fusion.1
  366.7 223.1 %all-reduce.2.cloned.1.call-done = f32[1024,1024]{1,0:T(8,128)} async-done(((f32[1024,1024]{1,0:T(8,128)}), f32[1024,1024]{1,0:T(8,128)}) %all-reduce.2.cloned.1.call-update) | async-done | bytes 4194320 | tf_op jit(solution)/shard_map/psum | solution.py:143
  (200 shorter events, 194.5 us)
Async XLA Ops:
  7.2 582.7 %all-reduce.2.cloned.1.call-start = ((), (), s32[]{:S(2)}) async-start(), calls=%async_computation | async-start | bytes 8388608 | tf_op jit(solution)/shard_map/psum | solution.py:143
  8.5 56.9 %collective-permute-start = (bf16[128,1024]{0,1:T(8,128)(2,1)S(1)}, bf16[128,1024]{0,1:T(8,128)(2,1)}, u32[]{:S(2)}, u32[]{:S(2)}) collective-permute-start(bf16[128,1024]{0,1:T(8,128)(2,1)S(1)} %bitcast.168), channel_id=1, source_target_pairs={{0,4},{1,5},{2,6},{3,7},{4,8},{5,9},{6,10},{7,11},{8,12},{9,13},{1... | collective-permute-start | bytes 786440 | tf_op jit(solution)/shard_map/ppermute | solution.py:15
  15.0 53.5 %collective-permute-start.1 = (bf16[128,1024]{0,1:T(8,128)(2,1)S(1)}, bf16[128,1024]{0,1:T(8,128)(2,1)}, u32[]{:S(2)}, u32[]{:S(2)}) collective-permute-start(bf16[128,1024]{0,1:T(8,128)(2,1)S(1)} %bitcast.169), channel_id=1, source_target_pairs={{0,3},{1,4},{2,5},{3,6},{4,7},{5,8},{6,9},{7,10},{8,11},{9,12},{10... | collective-permute-start | bytes 786440 | tf_op jit(solution)/shard_map/ppermute | solution.py:15
  20.2 51.4 %collective-permute-start.2 = (bf16[128,1024]{0,1:T(8,128)(2,1)S(1)}, bf16[128,1024]{0,1:T(8,128)(2,1)}, u32[]{:S(2)}, u32[]{:S(2)}) collective-permute-start(bf16[128,1024]{0,1:T(8,128)(2,1)S(1)} %bitcast.170), channel_id=1, source_target_pairs={{0,2},{1,3},{2,4},{3,5},{4,6},{5,7},{6,8},{7,9},{8,10},{9,11},{10,... | collective-permute-start | bytes 786440 | tf_op jit(solution)/shard_map/ppermute | solution.py:15
  39.9 37.0 %collective-permute-start.3 = (bf16[128,1024]{0,1:T(8,128)(2,1)S(1)}, bf16[128,1024]{0,1:T(8,128)(2,1)}, u32[]{:S(2)}, u32[]{:S(2)}) collective-permute-start(bf16[128,1024]{0,1:T(8,128)(2,1)S(1)} %bitcast.172), channel_id=1, source_target_pairs={{0,1},{1,2},{2,3},{3,4},{4,5},{5,6},{6,7},{7,8},{8,9},{9,10},{10,1... | collective-permute-start | bytes 786440 | tf_op jit(solution)/shard_map/ppermute | solution.py:15
  65.5 44.9 %collective-permute-start.9 = (bf16[384,1024]{0,1:T(8,128)(2,1)}, bf16[384,1024]{0,1:T(8,128)(2,1)}, u32[]{:S(2)}, u32[]{:S(2)}) collective-permute-start(bf16[384,1024]{0,1:T(8,128)(2,1)} %bitcast.154), channel_id=1, source_target_pairs={{0,1},{1,2},{2,3},{3,4},{4,5},{5,6},{6,7},{7,8},{8,9},{9,10},{10,1... | collective-permute-start | bytes 2359304 | tf_op jit(solution)/shard_map/ppermute | solution.py:15
  68.5 44.2 %collective-permute-start.8 = (bf16[384,1024]{0,1:T(8,128)(2,1)}, bf16[384,1024]{0,1:T(8,128)(2,1)}, u32[]{:S(2)}, u32[]{:S(2)}) collective-permute-start(bf16[384,1024]{0,1:T(8,128)(2,1)} %bitcast.155), channel_id=1, source_target_pairs={{0,2},{1,3},{2,4},{3,5},{4,6},{5,7},{6,8},{7,9},{8,10},{9,11},{10,... | collective-permute-start | bytes 2359304 | tf_op jit(solution)/shard_map/ppermute | solution.py:15
  71.7 26.1 %collective-permute-start.14 = (bf16[128,1024]{0,1:T(8,128)(2,1)S(1)}, bf16[128,1024]{0,1:T(8,128)(2,1)}, u32[]{:S(2)}, u32[]{:S(2)}) collective-permute-start(bf16[128,1024]{0,1:T(8,128)(2,1)S(1)} %bitcast.165), channel_id=1, source_target_pairs={{0,3},{1,4},{2,5},{3,6},{4,7},{5,8},{6,9},{7,10},{8,11},{9,12},{10... | collective-permute-start | bytes 786440 | tf_op jit(solution)/shard_map/ppermute | solution.py:15
  76.9 26.5 %collective-permute-start.15 = (bf16[128,1024]{0,1:T(8,128)(2,1)S(1)}, bf16[128,1024]{0,1:T(8,128)(2,1)}, u32[]{:S(2)}, u32[]{:S(2)}) collective-permute-start(bf16[128,1024]{0,1:T(8,128)(2,1)S(1)} %bitcast.166), channel_id=1, source_target_pairs={{0,2},{1,3},{2,4},{3,5},{4,6},{5,7},{6,8},{7,9},{8,10},{9,11},{10,... | collective-permute-start | bytes 786440 | tf_op jit(solution)/shard_map/ppermute | solution.py:15
  79.8 25.4 %collective-permute-start.16 = (bf16[128,1024]{0,1:T(8,128)(2,1)S(1)}, bf16[128,1024]{0,1:T(8,128)(2,1)}, u32[]{:S(2)}, u32[]{:S(2)}) collective-permute-start(bf16[128,1024]{0,1:T(8,128)(2,1)S(1)} %bitcast.167), channel_id=1, source_target_pairs={{0,1},{1,2},{2,3},{3,4},{4,5},{5,6},{6,7},{7,8},{8,9},{9,10},{10,1... | collective-permute-start | bytes 786440 | tf_op jit(solution)/shard_map/ppermute | solution.py:15
  144.7 44.5 %collective-permute-start.11 = (bf16[384,1024]{1,0:T(8,128)(2,1)}, bf16[384,1024]{1,0:T(8,128)(2,1)}, u32[]{:S(2)}, u32[]{:S(2)}) collective-permute-start(bf16[384,1024]{1,0:T(8,128)(2,1)} %copy.133), channel_id=1, source_target_pairs={{2,0},{3,1},{4,2},{5,3},{6,4},{7,5},{8,6},{9,7},{10,8},{11,9},{12,... | collective-permute-start | bytes 2359304 | tf_op jit(solution)/shard_map/ppermute | solution.py:15
  148.7 43.2 %collective-permute-start.10 = (bf16[384,1024]{1,0:T(8,128)(2,1)}, bf16[384,1024]{1,0:T(8,128)(2,1)}, u32[]{:S(2)}, u32[]{:S(2)}) collective-permute-start(bf16[384,1024]{1,0:T(8,128)(2,1)} %copy.131), channel_id=1, source_target_pairs={{1,0},{2,1},{3,2},{4,3},{5,4},{6,5},{7,6},{8,7},{9,8},{10,9},{11,1... | collective-permute-start | bytes 2359304 | tf_op jit(solution)/shard_map/ppermute | solution.py:15
  237.8 22.6 %collective-permute-start.25 = (bf16[1,1024]{1,0:T(2,128)(2,1)S(1)}, bf16[1,1024]{1,0:T(2,128)(2,1)S(1)}, u32[]{:S(2)}, u32[]{:S(2)}) collective-permute-start(bf16[1,1024]{1,0:T(2,128)(2,1)S(1)} %bitcast.190), channel_id=1, source_target_pairs={{0,1},{1,2},{2,3},{3,4},{4,5},{5,6},{6,7},{7,8},{8,9},{9,10},{10,1... | collective-permute-start | bytes 6152 | tf_op jit(solution)/shard_map/ppermute | solution.py:15
  251.0 40.6 %collective-permute-start.20 = (bf16[128,1024]{0,1:T(8,128)(2,1)}, bf16[128,1024]{0,1:T(8,128)(2,1)}, u32[]{:S(2)}, u32[]{:S(2)}) collective-permute-start(bf16[128,1024]{0,1:T(8,128)(2,1)} %bitcast.34), channel_id=1, source_target_pairs={{4,0},{5,1},{6,2},{7,3},{8,4},{9,5},{10,6},{11,7},{12,8},{13,9},{1... | collective-permute-start | bytes 786440 | tf_op jit(solution)/shard_map/ppermute | solution.py:15
  254.1 42.2 %collective-permute-start.19 = (bf16[128,1024]{0,1:T(8,128)(2,1)}, bf16[128,1024]{0,1:T(8,128)(2,1)}, u32[]{:S(2)}, u32[]{:S(2)}) collective-permute-start(bf16[128,1024]{0,1:T(8,128)(2,1)} %bitcast.33), channel_id=1, source_target_pairs={{3,0},{4,1},{5,2},{6,3},{7,4},{8,5},{9,6},{10,7},{11,8},{12,9},{13... | collective-permute-start | bytes 786440 | tf_op jit(solution)/shard_map/ppermute | solution.py:15
  257.2 40.6 %collective-permute-start.18 = (bf16[128,1024]{0,1:T(8,128)(2,1)}, bf16[128,1024]{0,1:T(8,128)(2,1)}, u32[]{:S(2)}, u32[]{:S(2)}) collective-permute-start(bf16[128,1024]{0,1:T(8,128)(2,1)} %bitcast.32), channel_id=1, source_target_pairs={{2,0},{3,1},{4,2},{5,3},{6,4},{7,5},{8,6},{9,7},{10,8},{11,9},{12,... | collective-permute-start | bytes 786440 | tf_op jit(solution)/shard_map/ppermute | solution.py:15
  272.3 31.1 %collective-permute-start.27 = (bf16[384,1024]{1,0:T(8,128)(2,1)}, bf16[384,1024]{1,0:T(8,128)(2,1)}, u32[]{:S(2)}, u32[]{:S(2)}) collective-permute-start(bf16[384,1024]{1,0:T(8,128)(2,1)} %fusion.15), channel_id=1, source_target_pairs={{0,1},{1,2},{2,3},{3,4},{4,5},{5,6},{6,7},{7,8},{8,9},{9,10},{10,1... | collective-permute-start | bytes 2359304 | tf_op jit(solution)/shard_map/ppermute | solution.py:15
  277.5 27.2 %collective-permute-start.26 = (bf16[384,1024]{1,0:T(8,128)(2,1)}, bf16[384,1024]{1,0:T(8,128)(2,1)}, u32[]{:S(2)}, u32[]{:S(2)}) collective-permute-start(bf16[384,1024]{1,0:T(8,128)(2,1)} %fusion.15), channel_id=1, source_target_pairs={{0,2},{1,3},{2,4},{3,5},{4,6},{5,7},{6,8},{7,9},{8,10},{9,11},{10,... | collective-permute-start | bytes 2359304 | tf_op jit(solution)/shard_map/ppermute | solution.py:15
  296.3 44.7 %collective-permute-start.24 = (bf16[128,1024]{1,0:T(8,128)(2,1)}, bf16[128,1024]{1,0:T(8,128)(2,1)}, u32[]{:S(2)}, u32[]{:S(2)}) collective-permute-start(bf16[128,1024]{1,0:T(8,128)(2,1)} %copy.161), channel_id=1, source_target_pairs={{4,0},{5,1},{6,2},{7,3},{8,4},{9,5},{10,6},{11,7},{12,8},{13,9},{1... | collective-permute-start | bytes 786440 | tf_op jit(solution)/shard_map/ppermute | solution.py:15
  297.7 44.8 %collective-permute-start.23 = (bf16[128,1024]{1,0:T(8,128)(2,1)}, bf16[128,1024]{1,0:T(8,128)(2,1)}, u32[]{:S(2)}, u32[]{:S(2)}) collective-permute-start(bf16[128,1024]{1,0:T(8,128)(2,1)} %copy.160), channel_id=1, source_target_pairs={{3,0},{4,1},{5,2},{6,3},{7,4},{8,5},{9,6},{10,7},{11,8},{12,9},{13... | collective-permute-start | bytes 786440 | tf_op jit(solution)/shard_map/ppermute | solution.py:15
  300.0 42.5 %collective-permute-start.22 = (bf16[128,1024]{1,0:T(8,128)(2,1)}, bf16[128,1024]{1,0:T(8,128)(2,1)}, u32[]{:S(2)}, u32[]{:S(2)}) collective-permute-start(bf16[128,1024]{1,0:T(8,128)(2,1)} %copy.159), channel_id=1, source_target_pairs={{2,0},{3,1},{4,2},{5,3},{6,4},{7,5},{8,6},{9,7},{10,8},{11,9},{12,... | collective-permute-start | bytes 786440 | tf_op jit(solution)/shard_map/ppermute | solution.py:15
  303.4 39.1 %collective-permute-start.21 = (bf16[128,1024]{1,0:T(8,128)(2,1)}, bf16[128,1024]{1,0:T(8,128)(2,1)}, u32[]{:S(2)}, u32[]{:S(2)}) collective-permute-start(bf16[128,1024]{1,0:T(8,128)(2,1)} %copy.157), channel_id=1, source_target_pairs={{1,0},{2,1},{3,2},{4,3},{5,4},{6,5},{7,6},{8,7},{9,8},{10,9},{11,1... | collective-permute-start | bytes 786440 | tf_op jit(solution)/shard_map/ppermute | solution.py:15
  337.4 24.7 %collective-permute-start.29 = (bf16[384,1024]{1,0:T(8,128)(2,1)}, bf16[384,1024]{1,0:T(8,128)(2,1)}, u32[]{:S(2)}, u32[]{:S(2)}) collective-permute-start(bf16[384,1024]{1,0:T(8,128)(2,1)} %copy.174), channel_id=1, source_target_pairs={{2,0},{3,1},{4,2},{5,3},{6,4},{7,5},{8,6},{9,7},{10,8},{11,9},{12,... | collective-permute-start | bytes 2359304 | tf_op jit(solution)/shard_map/ppermute | solution.py:15
  341.0 22.6 %collective-permute-start.28 = (bf16[384,1024]{1,0:T(8,128)(2,1)}, bf16[384,1024]{1,0:T(8,128)(2,1)}, u32[]{:S(2)}, u32[]{:S(2)}) collective-permute-start(bf16[384,1024]{1,0:T(8,128)(2,1)} %copy.172), channel_id=1, source_target_pairs={{1,0},{2,1},{3,2},{4,3},{5,4},{6,5},{7,6},{8,7},{9,8},{10,9},{11,1... | collective-permute-start | bytes 2359304 | tf_op jit(solution)/shard_map/ppermute | solution.py:15
  (32 other events, 695.0 us)
Sparse Core Ops, SparseCore 0:
  296.4 293.4 all-reduce.1
where the time goes:
time: 610 us; the launch traced here: 598 us
  waiting for transfers between devices  280 us (46%)
  local copies, waits for them, and re-layouts  110 us (18%)
  starting transfers between devices  93.7 us (15%)
  matrix products  69 us (11%)
  other arithmetic  30.3 us (5%)
  between operations  14.9 us (2%)
    psum x1, waiting for transfers between devices, shards(): link_all = lax.psum(link_term, ('dp', 'ctx'))  223 us
    ppermute x30, starting transfers between devices, shifted(): lax.ppermute(value, axis, [(source, source + steps) for source in range(i...  93.6 us
    ppermute x30, waiting for transfers between devices, shifted(): lax.ppermute(value, axis, [(source, source + steps) for source in range(i...  56.9 us
    unnamed x70, local copies, waits for them, and re-layouts  22 us
    sub x2, matrix products, attend(): expo = jnp.exp(scores - peak)  13.1 us
    dot_general x2, matrix products, key_side(): jnp.einsum('hqk,qhe->khe', weights, split_heads(cot), preferred_element_t...  12.3 us
  transfers between devices with their start and end apart: 31, of which 10 were waited for; matrix products, arithmetic and copies ran while one was open for 25% of the time, Pallas kernels for 0%

commit v1 on v0

v1 whole, which is shorter than its diff:
```python
import math

import jax
import jax.numpy as jnp
from jax import lax
from jax.experimental import pallas as pl
from jax.experimental.pallas import tpu as pltpu
from jax.sharding import PartitionSpec as P

H = 8
E = 128
S = 128
F = 384
REACH = 4
FREACH = 2
WIDTH = H * E
SPAN_M = (REACH + 1) * S
SPAN_F = (FREACH + 1) * F
WIN = FREACH * F
TILES = F // S
TILE_W = WIN + S
SCALE = E ** (-0.5)
LOG2 = SCALE * math.log2(math.e)
NEG = -1e30
F32 = jnp.float32
BF16 = jnp.bfloat16
PARAMS = pltpu.CompilerParams(vmem_limit_bytes=48 * 1024 * 1024)


def dot_nn(a, b):
    return lax.dot_general(a, b, (((1,), (0,)), ((), ())), preferred_element_type=F32)


def dot_nt(a, b):
    return lax.dot_general(a, b, (((1,), (1,)), ((), ())), preferred_element_type=F32)


def dot_tn(a, b):
    return lax.dot_general(a, b, (((0,), (0,)), ((), ())), preferred_element_type=F32)


def iota(shape, axis):
    return lax.broadcasted_iota(jnp.int32, shape, axis)


def to_column(row, size):
    return jnp.transpose(jnp.broadcast_to(row, (size, size)))


def split3(x):
    hi = x.astype(BF16)
    rest = x - hi.astype(F32)
    mid = rest.astype(BF16)
    return hi, mid, (rest - mid.astype(F32)).astype(BF16)


def head_spec(rows):
    return pl.BlockSpec((rows, E), lambda h: (0, h))


def whole_spec(shape):
    return pl.BlockSpec(shape, lambda h: (0,) * len(shape))


def mid_fwd_body(q, p4, p3, p2, p1, p0, out, att, stat, bias):
    pays = (p4, p3, p2, p1, p0)

    @pl.when(pl.program_id(0) == 0)
    def _():
        mine = to_column(p0[2 * S : 2 * S + 16, :].astype(F32)[0:1], S)
        for n, pay in enumerate(pays):
            ok = mine == pay[2 * S : 2 * S + 16, :].astype(F32)[0:1]
            if n == REACH:
                ok = ok & (iota((S, S), 0) >= iota((S, S), 1))
            bias[:, n * S : (n + 1) * S] = jnp.where(ok, 0.0, NEG)

    keys = jnp.concatenate([pay[0:S, :] for pay in pays], axis=0)
    values = jnp.concatenate([pay[S : 2 * S, :] for pay in pays], axis=0)
    scores = dot_nt(q[...], keys) * LOG2 + bias[...]
    peak = jnp.max(scores, axis=1, keepdims=True)
    expo = jnp.exp2(scores - peak)
    inv = 1.0 / jnp.sum(expo, axis=1, keepdims=True)
    attended = dot_nn((expo * inv).astype(BF16), values)
    att[...] = attended
    out[...] = attended.astype(BF16)
    stat[0:1, :] = jnp.transpose(jnp.broadcast_to(peak, (S, S)))[0:1]
    stat[1:2, :] = jnp.transpose(jnp.broadcast_to(inv, (S, S)))[0:1]
    stat[2:8, :] = jnp.zeros((6, S), F32)


def mid_forward(q, pays):
    return pl.pallas_call(
        mid_fwd_body,
        grid=(H,),
        in_specs=[head_spec(S)] + [head_spec(2 * S + 16)] * 5,
        out_specs=[head_spec(S), head_spec(S), head_spec(8)],
        out_shape=[
            jax.ShapeDtypeStruct((S, WIDTH), BF16),
            jax.ShapeDtypeStruct((S, WIDTH), F32),
            jax.ShapeDtypeStruct((8, WIDTH), F32),
        ],
        scratch_shapes=[pltpu.VMEM((S, SPAN_M), F32)],
        compiler_params=PARAMS,
        cost_estimate=pl.CostEstimate(flops=700_000_000, bytes_accessed=4_000_000, transcendentals=0),
        name="mid_forward",
    )(q, *pays)


def full_mask(bias, docs, own_rows):
    spread = (iota((S, F), 1) // 3 == iota((S, F), 0)).astype(BF16)
    spread_t = (iota((F, S), 0) // 3 == iota((F, S), 1)).astype(BF16)
    rows = jnp.concatenate(
        [dot_nn(jnp.broadcast_to(d, (16, S)), spread)[0:1] for d in docs], axis=1
    )
    column = dot_nn(spread_t, to_column(own_rows.astype(F32), S).astype(BF16))
    for t in range(TILES):
        lo = t * S
        mine = jnp.concatenate([column[lo : lo + S]] * (TILE_W // S), axis=1)
        gap = iota((S, TILE_W), 1) - iota((S, TILE_W), 0)
        ok = (mine == rows[:, lo : lo + TILE_W]) & (gap >= 0) & (gap < WIN)
        bias[t] = jnp.where(ok, 0.0, NEG)


def doc_row(ref):
    return ref[S : S + 16, :][0:1]


def stats_body(k, base, mid, edge, w, q0, q1, q2, c0, c1, c2, m0, m1, m2, values, s0, s1, s2, bias, ext, part):
    head = pl.program_id(0)

    @pl.when(head == 0)
    def _():
        docs = [doc_row(ref) for ref in (m0, m1, m2)]
        full_mask(bias, docs, docs[0])
        for t in range(TILES):
            part[t, 0:H, :] = jnp.full((H, SPAN_F), NEG, F32)
            part[t, H : 3 * H, :] = jnp.zeros((2 * H, SPAN_F), F32)

    linked = dot_nn(mid[...], w[...])
    for n in range(2, 5):
        ext[pl.ds(n, S, stride=3), :] = linked
    ext[0:2, :] = jnp.broadcast_to(dot_nn(edge[...], w[...])[15:16], (2, E))
    v = (base[...].astype(F32) + ext[0:F, :]).astype(BF16)
    values[...] = v
    queries = jnp.concatenate([q0[...], q1[...], q2[...]], axis=0)
    cots = jnp.concatenate([c0[...], c1[...], c2[...]], axis=0)
    for t in range(TILES):
        lo = t * S
        scores = dot_nt(k[lo : lo + S, :], queries[lo : lo + TILE_W]) * LOG2 + bias[t]
        peak = jnp.max(scores, axis=0, keepdims=True)
        expo = jnp.exp2(scores - peak)
        dots = dot_nt(v[lo : lo + S], cots[lo : lo + TILE_W])
        part[t, pl.ds(head, 1), lo : lo + TILE_W] = peak
        part[t, pl.ds(H + head, 1), lo : lo + TILE_W] = jnp.sum(expo, axis=0, keepdims=True)
        part[t, pl.ds(2 * H + head, 1), lo : lo + TILE_W] = jnp.sum(expo * dots, axis=0, keepdims=True)

    @pl.when(head == H - 1)
    def _():
        for n, out in enumerate((s0, s1, s2)):
            cols = slice(n * F, (n + 1) * F)
            merged = merge([(part[t, 0:H, cols], part[t, H : 2 * H, cols], part[t, 2 * H : 3 * H, cols]) for t in range(TILES)])
            for j in range(3):
                out[j * H : (j + 1) * H, :] = merged[j]


def merge(parts):
    peak = parts[0][0]
    for part in parts[1:]:
        peak = jnp.maximum(peak, part[0])
    total, dots = 0.0, 0.0
    for part in parts:
        factor = jnp.exp2(part[0] - peak)
        total = total + part[1] * factor
        dots = dots + part[2] * factor
    return peak, total, dots


def full_stats(k, base, mid, edge, w, qs, cs, ms):
    stat = jax.ShapeDtypeStruct((3 * H, F), F32)
    return pl.pallas_call(
        stats_body,
        grid=(H,),
        in_specs=[head_spec(F), head_spec(F), whole_spec((S, WIDTH)), whole_spec((16, WIDTH)), head_spec(WIDTH)]
        + [head_spec(F)] * 6
        + [pl.BlockSpec((S + 16, E), lambda h: (0, 0))] * 3,
        out_specs=[head_spec(F)] + [whole_spec((3 * H, F))] * 3,
        out_shape=[jax.ShapeDtypeStruct((F, WIDTH), BF16), stat, stat, stat],
        scratch_shapes=[
            pltpu.VMEM((TILES, S, TILE_W), F32),
            pltpu.VMEM((400, E), F32),
            pltpu.VMEM((TILES, 3 * H, SPAN_F), F32),
        ],
        compiler_params=PARAMS,
        cost_estimate=pl.CostEstimate(flops=3_000_000_000, bytes_accessed=10_000_000, transcendentals=0),
        name="full_stats",
    )(k, base, mid, edge, w, *qs, *cs, *ms)


def grads_body(
    k, v, q0, q1, q2, c0, c1, c2, m0, m1, m2, s0, s1, s2, up1, up2, down1, down2,
    dk, dv, dq0, dq1, dq2, sums, link, tail, bias, ext, glob, kept,
):
    head = pl.program_id(0)

    @pl.when(head == 0)
    def _():
        docs = [doc_row(ref) for ref in (m0, m1, m2)]
        full_mask(bias, docs, docs[0])

        def triple(ref, base):
            peak, total, dots = (ref[base + j * H : base + (j + 1) * H, :] for j in range(3))
            return jnp.where(total > 0.0, peak, NEG), total, dots

        groups = (
            [triple(s0, 0), triple(up1, 0), triple(up2, 0)],
            [triple(s1, 0), triple(up1, 3 * H), triple(down1, 0)],
            [triple(s2, 0), triple(down1, 3 * H), triple(down2, 0)],
        )
        for n, group in enumerate(groups):
            cols = slice(n * F, (n + 1) * F)
            peak, total, dots = merge(group)
            inv = jnp.where(total > 0.0, 1.0 / total, 0.0)
            glob[0:H, cols] = peak
            glob[H : 2 * H, cols] = inv
            glob[2 * H : 3 * H, cols] = dots * inv
        kept[...] = jnp.zeros((F, SPAN_F), BF16)
        ext[F:400, :] = jnp.zeros((400 - F, E), F32)

    queries = jnp.concatenate([q0[...], q1[...], q2[...]], axis=0)
    cots = jnp.concatenate([c0[...], c1[...], c2[...]], axis=0)
    for t in range(TILES):
        lo = t * S
        cols = slice(lo, lo + TILE_W)
        scores = dot_nt(k[lo : lo + S, :], queries[cols]) * LOG2 + bias[t]
        probs = jnp.exp2(scores - glob[pl.ds(head, 1), cols]) * glob[pl.ds(H + head, 1), cols]
        dots = dot_nt(v[lo : lo + S, :], cots[cols])
        grads = (probs * (dots - glob[pl.ds(2 * H + head, 1), cols])).astype(BF16)
        kept[lo : lo + S, cols] = grads
        dk[lo : lo + S, :] = (dot_nn(grads, queries[cols]) * SCALE).astype(BF16)
        grad_v = dot_nn(probs.astype(BF16), cots[cols]).astype(BF16)
        dv[lo : lo + S, :] = grad_v
        ext[lo : lo + S, :] = grad_v.astype(F32)
    for n, out in enumerate((dq0, dq1, dq2)):
        part = dot_tn(kept[:, n * F : (n + 1) * F], k[...]) * SCALE
        out[...] = part.astype(out.dtype)
    total = ext[pl.ds(2, S, stride=3), :] + ext[pl.ds(3, S, stride=3), :] + ext[pl.ds(4, S, stride=3), :]
    sums[...] = total
    first = ext[0:1, :] + ext[1:2, :]
    tail[...] = jnp.broadcast_to(first, (8, E))
    link[0:S, :] = total.astype(BF16)
    link[S : S + 16, :] = jnp.where(iota((16, E), 0) == 15, first, 0.0).astype(BF16)


def full_grads(k, v, qs, cs, ms, stats):
    return pl.pallas_call(
        grads_body,
        grid=(H,),
        in_specs=[head_spec(F), head_spec(F)]
        + [head_spec(F)] * 6
        + [pl.BlockSpec((S + 16, E), lambda h: (0, 0))] * 3
        + [whole_spec(s.shape) for s in stats],
        out_specs=[head_spec(F)] * 5 + [head_spec(S), head_spec(S + 16), head_spec(8)],
        out_shape=[
            jax.ShapeDtypeStruct((F, WIDTH), BF16),
            jax.ShapeDtypeStruct((F, WIDTH), BF16),
            jax.ShapeDtypeStruct((F, WIDTH), F32),
            jax.ShapeDtypeStruct((F, WIDTH), BF16),
            jax.ShapeDtypeStruct((F, WIDTH), BF16),
            jax.ShapeDtypeStruct((S, WIDTH), F32),
            jax.ShapeDtypeStruct((S + 16, WIDTH), BF16),
            jax.ShapeDtypeStruct((8, WIDTH), F32),
        ],
        scratch_shapes=[
            pltpu.VMEM((TILES, S, TILE_W), F32),
            pltpu.VMEM((400, E), F32),
            pltpu.VMEM((3 * H, SPAN_F), F32),
            pltpu.VMEM((F, SPAN_F), BF16),
        ],
        compiler_params=PARAMS,
        cost_estimate=pl.CostEstimate(flops=8_000_000_000, bytes_accessed=14_000_000, transcendentals=0),
        name="full_grads",
    )(k, v, *qs, *cs, *ms, *stats)


def mid_cot_body(sums, tail, w, att, stat, out):
    total = sums[...] + jnp.where(iota((S, WIDTH), 0) == S - 1, tail[0:1, :], 0.0)
    grad = dot_nt(total.astype(BF16), w[...]).astype(BF16)
    out[0:S, :] = grad
    weighed = grad.astype(F32) * att[...]
    for h in range(H):
        cols = slice(h * E, (h + 1) * E)
        delta = jnp.sum(jnp.transpose(weighed[:, cols]), axis=0, keepdims=True)
        rows = [*split3(stat[0:1, cols]), *split3(stat[1:2, cols]), *split3(delta)]
        rows = [row.astype(F32) for row in rows] + [jnp.zeros((7, E), F32)]
        out[S : S + 16, cols] = jnp.concatenate(rows, axis=0).astype(BF16)


def mid_cotangent(sums, tail, w, att, stat):
    return pl.pallas_call(
        mid_cot_body,
        out_shape=jax.ShapeDtypeStruct((S + 16, WIDTH), BF16),
        compiler_params=PARAMS,
        cost_estimate=pl.CostEstimate(flops=600_000_000, bytes_accessed=4_000_000, transcendentals=0),
        name="mid_cotangent",
    )(sums, tail, w, att, stat)


def mid_bwd_body(*refs):
    p4, p3, p2, p1, p0 = refs[0:5]
    ms = refs[5:10]
    gs = refs[10:15]
    dq, dk, dv, back, fore = refs[15:]
    pays = (p4, p3, p2, p1, p0)

    @pl.when(pl.program_id(0) == 0)
    def _():
        mine = p0[2 * S : 2 * S + 16, :].astype(F32)[0:1]
        column = to_column(mine, S)
        causal = iota((S, S), 1) >= iota((S, S), 0)
        for n, pay in enumerate(pays):
            ok = to_column(pay[2 * S : 2 * S + 16, :].astype(F32)[0:1], S) == mine
            if n == REACH:
                ok = ok & causal
            back[n * S : (n + 1) * S, :] = jnp.where(ok, 0.0, NEG)
        for n, pay in enumerate(ms):
            ok = column == doc_row(pay).astype(F32)
            if n == 0:
                ok = ok & causal
            fore[:, n * S : (n + 1) * S] = jnp.where(ok, 0.0, NEG)

    def stats(ref):
        rows = ref[S : S + 16, :].astype(F32)
        return [rows[j : j + 1] + rows[j + 1 : j + 2] + rows[j + 2 : j + 3] for j in (0, 3, 6)]

    k = p0[0:S, :]
    v = p0[S : 2 * S, :]
    keys = jnp.concatenate([pay[0:S, :] for pay in pays], axis=0)
    values = jnp.concatenate([pay[S : 2 * S, :] for pay in pays], axis=0)
    peak, inv, delta = stats(gs[0])
    scores = dot_nt(keys, ms[0][0:S, :]) * LOG2 + back[...]
    probs = jnp.exp2(scores - peak) * inv
    grads = (probs * (dot_nt(values, gs[0][0:S, :]) - delta)).astype(BF16)
    dq[...] = (dot_tn(grads, keys) * SCALE).astype(BF16)
    queries = jnp.concatenate([ref[0:S, :] for ref in ms], axis=0)
    cots = jnp.concatenate([ref[0:S, :] for ref in gs], axis=0)
    every = [stats(ref) for ref in gs]
    peak, inv, delta = (jnp.concatenate([one[j] for one in every], axis=1) for j in range(3))
    scores = dot_nt(k, queries) * LOG2 + fore[...]
    probs = jnp.exp2(scores - peak) * inv
    grads = (probs * (dot_nt(v, cots) - delta)).astype(BF16)
    dk[...] = (dot_nn(grads, queries) * SCALE).astype(BF16)
    dv[...] = dot_nn(probs.astype(BF16), cots).astype(BF16)


def mid_backward(pays, ms, gs):
    return pl.pallas_call(
        mid_bwd_body,
        grid=(H,),
        in_specs=[head_spec(2 * S + 16)] * 5 + [head_spec(S + 16)] * 10,
        out_specs=[head_spec(S)] * 3,
        out_shape=[jax.ShapeDtypeStruct((S, WIDTH), BF16)] * 3,
        scratch_shapes=[pltpu.VMEM((SPAN_M, S), F32), pltpu.VMEM((S, SPAN_M), F32)],
        compiler_params=PARAMS,
        cost_estimate=pl.CostEstimate(flops=3_000_000_000, bytes_accessed=6_000_000, transcendentals=0),
        name="mid_backward",
    )(*pays, *ms, *gs)


def shift(value, steps):
    count = lax.axis_size("ctx")
    first, last = max(0, -steps), min(count, count - steps)
    return lax.ppermute(value, "ctx", [(n, n + steps) for n in range(first, last)])


def swap(value, axis, bit):
    count = lax.axis_size(axis)
    return lax.ppermute(value, axis, [(n, n ^ bit) for n in range(count)])


def halves(value, high, axis):
    low, up = jnp.split(value, 2, axis=axis)
    return jnp.where(high, up, low), jnp.where(high, low, up)


def link_gradient(mid_ext, sum_ext, place):
    core = lax.axis_index("dp") % 2 == 1
    x = place // 16
    z = place // 2 % 8
    other_mid = swap(mid_ext, "dp", 1)
    keep, send = halves(sum_ext, core, 1)
    left = jnp.concatenate([mid_ext, other_mid], axis=0)
    right = jnp.concatenate([keep, swap(send, "dp", 1)], axis=0)
    term = dot_tn(left, right)
    blocks = term.reshape(4, 256, 512)
    outer = jnp.stack([blocks[0], blocks[3]])
    inner = jnp.stack([blocks[1], blocks[2]])
    is_outer = (x == 0) | (x == 3)
    keep = jnp.where(is_outer, outer, inner)
    send = jnp.where(is_outer, inner, outer).astype(BF16)
    got = lax.ppermute(send, "ctx", [(n, n ^ 16) for n in range(64)])
    term = keep + got.astype(F32)
    high = x >= 2
    keep = jnp.where(high, term[1], term[0])
    send = jnp.where(high, term[0], term[1]).astype(BF16)
    got = lax.ppermute(send, "ctx", [(n, n ^ 48) for n in range(64)])
    term = keep + got.astype(F32)
    for bit in (4, 2, 1):
        keep, send = halves(term, z & bit != 0, 0)
        term = keep + swap(send.astype(BF16), "ctx", 2 * bit).astype(F32)
    keep, send = halves(term, place % 2 == 1, 0)
    term = keep + swap(send, "ctx", 1)
    term = term + swap(term, "dp", 2)
    other = swap(term, "dp", 1)
    return jnp.concatenate([jnp.where(core, other, term), jnp.where(core, term, other)], axis=1)


def shards(q_mid, k_mid, v_mid, doc_ids, q_full, k_full, v_base, w_link, cotangent):
    place = lax.axis_index("ctx")
    upper = place % 2 == 1
    q_m, q_f, k_f, cot = q_mid[0], q_full[0], k_full[0], cotangent[0]
    ids = jnp.broadcast_to(jnp.tile((doc_ids + 1).astype(BF16), (1, H)), (16, WIDTH))
    own_kv = jnp.concatenate([k_mid[0], v_mid[0], ids], axis=0)
    own_q = jnp.concatenate([q_m, ids], axis=0)

    kv2 = shift(own_kv, 2)
    kv1 = swap(jnp.where(upper, kv2, own_kv), "ctx", 1)
    kv4 = shift(kv2, 2)
    kv3 = swap(jnp.where(upper, kv4, kv2), "ctx", 1)

    qf2 = shift(q_f, -2)
    qf1 = swap(jnp.where(upper, q_f, qf2), "ctx", 1)
    cf2 = shift(cot, -2)
    cf1 = swap(jnp.where(upper, cot, cf2), "ctx", 1)
    qm2 = shift(own_q, -2)
    qm1 = swap(jnp.where(upper, own_q, qm2), "ctx", 1)
    qm4 = shift(qm2, -2)
    qm3 = swap(jnp.where(upper, qm2, qm4), "ctx", 1)

    pays = (kv4, kv3, kv2, kv1, own_kv)
    mid_out, attended, mid_stat = mid_forward(q_m, pays)
    edge = shift(mid_out[S - 16 :], 1)

    qs, cs, ms = (q_f, qf1, qf2), (cot, cf1, cf2), (own_q, qm1, qm2)
    values, s0, s1, s2 = full_stats(k_f, v_base[0], mid_out, edge, w_link, qs, cs, ms)
    up1 = shift(jnp.concatenate([s1, s2], axis=0), 1)
    up2 = shift(s2, 2)
    down1 = shift(jnp.concatenate([s0, s1], axis=0), -1)
    down2 = shift(s0, -2)
    dk_f, dv_f, dq0, dq1, dq2, sums, sum_ext, tail = full_grads(
        k_f, values, qs, cs, ms, (s0, s1, s2, up1, up2, down1, down2)
    )

    cot_m = mid_cotangent(sums, shift(tail, -1), w_link, attended, mid_stat)
    g2 = shift(cot_m, -2)
    g1 = swap(jnp.where(upper, cot_m, g2), "ctx", 1)
    g4 = shift(g2, -2)
    g3 = swap(jnp.where(upper, g2, g4), "ctx", 1)
    dq_m, dk_m, dv_m = mid_backward(pays, (own_q, qm1, qm2, qm3, qm4), (cot_m, g1, g2, g3, g4))

    near = swap(dq1, "ctx", 1).astype(F32)
    passed = jnp.where(upper, dq2.astype(F32), dq2.astype(F32) + near)
    far = shift(passed.astype(BF16), 2).astype(F32)
    dq_f = (dq0 + far + jnp.where(upper, near, 0.0)).astype(BF16)

    factor = float(lax.axis_size("dp") * lax.axis_size("ctx") * F) ** (-0.5)
    grad_link = link_gradient(jnp.concatenate([mid_out, edge], axis=0), sum_ext, place) * factor
    return (dq_m[None], dk_m[None], dv_m[None], dq_f[None], dk_f[None], dv_f[None], grad_link)


def solution(mesh):
    rows = P("dp", "ctx", None)
    return jax.shard_map(
        shards,
        mesh=mesh,
        in_specs=(rows, rows, rows, P("dp", "ctx"), rows, rows, rows, P(), rows),
        out_specs=(rows,) * 6 + (P("ctx", None),),
        check_vma=False,
    )
```

time: 610 us -> 299 us (0.49); the launches traced: 598 us -> 296 us
  waiting for transfers between devices: 280 us -> 131 us
  local copies, waits for them, and re-layouts: 110 us -> 13.8 us
  matrix products: 69 us -> 1.7 us
  Pallas kernels: 0 us -> 40.7 us
  between operations: 14.9 us -> 1.17 us
  other arithmetic: 30.3 us -> 19.5 us
    psum x1 -> x0, waiting for transfers between devices: 223 us -> none  [shards(): link_all = lax.psum(link_term, ('dp', 'ctx'))]
    ppermute x30 -> x34, waiting for transfers between devices: 56.9 us -> 131 us  [the longest x17 68 us: swap(): return lax.ppermute(value, axis, [(n, n ^ bit) for n in range(count)])]
    dot_general x13 -> x1, matrix products: 55.9 us -> 1.7 us  [dot_tn(): lax.dot_general(a, b, (((0,), (0,)), ((), ())), preferred_element_type=F32)]
    pallas_call x0 -> x5, Pallas kernels: none -> 40.7 us  [the longest x1 15.4 us: full_grads(): pl.pallas_call(grads_body, grid=(H,), in_specs=[head_spec(F), head_spec(F...]
    slice x19 -> x2, local copies, waits for them, and re-layouts: 31.8 us -> 1.82 us  [the longest x1 1.2 us: link_gradient(): outer = jnp.stack([blocks[0], blocks[3]])]
    concatenate x16 -> x0, local copies, waits for them, and re-layouts: 23.1 us -> none  [the longest x6 8.28 us: shards(): keys_m = jnp.concatenate(near_keys[::-1], axis=0)]
    convert_element_type x9 -> x0, local copies, waits for them, and re-layouts: 14.7 us -> none  [the longest x2 4.78 us: shards(): dk_f[low:low + frows].astype(jnp.bfloat16)]
    sub x2 -> x0, matrix products: 13.1 us -> none  [attend(): expo = jnp.exp(scores - peak)]
  transfers between devices with their start and end apart: 31 -> 34, of which waited for: 10 -> 13; matrix products, arithmetic and copies ran while one was open for 25% -> 4% of each run, Pallas kernels for 0% -> 11%
where the time goes in v1:
time: 299 us; the launch traced here: 296 us
  waiting for transfers between devices  131 us (44%)
  starting transfers between devices  88.2 us (29%)
  Pallas kernels  40.7 us (14%)
  other arithmetic  19.5 us (7%)
  local copies, waits for them, and re-layouts  13.8 us (5%)
    ppermute x17, waiting for transfers between devices, swap(): return lax.ppermute(value, axis, [(n, n ^ bit) for n in range(count)])  68 us
    ppermute x15, waiting for transfers between devices, shift(): lax.ppermute(value, 'ctx', [(n, n + steps) for n in range(first, last)])  44.9 us
    ppermute x15, starting transfers between devices, shift(): lax.ppermute(value, 'ctx', [(n, n + steps) for n in range(first, last)])  37.6 us
    ppermute x17, starting transfers between devices, swap(): return lax.ppermute(value, axis, [(n, n ^ bit) for n in range(count)])  36 us
    pallas_call x1, Pallas kernels, full_grads(): pl.pallas_call(grads_body, grid=(H,), in_specs=[head_spec(F), head_spec(F...  15.4 us
    ppermute x1, waiting for transfers between devices, link_gradient(): got = lax.ppermute(send, 'ctx', [(n, n ^ 16) for n in range(64)])  12.3 us
    unnamed x72, local copies, waits for them, and re-layouts  12 us
    ppermute x1, starting transfers between devices, link_gradient(): got = lax.ppermute(send, 'ctx', [(n, n ^ 16) for n in range(64)])  11.6 us
  transfers between devices with their start and end apart: 34, of which 13 were waited for; matrix products, arithmetic and copies ran while one was open for 4% of the time, Pallas kernels for 11%

profile of v1, /device:TPU:1, one launch (start us, length us, event | category | flops | bytes accessed | tf_op | source)
XLA Modules:
  0.0 295.8 jit_solution(12492149824381409790)
XLA Ops:
  3.8 5.0 %collective-permute-start = (bf16[272,1024]{1,0:T(8,128)(2,1)S(1)}, bf16[272,1024]{1,0:T(8,128)(2,1)S(1)}, u32[]{:S(2)}, u32[]{:S(2)}) collective-permute-start(bf16[272,1024]{1,0:T(8,128)(2,1)S(1)} %pad_maximum_fusion.2.p0.refs_4_), channel_id=1, source_target_pairs={{0,2},{1,3},{2,4},{3,5},{4,6},{5,7},{6,8},{7,9},{8,10},{9,11},{10,... | collective-permute-start | bytes 1671176 | tf_op jit(solution)/shard_map/ppermute | solution.py:372
  13.2 30.7 %collective-permute-done.4.m2.refs_7_ = bf16[144,1024]{1,0:T(8,128)(2,1)S(1)} collective-permute-done((bf16[144,1024]{1,0:T(8,128)(2,1)S(1)}, bf16[144,1024]{1,0:T(8,128)(2,1)S(1)}, u32[]{:S(2)}, u32[]{:S(2)}) %collective-permute-start.4) | collective-permute-done | bytes 294944 | tf_op jit(solution)/shard_map/ppermute | solution.py:372
  45.2 6.0 %collective-permute-start.1 = (bf16[272,1024]{1,0:T(8,128)(2,1)S(1)}, bf16[272,1024]{1,0:T(8,128)(2,1)S(1)}, u32[]{:S(2)}, u32[]{:S(2)}) collective-permute-start(bf16[272,1024]{1,0:T(8,128)(2,1)S(1)} %collective-permute-done.p2.refs_2_), channel_id=1, source_target_pairs={{0,2},{1,3},{2,4},{3,5},{4,6},{5,7},{6,8},{7,9},{8,10},{9,11},{10,... | collective-permute-start | bytes 1671176 | tf_op jit(solution)/shard_map/ppermute | solution.py:372
  55.7 5.9 %collective-permute-done.1.p4.refs_0_ = bf16[272,1024]{1,0:T(8,128)(2,1)S(1)} collective-permute-done((bf16[272,1024]{1,0:T(8,128)(2,1)S(1)}, bf16[272,1024]{1,0:T(8,128)(2,1)S(1)}, u32[]{:S(2)}, u32[]{:S(2)}) %collective-permute-start.1) | collective-permute-done | bytes 557088 | tf_op jit(solution)/shard_map/ppermute | solution.py:372
  65.9 32.8 %collective-permute-done.2.p3.refs_1_ = bf16[272,1024]{1,0:T(8,128)(2,1)S(1)} collective-permute-done((bf16[272,1024]{1,0:T(8,128)(2,1)S(1)}, bf16[272,1024]{1,0:T(8,128)(2,1)S(1)}, u32[]{:S(2)}, u32[]{:S(2)}) %collective-permute-start.2) | collective-permute-done | bytes 557088 | tf_op jit(solution)/shard_map/ppermute | solution.py:377
  98.7 11.9 %collective-permute-done.3.p1.refs_3_ = bf16[272,1024]{1,0:T(8,128)(2,1)S(1)} collective-permute-done((bf16[272,1024]{1,0:T(8,128)(2,1)S(1)}, bf16[272,1024]{1,0:T(8,128)(2,1)S(1)}, u32[]{:S(2)}, u32[]{:S(2)}) %collective-permute-start.3) | collective-permute-done | bytes 557088 | tf_op jit(solution)/shard_map/ppermute | solution.py:377
  110.6 5.7 %mid_forward.1 = (bf16[128,1024]{1,0:T(8,128)(2,1)S(1)}, f32[128,1024]{1,0:T(8,128)S(1)}, f32[8,1024]{1,0:T(8,128)S(1)}) custom-call(bf16[128,1024]{1,0:T(8,128)(2,1)S(1)} %bitcast.34, bf16[272,1024]{1,0:T(8,128)(2,1)S(1)} %collective-permute-done.1.p4.refs_0_, bf16[272,1024]{1,0:T(8,128)(2,1)S(1)} %collective-permute-done.2.p3.refs_1_, ...), custom_call_target="tpu_custom_call" | custom-call | flops 700000000 | bytes 4000000 | tf_op jit(solution)/shard_map/mid_forward/pallas_call | solution.py:92
  117.8 3.8 %collective-permute-start.8 = (bf16[16,1024]{1,0:T(8,128)(2,1)}, bf16[16,1024]{1,0:T(8,128)(2,1)}, u32[]{:S(2)}, u32[]{:S(2)}) collective-permute-start(bf16[16,1024]{1,0:T(8,128)(2,1)} %slice.35), channel_id=1, source_target_pairs={{0,1},{1,2},{2,3},{3,4},{4,5},{5,6},{6,7},{7,8},{8,9},{9,10},{10,1... | collective-permute-start | bytes 98312 | tf_op jit(solution)/shard_map/ppermute | solution.py:372
  126.5 9.6 %full_stats.1 = (bf16[384,1024]{1,0:T(8,128)(2,1)S(1)}, f32[24,384]{1,0:T(8,128)S(1)}, f32[24,384]{1,0:T(8,128)S(1)}, f32[24,384]{1,0:T(8,128)S(1)}) custom-call(bf16[384,1024]{1,0:T(8,128)(2,1)S(1)} %bitcast.39, bf16[384,1024]{1,0:T(8,128)(2,1)S(1)} %bitcast.38, bf16[128,1024]{1,0:T(8,128)(2,1)S(1)} %get-tuple-element.25.mid, ...), custom_call_target="tpu_custom_call" | custom-call | flops 3000000000 | bytes 10000000 | tf_op jit(solution)/shard_map/full_stats/pallas_call | solution.py:180
  136.1 4.9 %collective-permute-start.14 = (f32[24,384]{1,0:T(8,128)S(1)}, f32[24,384]{1,0:T(8,128)S(1)}, u32[]{:S(2)}, u32[]{:S(2)}) collective-permute-start(f32[24,384]{1,0:T(8,128)S(1)} %get-tuple-element.29.s2), channel_id=1, source_target_pairs={{0,2},{1,3},{2,4},{3,5},{4,6},{5,7},{6,8},{7,9},{8,10},{9,11},{10,... | collective-permute-start | bytes 110600 | tf_op jit(solution)/shard_map/ppermute | solution.py:372
  148.5 6.1 %collective-permute-start.24 = (bf16[144,1024]{1,0:T(8,128)(2,1)}, bf16[144,1024]{1,0:T(8,128)(2,1)}, u32[]{:S(2)}, u32[]{:S(2)}) collective-permute-start(bf16[144,1024]{1,0:T(8,128)(2,1)} %pad_maximum_fusion.4), channel_id=1, source_target_pairs={{0,64},{64,0},{128,192},{192,128},{1,65},{65,1},{129,193},{193,129... | collective-permute-start | bytes 884744 | tf_op jit(solution)/shard_map/ppermute | solution.py:377
  154.6 15.4 %full_grads.1 = (bf16[384,1024]{1,0:T(8,128)(2,1)}, bf16[384,1024]{1,0:T(8,128)(2,1)}, f32[384,1024]{1,0:T(8,128)}, bf16[384,1024]{1,0:T(8,128)(2,1)S(1)}, bf16[...) custom-call(bf16[384,1024]{1,0:T(8,128)(2,1)S(1)} %bitcast.40, ...), custom_call_target="tpu_custom_call" | custom-call | flops 8000000000 | bytes 14000000 | tf_op jit(solution)/shard_map/full_grads/pallas_call | solution.py:255
  171.7 5.2 %collective-permute-start.25 = (bf16[144,512]{1,0:T(8,128)(2,1)S(1)}, bf16[144,512]{1,0:T(8,128)(2,1)S(1)}, u32[]{:S(2)}, u32[]{:S(2)}) collective-permute-start(bf16[144,512]{1,0:T(8,128)(2,1)S(1)} %get-tuple-element.50), channel_id=1, source_target_pairs={{0,64},{64,0},{128,192},{192,128},{1,65},{65,1},{129,193},{193,129... | collective-permute-start | bytes 442376 | tf_op jit(solution)/shard_map/ppermute | solution.py:377
  183.8 11.6 %collective-permute-start.26 = (bf16[2,256,512]{2,1,0:T(8,128)(2,1)}, bf16[2,256,512]{2,1,0:T(8,128)(2,1)}, u32[]{:S(2)}, u32[]{:S(2)}) collective-permute-start(bf16[2,256,512]{2,1,0:T(8,128)(2,1)} %select_convert_fusion), channel_id=1, source_target_pairs={{0,16},{1,17},{2,18},{3,19},{4,20},{5,21},{6,22},{7,23},{8,24},{9,... | collective-permute-start | bytes 1572872 | tf_op jit(solution)/shard_map/ppermute | solution.py:400
  195.4 12.3 %collective-permute-done.26 = bf16[2,256,512]{2,1,0:T(8,128)(2,1)} collective-permute-done((bf16[2,256,512]{2,1,0:T(8,128)(2,1)}, bf16[2,256,512]{2,1,0:T(8,128)(2,1)}, u32[]{:S(2)}, u32[]{:S(2)}) %collective-permute-start.26) | collective-permute-done | bytes 524320 | tf_op jit(solution)/shard_map/ppermute | solution.py:400
  214.8 5.4 %collective-permute-done.27 = bf16[256,512]{1,0:T(8,128)(2,1)S(1)} collective-permute-done((bf16[256,512]{1,0:T(8,128)(2,1)S(1)}, bf16[256,512]{1,0:T(8,128)(2,1)S(1)}, u32[]{:S(2)}, u32[]{:S(2)}) %collective-permute-start.27) | collective-permute-done | bytes 262176 | tf_op jit(solution)/shard_map/ppermute | solution.py:405
  235.9 4.8 %collective-permute-start.7 = (bf16[144,1024]{1,0:T(8,128)(2,1)}, bf16[144,1024]{1,0:T(8,128)(2,1)S(1)}, u32[]{:S(2)}, u32[]{:S(2)}) collective-permute-start(bf16[144,1024]{1,0:T(8,128)(2,1)} %get-tuple-element.53), channel_id=1, source_target_pairs={{0,1},{1,0},{2,3},{3,2},{4,5},{5,4},{6,7},{7,6},{8,9},{9,8},{10,11... | collective-permute-start | bytes 884744 | tf_op jit(solution)/shard_map/ppermute | solution.py:377
  242.1 4.1 %collective-permute-start.30 = (bf16[32,512]{1,0:T(8,128)(2,1)S(1)}, bf16[32,512]{1,0:T(8,128)(2,1)S(1)}, u32[]{:S(2)}, u32[]{:S(2)}) collective-permute-start(bf16[32,512]{1,0:T(8,128)(2,1)S(1)} %select_convert_fusion.4), channel_id=1, source_target_pairs={{0,2},{1,3},{2,0},{3,1},{4,6},{5,7},{6,4},{7,5},{8,10},{9,11},{10,... | collective-permute-start | bytes 98312 | tf_op jit(solution)/shard_map/ppermute | solution.py:377
  246.2 4.2 %collective-permute-done.20.refs_14_ = bf16[144,1024]{1,0:T(8,128)(2,1)S(1)} collective-permute-done((bf16[144,1024]{1,0:T(8,128)(2,1)S(1)}, bf16[144,1024]{1,0:T(8,128)(2,1)S(1)}, u32[]{:S(2)}, u32[]{:S(2)}) %collective-permute-start.20) | collective-permute-done | bytes 294944 | tf_op jit(solution)/shard_map/ppermute | solution.py:372
  250.6 3.7 %collective-permute-start.19 = (bf16[144,1024]{1,0:T(8,128)(2,1)S(1)}, bf16[144,1024]{1,0:T(8,128)(2,1)S(1)}, u32[]{:S(2)}, u32[]{:S(2)}) collective-permute-start(bf16[144,1024]{1,0:T(8,128)(2,1)S(1)} %get-tuple-element.52), channel_id=1, source_target_pairs={{0,1},{1,0},{2,3},{3,2},{4,5},{5,4},{6,7},{7,6},{8,9},{9,8},{10,11... | collective-permute-start | bytes 884744 | tf_op jit(solution)/shard_map/ppermute | solution.py:377
  255.9 8.0 %collective-permute-done.22 = bf16[384,1024]{1,0:T(8,128)(2,1)S(1)} collective-permute-done((bf16[384,1024]{1,0:T(8,128)(2,1)}, bf16[384,1024]{1,0:T(8,128)(2,1)S(1)}, u32[]{:S(2)}, u32[]{:S(2)}) %collective-permute-start.22) | collective-permute-done | bytes 786464 | tf_op jit(solution)/shard_map/ppermute | solution.py:377
  267.0 10.3 %collective-permute-done.31 = f32[16,512]{1,0:T(8,128)S(1)} collective-permute-done((f32[16,512]{1,0:T(8,128)S(1)}, f32[16,512]{1,0:T(8,128)S(1)}, u32[]{:S(2)}, u32[]{:S(2)}) %collective-permute-start.31) | collective-permute-done | bytes 32800 | tf_op jit(solution)/shard_map/ppermute | solution.py:377
  277.6 4.0 %collective-permute-done.32 = f32[16,512]{1,0:T(8,128)S(1)} collective-permute-done((f32[16,512]{1,0:T(8,128)S(1)}, f32[16,512]{1,0:T(8,128)S(1)}, u32[]{:S(2)}, u32[]{:S(2)}) %collective-permute-start.32) | collective-permute-done | bytes 32800 | tf_op jit(solution)/shard_map/ppermute | solution.py:377
  284.8 9.1 %mid_backward.1 = (bf16[128,1024]{1,0:T(8,128)(2,1)}, bf16[128,1024]{1,0:T(8,128)(2,1)}, bf16[128,1024]{1,0:T(8,128)(2,1)}) custom-call(bf16[272,1024]{1,0:T(8,128)(2,1)S(1)} %collective-permute-done.1.p4.refs_0_, bf16[272,1024]{1,0:T(8,128)(2,1)S(1)} %copy-done.5, bf16[272,1024]{1,0:T(8,128)(2,1)S(1)} %collective-permute-done.p2.refs_2_, ...), custom_call_target="tpu_custom_call" | custom-call | flops 3000000000 | bytes 6000000 | tf_op jit(solution)/shard_map/mid_backward/pallas_call | solution.py:356
  (154 shorter events, 74.0 us)
Async XLA Ops:
  0.6 50.6 %collective-permute-start.9 = (bf16[384,1024]{1,0:T(8,128)(2,1)}, bf16[384,1024]{1,0:T(8,128)(2,1)S(1)}, u32[]{:S(2)}, u32[]{:S(2)}) collective-permute-start(bf16[384,1024]{1,0:T(8,128)(2,1)} %bitcast.35), channel_id=1, source_target_pairs={{2,0},{3,1},{4,2},{5,3},{6,4},{7,5},{8,6},{9,7},{10,8},{11,9},{12,... | collective-permute-start | bytes 2359304 | tf_op jit(solution)/shard_map/ppermute | solution.py:372
  3.8 41.3 %collective-permute-start = (bf16[272,1024]{1,0:T(8,128)(2,1)S(1)}, bf16[272,1024]{1,0:T(8,128)(2,1)S(1)}, u32[]{:S(2)}, u32[]{:S(2)}) collective-permute-start(bf16[272,1024]{1,0:T(8,128)(2,1)S(1)} %pad_maximum_fusion.2.p0.refs_4_), channel_id=1, source_target_pairs={{0,2},{1,3},{2,4},{3,5},{4,6},{5,7},{6,8},{7,9},{8,10},{9,11},{10,... | collective-permute-start | bytes 1671176 | tf_op jit(solution)/shard_map/ppermute | solution.py:372
  8.9 44.8 %collective-permute-start.11 = (bf16[384,1024]{1,0:T(8,128)(2,1)}, bf16[384,1024]{1,0:T(8,128)(2,1)}, u32[]{:S(2)}, u32[]{:S(2)}) collective-permute-start(bf16[384,1024]{1,0:T(8,128)(2,1)} %bitcast.45), channel_id=1, source_target_pairs={{2,0},{3,1},{4,2},{5,3},{6,4},{7,5},{8,6},{9,7},{10,8},{11,9},{12,... | collective-permute-start | bytes 2359304 | tf_op jit(solution)/shard_map/ppermute | solution.py:372
  11.2 32.7 %collective-permute-start.4 = (bf16[144,1024]{1,0:T(8,128)(2,1)S(1)}, bf16[144,1024]{1,0:T(8,128)(2,1)S(1)}, u32[]{:S(2)}, u32[]{:S(2)}) collective-permute-start(bf16[144,1024]{1,0:T(8,128)(2,1)S(1)} %pad_maximum_fusion.3.m0.refs_5_), channel_id=1, source_target_pairs={{2,0},{3,1},{4,2},{5,3},{6,4},{7,5},{8,6},{9,7},{10,8},{11,9},{12,... | collective-permute-start | bytes 884744 | tf_op jit(solution)/shard_map/ppermute | solution.py:372
  43.9 19.7 %collective-permute-start.6 = (bf16[144,1024]{1,0:T(8,128)(2,1)S(1)}, bf16[144,1024]{1,0:T(8,128)(2,1)S(1)}, u32[]{:S(2)}, u32[]{:S(2)}) collective-permute-start(bf16[144,1024]{1,0:T(8,128)(2,1)S(1)} %collective-permute-done.4.m2.refs_7_), channel_id=1, source_target_pairs={{2,0},{3,1},{4,2},{5,3},{6,4},{7,5},{8,6},{9,7},{10,8},{11,9},{12,... | collective-permute-start | bytes 884744 | tf_op jit(solution)/shard_map/ppermute | solution.py:372
  45.2 16.5 %collective-permute-start.1 = (bf16[272,1024]{1,0:T(8,128)(2,1)S(1)}, bf16[272,1024]{1,0:T(8,128)(2,1)S(1)}, u32[]{:S(2)}, u32[]{:S(2)}) collective-permute-start(bf16[272,1024]{1,0:T(8,128)(2,1)S(1)} %collective-permute-done.p2.refs_2_), channel_id=1, source_target_pairs={{0,2},{1,3},{2,4},{3,5},{4,6},{5,7},{6,8},{7,9},{8,10},{9,11},{10,... | collective-permute-start | bytes 1671176 | tf_op jit(solution)/shard_map/ppermute | solution.py:372
  52.3 69.3 %collective-permute-start.10 = (bf16[384,1024]{1,0:T(8,128)(2,1)}, bf16[384,1024]{1,0:T(8,128)(2,1)}, u32[]{:S(2)}, u32[]{:S(2)}) collective-permute-start(bf16[384,1024]{1,0:T(8,128)(2,1)} %broadcast_select_fusion.1), channel_id=1, source_target_pairs={{0,1},{1,0},{2,3},{3,2},{4,5},{5,4},{6,7},{7,6},{8,9},{9,8},{10,11... | collective-permute-start | bytes 2359304 | tf_op jit(solution)/shard_map/ppermute | solution.py:377
  55.7 65.9 %collective-permute-start.12 = (bf16[384,1024]{1,0:T(8,128)(2,1)}, bf16[384,1024]{1,0:T(8,128)(2,1)}, u32[]{:S(2)}, u32[]{:S(2)}) collective-permute-start(bf16[384,1024]{1,0:T(8,128)(2,1)} %broadcast_select_fusion), channel_id=1, source_target_pairs={{0,1},{1,0},{2,3},{3,2},{4,5},{5,4},{6,7},{7,6},{8,9},{9,8},{10,11... | collective-permute-start | bytes 2359304 | tf_op jit(solution)/shard_map/ppermute | solution.py:377
  62.0 36.7 %collective-permute-start.2 = (bf16[272,1024]{1,0:T(8,128)(2,1)S(1)}, bf16[272,1024]{1,0:T(8,128)(2,1)S(1)}, u32[]{:S(2)}, u32[]{:S(2)}) collective-permute-start(bf16[272,1024]{1,0:T(8,128)(2,1)S(1)} %get-tuple-element.48), channel_id=1, source_target_pairs={{0,1},{1,0},{2,3},{3,2},{4,5},{5,4},{6,7},{7,6},{8,9},{9,8},{10,11... | collective-permute-start | bytes 1671176 | tf_op jit(solution)/shard_map/ppermute | solution.py:377
  63.4 47.2 %collective-permute-start.3 = (bf16[272,1024]{1,0:T(8,128)(2,1)S(1)}, bf16[272,1024]{1,0:T(8,128)(2,1)S(1)}, u32[]{:S(2)}, u32[]{:S(2)}) collective-permute-start(bf16[272,1024]{1,0:T(8,128)(2,1)S(1)} %get-tuple-element.47), channel_id=1, source_target_pairs={{0,1},{1,0},{2,3},{3,2},{4,5},{5,4},{6,7},{7,6},{8,9},{9,8},{10,11... | collective-permute-start | bytes 1671176 | tf_op jit(solution)/shard_map/ppermute | solution.py:377
  64.6 57.0 %collective-permute-start.5 = (bf16[144,1024]{1,0:T(8,128)(2,1)}, bf16[144,1024]{1,0:T(8,128)(2,1)}, u32[]{:S(2)}, u32[]{:S(2)}) collective-permute-start(bf16[144,1024]{1,0:T(8,128)(2,1)} %get-tuple-element.54), channel_id=1, source_target_pairs={{0,1},{1,0},{2,3},{3,2},{4,5},{5,4},{6,7},{7,6},{8,9},{9,8},{10,11... | collective-permute-start | bytes 884744 | tf_op jit(solution)/shard_map/ppermute | solution.py:377
  136.1 18.5 %collective-permute-start.14 = (f32[24,384]{1,0:T(8,128)S(1)}, f32[24,384]{1,0:T(8,128)S(1)}, u32[]{:S(2)}, u32[]{:S(2)}) collective-permute-start(f32[24,384]{1,0:T(8,128)S(1)} %get-tuple-element.29.s2), channel_id=1, source_target_pairs={{0,2},{1,3},{2,4},{3,5},{4,6},{5,7},{6,8},{7,9},{8,10},{9,11},{10,... | collective-permute-start | bytes 110600 | tf_op jit(solution)/shard_map/ppermute | solution.py:372
  140.9 13.6 %collective-permute-start.16 = (f32[24,384]{1,0:T(8,128)S(1)}, f32[24,384]{1,0:T(8,128)S(1)}, u32[]{:S(2)}, u32[]{:S(2)}) collective-permute-start(f32[24,384]{1,0:T(8,128)S(1)} %get-tuple-element.27.s0), channel_id=1, source_target_pairs={{2,0},{3,1},{4,2},{5,3},{6,4},{7,5},{8,6},{9,7},{10,8},{11,9},{12,... | collective-permute-start | bytes 110600 | tf_op jit(solution)/shard_map/ppermute | solution.py:372
  142.3 12.3 %collective-permute-start.13 = (f32[48,384]{1,0:T(8,128)S(1)}, f32[48,384]{1,0:T(8,128)S(1)}, u32[]{:S(2)}, u32[]{:S(2)}) collective-permute-start(f32[48,384]{1,0:T(8,128)S(1)} %get-tuple-element.58), channel_id=1, source_target_pairs={{0,1},{1,2},{2,3},{3,4},{4,5},{5,6},{6,7},{7,8},{8,9},{9,10},{10,1... | collective-permute-start | bytes 221192 | tf_op jit(solution)/shard_map/ppermute | solution.py:372
  148.5 29.5 %collective-permute-start.24 = (bf16[144,1024]{1,0:T(8,128)(2,1)}, bf16[144,1024]{1,0:T(8,128)(2,1)}, u32[]{:S(2)}, u32[]{:S(2)}) collective-permute-start(bf16[144,1024]{1,0:T(8,128)(2,1)} %pad_maximum_fusion.4), channel_id=1, source_target_pairs={{0,64},{64,0},{128,192},{192,128},{1,65},{65,1},{129,193},{193,129... | collective-permute-start | bytes 884744 | tf_op jit(solution)/shard_map/ppermute | solution.py:377
  183.8 23.9 %collective-permute-start.26 = (bf16[2,256,512]{2,1,0:T(8,128)(2,1)}, bf16[2,256,512]{2,1,0:T(8,128)(2,1)}, u32[]{:S(2)}, u32[]{:S(2)}) collective-permute-start(bf16[2,256,512]{2,1,0:T(8,128)(2,1)} %select_convert_fusion), channel_id=1, source_target_pairs={{0,16},{1,17},{2,18},{3,19},{4,20},{5,21},{6,22},{7,23},{8,24},{9,... | collective-permute-start | bytes 1572872 | tf_op jit(solution)/shard_map/ppermute | solution.py:400
  235.9 48.8 %collective-permute-start.7 = (bf16[144,1024]{1,0:T(8,128)(2,1)}, bf16[144,1024]{1,0:T(8,128)(2,1)S(1)}, u32[]{:S(2)}, u32[]{:S(2)}) collective-permute-start(bf16[144,1024]{1,0:T(8,128)(2,1)} %get-tuple-element.53), channel_id=1, source_target_pairs={{0,1},{1,0},{2,3},{3,2},{4,5},{5,4},{6,7},{7,6},{8,9},{9,8},{10,11... | collective-permute-start | bytes 884744 | tf_op jit(solution)/shard_map/ppermute | solution.py:377
  240.7 23.2 %collective-permute-start.22 = (bf16[384,1024]{1,0:T(8,128)(2,1)}, bf16[384,1024]{1,0:T(8,128)(2,1)S(1)}, u32[]{:S(2)}, u32[]{:S(2)}) collective-permute-start(bf16[384,1024]{1,0:T(8,128)(2,1)} %copy-done.24), channel_id=1, source_target_pairs={{0,1},{1,0},{2,3},{3,2},{4,5},{5,4},{6,7},{7,6},{8,9},{9,8},{10,11... | collective-permute-start | bytes 2359304 | tf_op jit(solution)/shard_map/ppermute | solution.py:377
  242.1 12.3 %collective-permute-start.30 = (bf16[32,512]{1,0:T(8,128)(2,1)S(1)}, bf16[32,512]{1,0:T(8,128)(2,1)S(1)}, u32[]{:S(2)}, u32[]{:S(2)}) collective-permute-start(bf16[32,512]{1,0:T(8,128)(2,1)S(1)} %select_convert_fusion.4), channel_id=1, source_target_pairs={{0,2},{1,3},{2,0},{3,1},{4,6},{5,7},{6,4},{7,5},{8,10},{9,11},{10,... | collective-permute-start | bytes 98312 | tf_op jit(solution)/shard_map/ppermute | solution.py:377
  250.6 34.1 %collective-permute-start.19 = (bf16[144,1024]{1,0:T(8,128)(2,1)S(1)}, bf16[144,1024]{1,0:T(8,128)(2,1)S(1)}, u32[]{:S(2)}, u32[]{:S(2)}) collective-permute-start(bf16[144,1024]{1,0:T(8,128)(2,1)S(1)} %get-tuple-element.52), channel_id=1, source_target_pairs={{0,1},{1,0},{2,3},{3,2},{4,5},{5,4},{6,7},{7,6},{8,9},{9,8},{10,11... | collective-permute-start | bytes 884744 | tf_op jit(solution)/shard_map/ppermute | solution.py:377
  254.3 30.4 %collective-permute-start.21 = (bf16[144,1024]{1,0:T(8,128)(2,1)S(1)}, bf16[144,1024]{1,0:T(8,128)(2,1)S(1)}, u32[]{:S(2)}, u32[]{:S(2)}) collective-permute-start(bf16[144,1024]{1,0:T(8,128)(2,1)S(1)} %get-tuple-element.51), channel_id=1, source_target_pairs={{0,1},{1,0},{2,3},{3,2},{4,5},{5,4},{6,7},{7,6},{8,9},{9,8},{10,11... | collective-permute-start | bytes 884744 | tf_op jit(solution)/shard_map/ppermute | solution.py:377
  254.4 22.8 %collective-permute-start.31 = (f32[16,512]{1,0:T(8,128)S(1)}, f32[16,512]{1,0:T(8,128)S(1)}, u32[]{:S(2)}, u32[]{:S(2)}) collective-permute-start(f32[16,512]{1,0:T(8,128)S(1)} %slice_select_fusion), channel_id=1, source_target_pairs={{0,1},{1,0},{2,3},{3,2},{4,5},{5,4},{6,7},{7,6},{8,9},{9,8},{10,11... | collective-permute-start | bytes 98312 | tf_op jit(solution)/shard_map/ppermute | solution.py:377
  264.2 30.3 %collective-permute-start.23 = (bf16[384,1024]{1,0:T(8,128)(2,1)S(1)}, bf16[384,1024]{1,0:T(8,128)(2,1)S(1)}, u32[]{:S(2)}, u32[]{:S(2)}) collective-permute-start(bf16[384,1024]{1,0:T(8,128)(2,1)S(1)} %fusion.2), channel_id=1, source_target_pairs={{0,2},{1,3},{2,4},{3,5},{4,6},{5,7},{6,8},{7,9},{8,10},{9,11},{10,... | collective-permute-start | bytes 2359304 | tf_op jit(solution)/shard_map/ppermute | solution.py:372
  281.6 12.3 %collective-permute-start.33 = (f32[16,512]{1,0:T(8,128)S(1)}, f32[16,512]{1,0:T(8,128)S(1)}, u32[]{:S(2)}, u32[]{:S(2)}) collective-permute-start(f32[16,512]{1,0:T(8,128)S(1)} %add.63), channel_id=1, source_target_pairs={{0,64},{64,0},{128,192},{192,128},{1,65},{65,1},{129,193},{193,129... | collective-permute-start | bytes 98312 | tf_op jit(solution)/shard_map/ppermute | solution.py:377
  (46 other events, 684.7 us)

commit v2 on v1

v2 whole, which is shorter than its diff:
```python
import math

import jax
import jax.numpy as jnp
from jax import lax
from jax.experimental import pallas as pl
from jax.experimental.pallas import tpu as pltpu
from jax.sharding import PartitionSpec as P

H = 8
E = 128
S = 128
F = 384
REACH = 4
FREACH = 2
WIDTH = H * E
SPAN_M = (REACH + 1) * S
SPAN_F = (FREACH + 1) * F
WIN = FREACH * F
KV = 2 * S + 32
TILES = F // S
TILE_W = WIN + S
SCALE = E ** (-0.5)
LOG2 = SCALE * math.log2(math.e)
NEG = -1e30
F32 = jnp.float32
BF16 = jnp.bfloat16
PARAMS = pltpu.CompilerParams(vmem_limit_bytes=48 * 1024 * 1024)


def dot_nn(a, b):
    return lax.dot_general(a, b, (((1,), (0,)), ((), ())), preferred_element_type=F32)


def dot_nt(a, b):
    return lax.dot_general(a, b, (((1,), (1,)), ((), ())), preferred_element_type=F32)


def dot_tn(a, b):
    return lax.dot_general(a, b, (((0,), (0,)), ((), ())), preferred_element_type=F32)


def iota(shape, axis):
    return lax.broadcasted_iota(jnp.int32, shape, axis)


def to_column(row, size):
    return jnp.transpose(jnp.broadcast_to(row, (size, size)))


def split3(x):
    hi = x.astype(BF16)
    rest = x - hi.astype(F32)
    mid = rest.astype(BF16)
    return hi, mid, (rest - mid.astype(F32)).astype(BF16)


def head_spec(rows):
    return pl.BlockSpec((rows, E), lambda h: (0, h))


def whole_spec(shape):
    return pl.BlockSpec(shape, lambda h: (0,) * len(shape))


def pack_body(flag, q, k, v, ids, qf, kv, qm, first):
    kv[0:S, :] = k[...]
    kv[S : 2 * S, :] = v[...]
    kv[2 * S : 2 * S + 16, :] = ids[...]
    kv[2 * S + 16 : KV, :] = q[S - 16 : S, :]
    qm[0:S, :] = q[...]
    qm[S : S + 16, :] = ids[...]
    first[...] = qf[...]

    @pl.when(flag[0] == 0)
    def _():
        first[0:KV, :] = kv[...]


def pack(flag, q, k, v, ids, qf):
    return pl.pallas_call(
        pack_body,
        grid=(H,),
        in_specs=[FLAG] + [head_spec(S)] * 3 + [whole_spec((16, E)), head_spec(F)],
        out_specs=[head_spec(KV), head_spec(S + 16), head_spec(F)],
        out_shape=[
            jax.ShapeDtypeStruct((KV, WIDTH), BF16),
            jax.ShapeDtypeStruct((S + 16, WIDTH), BF16),
            jax.ShapeDtypeStruct((F, WIDTH), BF16),
        ],
        compiler_params=PARAMS,
        name="pack",
    )(flag, q, k, v, ids, qf)


def pick(flag, upper, lower, rows):
    return jnp.where(flag[0] == 1, upper[0:rows, :], lower[0:rows, :])


def pair_slabs(flag, p4, p3, p2, first, second, p0):
    near = pick(flag, first, second, KV)
    return [p4[...], p3[...], p2[...], near, p0[...]]


def mid_fwd_body(flag, q, p4, p3, p2, first, second, p0, out, att, stat, bias):
    pays = pair_slabs(flag, p4, p3, p2, first, second, p0)

    @pl.when(pl.program_id(0) == 0)
    def _():
        def ids(n):
            return pays[n][2 * S : 2 * S + 16].astype(F32)[0:1]

        mine = to_column(ids(REACH), S)
        edge = to_column(ids(REACH - 1), S)[S - 16 : S]
        for n in range(REACH + 1):
            cols = slice(n * S, (n + 1) * S)
            ok = mine == ids(n)
            ok_edge = edge == ids(n)
            if n == REACH:
                ok = ok & (iota((S, S), 0) >= iota((S, S), 1))
                ok_edge = ok_edge & (iota((16, S), 1) < 0)
            if n == REACH - 1:
                ok_edge = ok_edge & (iota((16, S), 0) + (S - 16) >= iota((16, S), 1))
            bias[0:S, cols] = jnp.where(ok, 0.0, NEG)
            bias[S : S + 16, cols] = jnp.where(ok_edge, 0.0, NEG)

    keys = jnp.concatenate([pay[0:S] for pay in pays], axis=0)
    values = jnp.concatenate([pay[S : 2 * S] for pay in pays], axis=0)
    queries = jnp.concatenate([q[...], pays[REACH - 1][2 * S + 16 : KV]], axis=0)
    scores = dot_nt(queries, keys) * LOG2 + bias[...]
    peak = jnp.max(scores, axis=1, keepdims=True)
    expo = jnp.exp2(scores - peak)
    inv = 1.0 / jnp.sum(expo, axis=1, keepdims=True)
    attended = dot_nn((expo * inv).astype(BF16), values)
    att[...] = attended[0:S]
    out[...] = attended.astype(BF16)
    stat[0:1, :] = jnp.transpose(jnp.broadcast_to(peak[0:S], (S, S)))[0:1]
    stat[1:2, :] = jnp.transpose(jnp.broadcast_to(inv[0:S], (S, S)))[0:1]
    stat[2:8, :] = jnp.zeros((6, S), F32)


def mid_forward(flag, q, pays):
    return pl.pallas_call(
        mid_fwd_body,
        grid=(H,),
        in_specs=[FLAG, head_spec(S)] + PAY_SPECS,
        out_specs=[head_spec(S + 16), head_spec(S), head_spec(8)],
        out_shape=[
            jax.ShapeDtypeStruct((S + 16, WIDTH), BF16),
            jax.ShapeDtypeStruct((S, WIDTH), F32),
            jax.ShapeDtypeStruct((8, WIDTH), F32),
        ],
        scratch_shapes=[pltpu.VMEM((S + 16, SPAN_M), F32)],
        compiler_params=PARAMS,
        cost_estimate=pl.CostEstimate(flops=700_000_000, bytes_accessed=4_000_000, transcendentals=0),
        name="mid_forward",
    )(flag, q, *pays)


FLAG = pl.BlockSpec(memory_space=pltpu.SMEM)
PAY_SPECS = [head_spec(KV)] * 3 + [head_spec(F)] * 2 + [head_spec(KV)]


def full_mask(bias, docs, own_rows, tiles):
    spread = (iota((S, F), 1) // 3 == iota((S, F), 0)).astype(BF16)
    spread_t = (iota((F, S), 0) // 3 == iota((F, S), 1)).astype(BF16)
    rows = jnp.concatenate(
        [dot_nn(jnp.broadcast_to(d, (16, S)), spread)[0:1] for d in docs], axis=1
    )
    column = dot_nn(spread_t, to_column(own_rows.astype(F32), S).astype(BF16))
    for t in range(tiles):
        lo = t * S
        mine = jnp.concatenate([column[lo : lo + S]] * (TILE_W // S), axis=1)
        gap = iota((S, TILE_W), 1) - iota((S, TILE_W), 0)
        ok = (mine == rows[:, lo : lo + TILE_W]) & (gap >= 0) & (gap < WIN)
        bias[t] = jnp.where(ok, 0.0, NEG)


def doc_row(ref):
    return ref[...][0:1]


def stats_body(flag, k, base, mid, w, q0, q1a, q1b, q2, c0, c1, c2, m0, m1, m2, values, s0, s1, s2, bias, ext, part):
    head = pl.program_id(0)

    @pl.when(head == 0)
    def _():
        docs = [doc_row(ref) for ref in (m0, m1, m2)]
        full_mask(bias, docs, docs[0], TILES)
        for t in range(TILES):
            part[t, 0:H, :] = jnp.full((H, SPAN_F), NEG, F32)
            part[t, H : 3 * H, :] = jnp.zeros((2 * H, SPAN_F), F32)

    linked = dot_nn(mid[...], w[...])
    for n in range(2, 5):
        ext[pl.ds(n, S, stride=3), :] = linked[0:S]
    ext[0:2, :] = jnp.broadcast_to(linked[S + 15 : S + 16], (2, E))
    v = (base[...].astype(F32) + ext[0:F, :]).astype(BF16)
    values[...] = v
    queries = jnp.concatenate([q0[...], pick(flag, q1a, q1b, F), q2[...]], axis=0)
    cots = jnp.concatenate([c0[...], c1[...], c2[...]], axis=0)
    for t in range(TILES):
        lo = t * S
        scores = dot_nt(k[lo : lo + S, :], queries[lo : lo + TILE_W]) * LOG2 + bias[t]
        peak = jnp.max(scores, axis=0, keepdims=True)
        expo = jnp.exp2(scores - peak)
        dots = dot_nt(v[lo : lo + S], cots[lo : lo + TILE_W])
        part[t, pl.ds(head, 1), lo : lo + TILE_W] = peak
        part[t, pl.ds(H + head, 1), lo : lo + TILE_W] = jnp.sum(expo, axis=0, keepdims=True)
        part[t, pl.ds(2 * H + head, 1), lo : lo + TILE_W] = jnp.sum(expo * dots, axis=0, keepdims=True)

    @pl.when(head == H - 1)
    def _():
        for n, out in enumerate((s0, s1, s2)):
            cols = slice(n * F, (n + 1) * F)
            merged = merge([(part[t, 0:H, cols], part[t, H : 2 * H, cols], part[t, 2 * H : 3 * H, cols]) for t in range(TILES)])
            for j in range(3):
                out[j * H : (j + 1) * H, :] = merged[j]


def merge(parts):
    peak = parts[0][0]
    for part in parts[1:]:
        peak = jnp.maximum(peak, part[0])
    total, dots = 0.0, 0.0
    for part in parts:
        factor = jnp.exp2(part[0] - peak)
        total = total + part[1] * factor
        dots = dots + part[2] * factor
    return peak, total, dots


def full_stats(flag, k, base, mid, w, qs, cs, ms):
    stat = jax.ShapeDtypeStruct((3 * H, F), F32)
    return pl.pallas_call(
        stats_body,
        grid=(H,),
        in_specs=[FLAG, head_spec(F), head_spec(F), whole_spec((S + 16, WIDTH)), head_spec(WIDTH)]
        + [head_spec(F)] * 7
        + [whole_spec((16, E))] * 3,
        out_specs=[head_spec(F)] + [whole_spec((3 * H, F))] * 3,
        out_shape=[jax.ShapeDtypeStruct((F, WIDTH), BF16), stat, stat, stat],
        scratch_shapes=[
            pltpu.VMEM((TILES, S, TILE_W), F32),
            pltpu.VMEM((400, E), F32),
            pltpu.VMEM((TILES, 3 * H, SPAN_F), F32),
        ],
        compiler_params=PARAMS,
        cost_estimate=pl.CostEstimate(flops=3_000_000_000, bytes_accessed=10_000_000, transcendentals=0),
        name="full_stats",
    )(flag, k, base, mid, w, *qs, *cs, *ms)


def first_body(
    flag, k, v, q0, q1a, q1b, q2, c0, c1, c2, m0, m1, m2, s0, s1, s2, up1, up2, down1, down2, glob, tail, bias
):
    head = pl.program_id(0)

    @pl.when(head == 0)
    def _():
        docs = [doc_row(ref) for ref in (m0, m1, m2)]
        full_mask(bias, docs, docs[0], 1)

        def triple(ref, base):
            peak, total, dots = (ref[base + j * H : base + (j + 1) * H, :] for j in range(3))
            return jnp.where(total > 0.0, peak, NEG), total, dots

        groups = (
            [triple(s0, 0), triple(up1, 0), triple(up2, 0)],
            [triple(s1, 0), triple(up1, 3 * H), triple(down1, 0)],
            [triple(s2, 0), triple(down1, 3 * H), triple(down2, 0)],
        )
        for n, group in enumerate(groups):
            cols = slice(n * F, (n + 1) * F)
            peak, total, dots = merge(group)
            inv = jnp.where(total > 0.0, 1.0 / total, 0.0)
            glob[0:H, cols] = peak
            glob[H : 2 * H, cols] = inv
            glob[2 * H : 3 * H, cols] = dots * inv

    queries = jnp.concatenate([q0[...], pick(flag, q1a, q1b, F), q2[...]], axis=0)
    cots = jnp.concatenate([c0[...], c1[...], c2[...]], axis=0)
    scores = dot_nt(k[...], queries) * LOG2 + bias[0, 0:16, :]
    probs = jnp.exp2(scores - glob[pl.ds(head, 1), 0:TILE_W]) * glob[pl.ds(H + head, 1), 0:TILE_W]
    rows = dot_nn(probs.astype(BF16), cots).astype(BF16).astype(F32)
    tail[...] = jnp.broadcast_to(rows[0:1] + rows[1:2], (8, E))


def full_first(flag, k, v, qs, cs, ms, stats):
    return pl.pallas_call(
        first_body,
        grid=(H,),
        in_specs=[FLAG, head_spec(16), head_spec(16)]
        + [head_spec(F)] * 3 + [head_spec(S)]
        + [head_spec(F)] * 2 + [head_spec(S)]
        + [whole_spec((16, E))] * 3
        + [whole_spec(s.shape) for s in stats],
        out_specs=[whole_spec((3 * H, SPAN_F)), head_spec(8)],
        out_shape=[
            jax.ShapeDtypeStruct((3 * H, SPAN_F), F32),
            jax.ShapeDtypeStruct((8, WIDTH), F32),
        ],
        scratch_shapes=[pltpu.VMEM((1, S, TILE_W), F32)],
        compiler_params=PARAMS,
        cost_estimate=pl.CostEstimate(flops=200_000_000, bytes_accessed=4_000_000, transcendentals=0),
        name="full_first",
    )(flag, k, v, *qs, *cs, *ms, *stats)


def grads_body(
    flag, k, v, q0, q1a, q1b, q2, c0, c1, c2, m0, m1, m2, glob,
    dk, dv, dq0, dq1, dq2, sums, link, bias, ext, kept,
):
    head = pl.program_id(0)

    @pl.when(head == 0)
    def _():
        docs = [doc_row(ref) for ref in (m0, m1, m2)]
        full_mask(bias, docs, docs[0], TILES)
        kept[...] = jnp.zeros((F, SPAN_F), BF16)
        ext[F:400, :] = jnp.zeros((400 - F, E), F32)

    queries = jnp.concatenate([q0[...], pick(flag, q1a, q1b, F), q2[...]], axis=0)
    cots = jnp.concatenate([c0[...], c1[...], c2[...]], axis=0)
    for t in range(TILES):
        lo = t * S
        cols = slice(lo, lo + TILE_W)
        scores = dot_nt(k[lo : lo + S, :], queries[cols]) * LOG2 + bias[t]
        probs = jnp.exp2(scores - glob[pl.ds(head, 1), cols]) * glob[pl.ds(H + head, 1), cols]
        dots = dot_nt(v[lo : lo + S, :], cots[cols])
        grads = (probs * (dots - glob[pl.ds(2 * H + head, 1), cols])).astype(BF16)
        kept[lo : lo + S, cols] = grads
        dk[lo : lo + S, :] = (dot_nn(grads, queries[cols]) * SCALE).astype(BF16)
        grad_v = dot_nn(probs.astype(BF16), cots[cols]).astype(BF16)
        dv[lo : lo + S, :] = grad_v
        ext[lo : lo + S, :] = grad_v.astype(F32)
    for n, out in enumerate((dq0, dq1, dq2)):
        part = dot_tn(kept[:, n * F : (n + 1) * F], k[...]) * SCALE
        out[...] = part.astype(out.dtype)
    total = ext[pl.ds(2, S, stride=3), :] + ext[pl.ds(3, S, stride=3), :] + ext[pl.ds(4, S, stride=3), :]
    sums[...] = total
    first = ext[0:1, :] + ext[1:2, :]
    link[0:S, :] = total.astype(BF16)
    link[S : S + 16, :] = jnp.where(iota((16, E), 0) == 15, first, 0.0).astype(BF16)


def full_grads(flag, k, v, qs, cs, ms, glob):
    return pl.pallas_call(
        grads_body,
        grid=(H,),
        in_specs=[FLAG, head_spec(F), head_spec(F)]
        + [head_spec(F)] * 7
        + [whole_spec((16, E))] * 3
        + [whole_spec(glob.shape)],
        out_specs=[head_spec(F)] * 5 + [head_spec(S), head_spec(S + 16)],
        out_shape=[
            jax.ShapeDtypeStruct((F, WIDTH), BF16),
            jax.ShapeDtypeStruct((F, WIDTH), BF16),
            jax.ShapeDtypeStruct((F, WIDTH), F32),
            jax.ShapeDtypeStruct((F, WIDTH), BF16),
            jax.ShapeDtypeStruct((F, WIDTH), BF16),
            jax.ShapeDtypeStruct((S, WIDTH), F32),
            jax.ShapeDtypeStruct((S + 16, WIDTH), BF16),
        ],
        scratch_shapes=[
            pltpu.VMEM((TILES, S, TILE_W), F32),
            pltpu.VMEM((400, E), F32),
            pltpu.VMEM((F, SPAN_F), BF16),
        ],
        compiler_params=PARAMS,
        cost_estimate=pl.CostEstimate(flops=8_000_000_000, bytes_accessed=14_000_000, transcendentals=0),
        name="full_grads",
    )(flag, k, v, *qs, *cs, *ms, glob)


def mid_cot_body(sums, tail, w, att, stat, out):
    total = sums[...] + jnp.where(iota((S, WIDTH), 0) == S - 1, tail[0:1, :], 0.0)
    grad = dot_nt(total.astype(BF16), w[...]).astype(BF16)
    out[0:S, :] = grad
    weighed = grad.astype(F32) * att[...]
    for h in range(H):
        cols = slice(h * E, (h + 1) * E)
        delta = jnp.sum(jnp.transpose(weighed[:, cols]), axis=0, keepdims=True)
        rows = [*split3(stat[0:1, cols]), *split3(stat[1:2, cols]), *split3(delta)]
        rows = [row.astype(F32) for row in rows] + [jnp.zeros((7, E), F32)]
        out[S : S + 16, cols] = jnp.concatenate(rows, axis=0).astype(BF16)


def mid_cotangent(sums, tail, w, att, stat):
    return pl.pallas_call(
        mid_cot_body,
        out_shape=jax.ShapeDtypeStruct((S + 16, WIDTH), BF16),
        compiler_params=PARAMS,
        cost_estimate=pl.CostEstimate(flops=600_000_000, bytes_accessed=4_000_000, transcendentals=0),
        name="mid_cotangent",
    )(sums, tail, w, att, stat)


def mid_bwd_body(flag, p4, p3, p2, first, second, p0, *refs):
    ms = refs[0:5]
    gs = refs[5:10]
    dq, dk, dv, back, fore = refs[10:]
    pays = pair_slabs(flag, p4, p3, p2, first, second, p0)

    @pl.when(pl.program_id(0) == 0)
    def _():
        mine = p0[2 * S : 2 * S + 16, :].astype(F32)[0:1]
        column = to_column(mine, S)
        causal = iota((S, S), 1) >= iota((S, S), 0)
        for n, pay in enumerate(pays):
            ok = to_column(pay[2 * S : 2 * S + 16].astype(F32)[0:1], S) == mine
            if n == REACH:
                ok = ok & causal
            back[n * S : (n + 1) * S, :] = jnp.where(ok, 0.0, NEG)
        for n, pay in enumerate(ms):
            ok = column == pay[S : S + 16, :].astype(F32)[0:1]
            if n == 0:
                ok = ok & causal
            fore[:, n * S : (n + 1) * S] = jnp.where(ok, 0.0, NEG)

    def stats(ref):
        rows = ref[S : S + 16, :].astype(F32)
        return [rows[j : j + 1] + rows[j + 1 : j + 2] + rows[j + 2 : j + 3] for j in (0, 3, 6)]

    k = p0[0:S, :]
    v = p0[S : 2 * S, :]
    keys = jnp.concatenate([pay[0:S] for pay in pays], axis=0)
    values = jnp.concatenate([pay[S : 2 * S] for pay in pays], axis=0)
    peak, inv, delta = stats(gs[0])
    scores = dot_nt(keys, ms[0][0:S, :]) * LOG2 + back[...]
    probs = jnp.exp2(scores - peak) * inv
    grads = (probs * (dot_nt(values, gs[0][0:S, :]) - delta)).astype(BF16)
    dq[...] = (dot_tn(grads, keys) * SCALE).astype(BF16)
    queries = jnp.concatenate([ref[0:S, :] for ref in ms], axis=0)
    cots = jnp.concatenate([ref[0:S, :] for ref in gs], axis=0)
    every = [stats(ref) for ref in gs]
    peak, inv, delta = (jnp.concatenate([one[j] for one in every], axis=1) for j in range(3))
    scores = dot_nt(k, queries) * LOG2 + fore[...]
    probs = jnp.exp2(scores - peak) * inv
    grads = (probs * (dot_nt(v, cots) - delta)).astype(BF16)
    dk[...] = (dot_nn(grads, queries) * SCALE).astype(BF16)
    dv[...] = dot_nn(probs.astype(BF16), cots).astype(BF16)


def mid_backward(flag, pays, ms, gs):
    return pl.pallas_call(
        mid_bwd_body,
        grid=(H,),
        in_specs=[FLAG] + PAY_SPECS + [head_spec(S + 16)] * 10,
        out_specs=[head_spec(S)] * 3,
        out_shape=[jax.ShapeDtypeStruct((S, WIDTH), BF16)] * 3,
        scratch_shapes=[pltpu.VMEM((SPAN_M, S), F32), pltpu.VMEM((S, SPAN_M), F32)],
        compiler_params=PARAMS,
        cost_estimate=pl.CostEstimate(flops=3_000_000_000, bytes_accessed=6_000_000, transcendentals=0),
        name="mid_backward",
    )(flag, *pays, *ms, *gs)


def shift(value, steps):
    count = lax.axis_size("ctx")
    first, last = max(0, -steps), min(count, count - steps)
    return lax.ppermute(value, "ctx", [(n, n + steps) for n in range(first, last)])


def swap(value, axis, bit):
    count = lax.axis_size(axis)
    return lax.ppermute(value, axis, [(n, n ^ bit) for n in range(count)])


def together(*values):
    return lax.optimization_barrier(values)


def block(value, index, rows):
    return lax.dynamic_slice_in_dim(value, index * rows, rows, 0)


def link_left(mid_ext, place):
    x = place // 16
    parts = [lax.dynamic_slice_in_dim(mid_ext, x * 256, 256, 1)]
    for bits in (1, 2, 3):
        parts.append(swap(lax.dynamic_slice_in_dim(mid_ext, (x ^ bits) * 256, 256, 1), "ctx", 16 * bits))
    return jnp.concatenate(parts, axis=0)


def link_term(left, sum_ext):
    right = jnp.concatenate([sum_ext] + [swap(sum_ext, "ctx", 16 * bits) for bits in (1, 2, 3)], axis=0)
    return dot_tn(left, right)


def link_sum(term, early, late, place):
    z = place // 2 % 8
    total = block(term, z, 32)
    for bits in range(1, 8):
        send = block(early if bits < 4 else late, z ^ bits, 32)
        total = total + swap(send, "ctx", 2 * bits).astype(F32)
    total = block(total, place % 2, 16) + swap(block(total, (place + 1) % 2, 16), "ctx", 1)
    parts = [swap(total, "dp", bits) for bits in (1, 2, 3)]
    return total + parts[0] + parts[1] + parts[2]


def shards(q_mid, k_mid, v_mid, doc_ids, q_full, k_full, v_base, w_link, cotangent):
    place = lax.axis_index("ctx")
    upper = place % 2 == 1
    flag = (place % 2).astype(jnp.int32).reshape(1)
    q_m, q_f, k_f, cot = q_mid[0], q_full[0], k_full[0], cotangent[0]
    ids = jnp.broadcast_to((doc_ids + 1).astype(BF16), (16, S))
    own_kv, own_q, swap_a = pack(flag, q_m, k_mid[0], v_mid[0], ids, q_f)

    kv2 = shift(own_kv, 2)
    got_a = swap(swap_a, "ctx", 1)
    qf2 = shift(q_f, -2)
    late_cot, qf2, got_a = together(cot, qf2, got_a)
    swap_b = jnp.concatenate([jnp.where(upper, kv2, qf2[:KV]), qf2[KV:]], axis=0)
    got_b = swap(swap_b, "ctx", 1)
    kv4 = shift(kv2, 2)
    kv2, kv4 = together(kv2, kv4)
    kv3 = swap(jnp.where(upper, kv4, kv2), "ctx", 1)
    cf2 = shift(late_cot, -2)
    cf1 = swap(jnp.where(upper, cot, cf2), "ctx", 1)
    own_q, cf2 = together(own_q, cf2)
    qm2 = shift(own_q, -2)

    pays = (kv4, kv3, kv2, got_a, got_b, own_kv)
    mid_ext, attended, mid_stat = mid_forward(flag, q_m, pays)

    qm1 = swap(jnp.where(upper, own_q, qm2), "ctx", 1)
    qm4 = shift(qm2, -2)
    qm3 = swap(jnp.where(upper, qm2, qm4), "ctx", 1)

    qs, cs, ms = (q_f, got_b, got_a, qf2), (cot, cf1, cf2), (ids, shift(ids, -1), shift(ids, -2))
    values, s0, s1, s2 = full_stats(flag, k_f, v_base[0], mid_ext, w_link, qs, cs, ms)
    up1 = shift(jnp.concatenate([s1, s2], axis=0), 1)
    up2 = shift(s2, 2)
    down1 = shift(jnp.concatenate([s0, s1], axis=0), -1)
    down2 = shift(s0, -2)
    left = link_left(mid_ext, place)
    values, qm1, qm4, left = together(values, qm1, qm4, left)
    glob, tail = full_first(flag, k_f, values, qs, cs, ms, (s0, s1, s2, up1, up2, down1, down2))
    next_tail = shift(tail, -1)
    dk_f, dv_f, dq0, dq1, dq2, sums, sum_ext = full_grads(flag, k_f, values, qs, cs, ms, glob)
    sums, qm3 = together(sums, qm3)

    cot_m = mid_cotangent(sums, next_tail, w_link, attended, mid_stat)
    cot_m, sum_ext, dq1 = together(cot_m, sum_ext, dq1)
    g2 = shift(cot_m, -2)
    g1 = swap(jnp.where(upper, cot_m, g2), "ctx", 1)
    g4 = shift(g2, -2)
    g3 = swap(jnp.where(upper, g2, g4), "ctx", 1)
    term = link_term(left, sum_ext)
    early, g1 = together(term.astype(BF16), g1)
    late, g3 = together(early, g3)
    dq_m, dk_m, dv_m = mid_backward(flag, pays, (own_q, qm1, qm2, qm3, qm4), (cot_m, g1, g2, g3, g4))

    near = swap(dq1, "ctx", 1).astype(F32)
    passed = jnp.where(upper, dq2.astype(F32), dq2.astype(F32) + near)
    far = shift(passed.astype(BF16), 2).astype(F32)
    dq_f = (dq0 + far + jnp.where(upper, near, 0.0)).astype(BF16)

    factor = float(lax.axis_size("dp") * lax.axis_size("ctx") * F) ** (-0.5)
    grad_link = link_sum(term, early, late, place) * factor
    return (dq_m[None], dk_m[None], dv_m[None], dq_f[None], dk_f[None], dv_f[None], grad_link)


def solution(mesh):
    rows = P("dp", "ctx", None)
    return jax.shard_map(
        shards,
        mesh=mesh,
        in_specs=(rows, rows, rows, P("dp", "ctx"), rows, rows, rows, P(), rows),
        out_specs=(rows,) * 6 + (P("ctx", None),),
        check_vma=False,
    )
```

time: 299 us -> 250 us (0.84)
  waiting for transfers between devices: 131 us -> 57.4 us
  starting transfers between devices: 88.2 us -> 104 us
  Pallas kernels: 40.7 us -> 50.1 us
  other arithmetic: 19.5 us -> 15.3 us
  local copies, waits for them, and re-layouts: 13.8 us -> 16.9 us
    ppermute x17 -> x26, waiting for transfers between devices: 68 us -> 15.7 us  [swap(): return lax.ppermute(value, axis, [(n, n ^ bit) for n in range(count)])]
    ppermute x17 -> x26, starting transfers between devices: 36 us -> 73.6 us  [swap(): return lax.ppermute(value, axis, [(n, n ^ bit) for n in range(count)])]
    ppermute x2 -> x0, waiting for transfers between devices: 17.8 us -> none  [the longest x1 12.3 us: link_gradient(): got = lax.ppermute(send, 'ctx', [(n, n ^ 16) for n in range(64)])]
    ppermute x2 -> x0, starting transfers between devices: 14.5 us -> none  [the longest x1 11.6 us: link_gradient(): got = lax.ppermute(send, 'ctx', [(n, n ^ 16) for n in range(64)])]
    pallas_call x4 -> x6, Pallas kernels: 39.8 us -> 49.1 us  [the longest x1 15.3 us: full_grads(): pl.pallas_call(grads_body, grid=(H,), in_specs=[FLAG, head_spec(F), head_...]
    ppermute x15 -> x16, starting transfers between devices: 37.6 us -> 30.4 us  [shift(): lax.ppermute(value, 'ctx', [(n, n + steps) for n in range(first, last)])]
    unnamed x72 -> x84, local copies, waits for them, and re-layouts: 12 us -> 16.8 us
    convert_element_type x5 -> x0, other arithmetic: 4.21 us -> none  [the longest x1 2.18 us: link_gradient(): send = jnp.where(is_outer, inner, outer).astype(BF16)]
  transfers between devices with their start and end apart: 34 -> 42, of which waited for: 13 -> 11; matrix products, arithmetic and copies ran while one was open for 4% -> 6% of each run, Pallas kernels for 11% -> 19%
where the time goes in v2:
time: 250 us; the launch traced here: 248 us
  starting transfers between devices  104 us (42%)
  waiting for transfers between devices  57.4 us (23%)
  Pallas kernels  50.1 us (20%)
  local copies, waits for them, and re-layouts  16.9 us (7%)
  other arithmetic  15.3 us (6%)
  matrix products  2.73 us (1%)
    ppermute x26, starting transfers between devices, swap(): return lax.ppermute(value, axis, [(n, n ^ bit) for n in range(count)])  73.6 us
    ppermute x16, waiting for transfers between devices, shift(): lax.ppermute(value, 'ctx', [(n, n + steps) for n in range(first, last)])  41.7 us
    ppermute x16, starting transfers between devices, shift(): lax.ppermute(value, 'ctx', [(n, n + steps) for n in range(first, last)])  30.4 us
    unnamed x84, local copies, waits for them, and re-layouts  16.8 us
    ppermute x26, waiting for transfers between devices, swap(): return lax.ppermute(value, axis, [(n, n ^ bit) for n in range(count)])  15.7 us
    pallas_call x1, Pallas kernels, full_grads(): pl.pallas_call(grads_body, grid=(H,), in_specs=[FLAG, head_spec(F), head_...  15.3 us
    pallas_call x1, Pallas kernels, full_stats(): pl.pallas_call(stats_body, grid=(H,), in_specs=[FLAG, head_spec(F), head_...  9.52 us
    pallas_call x1, Pallas kernels, mid_backward(): pl.pallas_call(mid_bwd_body, grid=(H,), in_specs=[FLAG] + PAY_SPECS + [he...  9.52 us
  transfers between devices with their start and end apart: 42, of which 11 were waited for; matrix products, arithmetic and copies ran while one was open for 6% of the time, Pallas kernels for 19%

profile of v2, /device:TPU:1, one launch (start us, length us, event | category | flops | bytes accessed | tf_op | source)
XLA Modules:
  0.0 247.6 jit_solution(5159219185618059762)
XLA Ops:
  10.7 4.2 %collective-permute-start = (bf16[288,1024]{1,0:T(8,128)(2,1)S(1)}, bf16[288,1024]{1,0:T(8,128)(2,1)S(1)}, u32[]{:S(2)}, u32[]{:S(2)}) collective-permute-start(bf16[288,1024]{1,0:T(8,128)(2,1)S(1)} %get-tuple-element.49.p0), channel_id=1, source_target_pairs={{0,2},{1,3},{2,4},{3,5},{4,6},{5,7},{6,8},{7,9},{8,10},{9,11},{10,... | collective-permute-start | bytes 1769480 | tf_op jit(solution)/shard_map/ppermute | solution.py:462
  15.8 10.4 %collective-permute-done.p2 = bf16[288,1024]{1,0:T(8,128)(2,1)S(1)} collective-permute-done((bf16[288,1024]{1,0:T(8,128)(2,1)S(1)}, bf16[288,1024]{1,0:T(8,128)(2,1)S(1)}, u32[]{:S(2)}, u32[]{:S(2)}) %collective-permute-start) | collective-permute-done | bytes 589856 | tf_op jit(solution)/shard_map/ppermute | solution.py:462
  26.2 4.1 %collective-permute-start.1 = (bf16[288,1024]{1,0:T(8,128)(2,1)S(1)}, bf16[288,1024]{1,0:T(8,128)(2,1)S(1)}, u32[]{:S(2)}, u32[]{:S(2)}) collective-permute-start(bf16[288,1024]{1,0:T(8,128)(2,1)S(1)} %collective-permute-done.p2), channel_id=1, source_target_pairs={{0,2},{1,3},{2,4},{3,5},{4,6},{5,7},{6,8},{7,9},{8,10},{9,11},{10,... | collective-permute-start | bytes 1769480 | tf_op jit(solution)/shard_map/ppermute | solution.py:462
  32.8 8.0 %collective-permute-done.1.p4 = bf16[288,1024]{1,0:T(8,128)(2,1)S(1)} collective-permute-done((bf16[288,1024]{1,0:T(8,128)(2,1)S(1)}, bf16[288,1024]{1,0:T(8,128)(2,1)S(1)}, u32[]{:S(2)}, u32[]{:S(2)}) %collective-permute-start.1) | collective-permute-done | bytes 589856 | tf_op jit(solution)/shard_map/ppermute | solution.py:462
  41.6 8.0 %collective-permute-done.6.c2 = bf16[384,1024]{1,0:T(8,128)(2,1)} collective-permute-done((bf16[384,1024]{1,0:T(8,128)(2,1)S(1)}, bf16[384,1024]{1,0:T(8,128)(2,1)}, u32[]{:S(2)}, u32[]{:S(2)}) %collective-permute-start.6) | collective-permute-done | bytes 786464 | tf_op jit(solution)/shard_map/ppermute | solution.py:462
  53.1 5.4 %collective-permute-done.10.refs_2_ = bf16[144,1024]{1,0:T(8,128)(2,1)} collective-permute-done((bf16[144,1024]{1,0:T(8,128)(2,1)S(1)}, bf16[144,1024]{1,0:T(8,128)(2,1)}, u32[]{:S(2)}, u32[]{:S(2)}) %collective-permute-start.10) | collective-permute-done | bytes 294944 | tf_op jit(solution)/shard_map/ppermute | solution.py:462
  64.5 7.4 %mid_forward.1 = (bf16[144,1024]{1,0:T(8,128)(2,1)S(1)}, f32[128,1024]{1,0:T(8,128)S(1)}, f32[8,1024]{1,0:T(8,128)S(1)}) custom-call(s32[1]{0:T(128)} %bitcast.flag, bf16[128,1024]{1,0:T(8,128)(2,1)S(1)} %bitcast.29, bf16[288,1024]{1,0:T(8,128)(2,1)S(1)} %collective-permute-done.1.p4, bf16[288,1024]{1,0:T(8,128)(2,1)} %collective-permute-done.2.p3, ...), custom_call_target="tpu_custom_call" | custom-call | flops 700000000 | bytes 4000000 | tf_op jit(solution)/shard_map/mid_forward/pallas_call | solution.py:143
  72.0 15.0 %collective-permute-start.13 = (bf16[144,256]{1,0:T(8,128)(2,1)S(1)}, bf16[144,256]{1,0:T(8,128)(2,1)S(1)}, u32[]{:S(2)}, u32[]{:S(2)}) collective-permute-start(bf16[144,256]{1,0:T(8,128)(2,1)S(1)} %get-tuple-element.105), channel_id=1, source_target_pairs={{0,16},{1,17},{2,18},{3,19},{4,20},{5,21},{6,22},{7,23},{8,24},{9,... | collective-permute-start | bytes 221192 | tf_op jit(solution)/shard_map/ppermute | solution.py:467
  87.0 2.7 %collective-permute-start.14 = (bf16[144,256]{1,0:T(8,128)(2,1)S(1)}, bf16[144,256]{1,0:T(8,128)(2,1)S(1)}, u32[]{:S(2)}, u32[]{:S(2)}) collective-permute-start(bf16[144,256]{1,0:T(8,128)(2,1)S(1)} %get-tuple-element.104), channel_id=1, source_target_pairs={{0,32},{1,33},{2,34},{3,35},{4,36},{5,37},{6,38},{7,39},{8,40},{9,... | collective-permute-start | bytes 221192 | tf_op jit(solution)/shard_map/ppermute | solution.py:467
  92.5 9.5 %full_stats.1 = (bf16[384,1024]{1,0:T(8,128)(2,1)S(1)}, f32[24,384]{1,0:T(8,128)S(1)}, f32[24,384]{1,0:T(8,128)S(1)}, f32[24,384]{1,0:T(8,128)S(1)}) custom-call(s32[1]{0:T(128)} %bitcast.flag, bf16[384,1024]{1,0:T(8,128)(2,1)S(1)} %bitcast.30, bf16[384,1024]{1,0:T(8,128)(2,1)S(1)} %bitcast.35, bf16[144,1024]{1,0:T(8,128)(2,1)S(1)} %get-tuple-element.58.mid, ...), custom_call_target="tpu_custom_call" | custom-call | flops 3000000000 | bytes 10000000 | tf_op jit(solution)/shard_map/full_stats/pallas_call | solution.py:235
  102.0 3.4 %collective-permute-start.17 = (f32[24,384]{1,0:T(8,128)S(1)}, f32[24,384]{1,0:T(8,128)S(1)}, u32[]{:S(2)}, u32[]{:S(2)}) collective-permute-start(f32[24,384]{1,0:T(8,128)S(1)} %get-tuple-element.65.s2), channel_id=1, source_target_pairs={{0,2},{1,3},{2,4},{3,5},{4,6},{5,7},{6,8},{7,9},{8,10},{9,11},{10,... | collective-permute-start | bytes 110600 | tf_op jit(solution)/shard_map/ppermute | solution.py:462
  110.8 3.8 %collective-permute-start.20 = (bf16[144,1024]{1,0:T(8,128)(2,1)S(1)}, bf16[144,1024]{1,0:T(8,128)(2,1)S(1)}, u32[]{:S(2)}, u32[]{:S(2)}) collective-permute-start(bf16[144,1024]{1,0:T(8,128)(2,1)S(1)} %get-tuple-element.100), channel_id=1, source_target_pairs={{0,1},{1,0},{2,3},{3,2},{4,5},{5,4},{6,7},{7,6},{8,9},{9,8},{10,11... | collective-permute-start | bytes 884744 | tf_op jit(solution)/shard_map/ppermute | solution.py:467
  115.6 6.2 %full_first.1 = (f32[24,1152]{1,0:T(8,128)S(1)}, f32[8,1024]{1,0:T(8,128)S(1)}) custom-call(s32[1]{0:T(128)} %bitcast.flag, bf16[384,1024]{1,0:T(8,128)(2,1)S(1)} %bitcast.31, bf16[384,1024]{1,0:T(8,128)(2,1)S(1)} %get-tuple-element.62.v, bf16[384,1024]{1,0:T(8,128)(2,1)S(1)} %bitcast.26, bf16[384,1024]{1,0:T(8,128)(2,1)S(1)} %collective-permute-done.5.second.q1a, ...), custom_call_target="tpu_custom_call" | custom-call | flops 200000000 | bytes 4000000 | tf_op jit(solution)/shard_map/full_first/pallas_call | solution.py:290
  123.1 15.3 %full_grads.1 = (bf16[384,1024]{1,0:T(8,128)(2,1)}, bf16[384,1024]{1,0:T(8,128)(2,1)}, f32[384,1024]{1,0:T(8,128)}, bf16[384,1024]{1,0:T(8,128)(2,1)}, bf16[384,...) custom-call(s32[1]{0:T(128)} %bitcast.flag, bf16[384,1024]{1,0:T(8,128)(2,1)S(1)} %bitcast.32, ...), custom_call_target="tpu_custom_call" | custom-call | flops 8000000000 | bytes 14000000 | tf_op jit(solution)/shard_map/full_grads/pallas_call | solution.py:348
  141.9 8.8 %collective-permute-done.25.refs_7_ = bf16[144,1024]{1,0:T(8,128)(2,1)S(1)} collective-permute-done((bf16[144,1024]{1,0:T(8,128)(2,1)S(1)}, bf16[144,1024]{1,0:T(8,128)(2,1)S(1)}, u32[]{:S(2)}, u32[]{:S(2)}) %collective-permute-start.25) | collective-permute-done | bytes 294944 | tf_op jit(solution)/shard_map/ppermute | solution.py:462
  152.0 8.9 %collective-permute-start.22 = (bf16[144,1024]{1,0:T(8,128)(2,1)S(1)}, bf16[144,1024]{1,0:T(8,128)(2,1)}, u32[]{:S(2)}, u32[]{:S(2)}) collective-permute-start(bf16[144,1024]{1,0:T(8,128)(2,1)S(1)} %get-tuple-element.78), channel_id=1, source_target_pairs={{0,16},{1,17},{2,18},{3,19},{4,20},{5,21},{6,22},{7,23},{8,24},{9,... | collective-permute-start | bytes 884744 | tf_op jit(solution)/shard_map/ppermute | solution.py:467
  161.0 4.0 %collective-permute-start.23 = (bf16[144,1024]{1,0:T(8,128)(2,1)S(1)}, bf16[144,1024]{1,0:T(8,128)(2,1)}, u32[]{:S(2)}, u32[]{:S(2)}) collective-permute-start(bf16[144,1024]{1,0:T(8,128)(2,1)S(1)} %get-tuple-element.78), channel_id=1, source_target_pairs={{0,32},{1,33},{2,34},{3,35},{4,36},{5,37},{6,38},{7,39},{8,40},{9,... | collective-permute-start | bytes 884744 | tf_op jit(solution)/shard_map/ppermute | solution.py:467
  167.6 4.8 %collective-permute-done.23 = bf16[144,1024]{1,0:T(8,128)(2,1)} collective-permute-done((bf16[144,1024]{1,0:T(8,128)(2,1)S(1)}, bf16[144,1024]{1,0:T(8,128)(2,1)}, u32[]{:S(2)}, u32[]{:S(2)}) %collective-permute-start.23) | collective-permute-done | bytes 294944 | tf_op jit(solution)/shard_map/ppermute | solution.py:467
  178.0 3.4 %collective-permute-start.33 = (bf16[32,1024]{1,0:T(8,128)(2,1)S(1)}, bf16[32,1024]{1,0:T(8,128)(2,1)}, u32[]{:S(2)}, u32[]{:S(2)}) collective-permute-start(bf16[32,1024]{1,0:T(8,128)(2,1)S(1)} %get-tuple-element.92), channel_id=1, source_target_pairs={{0,6},{1,7},{2,4},{3,5},{4,2},{5,3},{6,0},{7,1},{8,14},{9,15},{10,... | collective-permute-start | bytes 196616 | tf_op jit(solution)/shard_map/ppermute | solution.py:467
  181.4 4.0 %collective-permute-done.28.refs_8_ = bf16[144,1024]{1,0:T(8,128)(2,1)S(1)} collective-permute-done((bf16[144,1024]{1,0:T(8,128)(2,1)}, bf16[144,1024]{1,0:T(8,128)(2,1)S(1)}, u32[]{:S(2)}, u32[]{:S(2)}) %collective-permute-start.28) | collective-permute-done | bytes 294944 | tf_op jit(solution)/shard_map/ppermute | solution.py:467
  187.3 2.7 %collective-permute-start.35 = (bf16[32,1024]{1,0:T(8,128)(2,1)S(1)}, bf16[32,1024]{1,0:T(8,128)(2,1)S(1)}, u32[]{:S(2)}, u32[]{:S(2)}) collective-permute-start(bf16[32,1024]{1,0:T(8,128)(2,1)S(1)} %get-tuple-element.97), channel_id=1, source_target_pairs={{0,10},{1,11},{2,8},{3,9},{4,14},{5,15},{6,12},{7,13},{8,2},{9,3},... | collective-permute-start | bytes 196616 | tf_op jit(solution)/shard_map/ppermute | solution.py:467
  190.1 8.2 %collective-permute-start.36 = (bf16[32,1024]{1,0:T(8,128)(2,1)S(1)}, bf16[32,1024]{1,0:T(8,128)(2,1)S(1)}, u32[]{:S(2)}, u32[]{:S(2)}) collective-permute-start(bf16[32,1024]{1,0:T(8,128)(2,1)S(1)} %get-tuple-element.96), channel_id=1, source_target_pairs={{0,12},{1,13},{2,14},{3,15},{4,8},{5,9},{6,10},{7,11},{8,4},{9,5},... | collective-permute-start | bytes 196616 | tf_op jit(solution)/shard_map/ppermute | solution.py:467
  210.2 14.4 %collective-permute-start.39 = (f32[16,1024]{1,0:T(8,128)S(1)}, f32[16,1024]{1,0:T(8,128)S(1)}, u32[]{:S(2)}, u32[]{:S(2)}) collective-permute-start(f32[16,1024]{1,0:T(8,128)S(1)} %dynamic-slice_add_fusion), channel_id=1, source_target_pairs={{0,64},{64,0},{128,192},{192,128},{1,65},{65,1},{129,193},{193,129... | collective-permute-start | bytes 196616 | tf_op jit(solution)/shard_map/ppermute | solution.py:467
  234.7 9.5 %mid_backward.1 = (bf16[128,1024]{1,0:T(8,128)(2,1)}, bf16[128,1024]{1,0:T(8,128)(2,1)}, bf16[128,1024]{1,0:T(8,128)(2,1)}) custom-call(s32[1]{0:T(128)} %bitcast.flag, bf16[288,1024]{1,0:T(8,128)(2,1)S(1)} %collective-permute-done.1.p4, bf16[288,1024]{1,0:T(8,128)(2,1)} %collective-permute-done.2.p3, bf16[288,1024]{1,0:T(8,128)(2,1)S(1)} %collective-permute-done.p2, ...), custom_call_target="tpu_custom_call" | custom-call | flops 3000000000 | bytes 6000000 | tf_op jit(solution)/shard_map/mid_backward/pallas_call | solution.py:446
  (172 shorter events, 74.0 us)
Async XLA Ops:
  7.3 23.0 %collective-permute-start.4 = (bf16[384,1024]{1,0:T(8,128)(2,1)S(1)}, bf16[384,1024]{1,0:T(8,128)(2,1)S(1)}, u32[]{:S(2)}, u32[]{:S(2)}) collective-permute-start(bf16[384,1024]{1,0:T(8,128)(2,1)S(1)} %get-tuple-element.52), channel_id=1, source_target_pairs={{0,1},{1,0},{2,3},{3,2},{4,5},{5,4},{6,7},{7,6},{8,9},{9,8},{10,11... | collective-permute-start | bytes 2359304 | tf_op jit(solution)/shard_map/ppermute | solution.py:467
  9.4 21.0 %collective-permute-start.3 = (bf16[384,1024]{1,0:T(8,128)(2,1)S(1)}, bf16[384,1024]{1,0:T(8,128)(2,1)S(1)}, u32[]{:S(2)}, u32[]{:S(2)}) collective-permute-start(bf16[384,1024]{1,0:T(8,128)(2,1)S(1)} %bitcast.24), channel_id=1, source_target_pairs={{2,0},{3,1},{4,2},{5,3},{6,4},{7,5},{8,6},{9,7},{10,8},{11,9},{12,... | collective-permute-start | bytes 2359304 | tf_op jit(solution)/shard_map/ppermute | solution.py:462
  10.7 15.5 %collective-permute-start = (bf16[288,1024]{1,0:T(8,128)(2,1)S(1)}, bf16[288,1024]{1,0:T(8,128)(2,1)S(1)}, u32[]{:S(2)}, u32[]{:S(2)}) collective-permute-start(bf16[288,1024]{1,0:T(8,128)(2,1)S(1)} %get-tuple-element.49.p0), channel_id=1, source_target_pairs={{0,2},{1,3},{2,4},{3,5},{4,6},{5,7},{6,8},{7,9},{8,10},{9,11},{10,... | collective-permute-start | bytes 1769480 | tf_op jit(solution)/shard_map/ppermute | solution.py:462
  30.4 19.3 %collective-permute-start.6 = (bf16[384,1024]{1,0:T(8,128)(2,1)S(1)}, bf16[384,1024]{1,0:T(8,128)(2,1)}, u32[]{:S(2)}, u32[]{:S(2)}) collective-permute-start(bf16[384,1024]{1,0:T(8,128)(2,1)S(1)} %bitcast.21), channel_id=1, source_target_pairs={{2,0},{3,1},{4,2},{5,3},{6,4},{7,5},{8,6},{9,7},{10,8},{11,9},{12,... | collective-permute-start | bytes 2359304 | tf_op jit(solution)/shard_map/ppermute | solution.py:462
  32.8 28.4 %collective-permute-start.5 = (bf16[384,1024]{1,0:T(8,128)(2,1)}, bf16[384,1024]{1,0:T(8,128)(2,1)S(1)}, u32[]{:S(2)}, u32[]{:S(2)}) collective-permute-start(bf16[384,1024]{1,0:T(8,128)(2,1)} %pad_maximum_fusion), channel_id=1, source_target_pairs={{0,1},{1,0},{2,3},{3,2},{4,5},{5,4},{6,7},{7,6},{8,9},{9,8},{10,11... | collective-permute-start | bytes 2359304 | tf_op jit(solution)/shard_map/ppermute | solution.py:467
  41.6 20.8 %collective-permute-start.2 = (bf16[288,1024]{1,0:T(8,128)(2,1)}, bf16[288,1024]{1,0:T(8,128)(2,1)}, u32[]{:S(2)}, u32[]{:S(2)}) collective-permute-start(bf16[288,1024]{1,0:T(8,128)(2,1)} %broadcast_select_fusion.1), channel_id=1, source_target_pairs={{0,1},{1,0},{2,3},{3,2},{4,5},{5,4},{6,7},{7,6},{8,9},{9,8},{10,11... | collective-permute-start | bytes 1769480 | tf_op jit(solution)/shard_map/ppermute | solution.py:467
  53.1 39.4 %collective-permute-start.7 = (bf16[384,1024]{1,0:T(8,128)(2,1)}, bf16[384,1024]{1,0:T(8,128)(2,1)}, u32[]{:S(2)}, u32[]{:S(2)}) collective-permute-start(bf16[384,1024]{1,0:T(8,128)(2,1)} %broadcast_select_fusion), channel_id=1, source_target_pairs={{0,1},{1,0},{2,3},{3,2},{4,5},{5,4},{6,7},{7,6},{8,9},{9,8},{10,11... | collective-permute-start | bytes 2359304 | tf_op jit(solution)/shard_map/ppermute | solution.py:467
  58.5 28.5 %collective-permute-start.12 = (bf16[144,1024]{1,0:T(8,128)(2,1)}, bf16[144,1024]{1,0:T(8,128)(2,1)}, u32[]{:S(2)}, u32[]{:S(2)}) collective-permute-start(bf16[144,1024]{1,0:T(8,128)(2,1)} %collective-permute-done.10.refs_2_), channel_id=1, source_target_pairs={{2,0},{3,1},{4,2},{5,3},{6,4},{7,5},{8,6},{9,7},{10,8},{11,9},{12,... | collective-permute-start | bytes 884744 | tf_op jit(solution)/shard_map/ppermute | solution.py:462
  59.8 31.1 %collective-permute-start.8 = (bf16[16,128]{1,0:T(8,128)(2,1)S(1)}, bf16[16,128]{1,0:T(8,128)(2,1)S(1)}, u32[]{:S(2)}, u32[]{:S(2)}) collective-permute-start(bf16[16,128]{1,0:T(8,128)(2,1)S(1)} %broadcast_in_dim.30.ids.m0), channel_id=1, source_target_pairs={{1,0},{2,1},{3,2},{4,3},{5,4},{6,5},{7,6},{8,7},{9,8},{10,9},{11,1... | collective-permute-start | bytes 12296 | tf_op jit(solution)/shard_map/ppermute | solution.py:462
  61.2 30.8 %collective-permute-start.9 = (bf16[16,128]{1,0:T(8,128)(2,1)S(1)}, bf16[16,128]{1,0:T(8,128)(2,1)S(1)}, u32[]{:S(2)}, u32[]{:S(2)}) collective-permute-start(bf16[16,128]{1,0:T(8,128)(2,1)S(1)} %broadcast_in_dim.30.ids.m0), channel_id=1, source_target_pairs={{2,0},{3,1},{4,2},{5,3},{6,4},{7,5},{8,6},{9,7},{10,8},{11,9},{12,... | collective-permute-start | bytes 12296 | tf_op jit(solution)/shard_map/ppermute | solution.py:462
  72.0 33.4 %collective-permute-start.13 = (bf16[144,256]{1,0:T(8,128)(2,1)S(1)}, bf16[144,256]{1,0:T(8,128)(2,1)S(1)}, u32[]{:S(2)}, u32[]{:S(2)}) collective-permute-start(bf16[144,256]{1,0:T(8,128)(2,1)S(1)} %get-tuple-element.105), channel_id=1, source_target_pairs={{0,16},{1,17},{2,18},{3,19},{4,20},{5,21},{6,22},{7,23},{8,24},{9,... | collective-permute-start | bytes 221192 | tf_op jit(solution)/shard_map/ppermute | solution.py:467
  87.0 19.7 %collective-permute-start.14 = (bf16[144,256]{1,0:T(8,128)(2,1)S(1)}, bf16[144,256]{1,0:T(8,128)(2,1)S(1)}, u32[]{:S(2)}, u32[]{:S(2)}) collective-permute-start(bf16[144,256]{1,0:T(8,128)(2,1)S(1)} %get-tuple-element.104), channel_id=1, source_target_pairs={{0,32},{1,33},{2,34},{3,35},{4,36},{5,37},{6,38},{7,39},{8,40},{9,... | collective-permute-start | bytes 221192 | tf_op jit(solution)/shard_map/ppermute | solution.py:467
  90.9 17.9 %collective-permute-start.15 = (bf16[144,256]{1,0:T(8,128)(2,1)S(1)}, bf16[144,256]{1,0:T(8,128)(2,1)S(1)}, u32[]{:S(2)}, u32[]{:S(2)}) collective-permute-start(bf16[144,256]{1,0:T(8,128)(2,1)S(1)} %get-tuple-element.103), channel_id=1, source_target_pairs={{0,48},{1,49},{2,50},{3,51},{4,52},{5,53},{6,54},{7,55},{8,56},{9,... | collective-permute-start | bytes 221192 | tf_op jit(solution)/shard_map/ppermute | solution.py:467
  91.9 18.9 %collective-permute-start.11 = (bf16[144,1024]{1,0:T(8,128)(2,1)S(1)}, bf16[144,1024]{1,0:T(8,128)(2,1)S(1)}, u32[]{:S(2)}, u32[]{:S(2)}) collective-permute-start(bf16[144,1024]{1,0:T(8,128)(2,1)S(1)} %get-tuple-element.101), channel_id=1, source_target_pairs={{0,1},{1,0},{2,3},{3,2},{4,5},{5,4},{6,7},{7,6},{8,9},{9,8},{10,11... | collective-permute-start | bytes 884744 | tf_op jit(solution)/shard_map/ppermute | solution.py:467
  110.8 28.5 %collective-permute-start.20 = (bf16[144,1024]{1,0:T(8,128)(2,1)S(1)}, bf16[144,1024]{1,0:T(8,128)(2,1)S(1)}, u32[]{:S(2)}, u32[]{:S(2)}) collective-permute-start(bf16[144,1024]{1,0:T(8,128)(2,1)S(1)} %get-tuple-element.100), channel_id=1, source_target_pairs={{0,1},{1,0},{2,3},{3,2},{4,5},{5,4},{6,7},{7,6},{8,9},{9,8},{10,11... | collective-permute-start | bytes 884744 | tf_op jit(solution)/shard_map/ppermute | solution.py:467
  121.8 17.5 %collective-permute-start.21 = (f32[8,1024]{1,0:T(8,128)S(1)}, f32[8,1024]{1,0:T(8,128)S(1)}, u32[]{:S(2)}, u32[]{:S(2)}) collective-permute-start(f32[8,1024]{1,0:T(8,128)S(1)} %get-tuple-element.71), channel_id=1, source_target_pairs={{1,0},{2,1},{3,2},{4,3},{5,4},{6,5},{7,6},{8,7},{9,8},{10,9},{11,1... | collective-permute-start | bytes 98312 | tf_op jit(solution)/shard_map/ppermute | solution.py:462
  152.0 15.3 %collective-permute-start.22 = (bf16[144,1024]{1,0:T(8,128)(2,1)S(1)}, bf16[144,1024]{1,0:T(8,128)(2,1)}, u32[]{:S(2)}, u32[]{:S(2)}) collective-permute-start(bf16[144,1024]{1,0:T(8,128)(2,1)S(1)} %get-tuple-element.78), channel_id=1, source_target_pairs={{0,16},{1,17},{2,18},{3,19},{4,20},{5,21},{6,22},{7,23},{8,24},{9,... | collective-permute-start | bytes 884744 | tf_op jit(solution)/shard_map/ppermute | solution.py:467
  166.2 38.7 %collective-permute-start.29 = (bf16[384,1024]{1,0:T(8,128)(2,1)}, bf16[384,1024]{1,0:T(8,128)(2,1)}, u32[]{:S(2)}, u32[]{:S(2)}) collective-permute-start(bf16[384,1024]{1,0:T(8,128)(2,1)} %get-tuple-element.87), channel_id=1, source_target_pairs={{0,1},{1,0},{2,3},{3,2},{4,5},{5,4},{6,7},{7,6},{8,9},{9,8},{10,11... | collective-permute-start | bytes 2359304 | tf_op jit(solution)/shard_map/ppermute | solution.py:467
  167.3 18.0 %collective-permute-start.28 = (bf16[144,1024]{1,0:T(8,128)(2,1)}, bf16[144,1024]{1,0:T(8,128)(2,1)S(1)}, u32[]{:S(2)}, u32[]{:S(2)}) collective-permute-start(bf16[144,1024]{1,0:T(8,128)(2,1)} %get-tuple-element.98), channel_id=1, source_target_pairs={{0,1},{1,0},{2,3},{3,2},{4,5},{5,4},{6,7},{7,6},{8,9},{9,8},{10,11... | collective-permute-start | bytes 884744 | tf_op jit(solution)/shard_map/ppermute | solution.py:467
  178.0 20.3 %collective-permute-start.33 = (bf16[32,1024]{1,0:T(8,128)(2,1)S(1)}, bf16[32,1024]{1,0:T(8,128)(2,1)}, u32[]{:S(2)}, u32[]{:S(2)}) collective-permute-start(bf16[32,1024]{1,0:T(8,128)(2,1)S(1)} %get-tuple-element.92), channel_id=1, source_target_pairs={{0,6},{1,7},{2,4},{3,5},{4,2},{5,3},{6,0},{7,1},{8,14},{9,15},{10,... | collective-permute-start | bytes 196616 | tf_op jit(solution)/shard_map/ppermute | solution.py:467
  207.2 37.7 %collective-permute-start.30 = (bf16[384,1024]{1,0:T(8,128)(2,1)}, bf16[384,1024]{1,0:T(8,128)(2,1)}, u32[]{:S(2)}, u32[]{:S(2)}) collective-permute-start(bf16[384,1024]{1,0:T(8,128)(2,1)} %fusion.2), channel_id=1, source_target_pairs={{0,2},{1,3},{2,4},{3,5},{4,6},{5,7},{6,8},{7,9},{8,10},{9,11},{10,... | collective-permute-start | bytes 2359304 | tf_op jit(solution)/shard_map/ppermute | solution.py:462
  210.2 34.0 %collective-permute-start.39 = (f32[16,1024]{1,0:T(8,128)S(1)}, f32[16,1024]{1,0:T(8,128)S(1)}, u32[]{:S(2)}, u32[]{:S(2)}) collective-permute-start(f32[16,1024]{1,0:T(8,128)S(1)} %dynamic-slice_add_fusion), channel_id=1, source_target_pairs={{0,64},{64,0},{128,192},{192,128},{1,65},{65,1},{129,193},{193,129... | collective-permute-start | bytes 196616 | tf_op jit(solution)/shard_map/ppermute | solution.py:467
  224.6 19.6 %collective-permute-start.40 = (f32[16,1024]{1,0:T(8,128)S(1)}, f32[16,1024]{1,0:T(8,128)S(1)}, u32[]{:S(2)}, u32[]{:S(2)}) collective-permute-start(f32[16,1024]{1,0:T(8,128)S(1)} %dynamic-slice_add_fusion), channel_id=1, source_target_pairs={{0,128},{64,192},{128,0},{192,64},{1,129},{65,193},{129,1},{193,65... | collective-permute-start | bytes 196616 | tf_op jit(solution)/shard_map/ppermute | solution.py:467
  227.3 17.0 %collective-permute-start.41 = (f32[16,1024]{1,0:T(8,128)S(1)}, f32[16,1024]{1,0:T(8,128)S(1)}, u32[]{:S(2)}, u32[]{:S(2)}) collective-permute-start(f32[16,1024]{1,0:T(8,128)S(1)} %dynamic-slice_add_fusion), channel_id=1, source_target_pairs={{0,192},{64,128},{128,64},{192,0},{1,193},{65,129},{129,65},{193,1... | collective-permute-start | bytes 196616 | tf_op jit(solution)/shard_map/ppermute | solution.py:467
  (60 other events, 761.0 us)

commit v3 on v2

--- a/solution.py
+++ b/solution.py
@@ -25,7 +25,7 @@
 NEG = -1e30
 F32 = jnp.float32
 BF16 = jnp.bfloat16
-PARAMS = pltpu.CompilerParams(vmem_limit_bytes=48 * 1024 * 1024)
+PARAMS = pltpu.CompilerParams(vmem_limit_bytes=16 * 1024 * 1024)
 
 
 def dot_nn(a, b):
@@ -88,7 +88,7 @@
             jax.ShapeDtypeStruct((S + 16, WIDTH), BF16),
             jax.ShapeDtypeStruct((F, WIDTH), BF16),
         ],
-        compiler_params=PARAMS,
+        compiler_params=pltpu.CompilerParams(vmem_limit_bytes=60 * 1024 * 1024),
         name="pack",
     )(flag, q, k, v, ids, qf)
 
@@ -476,27 +476,21 @@
 
 
 def link_left(mid_ext, place):
-    x = place // 16
-    parts = [lax.dynamic_slice_in_dim(mid_ext, x * 256, 256, 1)]
-    for bits in (1, 2, 3):
-        parts.append(swap(lax.dynamic_slice_in_dim(mid_ext, (x ^ bits) * 256, 256, 1), "ctx", 16 * bits))
-    return jnp.concatenate(parts, axis=0)
+    groups = [[first + 16 * n for n in range(4)] for first in range(16)]
+    every = lax.all_gather(mid_ext, "ctx", axis_index_groups=groups, tiled=True)
+    return lax.dynamic_slice_in_dim(every, place // 16 * 256, 256, 1)
 
 
 def link_term(left, sum_ext):
-    right = jnp.concatenate([sum_ext] + [swap(sum_ext, "ctx", 16 * bits) for bits in (1, 2, 3)], axis=0)
+    groups = [[first + 16 * n for n in range(4)] for first in range(16)]
+    right = lax.all_gather(sum_ext, "ctx", axis_index_groups=groups, tiled=True)
     return dot_tn(left, right)
 
 
-def link_sum(term, early, late, place):
-    z = place // 2 % 8
-    total = block(term, z, 32)
-    for bits in range(1, 8):
-        send = block(early if bits < 4 else late, z ^ bits, 32)
-        total = total + swap(send, "ctx", 2 * bits).astype(F32)
-    total = block(total, place % 2, 16) + swap(block(total, (place + 1) % 2, 16), "ctx", 1)
-    parts = [swap(total, "dp", bits) for bits in (1, 2, 3)]
-    return total + parts[0] + parts[1] + parts[2]
+def link_sum(term):
+    groups = [[16 * first + n for n in range(16)] for first in range(4)]
+    rows = lax.psum_scatter(term, "ctx", scatter_dimension=0, axis_index_groups=groups, tiled=True)
+    return lax.psum(rows, "dp")
 
 
 def shards(q_mid, k_mid, v_mid, doc_ids, q_full, k_full, v_base, w_link, cotangent):
@@ -542,14 +536,12 @@
     sums, qm3 = together(sums, qm3)
 
     cot_m = mid_cotangent(sums, next_tail, w_link, attended, mid_stat)
-    cot_m, sum_ext, dq1 = together(cot_m, sum_ext, dq1)
+    cot_m, dq1 = together(cot_m, dq1)
     g2 = shift(cot_m, -2)
     g1 = swap(jnp.where(upper, cot_m, g2), "ctx", 1)
     g4 = shift(g2, -2)
     g3 = swap(jnp.where(upper, g2, g4), "ctx", 1)
     term = link_term(left, sum_ext)
-    early, g1 = together(term.astype(BF16), g1)
-    late, g3 = together(early, g3)
     dq_m, dk_m, dv_m = mid_backward(flag, pays, (own_q, qm1, qm2, qm3, qm4), (cot_m, g1, g2, g3, g4))
 
     near = swap(dq1, "ctx", 1).astype(F32)
@@ -558,7 +550,7 @@
     dq_f = (dq0 + far + jnp.where(upper, near, 0.0)).astype(BF16)
 
     factor = float(lax.axis_size("dp") * lax.axis_size("ctx") * F) ** (-0.5)
-    grad_link = link_sum(term, early, late, place) * factor
+    grad_link = link_sum(term) * factor
     return (dq_m[None], dk_m[None], dv_m[None], dq_f[None], dk_f[None], dv_f[None], grad_link)
 
 

time: 250 us -> 344 us (1.38)
  waiting for transfers between devices: 57.4 us -> 183 us
  starting transfers between devices: 104 us -> 47.3 us
  between operations: 1.27 us -> 14.2 us
  local copies, waits for them, and re-layouts: 16.9 us -> 27.1 us
  Pallas kernels: 50.1 us -> 56 us
    ppermute x26 -> x9, starting transfers between devices: 73.6 us -> 9.11 us  [swap(): return lax.ppermute(value, axis, [(n, n ^ bit) for n in range(count)])]
    psum x0 -> x1, waiting for transfers between devices: none -> 51.1 us  [link_sum(): return lax.psum(rows, 'dp')]
    all_gather x0 -> x2, waiting for transfers between devices: none -> 43.1 us  [the longest x1 43.1 us: link_term(): right = lax.all_gather(sum_ext, 'ctx', axis_index_groups=groups, tiled=True)]
    ppermute x26 -> x9, waiting for transfers between devices: 15.7 us -> 46.5 us  [swap(): return lax.ppermute(value, axis, [(n, n ^ bit) for n in range(count)])]
    unnamed x84 -> x80, local copies, waits for them, and re-layouts: 16.8 us -> 24.8 us
    ppermute x16, starting transfers between devices: 30.4 us -> 38 us  [shift(): lax.ppermute(value, 'ctx', [(n, n + steps) for n in range(first, last)])]
    pallas_call x1, Pallas kernels: 1.19 us -> 5.57 us  [pack(): pl.pallas_call(pack_body, grid=(H,), in_specs=[FLAG] + [head_spec(S)] * 3...]
  transfers between devices with their start and end apart: 42 -> 29, of which waited for: 11 -> 14; matrix products, arithmetic and copies ran while one was open for 6% -> 5% of each run, Pallas kernels for 19% -> 10%
where the time goes in v3:
time: 344 us; the launch traced here: 342 us
  waiting for transfers between devices  183 us (53%)
  Pallas kernels  56 us (16%)
  starting transfers between devices  47.3 us (14%)
  local copies, waits for them, and re-layouts  27.1 us (8%)
  between operations  14.2 us (4%)
  other arithmetic  11.9 us (3%)
    psum x1, waiting for transfers between devices, link_sum(): return lax.psum(rows, 'dp')  51.1 us
    ppermute x9, waiting for transfers between devices, swap(): return lax.ppermute(value, axis, [(n, n ^ bit) for n in range(count)])  46.5 us
    all_gather x1, waiting for transfers between devices, link_term(): right = lax.all_gather(sum_ext, 'ctx', axis_index_groups=groups, tiled=True)  43.1 us
    ppermute x16, waiting for transfers between devices, shift(): lax.ppermute(value, 'ctx', [(n, n + steps) for n in range(first, last)])  41.9 us
    ppermute x16, starting transfers between devices, shift(): lax.ppermute(value, 'ctx', [(n, n + steps) for n in range(first, last)])  38 us
    unnamed x80, local copies, waits for them, and re-layouts  24.8 us
    pallas_call x1, Pallas kernels, full_grads(): pl.pallas_call(grads_body, grid=(H,), in_specs=[FLAG, head_spec(F), head_...  15.8 us
    pallas_call x1, Pallas kernels, full_stats(): pl.pallas_call(stats_body, grid=(H,), in_specs=[FLAG, head_spec(F), head_...  10.7 us
  transfers between devices with their start and end apart: 29, of which 14 were waited for; matrix products, arithmetic and copies ran while one was open for 5% of the time, Pallas kernels for 10%

profile of v3, /device:TPU:1, one launch (start us, length us, event | category | flops | bytes accessed | tf_op | source)
XLA Modules:
  0.0 342.0 jit_solution(18255749030420773710)
XLA Ops:
  9.8 5.6 %pack.1 = (bf16[288,1024]{1,0:T(8,128)(2,1)}, bf16[144,1024]{1,0:T(8,128)(2,1)}, bf16[384,1024]{1,0:T(8,128)(2,1)}) custom-call(s32[1]{0:T(128)} %bitcast.flag, bf16[128,1024]{1,0:T(8,128)(2,1)} %bitcast.29, bf16[128,1024]{1,0:T(8,128)(2,1)} %bitcast.35, bf16[128,1024]{1,0:T(8,128)(2,1)} %bitcast.36, bf16[16,128]{1,0:T(8,128)(2,1)} %broadcast_in_dim.30.ids.m0, ...), custom_call_target="tpu_custom_call" | custom-call | tf_op jit(solution)/shard_map/pack/pallas_call | solution.py:81
  17.5 4.2 %collective-permute-start = (bf16[288,1024]{1,0:T(8,128)(2,1)}, bf16[288,1024]{1,0:T(8,128)(2,1)S(1)}, u32[]{:S(2)}, u32[]{:S(2)}) collective-permute-start(bf16[288,1024]{1,0:T(8,128)(2,1)} %get-tuple-element.44.p0), channel_id=1, source_target_pairs={{0,2},{1,3},{2,4},{3,5},{4,6},{5,7},{6,8},{7,9},{8,10},{9,11},{10,... | collective-permute-start | bytes 1769480 | tf_op jit(solution)/shard_map/ppermute | solution.py:462
  21.7 11.6 %collective-permute-done.p2 = bf16[288,1024]{1,0:T(8,128)(2,1)S(1)} collective-permute-done((bf16[288,1024]{1,0:T(8,128)(2,1)}, bf16[288,1024]{1,0:T(8,128)(2,1)S(1)}, u32[]{:S(2)}, u32[]{:S(2)}) %collective-permute-start) | collective-permute-done | bytes 589856 | tf_op jit(solution)/shard_map/ppermute | solution.py:462
  33.3 4.0 %collective-permute-start.1 = (bf16[288,1024]{1,0:T(8,128)(2,1)S(1)}, bf16[288,1024]{1,0:T(8,128)(2,1)S(1)}, u32[]{:S(2)}, u32[]{:S(2)}) collective-permute-start(bf16[288,1024]{1,0:T(8,128)(2,1)S(1)} %collective-permute-done.p2), channel_id=1, source_target_pairs={{0,2},{1,3},{2,4},{3,5},{4,6},{5,7},{6,8},{7,9},{8,10},{9,11},{10,... | collective-permute-start | bytes 1769480 | tf_op jit(solution)/shard_map/ppermute | solution.py:462
  38.5 9.2 %collective-permute-done.1.p4 = bf16[288,1024]{1,0:T(8,128)(2,1)S(1)} collective-permute-done((bf16[288,1024]{1,0:T(8,128)(2,1)S(1)}, bf16[288,1024]{1,0:T(8,128)(2,1)S(1)}, u32[]{:S(2)}, u32[]{:S(2)}) %collective-permute-start.1) | collective-permute-done | bytes 589856 | tf_op jit(solution)/shard_map/ppermute | solution.py:462
  49.2 5.9 %collective-permute-done.5.second.q1a = bf16[384,1024]{1,0:T(8,128)(2,1)S(1)} collective-permute-done((bf16[384,1024]{1,0:T(8,128)(2,1)S(1)}, bf16[384,1024]{1,0:T(8,128)(2,1)S(1)}, u32[]{:S(2)}, u32[]{:S(2)}) %collective-permute-start.5) | collective-permute-done | bytes 786464 | tf_op jit(solution)/shard_map/ppermute | solution.py:467
  55.1 12.7 %collective-permute-done.2.p3 = bf16[288,1024]{1,0:T(8,128)(2,1)S(1)} collective-permute-done((bf16[288,1024]{1,0:T(8,128)(2,1)S(1)}, bf16[288,1024]{1,0:T(8,128)(2,1)S(1)}, u32[]{:S(2)}, u32[]{:S(2)}) %collective-permute-start.2) | collective-permute-done | bytes 589856 | tf_op jit(solution)/shard_map/ppermute | solution.py:467
  67.8 6.7 %mid_forward.1 = (bf16[144,1024]{1,0:T(8,128)(2,1)S(1)}, f32[128,1024]{1,0:T(8,128)S(1)}, f32[8,1024]{1,0:T(8,128)S(1)}) custom-call(s32[1]{0:T(128)} %bitcast.flag, bf16[128,1024]{1,0:T(8,128)(2,1)S(1)} %bitcast.30, bf16[288,1024]{1,0:T(8,128)(2,1)S(1)} %collective-permute-done.1.p4, bf16[288,1024]{1,0:T(8,128)(2,1)S(1)} %collective-permute-done.2.p3, ...), custom_call_target="tpu_custom_call" | custom-call | flops 700000000 | bytes 4000000 | tf_op jit(solution)/shard_map/mid_forward/pallas_call | solution.py:143
  80.1 4.9 %collective-permute-done.10.refs_2_ = bf16[144,1024]{1,0:T(8,128)(2,1)} collective-permute-done((bf16[144,1024]{1,0:T(8,128)(2,1)}, bf16[144,1024]{1,0:T(8,128)(2,1)}, u32[]{:S(2)}, u32[]{:S(2)}) %collective-permute-start.10) | collective-permute-done | bytes 294944 | tf_op jit(solution)/shard_map/ppermute | solution.py:462
  88.9 5.1 %collective-permute-done.12.refs_4_ = bf16[144,1024]{1,0:T(8,128)(2,1)} collective-permute-done((bf16[144,1024]{1,0:T(8,128)(2,1)}, bf16[144,1024]{1,0:T(8,128)(2,1)}, u32[]{:S(2)}, u32[]{:S(2)}) %collective-permute-start.12) | collective-permute-done | bytes 294944 | tf_op jit(solution)/shard_map/ppermute | solution.py:462
  103.5 10.7 %full_stats.1 = (bf16[384,1024]{1,0:T(8,128)(2,1)S(1)}, f32[24,384]{1,0:T(8,128)}, f32[24,384]{1,0:T(8,128)S(1)}, f32[24,384]{1,0:T(8,128)}) custom-call(s32[1]{0:T(128)} %bitcast.flag, bf16[384,1024]{1,0:T(8,128)(2,1)S(1)} %bitcast.31, bf16[384,1024]{1,0:T(8,128)(2,1)S(1)} %bitcast.34, bf16[144,1024]{1,0:T(8,128)(2,1)S(1)} %copy-done.27, ...), custom_call_target="tpu_custom_call" | custom-call | flops 3000000000 | bytes 10000000 | tf_op jit(solution)/shard_map/full_stats/pallas_call | solution.py:235
  116.3 6.2 %collective-permute-start.14 = (f32[24,384]{1,0:T(8,128)}, f32[24,384]{1,0:T(8,128)}, u32[]{:S(2)}, u32[]{:S(2)}) collective-permute-start(f32[24,384]{1,0:T(8,128)} %get-tuple-element.60.s2), channel_id=1, source_target_pairs={{0,2},{1,3},{2,4},{3,5},{4,6},{5,7},{6,8},{7,9},{8,10},{9,11},{10,... | collective-permute-start | bytes 110600 | tf_op jit(solution)/shard_map/ppermute | solution.py:462
  125.9 4.6 %collective-permute-start.13 = (f32[48,384]{1,0:T(8,128)}, f32[48,384]{1,0:T(8,128)}, u32[]{:S(2)}, u32[]{:S(2)}) collective-permute-start(f32[48,384]{1,0:T(8,128)} %get-tuple-element.86), channel_id=1, source_target_pairs={{0,1},{1,2},{2,3},{3,4},{4,5},{5,6},{6,7},{7,8},{8,9},{9,10},{10,1... | collective-permute-start | bytes 221192 | tf_op jit(solution)/shard_map/ppermute | solution.py:462
  137.6 6.7 %full_first.1 = (f32[24,1152]{1,0:T(8,128)S(1)}, f32[8,1024]{1,0:T(8,128)S(1)}) custom-call(s32[1]{0:T(128)} %bitcast.flag, bf16[384,1024]{1,0:T(8,128)(2,1)S(1)} %bitcast.32, bf16[384,1024]{1,0:T(8,128)(2,1)S(1)} %copy-done.16, bf16[384,1024]{1,0:T(8,128)(2,1)S(1)} %bitcast.27, bf16[384,1024]{1,0:T(8,128)(2,1)S(1)} %collective-permute-done.5.second.q1a, ...), custom_call_target="tpu_custom_call" | custom-call | flops 200000000 | bytes 4000000 | tf_op jit(solution)/shard_map/full_first/pallas_call | solution.py:290
  144.9 15.8 %full_grads.1 = (bf16[384,1024]{1,0:T(8,128)(2,1)}, bf16[384,1024]{1,0:T(8,128)(2,1)}, f32[384,1024]{1,0:T(8,128)S(1)}, bf16[384,1024]{1,0:T(8,128)(2,1)S(1)}, b...) custom-call(s32[1]{0:T(128)} %bitcast.flag, bf16[384,1024]{1,0:T(8,128)(2,1)S(1)} %bitcast.33, ...), custom_call_target="tpu_custom_call" | custom-call | flops 8000000000 | bytes 14000000 | tf_op jit(solution)/shard_map/full_grads/pallas_call | solution.py:348
  166.9 43.1 %all-gather.5.cloned.1.call-done = bf16[576,1024]{1,0:T(8,128)(2,1)} async-done(((bf16[144,1024]{1,0:T(8,128)(2,1)}), bf16[576,1024]{1,0:T(8,128)(2,1)}) %all-gather.5.cloned.1.call-update) | async-done | bytes 1179664 | tf_op jit(solution)/shard_map/all_gather | solution.py:486
  214.3 3.3 collective-permute-done.18.tail
  224.8 7.5 %collective-permute-done.19.refs_7_ = bf16[144,1024]{1,0:T(8,128)(2,1)S(1)} collective-permute-done((bf16[144,1024]{1,0:T(8,128)(2,1)S(1)}, bf16[144,1024]{1,0:T(8,128)(2,1)S(1)}, u32[]{:S(2)}, u32[]{:S(2)}) %collective-permute-start.19) | collective-permute-done | bytes 294944 | tf_op jit(solution)/shard_map/ppermute | solution.py:462
  233.8 12.5 %collective-permute-done.23 = bf16[384,1024]{1,0:T(8,128)(2,1)S(1)} collective-permute-done((bf16[384,1024]{1,0:T(8,128)(2,1)S(1)}, bf16[384,1024]{1,0:T(8,128)(2,1)S(1)}, u32[]{:S(2)}, u32[]{:S(2)}) %collective-permute-start.23) | collective-permute-done | bytes 786464 | tf_op jit(solution)/shard_map/ppermute | solution.py:467
  247.5 4.6 %collective-permute-start.24 = (bf16[384,1024]{1,0:T(8,128)(2,1)}, bf16[384,1024]{1,0:T(8,128)(2,1)}, u32[]{:S(2)}, u32[]{:S(2)}) collective-permute-start(bf16[384,1024]{1,0:T(8,128)(2,1)} %fusion.2), channel_id=1, source_target_pairs={{0,2},{1,3},{2,4},{3,5},{4,6},{5,7},{6,8},{7,9},{8,10},{9,11},{10,... | collective-permute-start | bytes 2359304 | tf_op jit(solution)/shard_map/ppermute | solution.py:462
  255.0 5.8 %collective-permute-done.22.refs_8_ = bf16[144,1024]{1,0:T(8,128)(2,1)S(1)} collective-permute-done((bf16[144,1024]{1,0:T(8,128)(2,1)S(1)}, bf16[144,1024]{1,0:T(8,128)(2,1)S(1)}, u32[]{:S(2)}, u32[]{:S(2)}) %collective-permute-start.22) | collective-permute-done | bytes 294944 | tf_op jit(solution)/shard_map/ppermute | solution.py:467
  260.8 9.5 %collective-permute-done.20.refs_6_ = bf16[144,1024]{1,0:T(8,128)(2,1)S(1)} collective-permute-done((bf16[144,1024]{1,0:T(8,128)(2,1)S(1)}, bf16[144,1024]{1,0:T(8,128)(2,1)S(1)}, u32[]{:S(2)}, u32[]{:S(2)}) %collective-permute-start.20) | collective-permute-done | bytes 294944 | tf_op jit(solution)/shard_map/ppermute | solution.py:467
  270.3 9.7 %mid_backward.1 = (bf16[128,1024]{1,0:T(8,128)(2,1)}, bf16[128,1024]{1,0:T(8,128)(2,1)}, bf16[128,1024]{1,0:T(8,128)(2,1)}) custom-call(s32[1]{0:T(128)} %bitcast.flag, bf16[288,1024]{1,0:T(8,128)(2,1)S(1)} %collective-permute-done.1.p4, bf16[288,1024]{1,0:T(8,128)(2,1)S(1)} %copy-done.21, bf16[288,1024]{1,0:T(8,128)(2,1)S(1)} %collective-permute-done.p2, ...), custom_call_target="tpu_custom_call" | custom-call | flops 3000000000 | bytes 6000000 | tf_op jit(solution)/shard_map/mid_backward/pallas_call | solution.py:446
  282.9 51.1 %all-reduce.2.cloned.1.call-done = f32[16,1024]{1,0:T(8,128)} async-done(((f32[16,1024]{1,0:T(8,128)}), f32[16,1024]{1,0:T(8,128)}) %all-reduce.2.cloned.1.call-update) | async-done | bytes 65552 | tf_op jit(solution)/shard_map/psum | solution.py:493
  (140 shorter events, 66.8 us)
Async XLA Ops:
  7.2 123.4 %all-gather.3.cloned.1.call-start = ((), (), s32[]{:S(2)}) async-start(), calls=%async_computation.1 | async-start | bytes 1474560 | tf_op jit(solution)/shard_map/all_gather | solution.py:480
  7.2 30.1 %collective-permute-start.3 = (bf16[384,1024]{1,0:T(8,128)(2,1)}, bf16[384,1024]{1,0:T(8,128)(2,1)S(1)}, u32[]{:S(2)}, u32[]{:S(2)}) collective-permute-start(bf16[384,1024]{1,0:T(8,128)(2,1)} %bitcast.24), channel_id=1, source_target_pairs={{2,0},{3,1},{4,2},{5,3},{6,4},{7,5},{8,6},{9,7},{10,8},{11,9},{12,... | collective-permute-start | bytes 2359304 | tf_op jit(solution)/shard_map/ppermute | solution.py:462
  15.3 22.0 %collective-permute-start.4 = (bf16[384,1024]{1,0:T(8,128)(2,1)}, bf16[384,1024]{1,0:T(8,128)(2,1)S(1)}, u32[]{:S(2)}, u32[]{:S(2)}) collective-permute-start(bf16[384,1024]{1,0:T(8,128)(2,1)} %get-tuple-element.47), channel_id=1, source_target_pairs={{0,1},{1,0},{2,3},{3,2},{4,5},{5,4},{6,7},{7,6},{8,9},{9,8},{10,11... | collective-permute-start | bytes 2359304 | tf_op jit(solution)/shard_map/ppermute | solution.py:467
  17.5 15.8 %collective-permute-start = (bf16[288,1024]{1,0:T(8,128)(2,1)}, bf16[288,1024]{1,0:T(8,128)(2,1)S(1)}, u32[]{:S(2)}, u32[]{:S(2)}) collective-permute-start(bf16[288,1024]{1,0:T(8,128)(2,1)} %get-tuple-element.44.p0), channel_id=1, source_target_pairs={{0,2},{1,3},{2,4},{3,5},{4,6},{5,7},{6,8},{7,9},{8,10},{9,11},{10,... | collective-permute-start | bytes 1769480 | tf_op jit(solution)/shard_map/ppermute | solution.py:462
  33.3 14.4 %collective-permute-start.1 = (bf16[288,1024]{1,0:T(8,128)(2,1)S(1)}, bf16[288,1024]{1,0:T(8,128)(2,1)S(1)}, u32[]{:S(2)}, u32[]{:S(2)}) collective-permute-start(bf16[288,1024]{1,0:T(8,128)(2,1)S(1)} %collective-permute-done.p2), channel_id=1, source_target_pairs={{0,2},{1,3},{2,4},{3,5},{4,6},{5,7},{6,8},{7,9},{8,10},{9,11},{10,... | collective-permute-start | bytes 1769480 | tf_op jit(solution)/shard_map/ppermute | solution.py:462
  38.4 16.7 %collective-permute-start.5 = (bf16[384,1024]{1,0:T(8,128)(2,1)S(1)}, bf16[384,1024]{1,0:T(8,128)(2,1)S(1)}, u32[]{:S(2)}, u32[]{:S(2)}) collective-permute-start(bf16[384,1024]{1,0:T(8,128)(2,1)S(1)} %pad_maximum_fusion), channel_id=1, source_target_pairs={{0,1},{1,0},{2,3},{3,2},{4,5},{5,4},{6,7},{7,6},{8,9},{9,8},{10,11... | collective-permute-start | bytes 2359304 | tf_op jit(solution)/shard_map/ppermute | solution.py:467
  47.8 20.0 %collective-permute-start.2 = (bf16[288,1024]{1,0:T(8,128)(2,1)S(1)}, bf16[288,1024]{1,0:T(8,128)(2,1)S(1)}, u32[]{:S(2)}, u32[]{:S(2)}) collective-permute-start(bf16[288,1024]{1,0:T(8,128)(2,1)S(1)} %broadcast_select_fusion.1), channel_id=1, source_target_pairs={{0,1},{1,0},{2,3},{3,2},{4,5},{5,4},{6,7},{7,6},{8,9},{9,8},{10,11... | collective-permute-start | bytes 1769480 | tf_op jit(solution)/shard_map/ppermute | solution.py:467
  47.9 28.8 %collective-permute-start.6 = (bf16[384,1024]{1,0:T(8,128)(2,1)S(1)}, bf16[384,1024]{1,0:T(8,128)(2,1)}, u32[]{:S(2)}, u32[]{:S(2)}) collective-permute-start(bf16[384,1024]{1,0:T(8,128)(2,1)S(1)} %bitcast.20), channel_id=1, source_target_pairs={{2,0},{3,1},{4,2},{5,3},{6,4},{7,5},{8,6},{9,7},{10,8},{11,9},{12,... | collective-permute-start | bytes 2359304 | tf_op jit(solution)/shard_map/ppermute | solution.py:462
  76.6 133.3 %all-gather.5.cloned.1.call-start = ((), (), s32[]{:S(2)}) async-start(), calls=%async_computation.2 | async-start | bytes 1474560 | tf_op jit(solution)/shard_map/all_gather | solution.py:486
  80.1 16.2 %collective-permute-start.7 = (bf16[384,1024]{1,0:T(8,128)(2,1)}, bf16[384,1024]{1,0:T(8,128)(2,1)}, u32[]{:S(2)}, u32[]{:S(2)}) collective-permute-start(bf16[384,1024]{1,0:T(8,128)(2,1)} %broadcast_select_fusion), channel_id=1, source_target_pairs={{0,1},{1,0},{2,3},{3,2},{4,5},{5,4},{6,7},{7,6},{8,9},{9,8},{10,11... | collective-permute-start | bytes 2359304 | tf_op jit(solution)/shard_map/ppermute | solution.py:467
  85.0 9.0 %collective-permute-start.12 = (bf16[144,1024]{1,0:T(8,128)(2,1)}, bf16[144,1024]{1,0:T(8,128)(2,1)}, u32[]{:S(2)}, u32[]{:S(2)}) collective-permute-start(bf16[144,1024]{1,0:T(8,128)(2,1)} %collective-permute-done.10.refs_2_), channel_id=1, source_target_pairs={{2,0},{3,1},{4,2},{5,3},{6,4},{7,5},{8,6},{9,7},{10,8},{11,9},{12,... | collective-permute-start | bytes 884744 | tf_op jit(solution)/shard_map/ppermute | solution.py:462
  86.3 9.8 %collective-permute-start.9 = (bf16[16,128]{1,0:T(8,128)(2,1)S(1)}, bf16[16,128]{1,0:T(8,128)(2,1)S(1)}, u32[]{:S(2)}, u32[]{:S(2)}) collective-permute-start(bf16[16,128]{1,0:T(8,128)(2,1)S(1)} %copy-done.32), channel_id=1, source_target_pairs={{2,0},{3,1},{4,2},{5,3},{6,4},{7,5},{8,6},{9,7},{10,8},{11,9},{12,... | collective-permute-start | bytes 12296 | tf_op jit(solution)/shard_map/ppermute | solution.py:462
  87.6 8.7 %collective-permute-start.8 = (bf16[16,128]{1,0:T(8,128)(2,1)S(1)}, bf16[16,128]{1,0:T(8,128)(2,1)S(1)}, u32[]{:S(2)}, u32[]{:S(2)}) collective-permute-start(bf16[16,128]{1,0:T(8,128)(2,1)S(1)} %copy-done.32), channel_id=1, source_target_pairs={{1,0},{2,1},{3,2},{4,3},{5,4},{6,5},{7,6},{8,7},{9,8},{10,9},{11,1... | collective-permute-start | bytes 12296 | tf_op jit(solution)/shard_map/ppermute | solution.py:462
  95.9 36.3 %collective-permute-start.11 = (bf16[144,1024]{1,0:T(8,128)(2,1)}, bf16[144,1024]{1,0:T(8,128)(2,1)}, u32[]{:S(2)}, u32[]{:S(2)}) collective-permute-start(bf16[144,1024]{1,0:T(8,128)(2,1)} %get-tuple-element.84), channel_id=1, source_target_pairs={{0,1},{1,0},{2,3},{3,2},{4,5},{5,4},{6,7},{7,6},{8,9},{9,8},{10,11... | collective-permute-start | bytes 884744 | tf_op jit(solution)/shard_map/ppermute | solution.py:467
  115.1 17.2 %collective-permute-start.16 = (f32[24,384]{1,0:T(8,128)}, f32[24,384]{1,0:T(8,128)}, u32[]{:S(2)}, u32[]{:S(2)}) collective-permute-start(f32[24,384]{1,0:T(8,128)} %get-tuple-element.58.s0), channel_id=1, source_target_pairs={{2,0},{3,1},{4,2},{5,3},{6,4},{7,5},{8,6},{9,7},{10,8},{11,9},{12,... | collective-permute-start | bytes 110600 | tf_op jit(solution)/shard_map/ppermute | solution.py:462
  116.3 15.9 %collective-permute-start.14 = (f32[24,384]{1,0:T(8,128)}, f32[24,384]{1,0:T(8,128)}, u32[]{:S(2)}, u32[]{:S(2)}) collective-permute-start(f32[24,384]{1,0:T(8,128)} %get-tuple-element.60.s2), channel_id=1, source_target_pairs={{0,2},{1,3},{2,4},{3,5},{4,6},{5,7},{6,8},{7,9},{8,10},{9,11},{10,... | collective-permute-start | bytes 110600 | tf_op jit(solution)/shard_map/ppermute | solution.py:462
  165.1 114.9 %reduce-scatter.2.cloned.1.call-start = ((), (), s32[]{:S(2)}) async-start(), calls=%async_computation.3 | async-start | bytes 1114112 | tf_op jit(solution)/shard_map/reduce_scatter | solution.py:492
  165.2 49.1 %collective-permute-start.17 = (bf16[144,1024]{1,0:T(8,128)(2,1)}, bf16[144,1024]{1,0:T(8,128)(2,1)}, u32[]{:S(2)}, u32[]{:S(2)}) collective-permute-start(bf16[144,1024]{1,0:T(8,128)(2,1)} %get-tuple-element.83), channel_id=1, source_target_pairs={{0,1},{1,0},{2,3},{3,2},{4,5},{5,4},{6,7},{7,6},{8,9},{9,8},{10,11... | collective-permute-start | bytes 884744 | tf_op jit(solution)/shard_map/ppermute | solution.py:467
  212.9 121.1 %all-reduce.2.cloned.1.call-start = ((), (), s32[]{:S(2)}) async-start(), calls=%async_computation.4 | async-start | bytes 131072 | tf_op jit(solution)/shard_map/psum | solution.py:493
  221.4 24.9 %collective-permute-start.23 = (bf16[384,1024]{1,0:T(8,128)(2,1)S(1)}, bf16[384,1024]{1,0:T(8,128)(2,1)S(1)}, u32[]{:S(2)}, u32[]{:S(2)}) collective-permute-start(bf16[384,1024]{1,0:T(8,128)(2,1)S(1)} %copy-done.37), channel_id=1, source_target_pairs={{0,1},{1,0},{2,3},{3,2},{4,5},{5,4},{6,7},{7,6},{8,9},{9,8},{10,11... | collective-permute-start | bytes 2359304 | tf_op jit(solution)/shard_map/ppermute | solution.py:467
  223.5 8.8 %collective-permute-start.19 = (bf16[144,1024]{1,0:T(8,128)(2,1)S(1)}, bf16[144,1024]{1,0:T(8,128)(2,1)S(1)}, u32[]{:S(2)}, u32[]{:S(2)}) collective-permute-start(bf16[144,1024]{1,0:T(8,128)(2,1)S(1)} %mid_cotangent.1.refs_5_), channel_id=1, source_target_pairs={{2,0},{3,1},{4,2},{5,3},{6,4},{7,5},{8,6},{9,7},{10,8},{11,9},{12,... | collective-permute-start | bytes 884744 | tf_op jit(solution)/shard_map/ppermute | solution.py:462
  232.3 19.8 %collective-permute-start.21 = (bf16[144,1024]{1,0:T(8,128)(2,1)S(1)}, bf16[144,1024]{1,0:T(8,128)(2,1)S(1)}, u32[]{:S(2)}, u32[]{:S(2)}) collective-permute-start(bf16[144,1024]{1,0:T(8,128)(2,1)S(1)} %collective-permute-done.19.refs_7_), channel_id=1, source_target_pairs={{2,0},{3,1},{4,2},{5,3},{6,4},{7,5},{8,6},{9,7},{10,8},{11,9},{12,... | collective-permute-start | bytes 884744 | tf_op jit(solution)/shard_map/ppermute | solution.py:462
  247.5 32.5 %collective-permute-start.24 = (bf16[384,1024]{1,0:T(8,128)(2,1)}, bf16[384,1024]{1,0:T(8,128)(2,1)}, u32[]{:S(2)}, u32[]{:S(2)}) collective-permute-start(bf16[384,1024]{1,0:T(8,128)(2,1)} %fusion.2), channel_id=1, source_target_pairs={{0,2},{1,3},{2,4},{3,5},{4,6},{5,7},{6,8},{7,9},{8,10},{9,11},{10,... | collective-permute-start | bytes 2359304 | tf_op jit(solution)/shard_map/ppermute | solution.py:462
  254.9 15.4 %collective-permute-start.20 = (bf16[144,1024]{1,0:T(8,128)(2,1)S(1)}, bf16[144,1024]{1,0:T(8,128)(2,1)S(1)}, u32[]{:S(2)}, u32[]{:S(2)}) collective-permute-start(bf16[144,1024]{1,0:T(8,128)(2,1)S(1)} %get-tuple-element.82), channel_id=1, source_target_pairs={{0,1},{1,0},{2,3},{3,2},{4,5},{5,4},{6,7},{7,6},{8,9},{9,8},{10,11... | collective-permute-start | bytes 884744 | tf_op jit(solution)/shard_map/ppermute | solution.py:467
  (45 other events, 411.7 us)
Sparse Core Ops, SparseCore 0:
  76.8 33.9 all-gather.2
  165.2 44.6 all-gather.4
  213.0 62.8 reduce-scatter.1
  280.2 53.8 all-reduce.1

commit v4 on v3

--- a/solution.py
+++ b/solution.py
@@ -18,6 +18,7 @@
 SPAN_F = (FREACH + 1) * F
 WIN = FREACH * F
 KV = 2 * S + 32
+CQ = F + S + 16
 TILES = F // S
 TILE_W = WIN + S
 SCALE = E ** (-0.5)
@@ -63,13 +64,14 @@
     return pl.BlockSpec(shape, lambda h: (0,) * len(shape))
 
 
-def pack_body(flag, q, k, v, ids, qf, kv, qm, first):
+def pack_body(flag, q, k, v, ids, qf, cot, kv, cq, first):
     kv[0:S, :] = k[...]
     kv[S : 2 * S, :] = v[...]
     kv[2 * S : 2 * S + 16, :] = ids[...]
     kv[2 * S + 16 : KV, :] = q[S - 16 : S, :]
-    qm[0:S, :] = q[...]
-    qm[S : S + 16, :] = ids[...]
+    cq[0:F, :] = cot[...]
+    cq[F : F + S, :] = q[...]
+    cq[F + S : CQ, :] = ids[...]
     first[...] = qf[...]
 
     @pl.when(flag[0] == 0)
@@ -77,20 +79,23 @@
         first[0:KV, :] = kv[...]
 
 
-def pack(flag, q, k, v, ids, qf):
+def pack(flag, q, k, v, ids, qf, cot):
+    def wide(rows):
+        return pl.BlockSpec((rows, 2 * E), lambda h: (0, h))
+
     return pl.pallas_call(
         pack_body,
-        grid=(H,),
-        in_specs=[FLAG] + [head_spec(S)] * 3 + [whole_spec((16, E)), head_spec(F)],
-        out_specs=[head_spec(KV), head_spec(S + 16), head_spec(F)],
+        grid=(H // 2,),
+        in_specs=[FLAG] + [wide(S)] * 3 + [whole_spec((16, 2 * E)), wide(F), wide(F)],
+        out_specs=[wide(KV), wide(CQ), wide(F)],
         out_shape=[
             jax.ShapeDtypeStruct((KV, WIDTH), BF16),
-            jax.ShapeDtypeStruct((S + 16, WIDTH), BF16),
+            jax.ShapeDtypeStruct((CQ, WIDTH), BF16),
             jax.ShapeDtypeStruct((F, WIDTH), BF16),
         ],
         compiler_params=pltpu.CompilerParams(vmem_limit_bytes=60 * 1024 * 1024),
         name="pack",
-    )(flag, q, k, v, ids, qf)
+    )(flag, q, k, v, ids, qf, cot)
 
 
 def pick(flag, upper, lower, rows):
@@ -161,14 +166,14 @@
 PAY_SPECS = [head_spec(KV)] * 3 + [head_spec(F)] * 2 + [head_spec(KV)]
 
 
-def full_mask(bias, docs, own_rows, tiles):
+def full_mask(bias, docs, own_rows):
     spread = (iota((S, F), 1) // 3 == iota((S, F), 0)).astype(BF16)
     spread_t = (iota((F, S), 0) // 3 == iota((F, S), 1)).astype(BF16)
     rows = jnp.concatenate(
         [dot_nn(jnp.broadcast_to(d, (16, S)), spread)[0:1] for d in docs], axis=1
     )
     column = dot_nn(spread_t, to_column(own_rows.astype(F32), S).astype(BF16))
-    for t in range(tiles):
+    for t in range(TILES):
         lo = t * S
         mine = jnp.concatenate([column[lo : lo + S]] * (TILE_W // S), axis=1)
         gap = iota((S, TILE_W), 1) - iota((S, TILE_W), 0)
@@ -177,16 +182,16 @@
 
 
 def doc_row(ref):
-    return ref[...][0:1]
-
-
-def stats_body(flag, k, base, mid, w, q0, q1a, q1b, q2, c0, c1, c2, m0, m1, m2, values, s0, s1, s2, bias, ext, part):
+    return ref[F + S : CQ, 0:S][0:1]
+
+
+def stats_body(flag, k, base, mid, w, q0, q1a, q1b, q2, c0, c1, c2, values, s0, s1, s2, bias, ext, part):
     head = pl.program_id(0)
 
     @pl.when(head == 0)
     def _():
-        docs = [doc_row(ref) for ref in (m0, m1, m2)]
-        full_mask(bias, docs, docs[0], TILES)
+        docs = [doc_row(ref) for ref in (c0, c1, c2)]
+        full_mask(bias, docs, docs[0])
         for t in range(TILES):
             part[t, 0:H, :] = jnp.full((H, SPAN_F), NEG, F32)
             part[t, H : 3 * H, :] = jnp.zeros((2 * H, SPAN_F), F32)
@@ -198,7 +203,7 @@
     v = (base[...].astype(F32) + ext[0:F, :]).astype(BF16)
     values[...] = v
     queries = jnp.concatenate([q0[...], pick(flag, q1a, q1b, F), q2[...]], axis=0)
-    cots = jnp.concatenate([c0[...], c1[...], c2[...]], axis=0)
+    cots = jnp.concatenate([c0[0:F, :], c1[0:F, :], c2[0:F, :]], axis=0)
     for t in range(TILES):
         lo = t * S
         scores = dot_nt(k[lo : lo + S, :], queries[lo : lo + TILE_W]) * LOG2 + bias[t]
@@ -230,14 +235,14 @@
     return peak, total, dots
 
 
-def full_stats(flag, k, base, mid, w, qs, cs, ms):
+def full_stats(flag, k, base, mid, w, qs, cs):
     stat = jax.ShapeDtypeStruct((3 * H, F), F32)
     return pl.pallas_call(
         stats_body,
         grid=(H,),
         in_specs=[FLAG, head_spec(F), head_spec(F), whole_spec((S + 16, WIDTH)), head_spec(WIDTH)]
-        + [head_spec(F)] * 7
-        + [whole_spec((16, E))] * 3,
+        + [head_spec(F)] * 4
+        + [head_spec(CQ)] * 3,
         out_specs=[head_spec(F)] + [whole_spec((3 * H, F))] * 3,
         out_shape=[jax.ShapeDtypeStruct((F, WIDTH), BF16), stat, stat, stat],
         scratch_shapes=[
@@ -248,18 +253,19 @@
         compiler_params=PARAMS,
         cost_estimate=pl.CostEstimate(flops=3_000_000_000, bytes_accessed=10_000_000, transcendentals=0),
         name="full_stats",
-    )(flag, k, base, mid, w, *qs, *cs, *ms)
-
-
-def first_body(
-    flag, k, v, q0, q1a, q1b, q2, c0, c1, c2, m0, m1, m2, s0, s1, s2, up1, up2, down1, down2, glob, tail, bias
+    )(flag, k, base, mid, w, *qs, *cs)
+
+
+def grads_body(
+    flag, k, v, q0, q1a, q1b, q2, c0, c1, c2, s0, s1, s2, up1, up2, down1, down2,
+    dk, dv, dq0, dq1, dq2, sums, link, tail, bias, ext, glob, kept,
 ):
     head = pl.program_id(0)
 
     @pl.when(head == 0)
     def _():
-        docs = [doc_row(ref) for ref in (m0, m1, m2)]
-        full_mask(bias, docs, docs[0], 1)
+        docs = [doc_row(ref) for ref in (c0, c1, c2)]
+        full_mask(bias, docs, docs[0])
 
         def triple(ref, base):
             peak, total, dots = (ref[base + j * H : base + (j + 1) * H, :] for j in range(3))
@@ -277,51 +283,11 @@
             glob[0:H, cols] = peak
             glob[H : 2 * H, cols] = inv
             glob[2 * H : 3 * H, cols] = dots * inv
-
-    queries = jnp.concatenate([q0[...], pick(flag, q1a, q1b, F), q2[...]], axis=0)
-    cots = jnp.concatenate([c0[...], c1[...], c2[...]], axis=0)
-    scores = dot_nt(k[...], queries) * LOG2 + bias[0, 0:16, :]
-    probs = jnp.exp2(scores - glob[pl.ds(head, 1), 0:TILE_W]) * glob[pl.ds(H + head, 1), 0:TILE_W]
-    rows = dot_nn(probs.astype(BF16), cots).astype(BF16).astype(F32)
-    tail[...] = jnp.broadcast_to(rows[0:1] + rows[1:2], (8, E))
-
-
-def full_first(flag, k, v, qs, cs, ms, stats):
-    return pl.pallas_call(
-        first_body,
-        grid=(H,),
-        in_specs=[FLAG, head_spec(16), head_spec(16)]
-        + [head_spec(F)] * 3 + [head_spec(S)]
-        + [head_spec(F)] * 2 + [head_spec(S)]
-        + [whole_spec((16, E))] * 3
-        + [whole_spec(s.shape) for s in stats],
-        out_specs=[whole_spec((3 * H, SPAN_F)), head_spec(8)],
-        out_shape=[
-            jax.ShapeDtypeStruct((3 * H, SPAN_F), F32),
-            jax.ShapeDtypeStruct((8, WIDTH), F32),
-        ],
-        scratch_shapes=[pltpu.VMEM((1, S, TILE_W), F32)],
-        compiler_params=PARAMS,
-        cost_estimate=pl.CostEstimate(flops=200_000_000, bytes_accessed=4_000_000, transcendentals=0),
-        name="full_first",
-    )(flag, k, v, *qs, *cs, *ms, *stats)
-
-
-def grads_body(
-    flag, k, v, q0, q1a, q1b, q2, c0, c1, c2, m0, m1, m2, glob,
-    dk, dv, dq0, dq1, dq2, sums, link, bias, ext, kept,
-):
-    head = pl.program_id(0)
-
-    @pl.when(head == 0)
-    def _():
-        docs = [doc_row(ref) for ref in (m0, m1, m2)]
-        full_mask(bias, docs, docs[0], TILES)
         kept[...] = jnp.zeros((F, SPAN_F), BF16)
         ext[F:400, :] = jnp.zeros((400 - F, E), F32)
 
     queries = jnp.concatenate([q0[...], pick(flag, q1a, q1b, F), q2[...]], axis=0)
-    cots = jnp.concatenate([c0[...], c1[...], c2[...]], axis=0)
+    cots = jnp.concatenate([c0[0:F, :], c1[0:F, :], c2[0:F, :]], axis=0)
     for t in range(TILES):
         lo = t * S
         cols = slice(lo, lo + TILE_W)
@@ -340,19 +306,20 @@
     total = ext[pl.ds(2, S, stride=3), :] + ext[pl.ds(3, S, stride=3), :] + ext[pl.ds(4, S, stride=3), :]
     sums[...] = total
     first = ext[0:1, :] + ext[1:2, :]
+    tail[...] = jnp.broadcast_to(first, (8, E))
     link[0:S, :] = total.astype(BF16)
     link[S : S + 16, :] = jnp.where(iota((16, E), 0) == 15, first, 0.0).astype(BF16)
 
 
-def full_grads(flag, k, v, qs, cs, ms, glob):
+def full_grads(flag, k, v, qs, cs, stats):
     return pl.pallas_call(
         grads_body,
         grid=(H,),
         in_specs=[FLAG, head_spec(F), head_spec(F)]
-        + [head_spec(F)] * 7
-        + [whole_spec((16, E))] * 3
-        + [whole_spec(glob.shape)],
-        out_specs=[head_spec(F)] * 5 + [head_spec(S), head_spec(S + 16)],
+        + [head_spec(F)] * 4
+        + [head_spec(CQ)] * 3
+        + [whole_spec(s.shape) for s in stats],
+        out_specs=[head_spec(F)] * 5 + [head_spec(S), head_spec(S + 16), head_spec(8)],
         out_shape=[
             jax.ShapeDtypeStruct((F, WIDTH), BF16),
             jax.ShapeDtypeStruct((F, WIDTH), BF16),
@@ -361,16 +328,18 @@
             jax.ShapeDtypeStruct((F, WIDTH), BF16),
             jax.ShapeDtypeStruct((S, WIDTH), F32),
             jax.ShapeDtypeStruct((S + 16, WIDTH), BF16),
+            jax.ShapeDtypeStruct((8, WIDTH), F32),
         ],
         scratch_shapes=[
             pltpu.VMEM((TILES, S, TILE_W), F32),
             pltpu.VMEM((400, E), F32),
+            pltpu.VMEM((3 * H, SPAN_F), F32),
             pltpu.VMEM((F, SPAN_F), BF16),
         ],
         compiler_params=PARAMS,
         cost_estimate=pl.CostEstimate(flops=8_000_000_000, bytes_accessed=14_000_000, transcendentals=0),
         name="full_grads",
-    )(flag, k, v, *qs, *cs, *ms, glob)
+    )(flag, k, v, *qs, *cs, *stats)
 
 
 def mid_cot_body(sums, tail, w, att, stat, out):
@@ -397,7 +366,7 @@
 
 
 def mid_bwd_body(flag, p4, p3, p2, first, second, p0, *refs):
-    ms = refs[0:5]
+    ms = [ref[F:CQ, :] for ref in refs[0:3]] + [ref[...] for ref in refs[3:5]]
     gs = refs[5:10]
     dq, dk, dv, back, fore = refs[10:]
     pays = pair_slabs(flag, p4, p3, p2, first, second, p0)
@@ -413,7 +382,7 @@
                 ok = ok & causal
             back[n * S : (n + 1) * S, :] = jnp.where(ok, 0.0, NEG)
         for n, pay in enumerate(ms):
-            ok = column == pay[S : S + 16, :].astype(F32)[0:1]
+            ok = column == pay[S : S + 16].astype(F32)[0:1]
             if n == 0:
                 ok = ok & causal
             fore[:, n * S : (n + 1) * S] = jnp.where(ok, 0.0, NEG)
@@ -427,11 +396,11 @@
     keys = jnp.concatenate([pay[0:S] for pay in pays], axis=0)
     values = jnp.concatenate([pay[S : 2 * S] for pay in pays], axis=0)
     peak, inv, delta = stats(gs[0])
-    scores = dot_nt(keys, ms[0][0:S, :]) * LOG2 + back[...]
+    scores = dot_nt(keys, ms[0][0:S]) * LOG2 + back[...]
     probs = jnp.exp2(scores - peak) * inv
     grads = (probs * (dot_nt(values, gs[0][0:S, :]) - delta)).astype(BF16)
     dq[...] = (dot_tn(grads, keys) * SCALE).astype(BF16)
-    queries = jnp.concatenate([ref[0:S, :] for ref in ms], axis=0)
+    queries = jnp.concatenate([one[0:S] for one in ms], axis=0)
     cots = jnp.concatenate([ref[0:S, :] for ref in gs], axis=0)
     every = [stats(ref) for ref in gs]
     peak, inv, delta = (jnp.concatenate([one[j] for one in every], axis=1) for j in range(3))
@@ -446,7 +415,7 @@
     return pl.pallas_call(
         mid_bwd_body,
         grid=(H,),
-        in_specs=[FLAG] + PAY_SPECS + [head_spec(S + 16)] * 10,
+        in_specs=[FLAG] + PAY_SPECS + [head_spec(CQ)] * 3 + [head_spec(S + 16)] * 7,
         out_specs=[head_spec(S)] * 3,
         out_shape=[jax.ShapeDtypeStruct((S, WIDTH), BF16)] * 3,
         scratch_shapes=[pltpu.VMEM((SPAN_M, S), F32), pltpu.VMEM((S, SPAN_M), F32)],
@@ -475,82 +444,76 @@
     return lax.dynamic_slice_in_dim(value, index * rows, rows, 0)
 
 
-def link_left(mid_ext, place):
-    groups = [[first + 16 * n for n in range(4)] for first in range(16)]
-    every = lax.all_gather(mid_ext, "ctx", axis_index_groups=groups, tiled=True)
-    return lax.dynamic_slice_in_dim(every, place // 16 * 256, 256, 1)
-
-
-def link_term(left, sum_ext):
-    groups = [[first + 16 * n for n in range(4)] for first in range(16)]
-    right = lax.all_gather(sum_ext, "ctx", axis_index_groups=groups, tiled=True)
-    return dot_tn(left, right)
-
-
-def link_sum(term):
-    groups = [[16 * first + n for n in range(16)] for first in range(4)]
-    rows = lax.psum_scatter(term, "ctx", scatter_dimension=0, axis_index_groups=groups, tiled=True)
-    return lax.psum(rows, "dp")
+X_GROUPS = [[first + 16 * n for n in range(4)] for first in range(16)]
+YZ_GROUPS = [[16 * first + n for n in range(16)] for first in range(4)]
+
+
+def exchange(value, axis, groups):
+    return lax.all_to_all(value, axis, 0, 0, axis_index_groups=groups, tiled=True)
 
 
 def shards(q_mid, k_mid, v_mid, doc_ids, q_full, k_full, v_base, w_link, cotangent):
     place = lax.axis_index("ctx")
     upper = place % 2 == 1
     flag = (place % 2).astype(jnp.int32).reshape(1)
-    q_m, q_f, k_f, cot = q_mid[0], q_full[0], k_full[0], cotangent[0]
-    ids = jnp.broadcast_to((doc_ids + 1).astype(BF16), (16, S))
-    own_kv, own_q, swap_a = pack(flag, q_m, k_mid[0], v_mid[0], ids, q_f)
+    q_m, q_f, k_f = q_mid[0], q_full[0], k_full[0]
+    ids = jnp.broadcast_to(jnp.tile((doc_ids + 1).astype(BF16), (1, 2)), (16, 2 * S))
+    own_kv, own_cq, swap_a = pack(flag, q_m, k_mid[0], v_mid[0], ids, q_f, cotangent[0])
 
     kv2 = shift(own_kv, 2)
     got_a = swap(swap_a, "ctx", 1)
     qf2 = shift(q_f, -2)
-    late_cot, qf2, got_a = together(cot, qf2, got_a)
+    late_cq, qf2, kv2, got_a = together(own_cq, qf2, kv2, got_a)
     swap_b = jnp.concatenate([jnp.where(upper, kv2, qf2[:KV]), qf2[KV:]], axis=0)
     got_b = swap(swap_b, "ctx", 1)
     kv4 = shift(kv2, 2)
     kv2, kv4 = together(kv2, kv4)
     kv3 = swap(jnp.where(upper, kv4, kv2), "ctx", 1)
-    cf2 = shift(late_cot, -2)
-    cf1 = swap(jnp.where(upper, cot, cf2), "ctx", 1)
-    own_q, cf2 = together(own_q, cf2)
-    qm2 = shift(own_q, -2)
+    cq2 = shift(late_cq, -2)
+    cq2, got_b = together(cq2, got_b)
+    cq1 = swap(jnp.where(upper, late_cq, cq2), "ctx", 1)
 
     pays = (kv4, kv3, kv2, got_a, got_b, own_kv)
     mid_ext, attended, mid_stat = mid_forward(flag, q_m, pays)
-
-    qm1 = swap(jnp.where(upper, own_q, qm2), "ctx", 1)
+    parts = jnp.concatenate([mid_ext[:, n * 256 : (n + 1) * 256] for n in range(4)], axis=0)
+    left, cq1 = together(exchange(parts, "ctx", X_GROUPS), cq1)
+    qm2, cq1 = together(cq2[F:], cq1)
     qm4 = shift(qm2, -2)
-    qm3 = swap(jnp.where(upper, qm2, qm4), "ctx", 1)
-
-    qs, cs, ms = (q_f, got_b, got_a, qf2), (cot, cf1, cf2), (ids, shift(ids, -1), shift(ids, -2))
-    values, s0, s1, s2 = full_stats(flag, k_f, v_base[0], mid_ext, w_link, qs, cs, ms)
+    qs, cs = (q_f, got_b, got_a, qf2), (late_cq, cq1, cq2)
+    values, s0, s1, s2 = full_stats(flag, k_f, v_base[0], mid_ext, w_link, qs, cs)
     up1 = shift(jnp.concatenate([s1, s2], axis=0), 1)
     up2 = shift(s2, 2)
     down1 = shift(jnp.concatenate([s0, s1], axis=0), -1)
     down2 = shift(s0, -2)
-    left = link_left(mid_ext, place)
-    values, qm1, qm4, left = together(values, qm1, qm4, left)
-    glob, tail = full_first(flag, k_f, values, qs, cs, ms, (s0, s1, s2, up1, up2, down1, down2))
+
+    qm4, up1 = together(qm4, up1)
+    qm3 = swap(jnp.where(upper, qm2, qm4), "ctx", 1)
+    dk_f, dv_f, dq0, dq1, dq2, sums, sum_ext, tail = full_grads(
+        flag, k_f, values, qs, cs, (s0, s1, s2, up1, up2, down1, down2)
+    )
+
     next_tail = shift(tail, -1)
-    dk_f, dv_f, dq0, dq1, dq2, sums, sum_ext = full_grads(flag, k_f, values, qs, cs, ms, glob)
-    sums, qm3 = together(sums, qm3)
-
+    near = swap(dq1, "ctx", 1)
+    right = exchange(jnp.concatenate([sum_ext] * 4, axis=0), "ctx", X_GROUPS)
+    sums, right, qm3 = together(sums, right, qm3)
     cot_m = mid_cotangent(sums, next_tail, w_link, attended, mid_stat)
-    cot_m, dq1 = together(cot_m, dq1)
     g2 = shift(cot_m, -2)
+    term = dot_tn(left, right).astype(BF16)
+    term, g2, near = together(term, g2, near)
     g1 = swap(jnp.where(upper, cot_m, g2), "ctx", 1)
     g4 = shift(g2, -2)
+    total = jnp.sum(exchange(term, "ctx", YZ_GROUPS).astype(F32).reshape(16, 16, WIDTH), axis=0)
+    total, g4 = together(total, g4)
     g3 = swap(jnp.where(upper, g2, g4), "ctx", 1)
-    term = link_term(left, sum_ext)
-    dq_m, dk_m, dv_m = mid_backward(flag, pays, (own_q, qm1, qm2, qm3, qm4), (cot_m, g1, g2, g3, g4))
-
-    near = swap(dq1, "ctx", 1).astype(F32)
+    every = exchange(jnp.concatenate([total] * 4, axis=0), "dp", None)
+    factor = float(lax.axis_size("dp") * lax.axis_size("ctx") * F) ** (-0.5)
+    grad_link = jnp.sum(every.reshape(4, 16, WIDTH), axis=0) * factor
+    dq_m, dk_m, dv_m = mid_backward(flag, pays, (late_cq, cq1, cq2, qm3, qm4), (cot_m, g1, g2, g3, g4))
+
+    near = near.astype(F32)
     passed = jnp.where(upper, dq2.astype(F32), dq2.astype(F32) + near)
     far = shift(passed.astype(BF16), 2).astype(F32)
     dq_f = (dq0 + far + jnp.where(upper, near, 0.0)).astype(BF16)
-
-    factor = float(lax.axis_size("dp") * lax.axis_size("ctx") * F) ** (-0.5)
-    grad_link = link_sum(term) * factor
     return (dq_m[None], dk_m[None], dv_m[None], dq_f[None], dk_f[None], dv_f[None], grad_link)
 
 

time: 344 us -> 264 us (0.77)
  waiting for transfers between devices: 183 us -> 80.3 us
  starting transfers between devices: 47.3 us -> 83.3 us
  between operations: 14.2 us -> 1.08 us
  Pallas kernels: 56 us -> 48.4 us
    psum x1 -> x0, waiting for transfers between devices: 51.1 us -> none  [link_sum(): return lax.psum(rows, 'dp')]
    all_gather x2 -> x0, waiting for transfers between devices: 43.1 us -> none  [the longest x1 43.1 us: link_term(): right = lax.all_gather(sum_ext, 'ctx', axis_index_groups=groups, tiled=True)]
    all_to_all x0 -> x4, starting transfers between devices: none -> 39.4 us  [exchange(): lax.all_to_all(value, axis, 0, 0, axis_index_groups=groups, tiled=True)]
    ppermute x9 -> x8, waiting for transfers between devices: 46.5 us -> 33.4 us  [swap(): return lax.ppermute(value, axis, [(n, n ^ bit) for n in range(count)])]
    all_to_all x0 -> x4, waiting for transfers between devices: none -> 9.51 us  [exchange(): lax.all_to_all(value, axis, 0, 0, axis_index_groups=groups, tiled=True)]
    pallas_call x2 -> x1, Pallas kernels: 12.2 us -> 3.95 us  [pack(): pl.pallas_call(pack_body, grid=(H // 2,), in_specs=[FLAG] + [wide(S)] * 3...]
    ppermute x16 -> x13, starting transfers between devices: 38 us -> 32.4 us  [shift(): lax.ppermute(value, 'ctx', [(n, n + steps) for n in range(first, last)])]
    ppermute x16 -> x13, waiting for transfers between devices: 41.9 us -> 37.4 us  [shift(): lax.ppermute(value, 'ctx', [(n, n + steps) for n in range(first, last)])]
  transfers between devices with their start and end apart: 29 -> 25, of which waited for: 14 -> 15; matrix products, arithmetic and copies ran while one was open for 5% -> 7% of each run, Pallas kernels for 10% -> 8%
where the time goes in v4:
time: 264 us; the launch traced here: 259 us
  starting transfers between devices  83.3 us (32%)
  waiting for transfers between devices  80.3 us (30%)
  Pallas kernels  48.4 us (18%)
  local copies, waits for them, and re-layouts  29 us (11%)
  other arithmetic  14.1 us (5%)
  matrix products  2.77 us (1%)
    all_to_all x4, starting transfers between devices, exchange(): lax.all_to_all(value, axis, 0, 0, axis_index_groups=groups, tiled=True)  39.4 us
    ppermute x13, waiting for transfers between devices, shift(): lax.ppermute(value, 'ctx', [(n, n + steps) for n in range(first, last)])  37.4 us
    ppermute x8, waiting for transfers between devices, swap(): return lax.ppermute(value, axis, [(n, n ^ bit) for n in range(count)])  33.4 us
    ppermute x13, starting transfers between devices, shift(): lax.ppermute(value, 'ctx', [(n, n + steps) for n in range(first, last)])  32.4 us
    unnamed x98, local copies, waits for them, and re-layouts  26.7 us
    pallas_call x1, Pallas kernels, full_grads(): pl.pallas_call(grads_body, grid=(H,), in_specs=[FLAG, head_spec(F), head_...  16.2 us
    ppermute x8, starting transfers between devices, swap(): return lax.ppermute(value, axis, [(n, n ^ bit) for n in range(count)])  11.6 us
    pallas_call x1, Pallas kernels, full_stats(): pl.pallas_call(stats_body, grid=(H,), in_specs=[FLAG, head_spec(F), head_...  10.4 us
  transfers between devices with their start and end apart: 25, of which 15 were waited for; matrix products, arithmetic and copies ran while one was open for 7% of the time, Pallas kernels for 8%

profile of v4, /device:TPU:1, one launch (start us, length us, event | category | flops | bytes accessed | tf_op | source)
XLA Modules:
  0.0 259.0 jit_solution(11136206701923708582)
XLA Ops:
  3.2 4.0 %pack.1 = (bf16[288,1024]{1,0:T(8,128)(2,1)}, bf16[528,1024]{1,0:T(8,128)(2,1)}, bf16[384,1024]{1,0:T(8,128)(2,1)}) custom-call(s32[1]{0:T(128)} %bitcast.flag, bf16[128,1024]{1,0:T(8,128)(2,1)} %bitcast.27, bf16[128,1024]{1,0:T(8,128)(2,1)} %bitcast.40, bf16[128,1024]{1,0:T(8,128)(2,1)} %bitcast.41, bf16[16,256]{1,0:T(8,128)(2,1)} %broadcast_in_dim.27.ids, ...), custom_call_target="tpu_custom_call" | custom-call | tf_op jit(solution)/shard_map/pack/pallas_call | solution.py:86
  9.3 4.2 %collective-permute-start.1 = (bf16[288,1024]{1,0:T(8,128)(2,1)}, bf16[288,1024]{1,0:T(8,128)(2,1)S(1)}, u32[]{:S(2)}, u32[]{:S(2)}) collective-permute-start(bf16[288,1024]{1,0:T(8,128)(2,1)} %get-tuple-element.51.p0), channel_id=1, source_target_pairs={{0,2},{1,3},{2,4},{3,5},{4,6},{5,7},{6,8},{7,9},{8,10},{9,11},{10,... | collective-permute-start | bytes 1769480 | tf_op jit(solution)/shard_map/ppermute | solution.py:431
  13.5 11.6 %collective-permute-done.1.p2 = bf16[288,1024]{1,0:T(8,128)(2,1)S(1)} collective-permute-done((bf16[288,1024]{1,0:T(8,128)(2,1)}, bf16[288,1024]{1,0:T(8,128)(2,1)S(1)}, u32[]{:S(2)}, u32[]{:S(2)}) %collective-permute-start.1) | collective-permute-done | bytes 589856 | tf_op jit(solution)/shard_map/ppermute | solution.py:431
  25.6 4.1 %collective-permute-start.3 = (bf16[288,1024]{1,0:T(8,128)(2,1)S(1)}, bf16[288,1024]{1,0:T(8,128)(2,1)S(1)}, u32[]{:S(2)}, u32[]{:S(2)}) collective-permute-start(bf16[288,1024]{1,0:T(8,128)(2,1)S(1)} %collective-permute-done.1.p2), channel_id=1, source_target_pairs={{0,2},{1,3},{2,4},{3,5},{4,6},{5,7},{6,8},{7,9},{8,10},{9,11},{10,... | collective-permute-start | bytes 1769480 | tf_op jit(solution)/shard_map/ppermute | solution.py:431
  33.4 6.2 %collective-permute-done.3.p4 = bf16[288,1024]{1,0:T(8,128)(2,1)S(1)} collective-permute-done((bf16[288,1024]{1,0:T(8,128)(2,1)S(1)}, bf16[288,1024]{1,0:T(8,128)(2,1)S(1)}, u32[]{:S(2)}, u32[]{:S(2)}) %collective-permute-start.3) | collective-permute-done | bytes 589856 | tf_op jit(solution)/shard_map/ppermute | solution.py:431
  42.7 5.9 %collective-permute-done.6.second.q1a = bf16[384,1024]{1,0:T(8,128)(2,1)S(1)} collective-permute-done((bf16[384,1024]{1,0:T(8,128)(2,1)S(1)}, bf16[384,1024]{1,0:T(8,128)(2,1)S(1)}, u32[]{:S(2)}, u32[]{:S(2)}) %collective-permute-start.6) | collective-permute-done | bytes 786464 | tf_op jit(solution)/shard_map/ppermute | solution.py:436
  48.6 8.0 %collective-permute-done.5.c2.refs_2_ = bf16[528,1024]{1,0:T(8,128)(2,1)S(1)} collective-permute-done((bf16[528,1024]{1,0:T(8,128)(2,1)}, bf16[528,1024]{1,0:T(8,128)(2,1)S(1)}, u32[]{:S(2)}, u32[]{:S(2)}) %collective-permute-start.5) | collective-permute-done | bytes 1081376 | tf_op jit(solution)/shard_map/ppermute | solution.py:431
  61.3 6.7 %mid_forward.1 = (bf16[144,1024]{1,0:T(8,128)(2,1)S(1)}, f32[128,1024]{1,0:T(8,128)S(1)}, f32[8,1024]{1,0:T(8,128)S(1)}) custom-call(s32[1]{0:T(128)} %bitcast.flag, bf16[128,1024]{1,0:T(8,128)(2,1)S(1)} %bitcast.28, bf16[288,1024]{1,0:T(8,128)(2,1)S(1)} %collective-permute-done.3.p4, bf16[288,1024]{1,0:T(8,128)(2,1)S(1)} %collective-permute-done.4.p3, ...), custom_call_target="tpu_custom_call" | custom-call | flops 700000000 | bytes 4000000 | tf_op jit(solution)/shard_map/mid_forward/pallas_call | solution.py:148
  70.3 12.7 %all-to-all-start = ((bf16[4,144,256]{2,1,0:T(8,128)(2,1)}), bf16[4,144,256]{2,1,0:T(8,128)(2,1)}, u32[]{:S(2)}, u32[]{:S(2)}) async-start(bf16[4,144,256]{2,1,0:T(8,128)(2,1)} %bitcast.37), calls=%async_computation | async-start | bytes 589824 | tf_op jit(solution)/shard_map/all_to_all | solution.py:452
  84.6 4.1 %all-to-all-done = bf16[4,144,256]{2,1,0:T(8,128)(2,1)} async-done(((bf16[4,144,256]{2,1,0:T(8,128)(2,1)}), bf16[4,144,256]{2,1,0:T(8,128)(2,1)}, u32[]{:S(2)}, u32[]{:S(2)}) %all-to-all-start) | async-done | bytes 294944 | tf_op jit(solution)/shard_map/all_to_all | solution.py:452
  100.3 10.4 %full_stats.1 = (bf16[384,1024]{1,0:T(8,128)(2,1)S(1)}, f32[24,384]{1,0:T(8,128)S(1)}, f32[24,384]{1,0:T(8,128)S(1)}, f32[24,384]{1,0:T(8,128)S(1)}) custom-call(s32[1]{0:T(128)} %bitcast.flag, bf16[384,1024]{1,0:T(8,128)(2,1)S(1)} %bitcast.34, bf16[384,1024]{1,0:T(8,128)(2,1)S(1)} %bitcast.33, bf16[144,1024]{1,0:T(8,128)(2,1)S(1)} %copy-done.38, ...), custom_call_target="tpu_custom_call" | custom-call | flops 3000000000 | bytes 10000000 | tf_op jit(solution)/shard_map/full_stats/pallas_call | solution.py:240
  116.0 6.8 %collective-permute-start.10 = (f32[24,384]{1,0:T(8,128)S(1)}, f32[24,384]{1,0:T(8,128)S(1)}, u32[]{:S(2)}, u32[]{:S(2)}) collective-permute-start(f32[24,384]{1,0:T(8,128)S(1)} %get-tuple-element.67.s2), channel_id=1, source_target_pairs={{0,2},{1,3},{2,4},{3,5},{4,6},{5,7},{6,8},{7,9},{8,10},{9,11},{10,... | collective-permute-start | bytes 110600 | tf_op jit(solution)/shard_map/ppermute | solution.py:431
  123.9 16.2 %full_grads.1 = (bf16[384,1024]{1,0:T(8,128)(2,1)}, bf16[384,1024]{1,0:T(8,128)(2,1)}, f32[384,1024]{1,0:T(8,128)S(1)}, bf16[384,1024]{1,0:T(8,128)(2,1)S(1)}, b...) custom-call(s32[1]{0:T(128)} %bitcast.flag, ...), custom_call_target="tpu_custom_call" | custom-call | flops 8000000000 | bytes 14000000 | tf_op jit(solution)/shard_map/full_grads/pallas_call | solution.py:315
  144.3 13.3 %all-to-all-start.1 = ((bf16[4,144,1024]{2,1,0:T(8,128)(2,1)}), bf16[4,144,1024]{2,1,0:T(8,128)(2,1)}, u32[]{:S(2)}, u32[]{:S(2)}) async-start(bf16[4,144,1024]{2,1,0:T(8,128)(2,1)} %bitcast.36), calls=%async_computation.1 | async-start | bytes 2359296 | tf_op jit(solution)/shard_map/all_to_all | solution.py:452
  161.5 16.3 %collective-permute-done.13.refs_3_ = bf16[144,1024]{1,0:T(8,128)(2,1)S(1)} collective-permute-done((bf16[144,1024]{1,0:T(8,128)(2,1)S(1)}, bf16[144,1024]{1,0:T(8,128)(2,1)S(1)}, u32[]{:S(2)}, u32[]{:S(2)}) %collective-permute-start.13) | collective-permute-done | bytes 294944 | tf_op jit(solution)/shard_map/ppermute | solution.py:436
  186.5 3.4 %collective-permute-done.15.refs_7_ = bf16[144,1024]{1,0:T(8,128)(2,1)S(1)} collective-permute-done((bf16[144,1024]{1,0:T(8,128)(2,1)S(1)}, bf16[144,1024]{1,0:T(8,128)(2,1)S(1)}, u32[]{:S(2)}, u32[]{:S(2)}) %collective-permute-start.15) | collective-permute-done | bytes 294944 | tf_op jit(solution)/shard_map/ppermute | solution.py:431
  189.9 4.9 %all-to-all-start.2 = ((bf16[16,16,1024]{2,1,0:T(8,128)(2,1)}), bf16[16,16,1024]{2,1,0:T(8,128)(2,1)S(1)}, u32[]{:S(2)}, u32[]{:S(2)}) async-start(bf16[16,16,1024]{2,1,0:T(8,128)(2,1)} %bitcast.39), calls=%async_computation.2 | async-start | bytes 1048576 | tf_op jit(solution)/shard_map/all_to_all | solution.py:452
  197.1 4.1 %collective-permute-start.20 = (bf16[384,1024]{1,0:T(8,128)(2,1)}, bf16[384,1024]{1,0:T(8,128)(2,1)}, u32[]{:S(2)}, u32[]{:S(2)}) collective-permute-start(bf16[384,1024]{1,0:T(8,128)(2,1)} %fusion.2), channel_id=1, source_target_pairs={{0,2},{1,3},{2,4},{3,5},{4,6},{5,7},{6,8},{7,9},{8,10},{9,11},{10,... | collective-permute-start | bytes 2359304 | tf_op jit(solution)/shard_map/ppermute | solution.py:431
  202.5 4.2 %all-to-all-done.2 = bf16[16,16,1024]{2,1,0:T(8,128)(2,1)S(1)} async-done(((bf16[16,16,1024]{2,1,0:T(8,128)(2,1)}), bf16[16,16,1024]{2,1,0:T(8,128)(2,1)S(1)}, u32[]{:S(2)}, u32[]{:S(2)}) %all-to-all-start.2) | async-done | bytes 524320 | tf_op jit(solution)/shard_map/all_to_all | solution.py:452
  206.9 7.1 %collective-permute-done.18.refs_9_ = bf16[144,1024]{1,0:T(8,128)(2,1)S(1)} collective-permute-done((bf16[144,1024]{1,0:T(8,128)(2,1)S(1)}, bf16[144,1024]{1,0:T(8,128)(2,1)S(1)}, u32[]{:S(2)}, u32[]{:S(2)}) %collective-permute-start.18) | collective-permute-done | bytes 294944 | tf_op jit(solution)/shard_map/ppermute | solution.py:431
  214.8 8.5 %all-to-all-start.3 = ((f32[4,16,1024]{2,1,0:T(8,128)}), f32[4,16,1024]{2,1,0:T(8,128)}, u32[]{:S(2)}, u32[]{:S(2)}) async-start(f32[4,16,1024]{2,1,0:T(8,128)} %bitcast.21), calls=%async_computation.3 | async-start | bytes 524288 | tf_op jit(solution)/shard_map/all_to_all | solution.py:452
  225.6 3.2 %fusion.3 = bf16[1,384,1024]{2,1,0:T(8,128)(2,1)} fusion(bf16[384,1024]{1,0:T(8,128)(2,1)} %collective-permute-done.16, f32[384,1024]{1,0:T(8,128)} %copy-done.5, bf16[384,1024]{1,0:T(8,128)(2,1)} %collective-permute-done.20, pred[]{:T(512)S(6)} %eq.6), kind=kLoop, calls=%fused_computation.9 | loop fusion | flops 2359296 | bytes 3932161 | tf_op jit(solution)/shard_map/broadcast_in_dim | solution.py:517
  234.1 6.3 %collective-permute-done.17.refs_6_ = bf16[144,1024]{1,0:T(8,128)(2,1)} collective-permute-done((bf16[144,1024]{1,0:T(8,128)(2,1)}, bf16[144,1024]{1,0:T(8,128)(2,1)}, u32[]{:S(2)}, u32[]{:S(2)}) %collective-permute-start.17) | collective-permute-done | bytes 294944 | tf_op jit(solution)/shard_map/ppermute | solution.py:436
  248.7 10.2 %mid_backward.1 = (bf16[128,1024]{1,0:T(8,128)(2,1)}, bf16[128,1024]{1,0:T(8,128)(2,1)}, bf16[128,1024]{1,0:T(8,128)(2,1)}) custom-call(s32[1]{0:T(128)} %bitcast.flag, bf16[288,1024]{1,0:T(8,128)(2,1)S(1)} %collective-permute-done.3.p4, bf16[288,1024]{1,0:T(8,128)(2,1)S(1)} %copy-done.30, bf16[288,1024]{1,0:T(8,128)(2,1)S(1)} %collective-permute-done.1.p2, ...), custom_call_target="tpu_custom_call" | custom-call | flops 3000000000 | bytes 6000000 | tf_op jit(solution)/shard_map/mid_backward/pallas_call | solution.py:415
  (152 shorter events, 75.4 us)
Async XLA Ops:
  0.6 24.5 %collective-permute-start = (bf16[384,1024]{1,0:T(8,128)(2,1)}, bf16[384,1024]{1,0:T(8,128)(2,1)S(1)}, u32[]{:S(2)}, u32[]{:S(2)}) collective-permute-start(bf16[384,1024]{1,0:T(8,128)(2,1)} %bitcast.29), channel_id=1, source_target_pairs={{2,0},{3,1},{4,2},{5,3},{6,4},{7,5},{8,6},{9,7},{10,8},{11,9},{12,... | collective-permute-start | bytes 2359304 | tf_op jit(solution)/shard_map/ppermute | solution.py:431
  7.2 18.4 %collective-permute-start.2 = (bf16[384,1024]{1,0:T(8,128)(2,1)}, bf16[384,1024]{1,0:T(8,128)(2,1)S(1)}, u32[]{:S(2)}, u32[]{:S(2)}) collective-permute-start(bf16[384,1024]{1,0:T(8,128)(2,1)} %get-tuple-element.52), channel_id=1, source_target_pairs={{0,1},{1,0},{2,3},{3,2},{4,5},{5,4},{6,7},{7,6},{8,9},{9,8},{10,11... | collective-permute-start | bytes 2359304 | tf_op jit(solution)/shard_map/ppermute | solution.py:436
  9.3 15.8 %collective-permute-start.1 = (bf16[288,1024]{1,0:T(8,128)(2,1)}, bf16[288,1024]{1,0:T(8,128)(2,1)S(1)}, u32[]{:S(2)}, u32[]{:S(2)}) collective-permute-start(bf16[288,1024]{1,0:T(8,128)(2,1)} %get-tuple-element.51.p0), channel_id=1, source_target_pairs={{0,2},{1,3},{2,4},{3,5},{4,6},{5,7},{6,8},{7,9},{8,10},{9,11},{10,... | collective-permute-start | bytes 1769480 | tf_op jit(solution)/shard_map/ppermute | solution.py:431
  25.6 14.0 %collective-permute-start.3 = (bf16[288,1024]{1,0:T(8,128)(2,1)S(1)}, bf16[288,1024]{1,0:T(8,128)(2,1)S(1)}, u32[]{:S(2)}, u32[]{:S(2)}) collective-permute-start(bf16[288,1024]{1,0:T(8,128)(2,1)S(1)} %collective-permute-done.1.p2), channel_id=1, source_target_pairs={{0,2},{1,3},{2,4},{3,5},{4,6},{5,7},{6,8},{7,9},{8,10},{9,11},{10,... | collective-permute-start | bytes 1769480 | tf_op jit(solution)/shard_map/ppermute | solution.py:431
  29.7 26.8 %collective-permute-start.5 = (bf16[528,1024]{1,0:T(8,128)(2,1)}, bf16[528,1024]{1,0:T(8,128)(2,1)S(1)}, u32[]{:S(2)}, u32[]{:S(2)}) collective-permute-start(bf16[528,1024]{1,0:T(8,128)(2,1)} %get-tuple-element.57.c0.refs_0_), channel_id=1, source_target_pairs={{2,0},{3,1},{4,2},{5,3},{6,4},{7,5},{8,6},{9,7},{10,8},{11,9},{12,... | collective-permute-start | bytes 3244040 | tf_op jit(solution)/shard_map/ppermute | solution.py:431
  31.2 17.4 %collective-permute-start.6 = (bf16[384,1024]{1,0:T(8,128)(2,1)S(1)}, bf16[384,1024]{1,0:T(8,128)(2,1)S(1)}, u32[]{:S(2)}, u32[]{:S(2)}) collective-permute-start(bf16[384,1024]{1,0:T(8,128)(2,1)S(1)} %pad_maximum_fusion.1), channel_id=1, source_target_pairs={{0,1},{1,0},{2,3},{3,2},{4,5},{5,4},{6,7},{7,6},{8,9},{9,8},{10,11... | collective-permute-start | bytes 2359304 | tf_op jit(solution)/shard_map/ppermute | solution.py:436
  39.7 21.5 %collective-permute-start.4 = (bf16[288,1024]{1,0:T(8,128)(2,1)S(1)}, bf16[288,1024]{1,0:T(8,128)(2,1)S(1)}, u32[]{:S(2)}, u32[]{:S(2)}) collective-permute-start(bf16[288,1024]{1,0:T(8,128)(2,1)S(1)} %broadcast_select_fusion.1), channel_id=1, source_target_pairs={{0,1},{1,0},{2,3},{3,2},{4,5},{5,4},{6,7},{7,6},{8,9},{9,8},{10,11... | collective-permute-start | bytes 1769480 | tf_op jit(solution)/shard_map/ppermute | solution.py:436
  58.0 30.8 %collective-permute-start.7 = (bf16[528,1024]{1,0:T(8,128)(2,1)}, bf16[528,1024]{1,0:T(8,128)(2,1)}, u32[]{:S(2)}, u32[]{:S(2)}) collective-permute-start(bf16[528,1024]{1,0:T(8,128)(2,1)} %broadcast_select_fusion), channel_id=1, source_target_pairs={{0,1},{1,0},{2,3},{3,2},{4,5},{5,4},{6,7},{7,6},{8,9},{9,8},{10,11... | collective-permute-start | bytes 3244040 | tf_op jit(solution)/shard_map/ppermute | solution.py:436
  70.3 18.5 %all-to-all-start = ((bf16[4,144,256]{2,1,0:T(8,128)(2,1)}), bf16[4,144,256]{2,1,0:T(8,128)(2,1)}, u32[]{:S(2)}, u32[]{:S(2)}) async-start(bf16[4,144,256]{2,1,0:T(8,128)(2,1)} %bitcast.37), calls=%async_computation | async-start | bytes 589824 | tf_op jit(solution)/shard_map/all_to_all | solution.py:452
  88.7 34.1 %collective-permute-start.8 = (bf16[144,1024]{1,0:T(8,128)(2,1)}, bf16[144,1024]{1,0:T(8,128)(2,1)S(1)}, u32[]{:S(2)}, u32[]{:S(2)}) collective-permute-start(bf16[144,1024]{1,0:T(8,128)(2,1)} %slice.23), channel_id=1, source_target_pairs={{2,0},{3,1},{4,2},{5,3},{6,4},{7,5},{8,6},{9,7},{10,8},{11,9},{12,... | collective-permute-start | bytes 884744 | tf_op jit(solution)/shard_map/ppermute | solution.py:431
  110.7 12.1 %collective-permute-start.9 = (f32[48,384]{1,0:T(8,128)S(1)}, f32[48,384]{1,0:T(8,128)S(1)}, u32[]{:S(2)}, u32[]{:S(2)}) collective-permute-start(f32[48,384]{1,0:T(8,128)S(1)} %get-tuple-element.100), channel_id=1, source_target_pairs={{0,1},{1,2},{2,3},{3,4},{4,5},{5,6},{6,7},{7,8},{8,9},{9,10},{10,1... | collective-permute-start | bytes 221192 | tf_op jit(solution)/shard_map/ppermute | solution.py:431
  113.4 10.5 %collective-permute-start.11 = (f32[48,384]{1,0:T(8,128)S(1)}, f32[48,384]{1,0:T(8,128)S(1)}, u32[]{:S(2)}, u32[]{:S(2)}) collective-permute-start(f32[48,384]{1,0:T(8,128)S(1)} %get-tuple-element.99), channel_id=1, source_target_pairs={{1,0},{2,1},{3,2},{4,3},{5,4},{6,5},{7,6},{8,7},{9,8},{10,9},{11,1... | collective-permute-start | bytes 221192 | tf_op jit(solution)/shard_map/ppermute | solution.py:431
  114.7 8.2 %collective-permute-start.12 = (f32[24,384]{1,0:T(8,128)S(1)}, f32[24,384]{1,0:T(8,128)S(1)}, u32[]{:S(2)}, u32[]{:S(2)}) collective-permute-start(f32[24,384]{1,0:T(8,128)S(1)} %get-tuple-element.65.s0), channel_id=1, source_target_pairs={{2,0},{3,1},{4,2},{5,3},{6,4},{7,5},{8,6},{9,7},{10,8},{11,9},{12,... | collective-permute-start | bytes 110600 | tf_op jit(solution)/shard_map/ppermute | solution.py:431
  116.0 7.9 %collective-permute-start.10 = (f32[24,384]{1,0:T(8,128)S(1)}, f32[24,384]{1,0:T(8,128)S(1)}, u32[]{:S(2)}, u32[]{:S(2)}) collective-permute-start(f32[24,384]{1,0:T(8,128)S(1)} %get-tuple-element.67.s2), channel_id=1, source_target_pairs={{0,2},{1,3},{2,4},{3,5},{4,6},{5,7},{6,8},{7,9},{8,10},{9,11},{10,... | collective-permute-start | bytes 110600 | tf_op jit(solution)/shard_map/ppermute | solution.py:431
  144.3 34.2 %all-to-all-start.1 = ((bf16[4,144,1024]{2,1,0:T(8,128)(2,1)}), bf16[4,144,1024]{2,1,0:T(8,128)(2,1)}, u32[]{:S(2)}, u32[]{:S(2)}) async-start(bf16[4,144,1024]{2,1,0:T(8,128)(2,1)} %bitcast.36), calls=%async_computation.1 | async-start | bytes 2359296 | tf_op jit(solution)/shard_map/all_to_all | solution.py:452
  157.6 28.8 %collective-permute-start.16 = (bf16[384,1024]{1,0:T(8,128)(2,1)}, bf16[384,1024]{1,0:T(8,128)(2,1)}, u32[]{:S(2)}, u32[]{:S(2)}) collective-permute-start(bf16[384,1024]{1,0:T(8,128)(2,1)} %copy-done.46), channel_id=1, source_target_pairs={{0,1},{1,0},{2,3},{3,2},{4,5},{5,4},{6,7},{7,6},{8,9},{9,8},{10,11... | collective-permute-start | bytes 2359304 | tf_op jit(solution)/shard_map/ppermute | solution.py:436
  158.9 18.9 %collective-permute-start.13 = (bf16[144,1024]{1,0:T(8,128)(2,1)S(1)}, bf16[144,1024]{1,0:T(8,128)(2,1)S(1)}, u32[]{:S(2)}, u32[]{:S(2)}) collective-permute-start(bf16[144,1024]{1,0:T(8,128)(2,1)S(1)} %broadcast_select_fusion.4), channel_id=1, source_target_pairs={{0,1},{1,0},{2,3},{3,2},{4,5},{5,4},{6,7},{7,6},{8,9},{9,8},{10,11... | collective-permute-start | bytes 884744 | tf_op jit(solution)/shard_map/ppermute | solution.py:436
  160.2 18.3 %collective-permute-start.14 = (f32[8,1024]{1,0:T(8,128)S(1)}, f32[8,1024]{1,0:T(8,128)S(1)}, u32[]{:S(2)}, u32[]{:S(2)}) collective-permute-start(f32[8,1024]{1,0:T(8,128)S(1)} %get-tuple-element.75), channel_id=1, source_target_pairs={{1,0},{2,1},{3,2},{4,3},{5,4},{6,5},{7,6},{8,7},{9,8},{10,9},{11,1... | collective-permute-start | bytes 98312 | tf_op jit(solution)/shard_map/ppermute | solution.py:431
  189.9 16.9 %all-to-all-start.2 = ((bf16[16,16,1024]{2,1,0:T(8,128)(2,1)}), bf16[16,16,1024]{2,1,0:T(8,128)(2,1)S(1)}, u32[]{:S(2)}, u32[]{:S(2)}) async-start(bf16[16,16,1024]{2,1,0:T(8,128)(2,1)} %bitcast.39), calls=%async_computation.2 | async-start | bytes 1048576 | tf_op jit(solution)/shard_map/all_to_all | solution.py:452
  197.1 28.5 %collective-permute-start.20 = (bf16[384,1024]{1,0:T(8,128)(2,1)}, bf16[384,1024]{1,0:T(8,128)(2,1)}, u32[]{:S(2)}, u32[]{:S(2)}) collective-permute-start(bf16[384,1024]{1,0:T(8,128)(2,1)} %fusion.2), channel_id=1, source_target_pairs={{0,2},{1,3},{2,4},{3,5},{4,6},{5,7},{6,8},{7,9},{8,10},{9,11},{10,... | collective-permute-start | bytes 2359304 | tf_op jit(solution)/shard_map/ppermute | solution.py:431
  201.3 12.7 %collective-permute-start.18 = (bf16[144,1024]{1,0:T(8,128)(2,1)S(1)}, bf16[144,1024]{1,0:T(8,128)(2,1)S(1)}, u32[]{:S(2)}, u32[]{:S(2)}) collective-permute-start(bf16[144,1024]{1,0:T(8,128)(2,1)S(1)} %collective-permute-done.15.refs_7_), channel_id=1, source_target_pairs={{2,0},{3,1},{4,2},{5,3},{6,4},{7,5},{8,6},{9,7},{10,8},{11,9},{12,... | collective-permute-start | bytes 884744 | tf_op jit(solution)/shard_map/ppermute | solution.py:431
  214.8 15.2 %all-to-all-start.3 = ((f32[4,16,1024]{2,1,0:T(8,128)}), f32[4,16,1024]{2,1,0:T(8,128)}, u32[]{:S(2)}, u32[]{:S(2)}) async-start(f32[4,16,1024]{2,1,0:T(8,128)} %bitcast.21), calls=%async_computation.3 | async-start | bytes 524288 | tf_op jit(solution)/shard_map/all_to_all | solution.py:452
  224.1 9.9 %collective-permute-start.19 = (bf16[144,1024]{1,0:T(8,128)(2,1)}, bf16[144,1024]{1,0:T(8,128)(2,1)}, u32[]{:S(2)}, u32[]{:S(2)}) collective-permute-start(bf16[144,1024]{1,0:T(8,128)(2,1)} %get-tuple-element.93), channel_id=1, source_target_pairs={{0,1},{1,0},{2,3},{3,2},{4,5},{5,4},{6,7},{7,6},{8,9},{9,8},{10,11... | collective-permute-start | bytes 884744 | tf_op jit(solution)/shard_map/ppermute | solution.py:436
  224.5 15.9 %collective-permute-start.17 = (bf16[144,1024]{1,0:T(8,128)(2,1)}, bf16[144,1024]{1,0:T(8,128)(2,1)}, u32[]{:S(2)}, u32[]{:S(2)}) collective-permute-start(bf16[144,1024]{1,0:T(8,128)(2,1)} %get-tuple-element.94), channel_id=1, source_target_pairs={{0,1},{1,0},{2,3},{3,2},{4,5},{5,4},{6,7},{7,6},{8,9},{9,8},{10,11... | collective-permute-start | bytes 884744 | tf_op jit(solution)/shard_map/ppermute | solution.py:436
  (50 other events, 462.3 us)

commit v5 on v4

--- a/solution.py
+++ b/solution.py
@@ -26,7 +26,6 @@
 NEG = -1e30
 F32 = jnp.float32
 BF16 = jnp.bfloat16
-PARAMS = pltpu.CompilerParams(vmem_limit_bytes=16 * 1024 * 1024)
 
 
 def dot_nn(a, b):
@@ -93,7 +92,6 @@
             jax.ShapeDtypeStruct((CQ, WIDTH), BF16),
             jax.ShapeDtypeStruct((F, WIDTH), BF16),
         ],
-        compiler_params=pltpu.CompilerParams(vmem_limit_bytes=60 * 1024 * 1024),
         name="pack",
     )(flag, q, k, v, ids, qf, cot)
 
@@ -156,7 +154,6 @@
             jax.ShapeDtypeStruct((8, WIDTH), F32),
         ],
         scratch_shapes=[pltpu.VMEM((S + 16, SPAN_M), F32)],
-        compiler_params=PARAMS,
         cost_estimate=pl.CostEstimate(flops=700_000_000, bytes_accessed=4_000_000, transcendentals=0),
         name="mid_forward",
     )(flag, q, *pays)
@@ -166,13 +163,13 @@
 PAY_SPECS = [head_spec(KV)] * 3 + [head_spec(F)] * 2 + [head_spec(KV)]
 
 
-def full_mask(bias, docs, own_rows):
+def full_mask(bias, docs):
     spread = (iota((S, F), 1) // 3 == iota((S, F), 0)).astype(BF16)
     spread_t = (iota((F, S), 0) // 3 == iota((F, S), 1)).astype(BF16)
     rows = jnp.concatenate(
         [dot_nn(jnp.broadcast_to(d, (16, S)), spread)[0:1] for d in docs], axis=1
     )
-    column = dot_nn(spread_t, to_column(own_rows.astype(F32), S).astype(BF16))
+    column = dot_nn(spread_t, to_column(docs[0].astype(F32), S).astype(BF16))
     for t in range(TILES):
         lo = t * S
         mine = jnp.concatenate([column[lo : lo + S]] * (TILE_W // S), axis=1)
@@ -185,16 +182,12 @@
     return ref[F + S : CQ, 0:S][0:1]
 
 
-def stats_body(flag, k, base, mid, w, q0, q1a, q1b, q2, c0, c1, c2, values, s0, s1, s2, bias, ext, part):
+def stats_body(k, base, mid, w, q0, q2, c0, c2, values, s0, s2, bias, ext, part):
     head = pl.program_id(0)
 
     @pl.when(head == 0)
     def _():
-        docs = [doc_row(ref) for ref in (c0, c1, c2)]
-        full_mask(bias, docs, docs[0])
-        for t in range(TILES):
-            part[t, 0:H, :] = jnp.full((H, SPAN_F), NEG, F32)
-            part[t, H : 3 * H, :] = jnp.zeros((2 * H, SPAN_F), F32)
+        full_mask(bias, [doc_row(ref) for ref in (c0, c0, c2)])
 
     linked = dot_nn(mid[...], w[...])
     for n in range(2, 5):
@@ -202,25 +195,55 @@
     ext[0:2, :] = jnp.broadcast_to(linked[S + 15 : S + 16], (2, E))
     v = (base[...].astype(F32) + ext[0:F, :]).astype(BF16)
     values[...] = v
-    queries = jnp.concatenate([q0[...], pick(flag, q1a, q1b, F), q2[...]], axis=0)
-    cots = jnp.concatenate([c0[0:F, :], c1[0:F, :], c2[0:F, :]], axis=0)
+    for t in range(TILES):
+        lo, first, last = t * S, F - t * S, (t + 1) * S
+        queries = jnp.concatenate([q0[lo:F, :], q2[0:last, :]], axis=0)
+        cots = jnp.concatenate([c0[lo:F, :], c2[0:last, :]], axis=0)
+        mask = jnp.concatenate([bias[t, :, 0:first], bias[t, :, first + F : first + F + last]], axis=1)
+        rows = partial_stats(k[lo : lo + S, :], v[lo : lo + S], queries, cots, mask)
+        for j, empty in enumerate((NEG, 0.0, 0.0)):
+            pieces = [jnp.full((1, lo), empty, F32)] if lo else []
+            pieces += [rows[j]] + ([jnp.full((1, F - last), empty, F32)] if last < F else [])
+            part[t, pl.ds(j * H + head, 1), :] = jnp.concatenate(pieces, axis=1)
+
+    @pl.when(head == H - 1)
+    def _():
+        for out, cols in ((s0, slice(0, F)), (s2, slice(F, 2 * F))):
+            merge_into(out, part, cols)
+
+
+def partial_stats(k, v, queries, cots, mask):
+    scores = dot_nt(k, queries) * LOG2 + mask
+    peak = jnp.max(scores, axis=0, keepdims=True)
+    expo = jnp.exp2(scores - peak)
+    dots = dot_nt(v, cots)
+    return peak, jnp.sum(expo, axis=0, keepdims=True), jnp.sum(expo * dots, axis=0, keepdims=True)
+
+
+def merge_into(out, part, cols):
+    merged = merge([tuple(part[t, j * H : (j + 1) * H, cols] for j in range(3)) for t in range(TILES)])
+    for j in range(3):
+        out[j * H : (j + 1) * H, :] = merged[j]
+
+
+def stats_next_body(flag, k, v, q1a, q1b, c0, c1, s1, bias, part):
+    head = pl.program_id(0)
+
+    @pl.when(head == 0)
+    def _():
+        full_mask(bias, [doc_row(ref) for ref in (c0, c1, c1)])
+
+    queries = pick(flag, q1a, q1b, F)
     for t in range(TILES):
         lo = t * S
-        scores = dot_nt(k[lo : lo + S, :], queries[lo : lo + TILE_W]) * LOG2 + bias[t]
-        peak = jnp.max(scores, axis=0, keepdims=True)
-        expo = jnp.exp2(scores - peak)
-        dots = dot_nt(v[lo : lo + S], cots[lo : lo + TILE_W])
-        part[t, pl.ds(head, 1), lo : lo + TILE_W] = peak
-        part[t, pl.ds(H + head, 1), lo : lo + TILE_W] = jnp.sum(expo, axis=0, keepdims=True)
-        part[t, pl.ds(2 * H + head, 1), lo : lo + TILE_W] = jnp.sum(expo * dots, axis=0, keepdims=True)
+        mask = bias[t, :, F - lo : 2 * F - lo]
+        rows = partial_stats(k[lo : lo + S, :], v[lo : lo + S, :], queries, c1[0:F, :], mask)
+        for j in range(3):
+            part[t, pl.ds(j * H + head, 1), :] = rows[j]
 
     @pl.when(head == H - 1)
     def _():
-        for n, out in enumerate((s0, s1, s2)):
-            cols = slice(n * F, (n + 1) * F)
-            merged = merge([(part[t, 0:H, cols], part[t, H : 2 * H, cols], part[t, 2 * H : 3 * H, cols]) for t in range(TILES)])
-            for j in range(3):
-                out[j * H : (j + 1) * H, :] = merged[j]
+        merge_into(s1, part, slice(0, F))
 
 
 def merge(parts):
@@ -235,50 +258,59 @@
     return peak, total, dots
 
 
-def full_stats(flag, k, base, mid, w, qs, cs):
+def full_stats(k, base, mid, w, q0, q2, c0, c2):
     stat = jax.ShapeDtypeStruct((3 * H, F), F32)
     return pl.pallas_call(
         stats_body,
         grid=(H,),
-        in_specs=[FLAG, head_spec(F), head_spec(F), whole_spec((S + 16, WIDTH)), head_spec(WIDTH)]
-        + [head_spec(F)] * 4
-        + [head_spec(CQ)] * 3,
-        out_specs=[head_spec(F)] + [whole_spec((3 * H, F))] * 3,
-        out_shape=[jax.ShapeDtypeStruct((F, WIDTH), BF16), stat, stat, stat],
+        in_specs=[head_spec(F), head_spec(F), whole_spec((S + 16, WIDTH)), head_spec(WIDTH)]
+        + [head_spec(F)] * 2
+        + [head_spec(CQ)] * 2,
+        out_specs=[head_spec(F)] + [whole_spec((3 * H, F))] * 2,
+        out_shape=[jax.ShapeDtypeStruct((F, WIDTH), BF16), stat, stat],
         scratch_shapes=[
             pltpu.VMEM((TILES, S, TILE_W), F32),
             pltpu.VMEM((400, E), F32),
-            pltpu.VMEM((TILES, 3 * H, SPAN_F), F32),
+            pltpu.VMEM((TILES, 3 * H, 2 * F), F32),
         ],
-        compiler_params=PARAMS,
-        cost_estimate=pl.CostEstimate(flops=3_000_000_000, bytes_accessed=10_000_000, transcendentals=0),
+        cost_estimate=pl.CostEstimate(flops=2_000_000_000, bytes_accessed=8_000_000, transcendentals=0),
         name="full_stats",
-    )(flag, k, base, mid, w, *qs, *cs)
+    )(k, base, mid, w, q0, q2, c0, c2)
+
+
+def next_stats(flag, k, v, q1a, q1b, c0, c1):
+    return pl.pallas_call(
+        stats_next_body,
+        grid=(H,),
+        in_specs=[FLAG] + [head_spec(F)] * 4 + [head_spec(CQ)] * 2,
+        out_specs=whole_spec((3 * H, F)),
+        out_shape=jax.ShapeDtypeStruct((3 * H, F), F32),
+        scratch_shapes=[
+            pltpu.VMEM((TILES, S, TILE_W), F32),
+            pltpu.VMEM((TILES, 3 * H, F), F32),
+        ],
+        cost_estimate=pl.CostEstimate(flops=1_000_000_000, bytes_accessed=6_000_000, transcendentals=0),
+        name="next_stats",
+    )(flag, k, v, q1a, q1b, c0, c1)
 
 
 def grads_body(
-    flag, k, v, q0, q1a, q1b, q2, c0, c1, c2, s0, s1, s2, up1, up2, down1, down2,
+    flag, k, v, q0, q1a, q1b, q2, c0, c1, c2, s0, s1, s2, up1, up1_far, up2, down1, down1_far, down2,
     dk, dv, dq0, dq1, dq2, sums, link, tail, bias, ext, glob, kept,
 ):
     head = pl.program_id(0)
 
     @pl.when(head == 0)
     def _():
-        docs = [doc_row(ref) for ref in (c0, c1, c2)]
-        full_mask(bias, docs, docs[0])
-
-        def triple(ref, base):
-            peak, total, dots = (ref[base + j * H : base + (j + 1) * H, :] for j in range(3))
+        full_mask(bias, [doc_row(ref) for ref in (c0, c1, c2)])
+
+        def triple(ref):
+            peak, total, dots = (ref[j * H : (j + 1) * H, :] for j in range(3))
             return jnp.where(total > 0.0, peak, NEG), total, dots
 
-        groups = (
-            [triple(s0, 0), triple(up1, 0), triple(up2, 0)],
-            [triple(s1, 0), triple(up1, 3 * H), triple(down1, 0)],
-            [triple(s2, 0), triple(down1, 3 * H), triple(down2, 0)],
-        )
-        for n, group in enumerate(groups):
+        for n, group in enumerate(((s0, up1, up2), (s1, up1_far, down1_far), (s2, down1, down2))):
             cols = slice(n * F, (n + 1) * F)
-            peak, total, dots = merge(group)
+            peak, total, dots = merge([triple(ref) for ref in group])
             inv = jnp.where(total > 0.0, 1.0 / total, 0.0)
             glob[0:H, cols] = peak
             glob[H : 2 * H, cols] = inv
@@ -336,7 +368,6 @@
             pltpu.VMEM((3 * H, SPAN_F), F32),
             pltpu.VMEM((F, SPAN_F), BF16),
         ],
-        compiler_params=PARAMS,
         cost_estimate=pl.CostEstimate(flops=8_000_000_000, bytes_accessed=14_000_000, transcendentals=0),
         name="full_grads",
     )(flag, k, v, *qs, *cs, *stats)
@@ -359,7 +390,6 @@
     return pl.pallas_call(
         mid_cot_body,
         out_shape=jax.ShapeDtypeStruct((S + 16, WIDTH), BF16),
-        compiler_params=PARAMS,
         cost_estimate=pl.CostEstimate(flops=600_000_000, bytes_accessed=4_000_000, transcendentals=0),
         name="mid_cotangent",
     )(sums, tail, w, att, stat)
@@ -419,7 +449,6 @@
         out_specs=[head_spec(S)] * 3,
         out_shape=[jax.ShapeDtypeStruct((S, WIDTH), BF16)] * 3,
         scratch_shapes=[pltpu.VMEM((SPAN_M, S), F32), pltpu.VMEM((S, SPAN_M), F32)],
-        compiler_params=PARAMS,
         cost_estimate=pl.CostEstimate(flops=3_000_000_000, bytes_accessed=6_000_000, transcendentals=0),
         name="mid_backward",
     )(flag, *pays, *ms, *gs)
@@ -470,35 +499,33 @@
     kv2, kv4 = together(kv2, kv4)
     kv3 = swap(jnp.where(upper, kv4, kv2), "ctx", 1)
     cq2 = shift(late_cq, -2)
-    cq2, got_b = together(cq2, got_b)
+    cq2, kv3_late = together(cq2, kv3)
     cq1 = swap(jnp.where(upper, late_cq, cq2), "ctx", 1)
 
     pays = (kv4, kv3, kv2, got_a, got_b, own_kv)
     mid_ext, attended, mid_stat = mid_forward(flag, q_m, pays)
-    parts = jnp.concatenate([mid_ext[:, n * 256 : (n + 1) * 256] for n in range(4)], axis=0)
-    left, cq1 = together(exchange(parts, "ctx", X_GROUPS), cq1)
-    qm2, cq1 = together(cq2[F:], cq1)
+    values, s0, s2 = full_stats(k_f, v_base[0], mid_ext, w_link, q_f, qf2, late_cq, cq2)
+    up2, up1_far = shift(s2, 2), shift(s2, 1)
+    down2, down1_far = shift(s0, -2), shift(s0, -1)
+    s1 = next_stats(flag, k_f, values, got_b, got_a, late_cq, cq1)
+    up1, down1 = shift(s1, 1), shift(s1, -1)
+
+    qm2, s1 = together(cq2[F:], s1)
     qm4 = shift(qm2, -2)
+    qm3 = swap(jnp.where(upper, qm2, qm4), "ctx", 1)
     qs, cs = (q_f, got_b, got_a, qf2), (late_cq, cq1, cq2)
-    values, s0, s1, s2 = full_stats(flag, k_f, v_base[0], mid_ext, w_link, qs, cs)
-    up1 = shift(jnp.concatenate([s1, s2], axis=0), 1)
-    up2 = shift(s2, 2)
-    down1 = shift(jnp.concatenate([s0, s1], axis=0), -1)
-    down2 = shift(s0, -2)
-
-    qm4, up1 = together(qm4, up1)
-    qm3 = swap(jnp.where(upper, qm2, qm4), "ctx", 1)
     dk_f, dv_f, dq0, dq1, dq2, sums, sum_ext, tail = full_grads(
-        flag, k_f, values, qs, cs, (s0, s1, s2, up1, up2, down1, down2)
+        flag, k_f, values, qs, cs, (s0, s1, s2, up1, up1_far, up2, down1, down1_far, down2)
     )
 
     next_tail = shift(tail, -1)
     near = swap(dq1, "ctx", 1)
-    right = exchange(jnp.concatenate([sum_ext] * 4, axis=0), "ctx", X_GROUPS)
-    sums, right, qm3 = together(sums, right, qm3)
+    parts = [jnp.concatenate([sum_ext, mid_ext[:, n * 256 : (n + 1) * 256]], axis=1) for n in range(4)]
+    parts = exchange(jnp.concatenate(parts, axis=0), "ctx", X_GROUPS)
+    sums, parts = together(sums, parts)
     cot_m = mid_cotangent(sums, next_tail, w_link, attended, mid_stat)
     g2 = shift(cot_m, -2)
-    term = dot_tn(left, right).astype(BF16)
+    term = dot_tn(parts[:, WIDTH:], parts[:, :WIDTH]).astype(BF16)
     term, g2, near = together(term, g2, near)
     g1 = swap(jnp.where(upper, cot_m, g2), "ctx", 1)
     g4 = shift(g2, -2)
@@ -508,6 +535,7 @@
     every = exchange(jnp.concatenate([total] * 4, axis=0), "dp", None)
     factor = float(lax.axis_size("dp") * lax.axis_size("ctx") * F) ** (-0.5)
     grad_link = jnp.sum(every.reshape(4, 16, WIDTH), axis=0) * factor
+    pays = (kv4, kv3_late, kv2, got_a, got_b, own_kv)
     dq_m, dk_m, dv_m = mid_backward(flag, pays, (late_cq, cq1, cq2, qm3, qm4), (cot_m, g1, g2, g3, g4))
 
     near = near.astype(F32)

time: 264 us -> 275 us (1.042)
  waiting for transfers between devices: 80.3 us -> 106 us
  local copies, waits for them, and re-layouts: 29 us -> 6.52 us
  Pallas kernels: 48.4 us -> 58.6 us
    unnamed x98 -> x46, local copies, waits for them, and re-layouts: 26.7 us -> 4.9 us
    ppermute x13 -> x15, waiting for transfers between devices: 37.4 us -> 51.3 us  [shift(): lax.ppermute(value, 'ctx', [(n, n + steps) for n in range(first, last)])]
    all_to_all x4 -> x3, waiting for transfers between devices: 9.51 us -> 16.8 us  [exchange(): lax.all_to_all(value, axis, 0, 0, axis_index_groups=groups, tiled=True)]
    pallas_call x1 -> x2, Pallas kernels: 10.4 us -> 17.4 us  [the longest x1 9.6 us: full_stats(): pl.pallas_call(stats_body, grid=(H,), in_specs=[head_spec(F), head_spec(F...]
    ppermute x8, waiting for transfers between devices: 33.4 us -> 38 us  [swap(): return lax.ppermute(value, axis, [(n, n ^ bit) for n in range(count)])]
    ppermute x13 -> x15, starting transfers between devices: 32.4 us -> 36.6 us  [shift(): lax.ppermute(value, 'ctx', [(n, n + steps) for n in range(first, last)])]
    ppermute x8, starting transfers between devices: 11.6 us -> 7.67 us  [swap(): return lax.ppermute(value, axis, [(n, n ^ bit) for n in range(count)])]
    all_to_all x4 -> x3, starting transfers between devices: 39.4 us -> 38.9 us  [exchange(): lax.all_to_all(value, axis, 0, 0, axis_index_groups=groups, tiled=True)]
  transfers between devices with their start and end apart: 25 -> 26, of which waited for: 15 -> 12; matrix products, arithmetic and copies ran while one was open for 7% -> 4% of each run, Pallas kernels for 8% -> 11%
where the time goes in v5:
time: 275 us; the launch traced here: 271 us
  waiting for transfers between devices  106 us (39%)
  starting transfers between devices  83.2 us (30%)
  Pallas kernels  58.6 us (21%)
  other arithmetic  13.8 us (5%)
  local copies, waits for them, and re-layouts  6.52 us (2%)
    ppermute x15, waiting for transfers between devices, shift(): lax.ppermute(value, 'ctx', [(n, n + steps) for n in range(first, last)])  51.3 us
    all_to_all x3, starting transfers between devices, exchange(): lax.all_to_all(value, axis, 0, 0, axis_index_groups=groups, tiled=True)  38.9 us
    ppermute x8, waiting for transfers between devices, swap(): return lax.ppermute(value, axis, [(n, n ^ bit) for n in range(count)])  38 us
    ppermute x15, starting transfers between devices, shift(): lax.ppermute(value, 'ctx', [(n, n + steps) for n in range(first, last)])  36.6 us
    all_to_all x3, waiting for transfers between devices, exchange(): lax.all_to_all(value, axis, 0, 0, axis_index_groups=groups, tiled=True)  16.8 us
    pallas_call x1, Pallas kernels, full_grads(): pl.pallas_call(grads_body, grid=(H,), in_specs=[FLAG, head_spec(F), head_...  14.9 us
    pallas_call x1, Pallas kernels, mid_backward(): pl.pallas_call(mid_bwd_body, grid=(H,), in_specs=[FLAG] + PAY_SPECS + [he...  10.1 us
    pallas_call x1, Pallas kernels, full_stats(): pl.pallas_call(stats_body, grid=(H,), in_specs=[head_spec(F), head_spec(F...  9.6 us
  transfers between devices with their start and end apart: 26, of which 12 were waited for; matrix products, arithmetic and copies ran while one was open for 4% of the time, Pallas kernels for 11%

profile of v5, /device:TPU:1, one launch (start us, length us, event | category | flops | bytes accessed | tf_op | source)
XLA Modules:
  0.0 270.7 jit_solution(453318776655515561)
XLA Ops:
  2.0 4.0 %pack.1 = (bf16[288,1024]{1,0:T(8,128)(2,1)}, bf16[528,1024]{1,0:T(8,128)(2,1)}, bf16[384,1024]{1,0:T(8,128)(2,1)}) custom-call(s32[1]{0:T(128)} %bitcast.flag, bf16[128,1024]{1,0:T(8,128)(2,1)} %bitcast.31, bf16[128,1024]{1,0:T(8,128)(2,1)} %bitcast.35, bf16[128,1024]{1,0:T(8,128)(2,1)} %bitcast.36, bf16[16,256]{1,0:T(8,128)(2,1)} %broadcast_in_dim.27.ids, ...), custom_call_target="tpu_custom_call" | custom-call | tf_op jit(solution)/shard_map/pack/pallas_call | solution.py:85
  9.4 4.2 %collective-permute-start.1 = (bf16[288,1024]{1,0:T(8,128)(2,1)}, bf16[288,1024]{1,0:T(8,128)(2,1)S(1)}, u32[]{:S(2)}, u32[]{:S(2)}) collective-permute-start(bf16[288,1024]{1,0:T(8,128)(2,1)} %get-tuple-element.45.p0), channel_id=1, source_target_pairs={{0,2},{1,3},{2,4},{3,5},{4,6},{5,7},{6,8},{7,9},{8,10},{9,11},{10,... | collective-permute-start | bytes 1769480 | tf_op jit(solution)/shard_map/ppermute | solution.py:460
  13.6 11.6 %collective-permute-done.1.p2 = bf16[288,1024]{1,0:T(8,128)(2,1)S(1)} collective-permute-done((bf16[288,1024]{1,0:T(8,128)(2,1)}, bf16[288,1024]{1,0:T(8,128)(2,1)S(1)}, u32[]{:S(2)}, u32[]{:S(2)}) %collective-permute-start.1) | collective-permute-done | bytes 589856 | tf_op jit(solution)/shard_map/ppermute | solution.py:460
  25.2 3.0 %collective-permute-done.q2 = bf16[384,1024]{1,0:T(8,128)(2,1)S(1)} collective-permute-done((bf16[384,1024]{1,0:T(8,128)(2,1)S(1)}, bf16[384,1024]{1,0:T(8,128)(2,1)S(1)}, u32[]{:S(2)}, u32[]{:S(2)}) %collective-permute-start) | collective-permute-done | bytes 786464 | tf_op jit(solution)/shard_map/ppermute | solution.py:460
  29.1 4.6 %collective-permute-start.3 = (bf16[288,1024]{1,0:T(8,128)(2,1)S(1)}, bf16[288,1024]{1,0:T(8,128)(2,1)}, u32[]{:S(2)}, u32[]{:S(2)}) collective-permute-start(bf16[288,1024]{1,0:T(8,128)(2,1)S(1)} %collective-permute-done.1.p2), channel_id=1, source_target_pairs={{0,2},{1,3},{2,4},{3,5},{4,6},{5,7},{6,8},{7,9},{8,10},{9,11},{10,... | collective-permute-start | bytes 1769480 | tf_op jit(solution)/shard_map/ppermute | solution.py:460
  35.1 8.7 %collective-permute-done.3.p4 = bf16[288,1024]{1,0:T(8,128)(2,1)} collective-permute-done((bf16[288,1024]{1,0:T(8,128)(2,1)S(1)}, bf16[288,1024]{1,0:T(8,128)(2,1)}, u32[]{:S(2)}, u32[]{:S(2)}) %collective-permute-start.3) | collective-permute-done | bytes 589856 | tf_op jit(solution)/shard_map/ppermute | solution.py:460
  45.3 14.1 %collective-permute-done.4.c2.refs_2_ = bf16[528,1024]{1,0:T(8,128)(2,1)S(1)} collective-permute-done((bf16[528,1024]{1,0:T(8,128)(2,1)}, bf16[528,1024]{1,0:T(8,128)(2,1)S(1)}, u32[]{:S(2)}, u32[]{:S(2)}) %collective-permute-start.4) | collective-permute-done | bytes 1081376 | tf_op jit(solution)/shard_map/ppermute | solution.py:460
  62.3 38.0 %collective-permute-done.6.second.q1a = bf16[384,1024]{1,0:T(8,128)(2,1)S(1)} collective-permute-done((bf16[384,1024]{1,0:T(8,128)(2,1)S(1)}, bf16[384,1024]{1,0:T(8,128)(2,1)S(1)}, u32[]{:S(2)}, u32[]{:S(2)}) %collective-permute-start.6) | collective-permute-done | bytes 786464 | tf_op jit(solution)/shard_map/ppermute | solution.py:465
  101.3 8.6 %mid_forward.1 = (bf16[144,1024]{1,0:T(8,128)(2,1)}, f32[128,1024]{1,0:T(8,128)}, f32[8,1024]{1,0:T(8,128)}) custom-call(s32[1]{0:T(128)} %bitcast.flag, bf16[128,1024]{1,0:T(8,128)(2,1)} %bitcast.32, bf16[288,1024]{1,0:T(8,128)(2,1)} %collective-permute-done.3.p4, bf16[288,1024]{1,0:T(8,128)(2,1)} %collective-permute-done.5.p3, ...), custom_call_target="tpu_custom_call" | custom-call | flops 700000000 | bytes 4000000 | tf_op jit(solution)/shard_map/mid_forward/pallas_call | solution.py:146
  110.0 9.6 %full_stats.1 = (bf16[384,1024]{1,0:T(8,128)(2,1)}, f32[24,384]{1,0:T(8,128)}, f32[24,384]{1,0:T(8,128)}) custom-call(bf16[384,1024]{1,0:T(8,128)(2,1)} %bitcast.23, bf16[384,1024]{1,0:T(8,128)(2,1)} %bitcast.33, bf16[144,1024]{1,0:T(8,128)(2,1)} %get-tuple-element.55.mid, bf16[1024,1024]{1,0:T(8,128)(2,1)} %w.3, bf16[384,1024]{1,0:T(8,128)(2,1)} %bitcast.27, ...), custom_call_target="tpu_custom_call" | custom-call | flops 2000000000 | bytes 8000000 | tf_op jit(solution)/shard_map/full_stats/pallas_call | solution.py:263
  121.7 4.7 %collective-permute-start.12 = (f32[24,384]{1,0:T(8,128)}, f32[24,384]{1,0:T(8,128)S(1)}, u32[]{:S(2)}, u32[]{:S(2)}) collective-permute-start(f32[24,384]{1,0:T(8,128)} %get-tuple-element.60.s2), channel_id=1, source_target_pairs={{0,2},{1,3},{2,4},{3,5},{4,6},{5,7},{6,8},{7,9},{8,10},{9,11},{10,... | collective-permute-start | bytes 110600 | tf_op jit(solution)/shard_map/ppermute | solution.py:460
  130.0 7.8 %next_stats.1.s1 = f32[24,384]{1,0:T(8,128)} custom-call(s32[1]{0:T(128)} %bitcast.flag, bf16[384,1024]{1,0:T(8,128)(2,1)} %bitcast.24, bf16[384,1024]{1,0:T(8,128)(2,1)} %get-tuple-element.56.v, bf16[384,1024]{1,0:T(8,128)(2,1)} %copy-done.4, bf16[384,1024]{1,0:T(8,128)(2,1)} %copy-done.3, bf16[528,1024]{1,0:T(8,128)(2,1)} %get-tuple-element.49.c0.refs_0_, ...), custom_call_target="tpu_custom_call" | custom-call | flops 1000000000 | bytes 6000000 | tf_op jit(solution)/shard_map/next_stats/pallas_call | solution.py:282
  137.8 4.4 %collective-permute-start.10 = (f32[24,384]{1,0:T(8,128)}, f32[24,384]{1,0:T(8,128)S(1)}, u32[]{:S(2)}, u32[]{:S(2)}) collective-permute-start(f32[24,384]{1,0:T(8,128)} %next_stats.1.s1), channel_id=1, source_target_pairs={{0,1},{1,2},{2,3},{3,4},{4,5},{5,6},{6,7},{7,8},{8,9},{9,10},{10,1... | collective-permute-start | bytes 110600 | tf_op jit(solution)/shard_map/ppermute | solution.py:460
  144.7 4.0 %collective-permute-done.13.down1 = f32[24,384]{1,0:T(8,128)S(1)} collective-permute-done((f32[24,384]{1,0:T(8,128)}, f32[24,384]{1,0:T(8,128)S(1)}, u32[]{:S(2)}, u32[]{:S(2)}) %collective-permute-start.13) | collective-permute-done | bytes 36896 | tf_op jit(solution)/shard_map/ppermute | solution.py:460
  149.4 14.9 %full_grads.1 = (bf16[384,1024]{1,0:T(8,128)(2,1)}, bf16[384,1024]{1,0:T(8,128)(2,1)}, f32[384,1024]{1,0:T(8,128)}, bf16[384,1024]{1,0:T(8,128)(2,1)}, bf16[384,...) custom-call(s32[1]{0:T(128)} %bitcast.flag, ...), custom_call_target="tpu_custom_call" | custom-call | flops 8000000000 | bytes 14000000 | tf_op jit(solution)/shard_map/full_grads/pallas_call | solution.py:347
  167.0 10.9 %all-to-all-start = ((bf16[4,144,1280]{2,1,0:T(8,128)(2,1)}), bf16[4,144,1280]{2,1,0:T(8,128)(2,1)S(1)}, u32[]{:S(2)}, u32[]{:S(2)}) async-start(bf16[4,144,1280]{2,1,0:T(8,128)(2,1)} %bitcast.10), calls=%async_computation | async-start | bytes 2949120 | tf_op jit(solution)/shard_map/all_to_all | solution.py:481
  179.2 11.9 %all-to-all-done = bf16[4,144,1280]{2,1,0:T(8,128)(2,1)S(1)} async-done(((bf16[4,144,1280]{2,1,0:T(8,128)(2,1)}), bf16[4,144,1280]{2,1,0:T(8,128)(2,1)S(1)}, u32[]{:S(2)}, u32[]{:S(2)}) %all-to-all-start) | async-done | bytes 1474592 | tf_op jit(solution)/shard_map/all_to_all | solution.py:481
  192.0 3.6 %mid_cotangent.1.refs_5_ = bf16[144,1024]{1,0:T(8,128)(2,1)} custom-call(f32[128,1024]{1,0:T(8,128)} %get-tuple-element.63.sums, f32[8,1024]{1,0:T(8,128)} %copy-done.13, bf16[1024,1024]{1,0:T(8,128)(2,1)} %w.3, f32[128,1024]{1,0:T(8,128)} %get-tuple-element.65.att, f32[8,1024]{1,0:T(8,128)} %get-tuple-element.66.stat), custom_call_target="tpu_custom_call" | custom-call | flops 600000000 | bytes 4000000 | tf_op jit(solution)/shard_map/mid_cotangent/pallas_call | solution.py:390
  198.3 5.1 %collective-permute-done.17.refs_7_ = bf16[144,1024]{1,0:T(8,128)(2,1)} collective-permute-done((bf16[144,1024]{1,0:T(8,128)(2,1)}, bf16[144,1024]{1,0:T(8,128)(2,1)}, u32[]{:S(2)}, u32[]{:S(2)}) %collective-permute-start.17) | collective-permute-done | bytes 294944 | tf_op jit(solution)/shard_map/ppermute | solution.py:460
  203.4 6.8 %all-to-all-start.1 = ((bf16[16,16,1024]{2,1,0:T(8,128)(2,1)}), bf16[16,16,1024]{2,1,0:T(8,128)(2,1)S(1)}, u32[]{:S(2)}, u32[]{:S(2)}) async-start(bf16[16,16,1024]{2,1,0:T(8,128)(2,1)} %bitcast.12), calls=%async_computation.1 | async-start | bytes 1048576 | tf_op jit(solution)/shard_map/all_to_all | solution.py:481
  213.9 4.9 %collective-permute-start.22 = (bf16[384,1024]{1,0:T(8,128)(2,1)}, bf16[384,1024]{1,0:T(8,128)(2,1)}, u32[]{:S(2)}, u32[]{:S(2)}) collective-permute-start(bf16[384,1024]{1,0:T(8,128)(2,1)} %fusion.2), channel_id=1, source_target_pairs={{0,2},{1,3},{2,4},{3,5},{4,6},{5,7},{6,8},{7,9},{8,10},{9,11},{10,... | collective-permute-start | bytes 2359304 | tf_op jit(solution)/shard_map/ppermute | solution.py:460
  230.7 21.1 %all-to-all-start.2 = ((f32[4,16,1024]{2,1,0:T(8,128)}), f32[4,16,1024]{2,1,0:T(8,128)S(1)}, u32[]{:S(2)}, u32[]{:S(2)}) async-start(f32[4,16,1024]{2,1,0:T(8,128)} %bitcast.19), calls=%async_computation.2 | async-start | bytes 524288 | tf_op jit(solution)/shard_map/all_to_all | solution.py:481
  254.2 4.9 %all-to-all-done.2 = f32[4,16,1024]{2,1,0:T(8,128)S(1)} async-done(((f32[4,16,1024]{2,1,0:T(8,128)}), f32[4,16,1024]{2,1,0:T(8,128)S(1)}, u32[]{:S(2)}, u32[]{:S(2)}) %all-to-all-start.2) | async-done | bytes 262176 | tf_op jit(solution)/shard_map/all_to_all | solution.py:481
  260.5 10.1 %mid_backward.1 = (bf16[128,1024]{1,0:T(8,128)(2,1)}, bf16[128,1024]{1,0:T(8,128)(2,1)}, bf16[128,1024]{1,0:T(8,128)(2,1)}) custom-call(s32[1]{0:T(128)} %bitcast.flag, bf16[288,1024]{1,0:T(8,128)(2,1)} %collective-permute-done.3.p4, bf16[288,1024]{1,0:T(8,128)(2,1)} %collective-permute-done.5.p3, bf16[288,1024]{1,0:T(8,128)(2,1)} %copy-done.2, ...), custom_call_target="tpu_custom_call" | custom-call | flops 3000000000 | bytes 6000000 | tf_op jit(solution)/shard_map/mid_backward/pallas_call | solution.py:445
  (102 shorter events, 48.0 us)
Async XLA Ops:
  6.0 19.2 %collective-permute-start.2 = (bf16[384,1024]{1,0:T(8,128)(2,1)}, bf16[384,1024]{1,0:T(8,128)(2,1)S(1)}, u32[]{:S(2)}, u32[]{:S(2)}) collective-permute-start(bf16[384,1024]{1,0:T(8,128)(2,1)} %get-tuple-element.46), channel_id=1, source_target_pairs={{0,1},{1,0},{2,3},{3,2},{4,5},{5,4},{6,7},{7,6},{8,9},{9,8},{10,11... | collective-permute-start | bytes 2359304 | tf_op jit(solution)/shard_map/ppermute | solution.py:465
  8.1 20.1 %collective-permute-start = (bf16[384,1024]{1,0:T(8,128)(2,1)S(1)}, bf16[384,1024]{1,0:T(8,128)(2,1)S(1)}, u32[]{:S(2)}, u32[]{:S(2)}) collective-permute-start(bf16[384,1024]{1,0:T(8,128)(2,1)S(1)} %bitcast.29), channel_id=1, source_target_pairs={{2,0},{3,1},{4,2},{5,3},{6,4},{7,5},{8,6},{9,7},{10,8},{11,9},{12,... | collective-permute-start | bytes 2359304 | tf_op jit(solution)/shard_map/ppermute | solution.py:460
  9.4 15.8 %collective-permute-start.1 = (bf16[288,1024]{1,0:T(8,128)(2,1)}, bf16[288,1024]{1,0:T(8,128)(2,1)S(1)}, u32[]{:S(2)}, u32[]{:S(2)}) collective-permute-start(bf16[288,1024]{1,0:T(8,128)(2,1)} %get-tuple-element.45.p0), channel_id=1, source_target_pairs={{0,2},{1,3},{2,4},{3,5},{4,6},{5,7},{6,8},{7,9},{8,10},{9,11},{10,... | collective-permute-start | bytes 1769480 | tf_op jit(solution)/shard_map/ppermute | solution.py:460
  29.1 14.7 %collective-permute-start.3 = (bf16[288,1024]{1,0:T(8,128)(2,1)S(1)}, bf16[288,1024]{1,0:T(8,128)(2,1)}, u32[]{:S(2)}, u32[]{:S(2)}) collective-permute-start(bf16[288,1024]{1,0:T(8,128)(2,1)S(1)} %collective-permute-done.1.p2), channel_id=1, source_target_pairs={{0,2},{1,3},{2,4},{3,5},{4,6},{5,7},{6,8},{7,9},{8,10},{9,11},{10,... | collective-permute-start | bytes 1769480 | tf_op jit(solution)/shard_map/ppermute | solution.py:460
  33.7 25.7 %collective-permute-start.4 = (bf16[528,1024]{1,0:T(8,128)(2,1)}, bf16[528,1024]{1,0:T(8,128)(2,1)S(1)}, u32[]{:S(2)}, u32[]{:S(2)}) collective-permute-start(bf16[528,1024]{1,0:T(8,128)(2,1)} %get-tuple-element.49.c0.refs_0_), channel_id=1, source_target_pairs={{2,0},{3,1},{4,2},{5,3},{6,4},{7,5},{8,6},{9,7},{10,8},{11,9},{12,... | collective-permute-start | bytes 3244040 | tf_op jit(solution)/shard_map/ppermute | solution.py:460
  43.9 15.5 %collective-permute-start.5 = (bf16[288,1024]{1,0:T(8,128)(2,1)S(1)}, bf16[288,1024]{1,0:T(8,128)(2,1)}, u32[]{:S(2)}, u32[]{:S(2)}) collective-permute-start(bf16[288,1024]{1,0:T(8,128)(2,1)S(1)} %broadcast_select_fusion.1), channel_id=1, source_target_pairs={{0,1},{1,0},{2,3},{3,2},{4,5},{5,4},{6,7},{7,6},{8,9},{9,8},{10,11... | collective-permute-start | bytes 1769480 | tf_op jit(solution)/shard_map/ppermute | solution.py:465
  60.7 68.3 %collective-permute-start.7 = (bf16[528,1024]{1,0:T(8,128)(2,1)}, bf16[528,1024]{1,0:T(8,128)(2,1)S(1)}, u32[]{:S(2)}, u32[]{:S(2)}) collective-permute-start(bf16[528,1024]{1,0:T(8,128)(2,1)} %broadcast_select_fusion), channel_id=1, source_target_pairs={{0,1},{1,0},{2,3},{3,2},{4,5},{5,4},{6,7},{7,6},{8,9},{9,8},{10,11... | collective-permute-start | bytes 3244040 | tf_op jit(solution)/shard_map/ppermute | solution.py:465
  61.0 39.4 %collective-permute-start.6 = (bf16[384,1024]{1,0:T(8,128)(2,1)S(1)}, bf16[384,1024]{1,0:T(8,128)(2,1)S(1)}, u32[]{:S(2)}, u32[]{:S(2)}) collective-permute-start(bf16[384,1024]{1,0:T(8,128)(2,1)S(1)} %pad_maximum_fusion), channel_id=1, source_target_pairs={{0,1},{1,0},{2,3},{3,2},{4,5},{5,4},{6,7},{7,6},{8,9},{9,8},{10,11... | collective-permute-start | bytes 2359304 | tf_op jit(solution)/shard_map/ppermute | solution.py:465
  119.6 22.7 %collective-permute-start.11 = (f32[24,384]{1,0:T(8,128)}, f32[24,384]{1,0:T(8,128)S(1)}, u32[]{:S(2)}, u32[]{:S(2)}) collective-permute-start(f32[24,384]{1,0:T(8,128)} %get-tuple-element.60.s2), channel_id=1, source_target_pairs={{0,1},{1,2},{2,3},{3,4},{4,5},{5,6},{6,7},{7,8},{8,9},{9,10},{10,1... | collective-permute-start | bytes 110600 | tf_op jit(solution)/shard_map/ppermute | solution.py:460
  121.7 22.9 %collective-permute-start.12 = (f32[24,384]{1,0:T(8,128)}, f32[24,384]{1,0:T(8,128)S(1)}, u32[]{:S(2)}, u32[]{:S(2)}) collective-permute-start(f32[24,384]{1,0:T(8,128)} %get-tuple-element.60.s2), channel_id=1, source_target_pairs={{0,2},{1,3},{2,4},{3,5},{4,6},{5,7},{6,8},{7,9},{8,10},{9,11},{10,... | collective-permute-start | bytes 110600 | tf_op jit(solution)/shard_map/ppermute | solution.py:460
  126.4 18.2 %collective-permute-start.14 = (f32[24,384]{1,0:T(8,128)}, f32[24,384]{1,0:T(8,128)S(1)}, u32[]{:S(2)}, u32[]{:S(2)}) collective-permute-start(f32[24,384]{1,0:T(8,128)} %get-tuple-element.58.s0), channel_id=1, source_target_pairs={{1,0},{2,1},{3,2},{4,3},{5,4},{6,5},{7,6},{8,7},{9,8},{10,9},{11,1... | collective-permute-start | bytes 110600 | tf_op jit(solution)/shard_map/ppermute | solution.py:460
  127.7 17.0 %collective-permute-start.15 = (f32[24,384]{1,0:T(8,128)}, f32[24,384]{1,0:T(8,128)S(1)}, u32[]{:S(2)}, u32[]{:S(2)}) collective-permute-start(f32[24,384]{1,0:T(8,128)} %get-tuple-element.58.s0), channel_id=1, source_target_pairs={{2,0},{3,1},{4,2},{5,3},{6,4},{7,5},{8,6},{9,7},{10,8},{11,9},{12,... | collective-permute-start | bytes 110600 | tf_op jit(solution)/shard_map/ppermute | solution.py:460
  167.0 24.1 %all-to-all-start = ((bf16[4,144,1280]{2,1,0:T(8,128)(2,1)}), bf16[4,144,1280]{2,1,0:T(8,128)(2,1)S(1)}, u32[]{:S(2)}, u32[]{:S(2)}) async-start(bf16[4,144,1280]{2,1,0:T(8,128)(2,1)} %bitcast.10), calls=%async_computation | async-start | bytes 2949120 | tf_op jit(solution)/shard_map/all_to_all | solution.py:481
  177.9 20.4 %collective-permute-start.18 = (bf16[384,1024]{1,0:T(8,128)(2,1)S(1)}, bf16[384,1024]{1,0:T(8,128)(2,1)S(1)}, u32[]{:S(2)}, u32[]{:S(2)}) collective-permute-start(bf16[384,1024]{1,0:T(8,128)(2,1)S(1)} %copy-done.14), channel_id=1, source_target_pairs={{0,1},{1,0},{2,3},{3,2},{4,5},{5,4},{6,7},{7,6},{8,9},{9,8},{10,11... | collective-permute-start | bytes 2359304 | tf_op jit(solution)/shard_map/ppermute | solution.py:465
  177.9 13.5 %collective-permute-start.16 = (f32[8,1024]{1,0:T(8,128)S(1)}, f32[8,1024]{1,0:T(8,128)S(1)}, u32[]{:S(2)}, u32[]{:S(2)}) collective-permute-start(f32[8,1024]{1,0:T(8,128)S(1)} %copy-done.22), channel_id=1, source_target_pairs={{1,0},{2,1},{3,2},{4,3},{5,4},{6,5},{7,6},{8,7},{9,8},{10,9},{11,1... | collective-permute-start | bytes 98312 | tf_op jit(solution)/shard_map/ppermute | solution.py:460
  195.6 7.8 %collective-permute-start.17 = (bf16[144,1024]{1,0:T(8,128)(2,1)}, bf16[144,1024]{1,0:T(8,128)(2,1)}, u32[]{:S(2)}, u32[]{:S(2)}) collective-permute-start(bf16[144,1024]{1,0:T(8,128)(2,1)} %mid_cotangent.1.refs_5_), channel_id=1, source_target_pairs={{2,0},{3,1},{4,2},{5,3},{6,4},{7,5},{8,6},{9,7},{10,8},{11,9},{12,... | collective-permute-start | bytes 884744 | tf_op jit(solution)/shard_map/ppermute | solution.py:460
  203.4 20.2 %all-to-all-start.1 = ((bf16[16,16,1024]{2,1,0:T(8,128)(2,1)}), bf16[16,16,1024]{2,1,0:T(8,128)(2,1)S(1)}, u32[]{:S(2)}, u32[]{:S(2)}) async-start(bf16[16,16,1024]{2,1,0:T(8,128)(2,1)} %bitcast.12), calls=%async_computation.1 | async-start | bytes 1048576 | tf_op jit(solution)/shard_map/all_to_all | solution.py:481
  210.3 11.3 %collective-permute-start.8 = (bf16[144,1024]{1,0:T(8,128)(2,1)S(1)}, bf16[144,1024]{1,0:T(8,128)(2,1)S(1)}, u32[]{:S(2)}, u32[]{:S(2)}) collective-permute-start(bf16[144,1024]{1,0:T(8,128)(2,1)S(1)} %slice.29), channel_id=1, source_target_pairs={{2,0},{3,1},{4,2},{5,3},{6,4},{7,5},{8,6},{9,7},{10,8},{11,9},{12,... | collective-permute-start | bytes 884744 | tf_op jit(solution)/shard_map/ppermute | solution.py:460
  213.9 37.9 %collective-permute-start.22 = (bf16[384,1024]{1,0:T(8,128)(2,1)}, bf16[384,1024]{1,0:T(8,128)(2,1)}, u32[]{:S(2)}, u32[]{:S(2)}) collective-permute-start(bf16[384,1024]{1,0:T(8,128)(2,1)} %fusion.2), channel_id=1, source_target_pairs={{0,2},{1,3},{2,4},{3,5},{4,6},{5,7},{6,8},{7,9},{8,10},{9,11},{10,... | collective-permute-start | bytes 2359304 | tf_op jit(solution)/shard_map/ppermute | solution.py:460
  218.8 7.8 %collective-permute-start.20 = (bf16[144,1024]{1,0:T(8,128)(2,1)}, bf16[144,1024]{1,0:T(8,128)(2,1)}, u32[]{:S(2)}, u32[]{:S(2)}) collective-permute-start(bf16[144,1024]{1,0:T(8,128)(2,1)} %collective-permute-done.17.refs_7_), channel_id=1, source_target_pairs={{2,0},{3,1},{4,2},{5,3},{6,4},{7,5},{8,6},{9,7},{10,8},{11,9},{12,... | collective-permute-start | bytes 884744 | tf_op jit(solution)/shard_map/ppermute | solution.py:460
  222.4 37.4 %collective-permute-start.9 = (bf16[144,1024]{1,0:T(8,128)(2,1)}, bf16[144,1024]{1,0:T(8,128)(2,1)}, u32[]{:S(2)}, u32[]{:S(2)}) collective-permute-start(bf16[144,1024]{1,0:T(8,128)(2,1)} %broadcast_select_fusion.4), channel_id=1, source_target_pairs={{0,1},{1,0},{2,3},{3,2},{4,5},{5,4},{6,7},{7,6},{8,9},{9,8},{10,11... | collective-permute-start | bytes 884744 | tf_op jit(solution)/shard_map/ppermute | solution.py:465
  228.5 31.3 %collective-permute-start.19 = (bf16[144,1024]{1,0:T(8,128)(2,1)}, bf16[144,1024]{1,0:T(8,128)(2,1)S(1)}, u32[]{:S(2)}, u32[]{:S(2)}) collective-permute-start(bf16[144,1024]{1,0:T(8,128)(2,1)} %get-tuple-element.82), channel_id=1, source_target_pairs={{0,1},{1,0},{2,3},{3,2},{4,5},{5,4},{6,7},{7,6},{8,9},{9,8},{10,11... | collective-permute-start | bytes 884744 | tf_op jit(solution)/shard_map/ppermute | solution.py:465
  230.0 29.9 %collective-permute-start.21 = (bf16[144,1024]{1,0:T(8,128)(2,1)}, bf16[144,1024]{1,0:T(8,128)(2,1)}, u32[]{:S(2)}, u32[]{:S(2)}) collective-permute-start(bf16[144,1024]{1,0:T(8,128)(2,1)} %get-tuple-element.81), channel_id=1, source_target_pairs={{0,1},{1,0},{2,3},{3,2},{4,5},{5,4},{6,7},{7,6},{8,9},{9,8},{10,11... | collective-permute-start | bytes 884744 | tf_op jit(solution)/shard_map/ppermute | solution.py:465
  230.7 28.4 %all-to-all-start.2 = ((f32[4,16,1024]{2,1,0:T(8,128)}), f32[4,16,1024]{2,1,0:T(8,128)S(1)}, u32[]{:S(2)}, u32[]{:S(2)}) async-start(f32[4,16,1024]{2,1,0:T(8,128)} %bitcast.19), calls=%async_computation.2 | async-start | bytes 524288 | tf_op jit(solution)/shard_map/all_to_all | solution.py:481
  (26 other events, 230.3 us)

commit v6 on v5

--- a/solution.py
+++ b/solution.py
@@ -21,6 +21,7 @@
 CQ = F + S + 16
 TILES = F // S
 TILE_W = WIN + S
+STEP = 2
 SCALE = E ** (-0.5)
 LOG2 = SCALE * math.log2(math.e)
 NEG = -1e30
@@ -56,7 +57,39 @@
 
 
 def head_spec(rows):
-    return pl.BlockSpec((rows, E), lambda h: (0, h))
+    return pl.BlockSpec((rows, STEP * E), lambda h: (0, h))
+
+
+def by_head(body, in_specs, out_specs):
+    split = [spec.block_shape is not None and spec.block_shape[-1] in (STEP * E, pl.Element(STEP * E)) for spec in in_specs + out_specs]
+
+    def run(*refs):
+        for sub in range(STEP):
+            views = [ref.at[:, pl.ds(sub * E, E)] if cut else ref for ref, cut in zip(refs, split)]
+            body(sub, pl.program_id(0) * STEP + sub, *views, *refs[len(split) :])
+
+    return run
+
+
+def call(body, name, flops, bytes_accessed, in_specs, out_specs, out_shape, scratch_shapes):
+    return pl.pallas_call(
+        by_head(body, in_specs, out_specs),
+        grid=(H // STEP,),
+        in_specs=in_specs,
+        out_specs=out_specs,
+        out_shape=out_shape,
+        scratch_shapes=scratch_shapes,
+        cost_estimate=pl.CostEstimate(flops=flops, bytes_accessed=bytes_accessed, transcendentals=0),
+        name=name,
+    )
+
+
+def on_first(sub):
+    return pl.when(pl.program_id(0) == 0) if sub == 0 else lambda build: None
+
+
+def on_last(sub):
+    return pl.when(pl.program_id(0) == H // STEP - 1) if sub == STEP - 1 else lambda build: None
 
 
 def whole_spec(shape):
@@ -105,10 +138,10 @@
     return [p4[...], p3[...], p2[...], near, p0[...]]
 
 
-def mid_fwd_body(flag, q, p4, p3, p2, first, second, p0, out, att, stat, bias):
+def mid_fwd_body(sub, head, flag, q, p4, p3, p2, first, second, p0, out, att, stat, bias):
     pays = pair_slabs(flag, p4, p3, p2, first, second, p0)
 
-    @pl.when(pl.program_id(0) == 0)
+    @on_first(sub)
     def _():
         def ids(n):
             return pays[n][2 * S : 2 * S + 16].astype(F32)[0:1]
@@ -143,9 +176,11 @@
 
 
 def mid_forward(flag, q, pays):
-    return pl.pallas_call(
+    return call(
         mid_fwd_body,
-        grid=(H,),
+        "mid_forward",
+        700_000_000,
+        4_000_000,
         in_specs=[FLAG, head_spec(S)] + PAY_SPECS,
         out_specs=[head_spec(S + 16), head_spec(S), head_spec(8)],
         out_shape=[
@@ -154,8 +189,6 @@
             jax.ShapeDtypeStruct((8, WIDTH), F32),
         ],
         scratch_shapes=[pltpu.VMEM((S + 16, SPAN_M), F32)],
-        cost_estimate=pl.CostEstimate(flops=700_000_000, bytes_accessed=4_000_000, transcendentals=0),
-        name="mid_forward",
     )(flag, q, *pays)
 
 
@@ -178,16 +211,17 @@
         bias[t] = jnp.where(ok, 0.0, NEG)
 
 
+DOCS = pl.BlockSpec((16, S), lambda h: ((F + S) // 16, 0))
+
+
 def doc_row(ref):
-    return ref[F + S : CQ, 0:S][0:1]
-
-
-def stats_body(k, base, mid, w, q0, q2, c0, c2, values, s0, s2, bias, ext, part):
-    head = pl.program_id(0)
-
-    @pl.when(head == 0)
-    def _():
-        full_mask(bias, [doc_row(ref) for ref in (c0, c0, c2)])
+    return ref[...][0:1]
+
+
+def stats_body(sub, head, k, base, mid, w, q0, q2, c0, c2, d0, d2, values, s0, s2, bias, ext, part):
+    @on_first(sub)
+    def _():
+        full_mask(bias, [doc_row(ref) for ref in (d0, d0, d2)])
 
     linked = dot_nn(mid[...], w[...])
     for n in range(2, 5):
@@ -206,7 +240,7 @@
             pieces += [rows[j]] + ([jnp.full((1, F - last), empty, F32)] if last < F else [])
             part[t, pl.ds(j * H + head, 1), :] = jnp.concatenate(pieces, axis=1)
 
-    @pl.when(head == H - 1)
+    @on_last(sub)
     def _():
         for out, cols in ((s0, slice(0, F)), (s2, slice(F, 2 * F))):
             merge_into(out, part, cols)
@@ -226,12 +260,10 @@
         out[j * H : (j + 1) * H, :] = merged[j]
 
 
-def stats_next_body(flag, k, v, q1a, q1b, c0, c1, s1, bias, part):
-    head = pl.program_id(0)
-
-    @pl.when(head == 0)
-    def _():
-        full_mask(bias, [doc_row(ref) for ref in (c0, c1, c1)])
+def stats_next_body(sub, head, flag, k, v, q1a, q1b, c1, d0, d1, s1, bias, part):
+    @on_first(sub)
+    def _():
+        full_mask(bias, [doc_row(ref) for ref in (d0, d1, d1)])
 
     queries = pick(flag, q1a, q1b, F)
     for t in range(TILES):
@@ -241,7 +273,7 @@
         for j in range(3):
             part[t, pl.ds(j * H + head, 1), :] = rows[j]
 
-    @pl.when(head == H - 1)
+    @on_last(sub)
     def _():
         merge_into(s1, part, slice(0, F))
 
@@ -260,12 +292,14 @@
 
 def full_stats(k, base, mid, w, q0, q2, c0, c2):
     stat = jax.ShapeDtypeStruct((3 * H, F), F32)
-    return pl.pallas_call(
+    return call(
         stats_body,
-        grid=(H,),
+        "full_stats",
+        2_000_000_000,
+        8_000_000,
         in_specs=[head_spec(F), head_spec(F), whole_spec((S + 16, WIDTH)), head_spec(WIDTH)]
-        + [head_spec(F)] * 2
-        + [head_spec(CQ)] * 2,
+        + [head_spec(F)] * 4
+        + [DOCS] * 2,
         out_specs=[head_spec(F)] + [whole_spec((3 * H, F))] * 2,
         out_shape=[jax.ShapeDtypeStruct((F, WIDTH), BF16), stat, stat],
         scratch_shapes=[
@@ -273,36 +307,32 @@
             pltpu.VMEM((400, E), F32),
             pltpu.VMEM((TILES, 3 * H, 2 * F), F32),
         ],
-        cost_estimate=pl.CostEstimate(flops=2_000_000_000, bytes_accessed=8_000_000, transcendentals=0),
-        name="full_stats",
-    )(k, base, mid, w, q0, q2, c0, c2)
+    )(k, base, mid, w, q0, q2, c0, c2, c0, c2)
 
 
 def next_stats(flag, k, v, q1a, q1b, c0, c1):
-    return pl.pallas_call(
+    return call(
         stats_next_body,
-        grid=(H,),
-        in_specs=[FLAG] + [head_spec(F)] * 4 + [head_spec(CQ)] * 2,
-        out_specs=whole_spec((3 * H, F)),
-        out_shape=jax.ShapeDtypeStruct((3 * H, F), F32),
+        "next_stats",
+        1_000_000_000,
+        6_000_000,
+        in_specs=[FLAG] + [head_spec(F)] * 5 + [DOCS] * 2,
+        out_specs=[whole_spec((3 * H, F))],
+        out_shape=[jax.ShapeDtypeStruct((3 * H, F), F32)],
         scratch_shapes=[
             pltpu.VMEM((TILES, S, TILE_W), F32),
             pltpu.VMEM((TILES, 3 * H, F), F32),
         ],
-        cost_estimate=pl.CostEstimate(flops=1_000_000_000, bytes_accessed=6_000_000, transcendentals=0),
-        name="next_stats",
-    )(flag, k, v, q1a, q1b, c0, c1)
+    )(flag, k, v, q1a, q1b, c1, c0, c1)[0]
 
 
 def grads_body(
-    flag, k, v, q0, q1a, q1b, q2, c0, c1, c2, s0, s1, s2, up1, up1_far, up2, down1, down1_far, down2,
+    sub, head, flag, k, v, q0, q1a, q1b, q2, c0, c1, c2, d0, d1, d2, s0, s1, s2, up1, up1_far, up2, down1, down1_far, down2,
     dk, dv, dq0, dq1, dq2, sums, link, tail, bias, ext, glob, kept,
 ):
-    head = pl.program_id(0)
-
-    @pl.when(head == 0)
-    def _():
-        full_mask(bias, [doc_row(ref) for ref in (c0, c1, c2)])
+    @on_first(sub)
+    def _():
+        full_mask(bias, [doc_row(ref) for ref in (d0, d1, d2)])
 
         def triple(ref):
             peak, total, dots = (ref[j * H : (j + 1) * H, :] for j in range(3))
@@ -344,12 +374,14 @@
 
 
 def full_grads(flag, k, v, qs, cs, stats):
-    return pl.pallas_call(
+    return call(
         grads_body,
-        grid=(H,),
+        "full_grads",
+        8_000_000_000,
+        14_000_000,
         in_specs=[FLAG, head_spec(F), head_spec(F)]
-        + [head_spec(F)] * 4
-        + [head_spec(CQ)] * 3
+        + [head_spec(F)] * 7
+        + [DOCS] * 3
         + [whole_spec(s.shape) for s in stats],
         out_specs=[head_spec(F)] * 5 + [head_spec(S), head_spec(S + 16), head_spec(8)],
         out_shape=[
@@ -368,40 +400,60 @@
             pltpu.VMEM((3 * H, SPAN_F), F32),
             pltpu.VMEM((F, SPAN_F), BF16),
         ],
-        cost_estimate=pl.CostEstimate(flops=8_000_000_000, bytes_accessed=14_000_000, transcendentals=0),
-        name="full_grads",
-    )(flag, k, v, *qs, *cs, *stats)
-
-
-def mid_cot_body(sums, tail, w, att, stat, out):
-    total = sums[...] + jnp.where(iota((S, WIDTH), 0) == S - 1, tail[0:1, :], 0.0)
-    grad = dot_nt(total.astype(BF16), w[...]).astype(BF16)
+    )(flag, k, v, *qs, *cs, *cs, *stats)
+
+
+def mid_cot_body(sub, head, w, att, stat, sums, tail, out, whole):
+    @on_first(sub)
+    def _():
+        total = sums[...] + jnp.where(iota((S, WIDTH), 0) == S - 1, tail[0:1, :], 0.0)
+        whole[...] = total.astype(BF16)
+
+    grad = dot_nt(whole[...], w[...]).astype(BF16)
     out[0:S, :] = grad
-    weighed = grad.astype(F32) * att[...]
-    for h in range(H):
-        cols = slice(h * E, (h + 1) * E)
-        delta = jnp.sum(jnp.transpose(weighed[:, cols]), axis=0, keepdims=True)
-        rows = [*split3(stat[0:1, cols]), *split3(stat[1:2, cols]), *split3(delta)]
-        rows = [row.astype(F32) for row in rows] + [jnp.zeros((7, E), F32)]
-        out[S : S + 16, cols] = jnp.concatenate(rows, axis=0).astype(BF16)
+    delta = jnp.sum(jnp.transpose(grad.astype(F32) * att[...]), axis=0, keepdims=True)
+    rows = [*split3(stat[0:1, :]), *split3(stat[1:2, :]), *split3(delta)]
+    rows = [row.astype(F32) for row in rows] + [jnp.zeros((7, E), F32)]
+    out[S : S + 16, :] = jnp.concatenate(rows, axis=0).astype(BF16)
 
 
 def mid_cotangent(sums, tail, w, att, stat):
+    body = mid_cot_body
+
+    def run(w_ref, *refs):
+        for sub in range(STEP):
+            cols = pl.ds(sub * E, E)
+            att_ref, stat_ref, sums_ref, tail_ref, out_ref, whole = refs
+            body(
+                sub, None, w_ref.at[cols, :], att_ref.at[:, cols], stat_ref.at[:, cols],
+                sums_ref, tail_ref, out_ref.at[:, cols], whole,
+            )
+
     return pl.pallas_call(
-        mid_cot_body,
+        run,
+        grid=(H // STEP,),
+        in_specs=[
+            pl.BlockSpec((STEP * E, WIDTH), lambda h: (h, 0)),
+            head_spec(S),
+            head_spec(8),
+            whole_spec((S, WIDTH)),
+            whole_spec((8, WIDTH)),
+        ],
+        out_specs=head_spec(S + 16),
         out_shape=jax.ShapeDtypeStruct((S + 16, WIDTH), BF16),
+        scratch_shapes=[pltpu.VMEM((S, WIDTH), BF16)],
         cost_estimate=pl.CostEstimate(flops=600_000_000, bytes_accessed=4_000_000, transcendentals=0),
         name="mid_cotangent",
-    )(sums, tail, w, att, stat)
-
-
-def mid_bwd_body(flag, p4, p3, p2, first, second, p0, *refs):
-    ms = [ref[F:CQ, :] for ref in refs[0:3]] + [ref[...] for ref in refs[3:5]]
+    )(w, att, stat, sums, tail)
+
+
+def mid_bwd_body(sub, head, flag, p4, p3, p2, first, second, p0, *refs):
+    ms = [ref[...] for ref in refs[0:5]]
     gs = refs[5:10]
     dq, dk, dv, back, fore = refs[10:]
     pays = pair_slabs(flag, p4, p3, p2, first, second, p0)
 
-    @pl.when(pl.program_id(0) == 0)
+    @on_first(sub)
     def _():
         mine = p0[2 * S : 2 * S + 16, :].astype(F32)[0:1]
         column = to_column(mine, S)
@@ -441,16 +493,19 @@
     dv[...] = dot_nn(probs.astype(BF16), cots).astype(BF16)
 
 
+QUERY_ROWS = pl.BlockSpec((pl.Element(S + 16), pl.Element(STEP * E)), lambda h: (F, h * STEP * E))
+
+
 def mid_backward(flag, pays, ms, gs):
-    return pl.pallas_call(
+    return call(
         mid_bwd_body,
-        grid=(H,),
-        in_specs=[FLAG] + PAY_SPECS + [head_spec(CQ)] * 3 + [head_spec(S + 16)] * 7,
+        "mid_backward",
+        3_000_000_000,
+        6_000_000,
+        in_specs=[FLAG] + PAY_SPECS + [QUERY_ROWS] * 3 + [head_spec(S + 16)] * 7,
         out_specs=[head_spec(S)] * 3,
         out_shape=[jax.ShapeDtypeStruct((S, WIDTH), BF16)] * 3,
         scratch_shapes=[pltpu.VMEM((SPAN_M, S), F32), pltpu.VMEM((S, SPAN_M), F32)],
-        cost_estimate=pl.CostEstimate(flops=3_000_000_000, bytes_accessed=6_000_000, transcendentals=0),
-        name="mid_backward",
     )(flag, *pays, *ms, *gs)
 
 
@@ -499,49 +554,47 @@
     kv2, kv4 = together(kv2, kv4)
     kv3 = swap(jnp.where(upper, kv4, kv2), "ctx", 1)
     cq2 = shift(late_cq, -2)
-    cq2, kv3_late = together(cq2, kv3)
+    cq2, got_b_late, kv3_late = together(cq2, got_b, kv3)
     cq1 = swap(jnp.where(upper, late_cq, cq2), "ctx", 1)
 
     pays = (kv4, kv3, kv2, got_a, got_b, own_kv)
     mid_ext, attended, mid_stat = mid_forward(flag, q_m, pays)
+    qm2 = cq2[F:]
+    qm4, mid_ext = together(shift(qm2, -2), mid_ext)
     values, s0, s2 = full_stats(k_f, v_base[0], mid_ext, w_link, q_f, qf2, late_cq, cq2)
     up2, up1_far = shift(s2, 2), shift(s2, 1)
     down2, down1_far = shift(s0, -2), shift(s0, -1)
-    s1 = next_stats(flag, k_f, values, got_b, got_a, late_cq, cq1)
+    s1 = next_stats(flag, k_f, values, got_b_late, got_a, late_cq, cq1)
     up1, down1 = shift(s1, 1), shift(s1, -1)
 
-    qm2, s1 = together(cq2[F:], s1)
-    qm4 = shift(qm2, -2)
     qm3 = swap(jnp.where(upper, qm2, qm4), "ctx", 1)
-    qs, cs = (q_f, got_b, got_a, qf2), (late_cq, cq1, cq2)
+    values, qm3 = together(values, qm3)
+    qs, cs = (q_f, got_b_late, got_a, qf2), (late_cq, cq1, cq2)
     dk_f, dv_f, dq0, dq1, dq2, sums, sum_ext, tail = full_grads(
         flag, k_f, values, qs, cs, (s0, s1, s2, up1, up1_far, up2, down1, down1_far, down2)
     )
 
-    next_tail = shift(tail, -1)
-    near = swap(dq1, "ctx", 1)
+    sums, next_tail, sum_ext, dq1, dq2 = together(sums, shift(tail, -1), sum_ext, dq1, dq2)
+    cot_m = mid_cotangent(sums, next_tail, w_link, attended, mid_stat)
+    cot_m, sum_ext, dq1, dq2 = together(cot_m, sum_ext, dq1, dq2)
+    g2 = shift(cot_m, -2)
+    near, far = shift(dq1, 1), shift(dq2, 2)
     parts = [jnp.concatenate([sum_ext, mid_ext[:, n * 256 : (n + 1) * 256]], axis=1) for n in range(4)]
     parts = exchange(jnp.concatenate(parts, axis=0), "ctx", X_GROUPS)
-    sums, parts = together(sums, parts)
-    cot_m = mid_cotangent(sums, next_tail, w_link, attended, mid_stat)
-    g2 = shift(cot_m, -2)
     term = dot_tn(parts[:, WIDTH:], parts[:, :WIDTH]).astype(BF16)
-    term, g2, near = together(term, g2, near)
+    term, g2 = together(term, g2)
     g1 = swap(jnp.where(upper, cot_m, g2), "ctx", 1)
     g4 = shift(g2, -2)
     total = jnp.sum(exchange(term, "ctx", YZ_GROUPS).astype(F32).reshape(16, 16, WIDTH), axis=0)
-    total, g4 = together(total, g4)
-    g3 = swap(jnp.where(upper, g2, g4), "ctx", 1)
+    g2_late, g4 = together(g2, g4)
+    g3 = swap(jnp.where(upper, g2_late, g4), "ctx", 1)
     every = exchange(jnp.concatenate([total] * 4, axis=0), "dp", None)
     factor = float(lax.axis_size("dp") * lax.axis_size("ctx") * F) ** (-0.5)
     grad_link = jnp.sum(every.reshape(4, 16, WIDTH), axis=0) * factor
     pays = (kv4, kv3_late, kv2, got_a, got_b, own_kv)
     dq_m, dk_m, dv_m = mid_backward(flag, pays, (late_cq, cq1, cq2, qm3, qm4), (cot_m, g1, g2, g3, g4))
 
-    near = near.astype(F32)
-    passed = jnp.where(upper, dq2.astype(F32), dq2.astype(F32) + near)
-    far = shift(passed.astype(BF16), 2).astype(F32)
-    dq_f = (dq0 + far + jnp.where(upper, near, 0.0)).astype(BF16)
+    dq_f = (dq0 + far.astype(F32) + near.astype(F32)).astype(BF16)
     return (dq_m[None], dk_m[None], dv_m[None], dq_f[None], dk_f[None], dv_f[None], grad_link)
 
 

time: 275 us -> 246 us (0.89)
  waiting for transfers between devices: 106 us -> 71.6 us
  starting transfers between devices: 83.2 us -> 105 us
  Pallas kernels: 58.6 us -> 50.8 us
  local copies, waits for them, and re-layouts: 6.52 us -> 3.56 us
    ppermute x8 -> x7, waiting for transfers between devices: 38 us -> 12.4 us  [swap(): return lax.ppermute(value, axis, [(n, n ^ bit) for n in range(count)])]
    ppermute x15 -> x16, waiting for transfers between devices: 51.3 us -> 37.4 us  [shift(): lax.ppermute(value, 'ctx', [(n, n + steps) for n in range(first, last)])]
    all_to_all x3, starting transfers between devices: 38.9 us -> 50.4 us  [exchange(): lax.all_to_all(value, axis, 0, 0, axis_index_groups=groups, tiled=True)]
    pallas_call x6, Pallas kernels: 54.7 us -> 46.8 us  [the longest x1 14.1 us: full_grads(): call(grads_body, 'full_grads', 8000000000, 14000000, in_specs=[FLAG, head...]
    ppermute x8 -> x7, starting transfers between devices: 7.67 us -> 12.9 us  [swap(): return lax.ppermute(value, axis, [(n, n ^ bit) for n in range(count)])]
    all_to_all x3, waiting for transfers between devices: 16.8 us -> 21.8 us  [exchange(): lax.all_to_all(value, axis, 0, 0, axis_index_groups=groups, tiled=True)]
    ppermute x15 -> x16, starting transfers between devices: 36.6 us -> 41.2 us  [shift(): lax.ppermute(value, 'ctx', [(n, n + steps) for n in range(first, last)])]
  transfers between devices with their start and end apart: 26 -> 26, of which waited for: 12 -> 11; matrix products, arithmetic and copies ran while one was open for 4% -> 3% of each run, Pallas kernels for 11% -> 13%
where the time goes in v6:
time: 246 us; the launch traced here: 244 us
  starting transfers between devices  105 us (43%)
  waiting for transfers between devices  71.6 us (29%)
  Pallas kernels  50.8 us (21%)
  other arithmetic  11.2 us (5%)
  local copies, waits for them, and re-layouts  3.56 us (1%)
    all_to_all x3, starting transfers between devices, exchange(): lax.all_to_all(value, axis, 0, 0, axis_index_groups=groups, tiled=True)  50.4 us
    ppermute x16, starting transfers between devices, shift(): lax.ppermute(value, 'ctx', [(n, n + steps) for n in range(first, last)])  41.2 us
    ppermute x16, waiting for transfers between devices, shift(): lax.ppermute(value, 'ctx', [(n, n + steps) for n in range(first, last)])  37.4 us
    all_to_all x3, waiting for transfers between devices, exchange(): lax.all_to_all(value, axis, 0, 0, axis_index_groups=groups, tiled=True)  21.8 us
    pallas_call x1, Pallas kernels, full_grads(): call(grads_body, 'full_grads', 8000000000, 14000000, in_specs=[FLAG, head...  14.1 us
    ppermute x7, starting transfers between devices, swap(): return lax.ppermute(value, axis, [(n, n ^ bit) for n in range(count)])  12.9 us
    ppermute x7, waiting for transfers between devices, swap(): return lax.ppermute(value, axis, [(n, n ^ bit) for n in range(count)])  12.4 us
    pallas_call x1, Pallas kernels, mid_backward(): call(mid_bwd_body, 'mid_backward', 3000000000, 6000000, in_specs=[FLAG] +...  8.16 us
  transfers between devices with their start and end apart: 26, of which 11 were waited for; matrix products, arithmetic and copies ran while one was open for 3% of the time, Pallas kernels for 13%

profile of v6, /device:TPU:1, one launch (start us, length us, event | category | flops | bytes accessed | tf_op | source)
XLA Modules:
  0.0 244.2 jit_solution(7558726374046516655)
XLA Ops:
  3.2 4.0 %pack.1 = (bf16[288,1024]{1,0:T(8,128)(2,1)}, bf16[528,1024]{1,0:T(8,128)(2,1)}, bf16[384,1024]{1,0:T(8,128)(2,1)}) custom-call(s32[1]{0:T(128)} %bitcast.flag.refs_0_, bf16[128,1024]{1,0:T(8,128)(2,1)} %bitcast.31, bf16[128,1024]{1,0:T(8,128)(2,1)} %bitcast.36, bf16[128,1024]{1,0:T(8,128)(2,1)} %bitcast.37, bf16[16,256]{1,0:T(8,128)(2,1)} %broadcast_in_dim.23.ids, ...), custom_call_target="tpu_custom_call" | custom-call | tf_op jit(solution)/shard_map/pack/pallas_call | solution.py:118
  9.3 4.2 %collective-permute-start.1 = (bf16[288,1024]{1,0:T(8,128)(2,1)}, bf16[288,1024]{1,0:T(8,128)(2,1)S(1)}, u32[]{:S(2)}, u32[]{:S(2)}) collective-permute-start(bf16[288,1024]{1,0:T(8,128)(2,1)} %get-tuple-element.54.refs_7_.refs_6_), channel_id=1, source_target_pairs={{0,2},{1,3},{2,4},{3,5},{4,6},{5,7},{6,8},{7,9},{8,10},{9,11},{10,... | collective-permute-start | bytes 1769480 | tf_op jit(solution)/shard_map/ppermute | solution.py:515
  13.5 11.6 %collective-permute-done.1.refs_4_.refs_3_ = bf16[288,1024]{1,0:T(8,128)(2,1)S(1)} collective-permute-done((bf16[288,1024]{1,0:T(8,128)(2,1)}, bf16[288,1024]{1,0:T(8,128)(2,1)S(1)}, u32[]{:S(2)}, u32[]{:S(2)}) %collective-permute-start.1) | collective-permute-done | bytes 589856 | tf_op jit(solution)/shard_map/ppermute | solution.py:515
  26.5 4.9 %collective-permute-start.3 = (bf16[288,1024]{1,0:T(8,128)(2,1)S(1)}, bf16[288,1024]{1,0:T(8,128)(2,1)}, u32[]{:S(2)}, u32[]{:S(2)}) collective-permute-start(bf16[288,1024]{1,0:T(8,128)(2,1)S(1)} %collective-permute-done.1.refs_4_.refs_3_), channel_id=1, source_target_pairs={{0,2},{1,3},{2,4},{3,5},{4,6},{5,7},{6,8},{7,9},{8,10},{9,11},{10,... | collective-permute-start | bytes 1769480 | tf_op jit(solution)/shard_map/ppermute | solution.py:515
  35.0 5.5 %collective-permute-done.3.refs_2_.refs_1_ = bf16[288,1024]{1,0:T(8,128)(2,1)} collective-permute-done((bf16[288,1024]{1,0:T(8,128)(2,1)S(1)}, bf16[288,1024]{1,0:T(8,128)(2,1)}, u32[]{:S(2)}, u32[]{:S(2)}) %collective-permute-start.3) | collective-permute-done | bytes 589856 | tf_op jit(solution)/shard_map/ppermute | solution.py:515
  40.5 4.1 %collective-permute-start.6 = (bf16[288,1024]{1,0:T(8,128)(2,1)S(1)}, bf16[288,1024]{1,0:T(8,128)(2,1)}, u32[]{:S(2)}, u32[]{:S(2)}) collective-permute-start(bf16[288,1024]{1,0:T(8,128)(2,1)S(1)} %broadcast_select_fusion.1), channel_id=1, source_target_pairs={{0,1},{1,0},{2,3},{3,2},{4,5},{5,4},{6,7},{7,6},{8,9},{9,8},{10,11... | collective-permute-start | bytes 1769480 | tf_op jit(solution)/shard_map/ppermute | solution.py:520
  44.6 5.7 %collective-permute-done.5.refs_6_.refs_3_.refs_4_.refs_5_ = bf16[384,1024]{1,0:T(8,128)(2,1)S(1)} collective-permute-done((bf16[384,1024]{1,0:T(8,128)(2,1)S(1)}, bf16[384,1024]{1,0:T(8,128)(2,1)S(1)}, u32[]{:S(2)}, u32[]{:S(2)}) %collective-permute-start.5) | collective-permute-done | bytes 786464 | tf_op jit(solution)/shard_map/ppermute | solution.py:520
  50.2 6.5 %collective-permute-done.4.refs_7_.refs_9_.refs_12_ = bf16[528,1024]{1,0:T(8,128)(2,1)S(1)} collective-permute-done((bf16[528,1024]{1,0:T(8,128)(2,1)}, bf16[528,1024]{1,0:T(8,128)(2,1)S(1)}, u32[]{:S(2)}, u32[]{:S(2)}) %collective-permute-start.4) | collective-permute-done | bytes 1081376 | tf_op jit(solution)/shard_map/ppermute | solution.py:515
  56.8 6.2 %collective-permute-done.6.refs_3_.refs_2_ = bf16[288,1024]{1,0:T(8,128)(2,1)} collective-permute-done((bf16[288,1024]{1,0:T(8,128)(2,1)S(1)}, bf16[288,1024]{1,0:T(8,128)(2,1)}, u32[]{:S(2)}, u32[]{:S(2)}) %collective-permute-start.6) | collective-permute-done | bytes 589856 | tf_op jit(solution)/shard_map/ppermute | solution.py:520
  66.9 6.7 %mid_forward.1 = (bf16[144,1024]{1,0:T(8,128)(2,1)}, f32[128,1024]{1,0:T(8,128)}, f32[8,1024]{1,0:T(8,128)}) custom-call(s32[1]{0:T(128)} %bitcast.flag.refs_0_, bf16[128,1024]{1,0:T(8,128)(2,1)} %bitcast.32, bf16[288,1024]{1,0:T(8,128)(2,1)} %collective-permute-done.3.refs_2_.refs_1_, bf16[288,1024]{1,0:T(8,128)(2,1)} %collective-permute-done.6.refs_3_.refs_2_, ...), custom_call_target="tpu_custom_call" | custom-call | flops 700000000 | bytes 4000000 | tf_op jit(solution)/shard_map/mid_forward/pallas_call | solution.py:179
  74.7 7.8 %full_stats.1 = (bf16[384,1024]{1,0:T(8,128)(2,1)}, f32[24,384]{1,0:T(8,128)}, f32[24,384]{1,0:T(8,128)}) custom-call(bf16[384,1024]{1,0:T(8,128)(2,1)} %bitcast.27, bf16[384,1024]{1,0:T(8,128)(2,1)} %bitcast.33, bf16[144,1024]{1,0:T(8,128)(2,1)} %get-tuple-element.65.refs_2_, bf16[1024,1024]{1,0:T(8,128)(2,1)} %w_ref.1, bf16[384,1024]{1,0:T(8,128)(2,1)} %bitcast.25, ...), custom_call_target="tpu_custom_call" | custom-call | flops 2000000000 | bytes 8000000 | tf_op jit(solution)/shard_map/full_stats/pallas_call | solution.py:295
  85.1 5.3 %collective-permute-start.12 = (f32[24,384]{1,0:T(8,128)}, f32[24,384]{1,0:T(8,128)S(1)}, u32[]{:S(2)}, u32[]{:S(2)}) collective-permute-start(f32[24,384]{1,0:T(8,128)} %get-tuple-element.74.refs_15_), channel_id=1, source_target_pairs={{0,2},{1,3},{2,4},{3,5},{4,6},{5,7},{6,8},{7,9},{8,10},{9,11},{10,... | collective-permute-start | bytes 110600 | tf_op jit(solution)/shard_map/ppermute | solution.py:515
  93.8 5.5 %next_stats.1.refs_14_ = f32[24,384]{1,0:T(8,128)} custom-call(s32[1]{0:T(128)} %bitcast.flag.refs_0_, bf16[384,1024]{1,0:T(8,128)(2,1)} %bitcast.28, bf16[384,1024]{1,0:T(8,128)(2,1)} %get-tuple-element.71.refs_2_, bf16[384,1024]{1,0:T(8,128)(2,1)} %copy-done.6, bf16[384,1024]{1,0:T(8,128)(2,1)} %copy-done.5, bf16[528,1024]{1,0:T(8,128)(2,1)} %copy-done.3, ...), custom_call_target="tpu_custom_call" | custom-call | flops 1000000000 | bytes 6000000 | tf_op jit(solution)/shard_map/next_stats/pallas_call | solution.py:314
  100.8 5.0 %collective-permute-start.10 = (f32[24,384]{1,0:T(8,128)}, f32[24,384]{1,0:T(8,128)S(1)}, u32[]{:S(2)}, u32[]{:S(2)}) collective-permute-start(f32[24,384]{1,0:T(8,128)} %next_stats.1.refs_14_), channel_id=1, source_target_pairs={{0,1},{1,2},{2,3},{3,4},{4,5},{5,6},{6,7},{7,8},{8,9},{9,10},{10,1... | collective-permute-start | bytes 110600 | tf_op jit(solution)/shard_map/ppermute | solution.py:515
  107.8 14.1 %full_grads.1 = (bf16[384,1024]{1,0:T(8,128)(2,1)}, bf16[384,1024]{1,0:T(8,128)(2,1)}, f32[384,1024]{1,0:T(8,128)}, bf16[384,1024]{1,0:T(8,128)(2,1)}, bf16[384,...) custom-call(s32[1]{0:T(128)} %bitcast.flag.refs_0_, ...), custom_call_target="tpu_custom_call" | custom-call | flops 8000000000 | bytes 14000000 | tf_op jit(solution)/shard_map/full_grads/pallas_call | solution.py:377
  123.4 4.2 %collective-permute-done.16.refs_3_ = f32[8,1024]{1,0:T(8,128)S(1)} collective-permute-done((f32[8,1024]{1,0:T(8,128)}, f32[8,1024]{1,0:T(8,128)S(1)}, u32[]{:S(2)}, u32[]{:S(2)}) %collective-permute-start.16) | collective-permute-done | bytes 32800 | tf_op jit(solution)/shard_map/ppermute | solution.py:515
  128.3 4.6 %mid_cotangent.1.refs_12_ = bf16[144,1024]{1,0:T(8,128)(2,1)} custom-call(bf16[1024,1024]{1,0:T(8,128)(2,1)} %w_ref.1, f32[128,1024]{1,0:T(8,128)} %get-tuple-element.69.refs_0_, f32[8,1024]{1,0:T(8,128)} %get-tuple-element.70.refs_1_, f32[128,1024]{1,0:T(8,128)} %get-tuple-element.80.refs_2_, f32[8,1024]{1,0:T(8,128)} %copy-done.14), custom_call_target="tpu_custom_call" | custom-call | flops 600000000 | bytes 4000000 | tf_op jit(solution)/shard_map/mid_cotangent/pallas_call | solution.py:432
  132.8 4.8 %maximum_maximum_fusion = bf16[576,1280]{1,0:T(8,128)(2,1)} fusion(bf16[144,256]{1,0:T(8,128)(2,1)S(1)} %get-tuple-element.100, bf16[144,1024]{1,0:T(8,128)(2,1)S(1)} %copy-done.13, bf16[144,256]{1,0:T(8,128)(2,1)S(1)} %get-tuple-element.101, bf16[144,256]{1,0:T(8,128)(2,1)S(1)} %get-tuple-element.102, bf16[144,256]{1,0:T(8,128)(2,1)S(1)} %get-tuple-element.99), kind=kLoop, calls=%fused_computation.1 | loop fusion | flops 11796480 | bytes 2064384 | tf_op jit(solution)/shard_map/concatenate | solution.py:583
  137.7 18.0 %all-to-all-start = ((bf16[4,144,1280]{2,1,0:T(8,128)(2,1)}), bf16[4,144,1280]{2,1,0:T(8,128)(2,1)S(1)}, u32[]{:S(2)}, u32[]{:S(2)}) async-start(bf16[4,144,1280]{2,1,0:T(8,128)(2,1)} %bitcast.10), calls=%async_computation | async-start | bytes 2949120 | tf_op jit(solution)/shard_map/all_to_all | solution.py:536
  157.0 4.0 %collective-permute-start.21 = (bf16[384,1024]{1,0:T(8,128)(2,1)}, bf16[384,1024]{1,0:T(8,128)(2,1)S(1)}, u32[]{:S(2)}, u32[]{:S(2)}) collective-permute-start(bf16[384,1024]{1,0:T(8,128)(2,1)} %get-tuple-element.94), channel_id=1, source_target_pairs={{0,2},{1,3},{2,4},{3,5},{4,6},{5,7},{6,8},{7,9},{8,10},{9,11},{10,... | collective-permute-start | bytes 2359304 | tf_op jit(solution)/shard_map/ppermute | solution.py:515
  163.7 21.8 %all-to-all-done = bf16[4,144,1280]{2,1,0:T(8,128)(2,1)S(1)} async-done(((bf16[4,144,1280]{2,1,0:T(8,128)(2,1)}), bf16[4,144,1280]{2,1,0:T(8,128)(2,1)S(1)}, u32[]{:S(2)}, u32[]{:S(2)}) %all-to-all-start) | async-done | bytes 1474592 | tf_op jit(solution)/shard_map/all_to_all | solution.py:536
  193.9 7.9 %collective-permute-done.19.refs_16_ = bf16[144,1024]{1,0:T(8,128)(2,1)S(1)} collective-permute-done((bf16[144,1024]{1,0:T(8,128)(2,1)S(1)}, bf16[144,1024]{1,0:T(8,128)(2,1)S(1)}, u32[]{:S(2)}, u32[]{:S(2)}) %collective-permute-start.19) | collective-permute-done | bytes 294944 | tf_op jit(solution)/shard_map/ppermute | solution.py:515
  206.7 28.7 %all-to-all-start.2 = ((f32[4,16,1024]{2,1,0:T(8,128)}), f32[4,16,1024]{2,1,0:T(8,128)S(1)}, u32[]{:S(2)}, u32[]{:S(2)}) async-start(f32[4,16,1024]{2,1,0:T(8,128)} %bitcast.19), calls=%async_computation.2 | async-start | bytes 524288 | tf_op jit(solution)/shard_map/all_to_all | solution.py:536
  235.3 8.2 %mid_backward.1 = (bf16[128,1024]{1,0:T(8,128)(2,1)}, bf16[128,1024]{1,0:T(8,128)(2,1)}, bf16[128,1024]{1,0:T(8,128)(2,1)}) custom-call(s32[1]{0:T(128)} %bitcast.flag.refs_0_, bf16[288,1024]{1,0:T(8,128)(2,1)} %collective-permute-done.3.refs_2_.refs_1_, bf16[288,1024]{1,0:T(8,128)(2,1)} %collective-permute-done.6.refs_3_.refs_2_, ...), custom_call_target="tpu_custom_call" | custom-call | flops 3000000000 | bytes 6000000 | tf_op jit(solution)/shard_map/mid_backward/pallas_call | solution.py:500
  (99 shorter events, 43.9 us)
Async XLA Ops:
  0.6 24.5 %collective-permute-start = (bf16[384,1024]{1,0:T(8,128)(2,1)}, bf16[384,1024]{1,0:T(8,128)(2,1)S(1)}, u32[]{:S(2)}, u32[]{:S(2)}) collective-permute-start(bf16[384,1024]{1,0:T(8,128)(2,1)} %bitcast.23), channel_id=1, source_target_pairs={{2,0},{3,1},{4,2},{5,3},{6,4},{7,5},{8,6},{9,7},{10,8},{11,9},{12,... | collective-permute-start | bytes 2359304 | tf_op jit(solution)/shard_map/ppermute | solution.py:515
  7.2 18.4 %collective-permute-start.2 = (bf16[384,1024]{1,0:T(8,128)(2,1)}, bf16[384,1024]{1,0:T(8,128)(2,1)S(1)}, u32[]{:S(2)}, u32[]{:S(2)}) collective-permute-start(bf16[384,1024]{1,0:T(8,128)(2,1)} %get-tuple-element.55), channel_id=1, source_target_pairs={{0,1},{1,0},{2,3},{3,2},{4,5},{5,4},{6,7},{7,6},{8,9},{9,8},{10,11... | collective-permute-start | bytes 2359304 | tf_op jit(solution)/shard_map/ppermute | solution.py:520
  9.3 15.8 %collective-permute-start.1 = (bf16[288,1024]{1,0:T(8,128)(2,1)}, bf16[288,1024]{1,0:T(8,128)(2,1)S(1)}, u32[]{:S(2)}, u32[]{:S(2)}) collective-permute-start(bf16[288,1024]{1,0:T(8,128)(2,1)} %get-tuple-element.54.refs_7_.refs_6_), channel_id=1, source_target_pairs={{0,2},{1,3},{2,4},{3,5},{4,6},{5,7},{6,8},{7,9},{8,10},{9,11},{10,... | collective-permute-start | bytes 1769480 | tf_op jit(solution)/shard_map/ppermute | solution.py:515
  26.5 14.0 %collective-permute-start.3 = (bf16[288,1024]{1,0:T(8,128)(2,1)S(1)}, bf16[288,1024]{1,0:T(8,128)(2,1)}, u32[]{:S(2)}, u32[]{:S(2)}) collective-permute-start(bf16[288,1024]{1,0:T(8,128)(2,1)S(1)} %collective-permute-done.1.refs_4_.refs_3_), channel_id=1, source_target_pairs={{0,2},{1,3},{2,4},{3,5},{4,6},{5,7},{6,8},{7,9},{8,10},{9,11},{10,... | collective-permute-start | bytes 1769480 | tf_op jit(solution)/shard_map/ppermute | solution.py:515
  31.3 25.4 %collective-permute-start.4 = (bf16[528,1024]{1,0:T(8,128)(2,1)}, bf16[528,1024]{1,0:T(8,128)(2,1)S(1)}, u32[]{:S(2)}, u32[]{:S(2)}) collective-permute-start(bf16[528,1024]{1,0:T(8,128)(2,1)} %get-tuple-element.58.refs_6_.refs_8_.refs_7_.refs_10_), channel_id=1, source_target_pairs={{2,0},{3,1},{4,2},{5,3},{6,4},{7,5},{8,6},{9,7},{10,8},{11,9},{12,... | collective-permute-start | bytes 3244040 | tf_op jit(solution)/shard_map/ppermute | solution.py:515
  32.8 17.4 %collective-permute-start.5 = (bf16[384,1024]{1,0:T(8,128)(2,1)S(1)}, bf16[384,1024]{1,0:T(8,128)(2,1)S(1)}, u32[]{:S(2)}, u32[]{:S(2)}) collective-permute-start(bf16[384,1024]{1,0:T(8,128)(2,1)S(1)} %pad_maximum_fusion), channel_id=1, source_target_pairs={{0,1},{1,0},{2,3},{3,2},{4,5},{5,4},{6,7},{7,6},{8,9},{9,8},{10,11... | collective-permute-start | bytes 2359304 | tf_op jit(solution)/shard_map/ppermute | solution.py:520
  40.5 22.5 %collective-permute-start.6 = (bf16[288,1024]{1,0:T(8,128)(2,1)S(1)}, bf16[288,1024]{1,0:T(8,128)(2,1)}, u32[]{:S(2)}, u32[]{:S(2)}) collective-permute-start(bf16[288,1024]{1,0:T(8,128)(2,1)S(1)} %broadcast_select_fusion.1), channel_id=1, source_target_pairs={{0,1},{1,0},{2,3},{3,2},{4,5},{5,4},{6,7},{7,6},{8,9},{9,8},{10,11... | collective-permute-start | bytes 1769480 | tf_op jit(solution)/shard_map/ppermute | solution.py:520
  63.1 27.3 %collective-permute-start.7 = (bf16[528,1024]{1,0:T(8,128)(2,1)S(1)}, bf16[528,1024]{1,0:T(8,128)(2,1)S(1)}, u32[]{:S(2)}, u32[]{:S(2)}) collective-permute-start(bf16[528,1024]{1,0:T(8,128)(2,1)S(1)} %broadcast_select_fusion), channel_id=1, source_target_pairs={{0,1},{1,0},{2,3},{3,2},{4,5},{5,4},{6,7},{7,6},{8,9},{9,8},{10,11... | collective-permute-start | bytes 3244040 | tf_op jit(solution)/shard_map/ppermute | solution.py:520
  65.6 8.3 %collective-permute-start.8 = (bf16[144,1024]{1,0:T(8,128)(2,1)}, bf16[144,1024]{1,0:T(8,128)(2,1)S(1)}, u32[]{:S(2)}, u32[]{:S(2)}) collective-permute-start(bf16[144,1024]{1,0:T(8,128)(2,1)} %slice.29), channel_id=1, source_target_pairs={{2,0},{3,1},{4,2},{5,3},{6,4},{7,5},{8,6},{9,7},{10,8},{11,9},{12,... | collective-permute-start | bytes 884744 | tf_op jit(solution)/shard_map/ppermute | solution.py:515
  74.7 26.0 %collective-permute-start.9 = (bf16[144,1024]{1,0:T(8,128)(2,1)}, bf16[144,1024]{1,0:T(8,128)(2,1)S(1)}, u32[]{:S(2)}, u32[]{:S(2)}) collective-permute-start(bf16[144,1024]{1,0:T(8,128)(2,1)} %broadcast_select_fusion.4), channel_id=1, source_target_pairs={{0,1},{1,0},{2,3},{3,2},{4,5},{5,4},{6,7},{7,6},{8,9},{9,8},{10,11... | collective-permute-start | bytes 884744 | tf_op jit(solution)/shard_map/ppermute | solution.py:520
  82.5 16.8 %collective-permute-start.15 = (f32[24,384]{1,0:T(8,128)}, f32[24,384]{1,0:T(8,128)S(1)}, u32[]{:S(2)}, u32[]{:S(2)}) collective-permute-start(f32[24,384]{1,0:T(8,128)} %get-tuple-element.73.refs_13_), channel_id=1, source_target_pairs={{2,0},{3,1},{4,2},{5,3},{6,4},{7,5},{8,6},{9,7},{10,8},{11,9},{12,... | collective-permute-start | bytes 110600 | tf_op jit(solution)/shard_map/ppermute | solution.py:515
  83.8 21.9 %collective-permute-start.14 = (f32[24,384]{1,0:T(8,128)}, f32[24,384]{1,0:T(8,128)S(1)}, u32[]{:S(2)}, u32[]{:S(2)}) collective-permute-start(f32[24,384]{1,0:T(8,128)} %get-tuple-element.73.refs_13_), channel_id=1, source_target_pairs={{1,0},{2,1},{3,2},{4,3},{5,4},{6,5},{7,6},{8,7},{9,8},{10,9},{11,1... | collective-permute-start | bytes 110600 | tf_op jit(solution)/shard_map/ppermute | solution.py:515
  85.1 20.7 %collective-permute-start.12 = (f32[24,384]{1,0:T(8,128)}, f32[24,384]{1,0:T(8,128)S(1)}, u32[]{:S(2)}, u32[]{:S(2)}) collective-permute-start(f32[24,384]{1,0:T(8,128)} %get-tuple-element.74.refs_15_), channel_id=1, source_target_pairs={{0,2},{1,3},{2,4},{3,5},{4,6},{5,7},{6,8},{7,9},{8,10},{9,11},{10,... | collective-permute-start | bytes 110600 | tf_op jit(solution)/shard_map/ppermute | solution.py:515
  90.4 15.4 %collective-permute-start.11 = (f32[24,384]{1,0:T(8,128)}, f32[24,384]{1,0:T(8,128)S(1)}, u32[]{:S(2)}, u32[]{:S(2)}) collective-permute-start(f32[24,384]{1,0:T(8,128)} %get-tuple-element.74.refs_15_), channel_id=1, source_target_pairs={{0,1},{1,2},{2,3},{3,4},{4,5},{5,6},{6,7},{7,8},{8,9},{9,10},{10,1... | collective-permute-start | bytes 110600 | tf_op jit(solution)/shard_map/ppermute | solution.py:515
  99.3 6.5 %collective-permute-start.13 = (f32[24,384]{1,0:T(8,128)}, f32[24,384]{1,0:T(8,128)S(1)}, u32[]{:S(2)}, u32[]{:S(2)}) collective-permute-start(f32[24,384]{1,0:T(8,128)} %next_stats.1.refs_14_), channel_id=1, source_target_pairs={{1,0},{2,1},{3,2},{4,3},{5,4},{6,5},{7,6},{8,7},{9,8},{10,9},{11,1... | collective-permute-start | bytes 110600 | tf_op jit(solution)/shard_map/ppermute | solution.py:515
  137.7 47.8 %all-to-all-start = ((bf16[4,144,1280]{2,1,0:T(8,128)(2,1)}), bf16[4,144,1280]{2,1,0:T(8,128)(2,1)S(1)}, u32[]{:S(2)}, u32[]{:S(2)}) async-start(bf16[4,144,1280]{2,1,0:T(8,128)(2,1)} %bitcast.10), calls=%async_computation | async-start | bytes 2949120 | tf_op jit(solution)/shard_map/all_to_all | solution.py:536
  155.7 31.2 %collective-permute-start.17 = (bf16[144,1024]{1,0:T(8,128)(2,1)S(1)}, bf16[144,1024]{1,0:T(8,128)(2,1)S(1)}, u32[]{:S(2)}, u32[]{:S(2)}) collective-permute-start(bf16[144,1024]{1,0:T(8,128)(2,1)S(1)} %copy-done.10), channel_id=1, source_target_pairs={{2,0},{3,1},{4,2},{5,3},{6,4},{7,5},{8,6},{9,7},{10,8},{11,9},{12,... | collective-permute-start | bytes 884744 | tf_op jit(solution)/shard_map/ppermute | solution.py:515
  157.0 46.5 %collective-permute-start.21 = (bf16[384,1024]{1,0:T(8,128)(2,1)}, bf16[384,1024]{1,0:T(8,128)(2,1)S(1)}, u32[]{:S(2)}, u32[]{:S(2)}) collective-permute-start(bf16[384,1024]{1,0:T(8,128)(2,1)} %get-tuple-element.94), channel_id=1, source_target_pairs={{0,2},{1,3},{2,4},{3,5},{4,6},{5,7},{6,8},{7,9},{8,10},{9,11},{10,... | collective-permute-start | bytes 2359304 | tf_op jit(solution)/shard_map/ppermute | solution.py:515
  161.0 42.4 %collective-permute-start.22 = (bf16[384,1024]{1,0:T(8,128)(2,1)}, bf16[384,1024]{1,0:T(8,128)(2,1)}, u32[]{:S(2)}, u32[]{:S(2)}) collective-permute-start(bf16[384,1024]{1,0:T(8,128)(2,1)} %get-tuple-element.95), channel_id=1, source_target_pairs={{0,1},{1,2},{2,3},{3,4},{4,5},{5,6},{6,7},{7,8},{8,9},{9,10},{10,1... | collective-permute-start | bytes 2359304 | tf_op jit(solution)/shard_map/ppermute | solution.py:515
  186.9 19.0 %all-to-all-start.1 = ((bf16[16,16,1024]{2,1,0:T(8,128)(2,1)}), bf16[16,16,1024]{2,1,0:T(8,128)(2,1)S(1)}, u32[]{:S(2)}, u32[]{:S(2)}) async-start(bf16[16,16,1024]{2,1,0:T(8,128)(2,1)} %bitcast.35), calls=%async_computation.1 | async-start | bytes 1048576 | tf_op jit(solution)/shard_map/all_to_all | solution.py:536
  190.6 11.2 %collective-permute-start.19 = (bf16[144,1024]{1,0:T(8,128)(2,1)S(1)}, bf16[144,1024]{1,0:T(8,128)(2,1)S(1)}, u32[]{:S(2)}, u32[]{:S(2)}) collective-permute-start(bf16[144,1024]{1,0:T(8,128)(2,1)S(1)} %collective-permute-done.17.refs_14_), channel_id=1, source_target_pairs={{2,0},{3,1},{4,2},{5,3},{6,4},{7,5},{8,6},{9,7},{10,8},{11,9},{12,... | collective-permute-start | bytes 884744 | tf_op jit(solution)/shard_map/ppermute | solution.py:515
  192.7 42.7 %collective-permute-start.18 = (bf16[144,1024]{1,0:T(8,128)(2,1)}, bf16[144,1024]{1,0:T(8,128)(2,1)}, u32[]{:S(2)}, u32[]{:S(2)}) collective-permute-start(bf16[144,1024]{1,0:T(8,128)(2,1)} %broadcast_select_fusion.3), channel_id=1, source_target_pairs={{0,1},{1,0},{2,3},{3,2},{4,5},{5,4},{6,7},{7,6},{8,9},{9,8},{10,11... | collective-permute-start | bytes 884744 | tf_op jit(solution)/shard_map/ppermute | solution.py:520
  201.9 33.4 %collective-permute-start.20 = (bf16[144,1024]{1,0:T(8,128)(2,1)S(1)}, bf16[144,1024]{1,0:T(8,128)(2,1)}, u32[]{:S(2)}, u32[]{:S(2)}) collective-permute-start(bf16[144,1024]{1,0:T(8,128)(2,1)S(1)} %broadcast_select_fusion.2), channel_id=1, source_target_pairs={{0,1},{1,0},{2,3},{3,2},{4,5},{5,4},{6,7},{7,6},{8,9},{9,8},{10,11... | collective-permute-start | bytes 884744 | tf_op jit(solution)/shard_map/ppermute | solution.py:520
  206.7 36.8 %all-to-all-start.2 = ((f32[4,16,1024]{2,1,0:T(8,128)}), f32[4,16,1024]{2,1,0:T(8,128)S(1)}, u32[]{:S(2)}, u32[]{:S(2)}) async-start(f32[4,16,1024]{2,1,0:T(8,128)} %bitcast.19), calls=%async_computation.2 | async-start | bytes 524288 | tf_op jit(solution)/shard_map/all_to_all | solution.py:536
  (24 other events, 221.2 us)

commit v7 on v6

--- a/solution.py
+++ b/solution.py
@@ -21,7 +21,7 @@
 CQ = F + S + 16
 TILES = F // S
 TILE_W = WIN + S
-STEP = 2
+STEP = 4
 SCALE = E ** (-0.5)
 LOG2 = SCALE * math.log2(math.e)
 NEG = -1e30
@@ -327,20 +327,25 @@
 
 
 def grads_body(
-    sub, head, flag, k, v, q0, q1a, q1b, q2, c0, c1, c2, d0, d1, d2, s0, s1, s2, up1, up1_far, up2, down1, down1_far, down2,
+    sub, head, flag, k, v, q0, q1a, q1b, q2, c0, c1, c2, d0, d1, d2, s0, s1, s2, up1, up2, down1, down2,
     dk, dv, dq0, dq1, dq2, sums, link, tail, bias, ext, glob, kept,
 ):
     @on_first(sub)
     def _():
         full_mask(bias, [doc_row(ref) for ref in (d0, d1, d2)])
 
-        def triple(ref):
-            peak, total, dots = (ref[j * H : (j + 1) * H, :] for j in range(3))
+        def triple(ref, base=0):
+            peak, total, dots = (ref[base + j * H : base + (j + 1) * H, :] for j in range(3))
             return jnp.where(total > 0.0, peak, NEG), total, dots
 
-        for n, group in enumerate(((s0, up1, up2), (s1, up1_far, down1_far), (s2, down1, down2))):
+        groups = (
+            (triple(s0), triple(up1), triple(up2)),
+            (triple(s1), triple(up1, 3 * H), triple(down1)),
+            (triple(s2), triple(down1, 3 * H), triple(down2)),
+        )
+        for n, group in enumerate(groups):
             cols = slice(n * F, (n + 1) * F)
-            peak, total, dots = merge([triple(ref) for ref in group])
+            peak, total, dots = merge(group)
             inv = jnp.where(total > 0.0, 1.0 / total, 0.0)
             glob[0:H, cols] = peak
             glob[H : 2 * H, cols] = inv
@@ -369,8 +374,11 @@
     sums[...] = total
     first = ext[0:1, :] + ext[1:2, :]
     tail[...] = jnp.broadcast_to(first, (8, E))
-    link[0:S, :] = total.astype(BF16)
-    link[S : S + 16, :] = jnp.where(iota((16, E), 0) == 15, first, 0.0).astype(BF16)
+    narrow = total.astype(BF16)
+    last = jnp.where(iota((16, E), 0) == 15, first, 0.0).astype(BF16)
+    for x in range(4):
+        link[x * (S + 16) : x * (S + 16) + S, :] = narrow
+        link[x * (S + 16) + S : (x + 1) * (S + 16), :] = last
 
 
 def full_grads(flag, k, v, qs, cs, stats):
@@ -383,7 +391,7 @@
         + [head_spec(F)] * 7
         + [DOCS] * 3
         + [whole_spec(s.shape) for s in stats],
-        out_specs=[head_spec(F)] * 5 + [head_spec(S), head_spec(S + 16), head_spec(8)],
+        out_specs=[head_spec(F)] * 5 + [head_spec(S), head_spec(4 * (S + 16)), head_spec(8)],
         out_shape=[
             jax.ShapeDtypeStruct((F, WIDTH), BF16),
             jax.ShapeDtypeStruct((F, WIDTH), BF16),
@@ -391,7 +399,7 @@
             jax.ShapeDtypeStruct((F, WIDTH), BF16),
             jax.ShapeDtypeStruct((F, WIDTH), BF16),
             jax.ShapeDtypeStruct((S, WIDTH), F32),
-            jax.ShapeDtypeStruct((S + 16, WIDTH), BF16),
+            jax.ShapeDtypeStruct((4 * (S + 16), WIDTH), BF16),
             jax.ShapeDtypeStruct((8, WIDTH), F32),
         ],
         scratch_shapes=[
@@ -442,6 +450,7 @@
         out_specs=head_spec(S + 16),
         out_shape=jax.ShapeDtypeStruct((S + 16, WIDTH), BF16),
         scratch_shapes=[pltpu.VMEM((S, WIDTH), BF16)],
+        compiler_params=pltpu.CompilerParams(vmem_limit_bytes=16 * 1024 * 1024),
         cost_estimate=pl.CostEstimate(flops=600_000_000, bytes_accessed=4_000_000, transcendentals=0),
         name="mid_cotangent",
     )(w, att, stat, sums, tail)
@@ -559,33 +568,36 @@
 
     pays = (kv4, kv3, kv2, got_a, got_b, own_kv)
     mid_ext, attended, mid_stat = mid_forward(flag, q_m, pays)
+    parts = jnp.concatenate([mid_ext[:, n * 256 : (n + 1) * 256] for n in range(4)], axis=0)
+    left = exchange(parts, "ctx", X_GROUPS)
     qm2 = cq2[F:]
     qm4, mid_ext = together(shift(qm2, -2), mid_ext)
     values, s0, s2 = full_stats(k_f, v_base[0], mid_ext, w_link, q_f, qf2, late_cq, cq2)
-    up2, up1_far = shift(s2, 2), shift(s2, 1)
-    down2, down1_far = shift(s0, -2), shift(s0, -1)
+    up2, down2 = shift(s2, 2), shift(s0, -2)
+    left, cq1, up2, down2 = together(left, cq1, up2, down2)
     s1 = next_stats(flag, k_f, values, got_b_late, got_a, late_cq, cq1)
-    up1, down1 = shift(s1, 1), shift(s1, -1)
+    up1 = shift(jnp.concatenate([s1, s2], axis=0), 1)
+    down1 = shift(jnp.concatenate([s0, s1], axis=0), -1)
 
     qm3 = swap(jnp.where(upper, qm2, qm4), "ctx", 1)
     values, qm3 = together(values, qm3)
     qs, cs = (q_f, got_b_late, got_a, qf2), (late_cq, cq1, cq2)
     dk_f, dv_f, dq0, dq1, dq2, sums, sum_ext, tail = full_grads(
-        flag, k_f, values, qs, cs, (s0, s1, s2, up1, up1_far, up2, down1, down1_far, down2)
+        flag, k_f, values, qs, cs, (s0, s1, s2, up1, up2, down1, down2)
     )
 
-    sums, next_tail, sum_ext, dq1, dq2 = together(sums, shift(tail, -1), sum_ext, dq1, dq2)
+    next_tail = shift(tail, -1)
+    near = swap(dq1, "ctx", 1)
     cot_m = mid_cotangent(sums, next_tail, w_link, attended, mid_stat)
-    cot_m, sum_ext, dq1, dq2 = together(cot_m, sum_ext, dq1, dq2)
     g2 = shift(cot_m, -2)
-    near, far = shift(dq1, 1), shift(dq2, 2)
-    parts = [jnp.concatenate([sum_ext, mid_ext[:, n * 256 : (n + 1) * 256]], axis=1) for n in range(4)]
-    parts = exchange(jnp.concatenate(parts, axis=0), "ctx", X_GROUPS)
-    term = dot_tn(parts[:, WIDTH:], parts[:, :WIDTH]).astype(BF16)
-    term, g2 = together(term, g2)
+    right = exchange(sum_ext, "ctx", X_GROUPS)
+    term = dot_tn(left, right).astype(BF16)
     g1 = swap(jnp.where(upper, cot_m, g2), "ctx", 1)
     g4 = shift(g2, -2)
     total = jnp.sum(exchange(term, "ctx", YZ_GROUPS).astype(F32).reshape(16, 16, WIDTH), axis=0)
+    near, total = together(near, total)
+    passed = jnp.where(upper, dq2.astype(F32), dq2.astype(F32) + near.astype(F32)).astype(BF16)
+    far = shift(passed, 2)
     g2_late, g4 = together(g2, g4)
     g3 = swap(jnp.where(upper, g2_late, g4), "ctx", 1)
     every = exchange(jnp.concatenate([total] * 4, axis=0), "dp", None)
@@ -594,7 +606,7 @@
     pays = (kv4, kv3_late, kv2, got_a, got_b, own_kv)
     dq_m, dk_m, dv_m = mid_backward(flag, pays, (late_cq, cq1, cq2, qm3, qm4), (cot_m, g1, g2, g3, g4))
 
-    dq_f = (dq0 + far.astype(F32) + near.astype(F32)).astype(BF16)
+    dq_f = (dq0 + far.astype(F32) + jnp.where(upper, near.astype(F32), 0.0)).astype(BF16)
     return (dq_m[None], dk_m[None], dv_m[None], dq_f[None], dk_f[None], dv_f[None], grad_link)
 
 

time: 246 us -> 226 us (0.919)
  starting transfers between devices: 105 us -> 78.9 us
  blocking collectives: 0 us -> 22.9 us
  waiting for transfers between devices: 71.6 us -> 58.6 us
  Pallas kernels: 50.8 us -> 47 us
    all_to_all x0 -> x1, blocking collectives: none -> 22.9 us  [exchange(): lax.all_to_all(value, axis, 0, 0, axis_index_groups=groups, tiled=True)]
    all_to_all x3, waiting for transfers between devices: 21.8 us -> 0.01 us  [exchange(): lax.all_to_all(value, axis, 0, 0, axis_index_groups=groups, tiled=True)]
    all_to_all x3, starting transfers between devices: 50.4 us -> 31.5 us  [exchange(): lax.all_to_all(value, axis, 0, 0, axis_index_groups=groups, tiled=True)]
    ppermute x16 -> x13, starting transfers between devices: 41.2 us -> 31.1 us  [shift(): lax.ppermute(value, 'ctx', [(n, n + steps) for n in range(first, last)])]
    ppermute x16 -> x13, waiting for transfers between devices: 37.4 us -> 46.2 us  [shift(): lax.ppermute(value, 'ctx', [(n, n + steps) for n in range(first, last)])]
    ppermute x7 -> x8, starting transfers between devices: 12.9 us -> 16.4 us  [swap(): return lax.ppermute(value, axis, [(n, n ^ bit) for n in range(count)])]
    pallas_call x1, Pallas kernels: 4.58 us -> 1.2 us  [mid_cotangent(): pl.pallas_call(run, grid=(H // STEP,), in_specs=[pl.BlockSpec((STEP * E,...]
    concatenate x1 -> x2, other arithmetic: 4.81 us -> 1.6 us  [the longest x1 0.86 us: shards(): down1 = shift(jnp.concatenate([s0, s1], axis=0), -1)]
  transfers between devices with their start and end apart: 26 -> 24, of which waited for: 11 -> 11; matrix products, arithmetic and copies ran while one was open for 3% -> 4% of each run, Pallas kernels for 13% -> 14%
where the time goes in v7:
time: 226 us; the launch traced here: 224 us
  starting transfers between devices  78.9 us (35%)
  waiting for transfers between devices  58.6 us (26%)
  Pallas kernels  47 us (21%)
  blocking collectives  22.9 us (10%)
  other arithmetic  10.3 us (5%)
  local copies, waits for them, and re-layouts  4.28 us (2%)
    ppermute x13, waiting for transfers between devices, shift(): lax.ppermute(value, 'ctx', [(n, n + steps) for n in range(first, last)])  46.2 us
    all_to_all x3, starting transfers between devices, exchange(): lax.all_to_all(value, axis, 0, 0, axis_index_groups=groups, tiled=True)  31.5 us
    ppermute x13, starting transfers between devices, shift(): lax.ppermute(value, 'ctx', [(n, n + steps) for n in range(first, last)])  31.1 us
    all_to_all x1, blocking collectives, exchange(): lax.all_to_all(value, axis, 0, 0, axis_index_groups=groups, tiled=True)  22.9 us
    ppermute x8, starting transfers between devices, swap(): return lax.ppermute(value, axis, [(n, n ^ bit) for n in range(count)])  16.4 us
    pallas_call x1, Pallas kernels, full_grads(): call(grads_body, 'full_grads', 8000000000, 14000000, in_specs=[FLAG, head...  15 us
    ppermute x8, waiting for transfers between devices, swap(): return lax.ppermute(value, axis, [(n, n ^ bit) for n in range(count)])  12.4 us
    pallas_call x1, Pallas kernels, mid_backward(): call(mid_bwd_body, 'mid_backward', 3000000000, 6000000, in_specs=[FLAG] +...  8.15 us
  transfers between devices with their start and end apart: 24, of which 11 were waited for; matrix products, arithmetic and copies ran while one was open for 4% of the time, Pallas kernels for 14%

profile of v7, /device:TPU:1, one launch (start us, length us, event | category | flops | bytes accessed | tf_op | source)
XLA Modules:
  0.0 224.4 jit_solution(8235407189011704462)
XLA Ops:
  3.2 4.0 %pack.1 = (bf16[288,1024]{1,0:T(8,128)(2,1)}, bf16[528,1024]{1,0:T(8,128)(2,1)}, bf16[384,1024]{1,0:T(8,128)(2,1)}) custom-call(s32[1]{0:T(128)} %bitcast.flag.refs_0_, bf16[128,1024]{1,0:T(8,128)(2,1)} %bitcast.36, bf16[128,1024]{1,0:T(8,128)(2,1)} %bitcast.42, bf16[128,1024]{1,0:T(8,128)(2,1)} %bitcast.43, bf16[16,256]{1,0:T(8,128)(2,1)} %broadcast_in_dim.27.ids, ...), custom_call_target="tpu_custom_call" | custom-call | tf_op jit(solution)/shard_map/pack/pallas_call | solution.py:118
  9.3 4.2 %collective-permute-start.1 = (bf16[288,1024]{1,0:T(8,128)(2,1)}, bf16[288,1024]{1,0:T(8,128)(2,1)S(1)}, u32[]{:S(2)}, u32[]{:S(2)}) collective-permute-start(bf16[288,1024]{1,0:T(8,128)(2,1)} %get-tuple-element.49.refs_7_.refs_6_), channel_id=1, source_target_pairs={{0,2},{1,3},{2,4},{3,5},{4,6},{5,7},{6,8},{7,9},{8,10},{9,11},{10,... | collective-permute-start | bytes 1769480 | tf_op jit(solution)/shard_map/ppermute | solution.py:524
  13.5 11.6 %collective-permute-done.1.refs_4_.refs_3_ = bf16[288,1024]{1,0:T(8,128)(2,1)S(1)} collective-permute-done((bf16[288,1024]{1,0:T(8,128)(2,1)}, bf16[288,1024]{1,0:T(8,128)(2,1)S(1)}, u32[]{:S(2)}, u32[]{:S(2)}) %collective-permute-start.1) | collective-permute-done | bytes 589856 | tf_op jit(solution)/shard_map/ppermute | solution.py:524
  26.5 4.9 %collective-permute-start.3 = (bf16[288,1024]{1,0:T(8,128)(2,1)S(1)}, bf16[288,1024]{1,0:T(8,128)(2,1)}, u32[]{:S(2)}, u32[]{:S(2)}) collective-permute-start(bf16[288,1024]{1,0:T(8,128)(2,1)S(1)} %collective-permute-done.1.refs_4_.refs_3_), channel_id=1, source_target_pairs={{0,2},{1,3},{2,4},{3,5},{4,6},{5,7},{6,8},{7,9},{8,10},{9,11},{10,... | collective-permute-start | bytes 1769480 | tf_op jit(solution)/shard_map/ppermute | solution.py:524
  35.0 5.4 %collective-permute-done.3.refs_2_.refs_1_ = bf16[288,1024]{1,0:T(8,128)(2,1)} collective-permute-done((bf16[288,1024]{1,0:T(8,128)(2,1)S(1)}, bf16[288,1024]{1,0:T(8,128)(2,1)}, u32[]{:S(2)}, u32[]{:S(2)}) %collective-permute-start.3) | collective-permute-done | bytes 589856 | tf_op jit(solution)/shard_map/ppermute | solution.py:524
  40.5 4.1 %collective-permute-start.6 = (bf16[288,1024]{1,0:T(8,128)(2,1)S(1)}, bf16[288,1024]{1,0:T(8,128)(2,1)}, u32[]{:S(2)}, u32[]{:S(2)}) collective-permute-start(bf16[288,1024]{1,0:T(8,128)(2,1)S(1)} %broadcast_select_fusion.1), channel_id=1, source_target_pairs={{0,1},{1,0},{2,3},{3,2},{4,5},{5,4},{6,7},{7,6},{8,9},{9,8},{10,11... | collective-permute-start | bytes 1769480 | tf_op jit(solution)/shard_map/ppermute | solution.py:529
  44.6 5.7 %collective-permute-done.5.refs_6_.refs_3_.refs_4_.refs_5_ = bf16[384,1024]{1,0:T(8,128)(2,1)S(1)} collective-permute-done((bf16[384,1024]{1,0:T(8,128)(2,1)S(1)}, bf16[384,1024]{1,0:T(8,128)(2,1)S(1)}, u32[]{:S(2)}, u32[]{:S(2)}) %collective-permute-start.5) | collective-permute-done | bytes 786464 | tf_op jit(solution)/shard_map/ppermute | solution.py:529
  50.2 6.5 %collective-permute-done.4.refs_7_.refs_9_.refs_12_ = bf16[528,1024]{1,0:T(8,128)(2,1)S(1)} collective-permute-done((bf16[528,1024]{1,0:T(8,128)(2,1)}, bf16[528,1024]{1,0:T(8,128)(2,1)S(1)}, u32[]{:S(2)}, u32[]{:S(2)}) %collective-permute-start.4) | collective-permute-done | bytes 1081376 | tf_op jit(solution)/shard_map/ppermute | solution.py:524
  56.8 6.2 %collective-permute-done.6.refs_3_.refs_2_ = bf16[288,1024]{1,0:T(8,128)(2,1)} collective-permute-done((bf16[288,1024]{1,0:T(8,128)(2,1)S(1)}, bf16[288,1024]{1,0:T(8,128)(2,1)}, u32[]{:S(2)}, u32[]{:S(2)}) %collective-permute-start.6) | collective-permute-done | bytes 589856 | tf_op jit(solution)/shard_map/ppermute | solution.py:529
  66.2 6.1 %mid_forward.1 = (bf16[144,1024]{1,0:T(8,128)(2,1)}, f32[128,1024]{1,0:T(8,128)}, f32[8,1024]{1,0:T(8,128)}) custom-call(s32[1]{0:T(128)} %bitcast.flag.refs_0_, bf16[128,1024]{1,0:T(8,128)(2,1)} %bitcast.37, bf16[288,1024]{1,0:T(8,128)(2,1)} %collective-permute-done.3.refs_2_.refs_1_, bf16[288,1024]{1,0:T(8,128)(2,1)} %collective-permute-done.6.refs_3_.refs_2_, ...), custom_call_target="tpu_custom_call" | custom-call | flops 700000000 | bytes 4000000 | tf_op jit(solution)/shard_map/mid_forward/pallas_call | solution.py:179
  74.0 12.2 %all-to-all-start = ((bf16[4,144,256]{2,1,0:T(8,128)(2,1)}), bf16[4,144,256]{2,1,0:T(8,128)(2,1)S(1)}, u32[]{:S(2)}, u32[]{:S(2)}) async-start(bf16[4,144,256]{2,1,0:T(8,128)(2,1)} %bitcast.8), calls=%async_computation | async-start | bytes 589824 | tf_op jit(solution)/shard_map/all_to_all | solution.py:545
  86.2 7.7 %full_stats.1 = (bf16[384,1024]{1,0:T(8,128)(2,1)}, f32[24,384]{1,0:T(8,128)}, f32[24,384]{1,0:T(8,128)}) custom-call(bf16[384,1024]{1,0:T(8,128)(2,1)} %bitcast.31, bf16[384,1024]{1,0:T(8,128)(2,1)} %bitcast.38, bf16[144,1024]{1,0:T(8,128)(2,1)} %get-tuple-element.60.refs_2_, bf16[1024,1024]{1,0:T(8,128)(2,1)} %w_ref.1, bf16[384,1024]{1,0:T(8,128)(2,1)} %bitcast.29, ...), custom_call_target="tpu_custom_call" | custom-call | flops 2000000000 | bytes 8000000 | tf_op jit(solution)/shard_map/full_stats/pallas_call | solution.py:295
  103.0 4.8 %next_stats.1.refs_14_ = f32[24,384]{1,0:T(8,128)} custom-call(s32[1]{0:T(128)} %bitcast.flag.refs_0_, bf16[384,1024]{1,0:T(8,128)(2,1)} %bitcast.32, bf16[384,1024]{1,0:T(8,128)(2,1)} %get-tuple-element.69.refs_2_, bf16[384,1024]{1,0:T(8,128)(2,1)} %copy-done.11, bf16[384,1024]{1,0:T(8,128)(2,1)} %copy-done.10, bf16[528,1024]{1,0:T(8,128)(2,1)} %copy-done.8, ...), custom_call_target="tpu_custom_call" | custom-call | flops 1000000000 | bytes 6000000 | tf_op jit(solution)/shard_map/next_stats/pallas_call | solution.py:314
  110.0 4.2 %collective-permute-start.12 = (f32[48,384]{1,0:T(8,128)S(1)}, f32[48,384]{1,0:T(8,128)S(1)}, u32[]{:S(2)}, u32[]{:S(2)}) collective-permute-start(f32[48,384]{1,0:T(8,128)S(1)} %get-tuple-element.94), channel_id=1, source_target_pairs={{0,1},{1,2},{2,3},{3,4},{4,5},{5,6},{6,7},{7,8},{8,9},{9,10},{10,1... | collective-permute-start | bytes 221192 | tf_op jit(solution)/shard_map/ppermute | solution.py:524
  116.0 15.0 %full_grads.1 = (bf16[384,1024]{1,0:T(8,128)(2,1)}, bf16[384,1024]{1,0:T(8,128)(2,1)}, f32[384,1024]{1,0:T(8,128)}, bf16[384,1024]{1,0:T(8,128)(2,1)}, bf16[384,...) custom-call(s32[1]{0:T(128)} %bitcast.flag.refs_0_, ...), custom_call_target="tpu_custom_call" | custom-call | flops 8000000000 | bytes 14000000 | tf_op jit(solution)/shard_map/full_grads/pallas_call | solution.py:385
  131.0 22.9 %all_to_all.42 = bf16[4,144,1024]{2,1,0:T(8,128)(2,1)S(1)} all-to-all(bf16[4,144,1024]{2,1,0:T(8,128)(2,1)} %bitcast.34), channel_id=1, replica_groups={{0,16,32,48},{1,17,33,49},{2,18,34,50},{3,19,35,51},{4,20,36,52},{5,21,..., dimensions={0} | all-to-all | bytes 2359296 | tf_op jit(solution)/shard_map/all_to_all | solution.py:545
  155.3 4.2 %all-to-all-start.2 = ((bf16[16,16,1024]{2,1,0:T(8,128)(2,1)}), bf16[16,16,1024]{2,1,0:T(8,128)(2,1)}, u32[]{:S(2)}, u32[]{:S(2)}) async-start(bf16[16,16,1024]{2,1,0:T(8,128)(2,1)} %bitcast.40), calls=%async_computation.2 | async-start | bytes 1048576 | tf_op jit(solution)/shard_map/all_to_all | solution.py:545
  160.8 3.4 %collective-permute-done.14.refs_3_ = f32[8,1024]{1,0:T(8,128)S(1)} collective-permute-done((f32[8,1024]{1,0:T(8,128)S(1)}, f32[8,1024]{1,0:T(8,128)S(1)}, u32[]{:S(2)}, u32[]{:S(2)}) %collective-permute-start.14) | collective-permute-done | bytes 32800 | tf_op jit(solution)/shard_map/ppermute | solution.py:524
  166.9 5.1 %collective-permute-start.19 = (bf16[384,1024]{1,0:T(8,128)(2,1)}, bf16[384,1024]{1,0:T(8,128)(2,1)S(1)}, u32[]{:S(2)}, u32[]{:S(2)}) collective-permute-start(bf16[384,1024]{1,0:T(8,128)(2,1)} %get-tuple-element.82), channel_id=1, source_target_pairs={{0,1},{1,0},{2,3},{3,2},{4,5},{5,4},{6,7},{7,6},{8,9},{9,8},{10,11... | collective-permute-start | bytes 2359304 | tf_op jit(solution)/shard_map/ppermute | solution.py:529
  172.0 8.6 %collective-permute-done.15.refs_14_ = bf16[144,1024]{1,0:T(8,128)(2,1)S(1)} collective-permute-done((bf16[144,1024]{1,0:T(8,128)(2,1)S(1)}, bf16[144,1024]{1,0:T(8,128)(2,1)S(1)}, u32[]{:S(2)}, u32[]{:S(2)}) %collective-permute-start.15) | collective-permute-done | bytes 294944 | tf_op jit(solution)/shard_map/ppermute | solution.py:524
  183.2 7.4 %collective-permute-done.17.refs_16_ = bf16[144,1024]{1,0:T(8,128)(2,1)S(1)} collective-permute-done((bf16[144,1024]{1,0:T(8,128)(2,1)S(1)}, bf16[144,1024]{1,0:T(8,128)(2,1)S(1)}, u32[]{:S(2)}, u32[]{:S(2)}) %collective-permute-start.17) | collective-permute-done | bytes 294944 | tf_op jit(solution)/shard_map/ppermute | solution.py:524
  193.0 4.4 %collective-permute-start.20 = (bf16[384,1024]{1,0:T(8,128)(2,1)S(1)}, bf16[384,1024]{1,0:T(8,128)(2,1)}, u32[]{:S(2)}, u32[]{:S(2)}) collective-permute-start(bf16[384,1024]{1,0:T(8,128)(2,1)S(1)} %fusion.2), channel_id=1, source_target_pairs={{0,2},{1,3},{2,4},{3,5},{4,6},{5,7},{6,8},{7,9},{8,10},{9,11},{10,... | collective-permute-start | bytes 2359304 | tf_op jit(solution)/shard_map/ppermute | solution.py:524
  198.1 15.1 %all-to-all-start.3 = ((f32[4,16,1024]{2,1,0:T(8,128)}), f32[4,16,1024]{2,1,0:T(8,128)S(1)}, u32[]{:S(2)}, u32[]{:S(2)}) async-start(f32[4,16,1024]{2,1,0:T(8,128)} %bitcast.21), calls=%async_computation.3 | async-start | bytes 524288 | tf_op jit(solution)/shard_map/all_to_all | solution.py:545
  213.1 8.2 %mid_backward.1 = (bf16[128,1024]{1,0:T(8,128)(2,1)}, bf16[128,1024]{1,0:T(8,128)(2,1)}, bf16[128,1024]{1,0:T(8,128)(2,1)}) custom-call(s32[1]{0:T(128)} %bitcast.flag.refs_0_, bf16[288,1024]{1,0:T(8,128)(2,1)} %collective-permute-done.3.refs_2_.refs_1_, bf16[288,1024]{1,0:T(8,128)(2,1)} %collective-permute-done.6.refs_3_.refs_2_, ...), custom_call_target="tpu_custom_call" | custom-call | flops 3000000000 | bytes 6000000 | tf_op jit(solution)/shard_map/mid_backward/pallas_call | solution.py:509
  (108 shorter events, 41.5 us)
Async XLA Ops:
  0.6 24.5 %collective-permute-start = (bf16[384,1024]{1,0:T(8,128)(2,1)}, bf16[384,1024]{1,0:T(8,128)(2,1)S(1)}, u32[]{:S(2)}, u32[]{:S(2)}) collective-permute-start(bf16[384,1024]{1,0:T(8,128)(2,1)} %bitcast.27), channel_id=1, source_target_pairs={{2,0},{3,1},{4,2},{5,3},{6,4},{7,5},{8,6},{9,7},{10,8},{11,9},{12,... | collective-permute-start | bytes 2359304 | tf_op jit(solution)/shard_map/ppermute | solution.py:524
  7.2 18.4 %collective-permute-start.2 = (bf16[384,1024]{1,0:T(8,128)(2,1)}, bf16[384,1024]{1,0:T(8,128)(2,1)S(1)}, u32[]{:S(2)}, u32[]{:S(2)}) collective-permute-start(bf16[384,1024]{1,0:T(8,128)(2,1)} %get-tuple-element.50), channel_id=1, source_target_pairs={{0,1},{1,0},{2,3},{3,2},{4,5},{5,4},{6,7},{7,6},{8,9},{9,8},{10,11... | collective-permute-start | bytes 2359304 | tf_op jit(solution)/shard_map/ppermute | solution.py:529
  9.3 15.8 %collective-permute-start.1 = (bf16[288,1024]{1,0:T(8,128)(2,1)}, bf16[288,1024]{1,0:T(8,128)(2,1)S(1)}, u32[]{:S(2)}, u32[]{:S(2)}) collective-permute-start(bf16[288,1024]{1,0:T(8,128)(2,1)} %get-tuple-element.49.refs_7_.refs_6_), channel_id=1, source_target_pairs={{0,2},{1,3},{2,4},{3,5},{4,6},{5,7},{6,8},{7,9},{8,10},{9,11},{10,... | collective-permute-start | bytes 1769480 | tf_op jit(solution)/shard_map/ppermute | solution.py:524
  26.5 14.0 %collective-permute-start.3 = (bf16[288,1024]{1,0:T(8,128)(2,1)S(1)}, bf16[288,1024]{1,0:T(8,128)(2,1)}, u32[]{:S(2)}, u32[]{:S(2)}) collective-permute-start(bf16[288,1024]{1,0:T(8,128)(2,1)S(1)} %collective-permute-done.1.refs_4_.refs_3_), channel_id=1, source_target_pairs={{0,2},{1,3},{2,4},{3,5},{4,6},{5,7},{6,8},{7,9},{8,10},{9,11},{10,... | collective-permute-start | bytes 1769480 | tf_op jit(solution)/shard_map/ppermute | solution.py:524
  31.4 25.4 %collective-permute-start.4 = (bf16[528,1024]{1,0:T(8,128)(2,1)}, bf16[528,1024]{1,0:T(8,128)(2,1)S(1)}, u32[]{:S(2)}, u32[]{:S(2)}) collective-permute-start(bf16[528,1024]{1,0:T(8,128)(2,1)} %get-tuple-element.53.refs_6_.refs_8_.refs_7_.refs_10_), channel_id=1, source_target_pairs={{2,0},{3,1},{4,2},{5,3},{6,4},{7,5},{8,6},{9,7},{10,8},{11,9},{12,... | collective-permute-start | bytes 3244040 | tf_op jit(solution)/shard_map/ppermute | solution.py:524
  32.8 17.4 %collective-permute-start.5 = (bf16[384,1024]{1,0:T(8,128)(2,1)S(1)}, bf16[384,1024]{1,0:T(8,128)(2,1)S(1)}, u32[]{:S(2)}, u32[]{:S(2)}) collective-permute-start(bf16[384,1024]{1,0:T(8,128)(2,1)S(1)} %pad_maximum_fusion), channel_id=1, source_target_pairs={{0,1},{1,0},{2,3},{3,2},{4,5},{5,4},{6,7},{7,6},{8,9},{9,8},{10,11... | collective-permute-start | bytes 2359304 | tf_op jit(solution)/shard_map/ppermute | solution.py:529
  40.5 22.5 %collective-permute-start.6 = (bf16[288,1024]{1,0:T(8,128)(2,1)S(1)}, bf16[288,1024]{1,0:T(8,128)(2,1)}, u32[]{:S(2)}, u32[]{:S(2)}) collective-permute-start(bf16[288,1024]{1,0:T(8,128)(2,1)S(1)} %broadcast_select_fusion.1), channel_id=1, source_target_pairs={{0,1},{1,0},{2,3},{3,2},{4,5},{5,4},{6,7},{7,6},{8,9},{9,8},{10,11... | collective-permute-start | bytes 1769480 | tf_op jit(solution)/shard_map/ppermute | solution.py:529
  63.1 38.8 %collective-permute-start.7 = (bf16[528,1024]{1,0:T(8,128)(2,1)S(1)}, bf16[528,1024]{1,0:T(8,128)(2,1)S(1)}, u32[]{:S(2)}, u32[]{:S(2)}) collective-permute-start(bf16[528,1024]{1,0:T(8,128)(2,1)S(1)} %broadcast_select_fusion), channel_id=1, source_target_pairs={{0,1},{1,0},{2,3},{3,2},{4,5},{5,4},{6,7},{7,6},{8,9},{9,8},{10,11... | collective-permute-start | bytes 3244040 | tf_op jit(solution)/shard_map/ppermute | solution.py:529
  64.9 21.3 %collective-permute-start.8 = (bf16[144,1024]{1,0:T(8,128)(2,1)S(1)}, bf16[144,1024]{1,0:T(8,128)(2,1)S(1)}, u32[]{:S(2)}, u32[]{:S(2)}) collective-permute-start(bf16[144,1024]{1,0:T(8,128)(2,1)S(1)} %slice.27), channel_id=1, source_target_pairs={{2,0},{3,1},{4,2},{5,3},{6,4},{7,5},{8,6},{9,7},{10,8},{11,9},{12,... | collective-permute-start | bytes 884744 | tf_op jit(solution)/shard_map/ppermute | solution.py:524
  74.0 25.9 %all-to-all-start = ((bf16[4,144,256]{2,1,0:T(8,128)(2,1)}), bf16[4,144,256]{2,1,0:T(8,128)(2,1)S(1)}, u32[]{:S(2)}, u32[]{:S(2)}) async-start(bf16[4,144,256]{2,1,0:T(8,128)(2,1)} %bitcast.8), calls=%async_computation | async-start | bytes 589824 | tf_op jit(solution)/shard_map/all_to_all | solution.py:545
  93.9 6.0 %collective-permute-start.9 = (f32[24,384]{1,0:T(8,128)}, f32[24,384]{1,0:T(8,128)S(1)}, u32[]{:S(2)}, u32[]{:S(2)}) collective-permute-start(f32[24,384]{1,0:T(8,128)} %get-tuple-element.61.refs_15_), channel_id=1, source_target_pairs={{0,2},{1,3},{2,4},{3,5},{4,6},{5,7},{6,8},{7,9},{8,10},{9,11},{10,... | collective-permute-start | bytes 110600 | tf_op jit(solution)/shard_map/ppermute | solution.py:524
  97.0 4.9 %collective-permute-start.10 = (f32[24,384]{1,0:T(8,128)}, f32[24,384]{1,0:T(8,128)S(1)}, u32[]{:S(2)}, u32[]{:S(2)}) collective-permute-start(f32[24,384]{1,0:T(8,128)} %get-tuple-element.62.refs_13_), channel_id=1, source_target_pairs={{2,0},{3,1},{4,2},{5,3},{6,4},{7,5},{8,6},{9,7},{10,8},{11,9},{12,... | collective-permute-start | bytes 110600 | tf_op jit(solution)/shard_map/ppermute | solution.py:524
  99.3 14.8 %collective-permute-start.11 = (bf16[144,1024]{1,0:T(8,128)(2,1)S(1)}, bf16[144,1024]{1,0:T(8,128)(2,1)S(1)}, u32[]{:S(2)}, u32[]{:S(2)}) collective-permute-start(bf16[144,1024]{1,0:T(8,128)(2,1)S(1)} %broadcast_select_fusion.4), channel_id=1, source_target_pairs={{0,1},{1,0},{2,3},{3,2},{4,5},{5,4},{6,7},{7,6},{8,9},{9,8},{10,11... | collective-permute-start | bytes 884744 | tf_op jit(solution)/shard_map/ppermute | solution.py:529
  108.7 5.5 %collective-permute-start.13 = (f32[48,384]{1,0:T(8,128)S(1)}, f32[48,384]{1,0:T(8,128)S(1)}, u32[]{:S(2)}, u32[]{:S(2)}) collective-permute-start(f32[48,384]{1,0:T(8,128)S(1)} %get-tuple-element.93), channel_id=1, source_target_pairs={{1,0},{2,1},{3,2},{4,3},{5,4},{6,5},{7,6},{8,7},{9,8},{10,9},{11,1... | collective-permute-start | bytes 221192 | tf_op jit(solution)/shard_map/ppermute | solution.py:524
  110.0 5.4 %collective-permute-start.12 = (f32[48,384]{1,0:T(8,128)S(1)}, f32[48,384]{1,0:T(8,128)S(1)}, u32[]{:S(2)}, u32[]{:S(2)}) collective-permute-start(f32[48,384]{1,0:T(8,128)S(1)} %get-tuple-element.94), channel_id=1, source_target_pairs={{0,1},{1,2},{2,3},{3,4},{4,5},{5,6},{6,7},{7,8},{8,9},{9,10},{10,1... | collective-permute-start | bytes 221192 | tf_op jit(solution)/shard_map/ppermute | solution.py:524
  155.3 36.2 %all-to-all-start.2 = ((bf16[16,16,1024]{2,1,0:T(8,128)(2,1)}), bf16[16,16,1024]{2,1,0:T(8,128)(2,1)}, u32[]{:S(2)}, u32[]{:S(2)}) async-start(bf16[16,16,1024]{2,1,0:T(8,128)(2,1)} %bitcast.40), calls=%async_computation.2 | async-start | bytes 1048576 | tf_op jit(solution)/shard_map/all_to_all | solution.py:545
  159.5 4.7 %collective-permute-start.14 = (f32[8,1024]{1,0:T(8,128)S(1)}, f32[8,1024]{1,0:T(8,128)S(1)}, u32[]{:S(2)}, u32[]{:S(2)}) collective-permute-start(f32[8,1024]{1,0:T(8,128)S(1)} %copy-done.26), channel_id=1, source_target_pairs={{1,0},{2,1},{3,2},{4,3},{5,4},{6,5},{7,6},{8,7},{9,8},{10,9},{11,1... | collective-permute-start | bytes 98312 | tf_op jit(solution)/shard_map/ppermute | solution.py:524
  165.4 15.2 %collective-permute-start.15 = (bf16[144,1024]{1,0:T(8,128)(2,1)S(1)}, bf16[144,1024]{1,0:T(8,128)(2,1)S(1)}, u32[]{:S(2)}, u32[]{:S(2)}) collective-permute-start(bf16[144,1024]{1,0:T(8,128)(2,1)S(1)} %mid_cotangent.1.refs_12_), channel_id=1, source_target_pairs={{2,0},{3,1},{4,2},{5,3},{6,4},{7,5},{8,6},{9,7},{10,8},{11,9},{12,... | collective-permute-start | bytes 884744 | tf_op jit(solution)/shard_map/ppermute | solution.py:524
  166.9 25.8 %collective-permute-start.19 = (bf16[384,1024]{1,0:T(8,128)(2,1)}, bf16[384,1024]{1,0:T(8,128)(2,1)S(1)}, u32[]{:S(2)}, u32[]{:S(2)}) collective-permute-start(bf16[384,1024]{1,0:T(8,128)(2,1)} %get-tuple-element.82), channel_id=1, source_target_pairs={{0,1},{1,0},{2,3},{3,2},{4,5},{5,4},{6,7},{7,6},{8,9},{9,8},{10,11... | collective-permute-start | bytes 2359304 | tf_op jit(solution)/shard_map/ppermute | solution.py:529
  180.6 10.1 %collective-permute-start.17 = (bf16[144,1024]{1,0:T(8,128)(2,1)S(1)}, bf16[144,1024]{1,0:T(8,128)(2,1)S(1)}, u32[]{:S(2)}, u32[]{:S(2)}) collective-permute-start(bf16[144,1024]{1,0:T(8,128)(2,1)S(1)} %collective-permute-done.15.refs_14_), channel_id=1, source_target_pairs={{2,0},{3,1},{4,2},{5,3},{6,4},{7,5},{8,6},{9,7},{10,8},{11,9},{12,... | collective-permute-start | bytes 884744 | tf_op jit(solution)/shard_map/ppermute | solution.py:524
  182.7 30.5 %collective-permute-start.16 = (bf16[144,1024]{1,0:T(8,128)(2,1)}, bf16[144,1024]{1,0:T(8,128)(2,1)}, u32[]{:S(2)}, u32[]{:S(2)}) collective-permute-start(bf16[144,1024]{1,0:T(8,128)(2,1)} %broadcast_select_fusion.3), channel_id=1, source_target_pairs={{0,1},{1,0},{2,3},{3,2},{4,5},{5,4},{6,7},{7,6},{8,9},{9,8},{10,11... | collective-permute-start | bytes 884744 | tf_op jit(solution)/shard_map/ppermute | solution.py:529
  191.5 21.6 %collective-permute-start.18 = (bf16[144,1024]{1,0:T(8,128)(2,1)}, bf16[144,1024]{1,0:T(8,128)(2,1)}, u32[]{:S(2)}, u32[]{:S(2)}) collective-permute-start(bf16[144,1024]{1,0:T(8,128)(2,1)} %broadcast_select_fusion.2), channel_id=1, source_target_pairs={{0,1},{1,0},{2,3},{3,2},{4,5},{5,4},{6,7},{7,6},{8,9},{9,8},{10,11... | collective-permute-start | bytes 884744 | tf_op jit(solution)/shard_map/ppermute | solution.py:529
  193.0 29.0 %collective-permute-start.20 = (bf16[384,1024]{1,0:T(8,128)(2,1)S(1)}, bf16[384,1024]{1,0:T(8,128)(2,1)}, u32[]{:S(2)}, u32[]{:S(2)}) collective-permute-start(bf16[384,1024]{1,0:T(8,128)(2,1)S(1)} %fusion.2), channel_id=1, source_target_pairs={{0,2},{1,3},{2,4},{3,5},{4,6},{5,7},{6,8},{7,9},{8,10},{9,11},{10,... | collective-permute-start | bytes 2359304 | tf_op jit(solution)/shard_map/ppermute | solution.py:524
  198.1 23.2 %all-to-all-start.3 = ((f32[4,16,1024]{2,1,0:T(8,128)}), f32[4,16,1024]{2,1,0:T(8,128)S(1)}, u32[]{:S(2)}, u32[]{:S(2)}) async-start(f32[4,16,1024]{2,1,0:T(8,128)} %bitcast.21), calls=%async_computation.3 | async-start | bytes 524288 | tf_op jit(solution)/shard_map/all_to_all | solution.py:545
  (27 other events, 341.0 us)

commit v8 on v7

--- a/solution.py
+++ b/solution.py
@@ -133,13 +133,12 @@
     return jnp.where(flag[0] == 1, upper[0:rows, :], lower[0:rows, :])
 
 
-def pair_slabs(flag, p4, p3, p2, first, second, p0):
-    near = pick(flag, first, second, KV)
-    return [p4[...], p3[...], p2[...], near, p0[...]]
-
-
-def mid_fwd_body(sub, head, flag, q, p4, p3, p2, first, second, p0, out, att, stat, bias):
-    pays = pair_slabs(flag, p4, p3, p2, first, second, p0)
+def pair_slabs(flag, p4, p2, a, b, c, p0):
+    return [p4[...], pick(flag, b, c, KV), p2[...], pick(flag, a, b, KV), p0[...]]
+
+
+def mid_fwd_body(sub, head, flag, q, p4, p2, a, b, c, p0, out, att, stat, bias):
+    pays = pair_slabs(flag, p4, p2, a, b, c, p0)
 
     @on_first(sub)
     def _():
@@ -193,7 +192,7 @@
 
 
 FLAG = pl.BlockSpec(memory_space=pltpu.SMEM)
-PAY_SPECS = [head_spec(KV)] * 3 + [head_spec(F)] * 2 + [head_spec(KV)]
+PAY_SPECS = [head_spec(KV)] * 6
 
 
 def full_mask(bias, docs):
@@ -456,11 +455,11 @@
     )(w, att, stat, sums, tail)
 
 
-def mid_bwd_body(sub, head, flag, p4, p3, p2, first, second, p0, *refs):
+def mid_bwd_body(sub, head, flag, p4, p2, a, b, c, p0, *refs):
     ms = [ref[...] for ref in refs[0:5]]
     gs = refs[5:10]
     dq, dk, dv, back, fore = refs[10:]
-    pays = pair_slabs(flag, p4, p3, p2, first, second, p0)
+    pays = pair_slabs(flag, p4, p2, a, b, c, p0)
 
     @on_first(sub)
     def _():
@@ -556,17 +555,15 @@
     kv2 = shift(own_kv, 2)
     got_a = swap(swap_a, "ctx", 1)
     qf2 = shift(q_f, -2)
+    got_b = swap(kv2, "ctx", 1)
     late_cq, qf2, kv2, got_a = together(own_cq, qf2, kv2, got_a)
-    swap_b = jnp.concatenate([jnp.where(upper, kv2, qf2[:KV]), qf2[KV:]], axis=0)
-    got_b = swap(swap_b, "ctx", 1)
-    kv4 = shift(kv2, 2)
-    kv2, kv4 = together(kv2, kv4)
-    kv3 = swap(jnp.where(upper, kv4, kv2), "ctx", 1)
+    kv4, got_b = together(shift(kv2, 2), got_b)
+    got_c = swap(jnp.concatenate([jnp.where(upper, kv4, qf2[:KV]), qf2[KV:]], axis=0), "ctx", 1)
     cq2 = shift(late_cq, -2)
-    cq2, got_b_late, kv3_late = together(cq2, got_b, kv3)
+    cq2, got_c_late = together(cq2, got_c)
     cq1 = swap(jnp.where(upper, late_cq, cq2), "ctx", 1)
 
-    pays = (kv4, kv3, kv2, got_a, got_b, own_kv)
+    pays = (kv4, kv2, got_a, got_b, got_c, own_kv)
     mid_ext, attended, mid_stat = mid_forward(flag, q_m, pays)
     parts = jnp.concatenate([mid_ext[:, n * 256 : (n + 1) * 256] for n in range(4)], axis=0)
     left = exchange(parts, "ctx", X_GROUPS)
@@ -575,25 +572,26 @@
     values, s0, s2 = full_stats(k_f, v_base[0], mid_ext, w_link, q_f, qf2, late_cq, cq2)
     up2, down2 = shift(s2, 2), shift(s0, -2)
     left, cq1, up2, down2 = together(left, cq1, up2, down2)
-    s1 = next_stats(flag, k_f, values, got_b_late, got_a, late_cq, cq1)
+    s1 = next_stats(flag, k_f, values, got_c_late, got_a, late_cq, cq1)
     up1 = shift(jnp.concatenate([s1, s2], axis=0), 1)
     down1 = shift(jnp.concatenate([s0, s1], axis=0), -1)
 
     qm3 = swap(jnp.where(upper, qm2, qm4), "ctx", 1)
     values, qm3 = together(values, qm3)
-    qs, cs = (q_f, got_b_late, got_a, qf2), (late_cq, cq1, cq2)
+    qs, cs = (q_f, got_c_late, got_a, qf2), (late_cq, cq1, cq2)
     dk_f, dv_f, dq0, dq1, dq2, sums, sum_ext, tail = full_grads(
         flag, k_f, values, qs, cs, (s0, s1, s2, up1, up2, down1, down2)
     )
 
     next_tail = shift(tail, -1)
+    cot_m = mid_cotangent(sums, next_tail, w_link, attended, mid_stat)
+    cot_m, dq1 = together(cot_m, dq1)
     near = swap(dq1, "ctx", 1)
-    cot_m = mid_cotangent(sums, next_tail, w_link, attended, mid_stat)
-    g2 = shift(cot_m, -2)
+    g2, sum_ext = together(shift(cot_m, -2), sum_ext)
     right = exchange(sum_ext, "ctx", X_GROUPS)
     term = dot_tn(left, right).astype(BF16)
     g1 = swap(jnp.where(upper, cot_m, g2), "ctx", 1)
-    g4 = shift(g2, -2)
+    term, g4 = together(term, shift(g2, -2))
     total = jnp.sum(exchange(term, "ctx", YZ_GROUPS).astype(F32).reshape(16, 16, WIDTH), axis=0)
     near, total = together(near, total)
     passed = jnp.where(upper, dq2.astype(F32), dq2.astype(F32) + near.astype(F32)).astype(BF16)
@@ -603,7 +601,6 @@
     every = exchange(jnp.concatenate([total] * 4, axis=0), "dp", None)
     factor = float(lax.axis_size("dp") * lax.axis_size("ctx") * F) ** (-0.5)
     grad_link = jnp.sum(every.reshape(4, 16, WIDTH), axis=0) * factor
-    pays = (kv4, kv3_late, kv2, got_a, got_b, own_kv)
     dq_m, dk_m, dv_m = mid_backward(flag, pays, (late_cq, cq1, cq2, qm3, qm4), (cot_m, g1, g2, g3, g4))
 
     dq_f = (dq0 + far.astype(F32) + jnp.where(upper, near.astype(F32), 0.0)).astype(BF16)

time: 226 us -> 230 us (1.018)
  blocking collectives: 22.9 us -> 0 us
  starting transfers between devices: 78.9 us -> 94.8 us
  waiting for transfers between devices: 58.6 us -> 67.8 us
    all_to_all x3 -> x4, starting transfers between devices: 31.5 us -> 56.1 us  [exchange(): lax.all_to_all(value, axis, 0, 0, axis_index_groups=groups, tiled=True)]
    all_to_all x1 -> x0, blocking collectives: 22.9 us -> none  [exchange(): lax.all_to_all(value, axis, 0, 0, axis_index_groups=groups, tiled=True)]
    all_to_all x3 -> x4, waiting for transfers between devices: 0.01 us -> 16.8 us  [exchange(): lax.all_to_all(value, axis, 0, 0, axis_index_groups=groups, tiled=True)]
    ppermute x8, starting transfers between devices: 16.4 us -> 8.19 us  [swap(): return lax.ppermute(value, axis, [(n, n ^ bit) for n in range(count)])]
    ppermute x13, waiting for transfers between devices: 46.2 us -> 42.1 us  [shift(): lax.ppermute(value, 'ctx', [(n, n + steps) for n in range(first, last)])]
    ppermute x8, waiting for transfers between devices: 12.4 us -> 8.82 us  [swap(): return lax.ppermute(value, axis, [(n, n ^ bit) for n in range(count)])]
  transfers between devices with their start and end apart: 24 -> 25, of which waited for: 11 -> 12; matrix products, arithmetic and copies ran while one was open for 4% -> 4% of each run, Pallas kernels for 14% -> 14%
where the time goes in v8:
time: 230 us; the launch traced here: 226 us
  starting transfers between devices  94.8 us (41%)
  waiting for transfers between devices  67.8 us (29%)
  Pallas kernels  46.8 us (20%)
  other arithmetic  9.1 us (4%)
  local copies, waits for them, and re-layouts  5.23 us (2%)
    all_to_all x4, starting transfers between devices, exchange(): lax.all_to_all(value, axis, 0, 0, axis_index_groups=groups, tiled=True)  56.1 us
    ppermute x13, waiting for transfers between devices, shift(): lax.ppermute(value, 'ctx', [(n, n + steps) for n in range(first, last)])  42.1 us
    ppermute x13, starting transfers between devices, shift(): lax.ppermute(value, 'ctx', [(n, n + steps) for n in range(first, last)])  30.5 us
    all_to_all x4, waiting for transfers between devices, exchange(): lax.all_to_all(value, axis, 0, 0, axis_index_groups=groups, tiled=True)  16.8 us
    pallas_call x1, Pallas kernels, full_grads(): call(grads_body, 'full_grads', 8000000000, 14000000, in_specs=[FLAG, head...  14.9 us
    ppermute x8, waiting for transfers between devices, swap(): return lax.ppermute(value, axis, [(n, n ^ bit) for n in range(count)])  8.82 us
    ppermute x8, starting transfers between devices, swap(): return lax.ppermute(value, axis, [(n, n ^ bit) for n in range(count)])  8.19 us
    pallas_call x1, Pallas kernels, mid_backward(): call(mid_bwd_body, 'mid_backward', 3000000000, 6000000, in_specs=[FLAG] +...  8.11 us
  transfers between devices with their start and end apart: 25, of which 12 were waited for; matrix products, arithmetic and copies ran while one was open for 4% of the time, Pallas kernels for 14%

profile of v8, /device:TPU:1, one launch (start us, length us, event | category | flops | bytes accessed | tf_op | source)
XLA Modules:
  0.0 226.1 jit_solution(12384138105189861574)
XLA Ops:
  3.2 4.0 %pack.1 = (bf16[288,1024]{1,0:T(8,128)(2,1)}, bf16[528,1024]{1,0:T(8,128)(2,1)}, bf16[384,1024]{1,0:T(8,128)(2,1)}) custom-call(s32[1]{0:T(128)} %bitcast.flag.refs_0_, bf16[128,1024]{1,0:T(8,128)(2,1)} %bitcast.36, bf16[128,1024]{1,0:T(8,128)(2,1)} %bitcast.41, bf16[128,1024]{1,0:T(8,128)(2,1)} %bitcast.42, bf16[16,256]{1,0:T(8,128)(2,1)} %broadcast_in_dim.27.ids, ...), custom_call_target="tpu_custom_call" | custom-call | tf_op jit(solution)/shard_map/pack/pallas_call | solution.py:118
  9.3 4.2 %collective-permute-start.1 = (bf16[288,1024]{1,0:T(8,128)(2,1)}, bf16[288,1024]{1,0:T(8,128)(2,1)S(1)}, u32[]{:S(2)}, u32[]{:S(2)}) collective-permute-start(bf16[288,1024]{1,0:T(8,128)(2,1)} %get-tuple-element.54.refs_7_.refs_6_), channel_id=1, source_target_pairs={{0,2},{1,3},{2,4},{3,5},{4,6},{5,7},{6,8},{7,9},{8,10},{9,11},{10,... | collective-permute-start | bytes 1769480 | tf_op jit(solution)/shard_map/ppermute | solution.py:523
  13.5 11.6 %collective-permute-done.1.refs_3_.refs_2_ = bf16[288,1024]{1,0:T(8,128)(2,1)S(1)} collective-permute-done((bf16[288,1024]{1,0:T(8,128)(2,1)}, bf16[288,1024]{1,0:T(8,128)(2,1)S(1)}, u32[]{:S(2)}, u32[]{:S(2)}) %collective-permute-start.1) | collective-permute-done | bytes 589856 | tf_op jit(solution)/shard_map/ppermute | solution.py:523
  25.6 4.1 %collective-permute-start.3 = (bf16[288,1024]{1,0:T(8,128)(2,1)S(1)}, bf16[288,1024]{1,0:T(8,128)(2,1)S(1)}, u32[]{:S(2)}, u32[]{:S(2)}) collective-permute-start(bf16[288,1024]{1,0:T(8,128)(2,1)S(1)} %collective-permute-done.1.refs_3_.refs_2_), channel_id=1, source_target_pairs={{0,2},{1,3},{2,4},{3,5},{4,6},{5,7},{6,8},{7,9},{8,10},{9,11},{10,... | collective-permute-start | bytes 1769480 | tf_op jit(solution)/shard_map/ppermute | solution.py:523
  31.2 6.7 %collective-permute-done.4.refs_5_.refs_4_ = bf16[288,1024]{1,0:T(8,128)(2,1)S(1)} collective-permute-done((bf16[288,1024]{1,0:T(8,128)(2,1)S(1)}, bf16[288,1024]{1,0:T(8,128)(2,1)S(1)}, u32[]{:S(2)}, u32[]{:S(2)}) %collective-permute-start.4) | collective-permute-done | bytes 589856 | tf_op jit(solution)/shard_map/ppermute | solution.py:528
  42.2 14.4 %collective-permute-done.6.refs_7_.refs_9_.refs_12_ = bf16[528,1024]{1,0:T(8,128)(2,1)S(1)} collective-permute-done((bf16[528,1024]{1,0:T(8,128)(2,1)}, bf16[528,1024]{1,0:T(8,128)(2,1)S(1)}, u32[]{:S(2)}, u32[]{:S(2)}) %collective-permute-start.6) | collective-permute-done | bytes 1081376 | tf_op jit(solution)/shard_map/ppermute | solution.py:523
  59.0 6.0 %mid_forward.1 = (bf16[144,1024]{1,0:T(8,128)(2,1)}, f32[128,1024]{1,0:T(8,128)}, f32[8,1024]{1,0:T(8,128)}) custom-call(s32[1]{0:T(128)} %bitcast.flag.refs_0_, bf16[128,1024]{1,0:T(8,128)(2,1)} %bitcast.37, bf16[288,1024]{1,0:T(8,128)(2,1)} %copy-done.9, bf16[288,1024]{1,0:T(8,128)(2,1)} %copy-done.13, ...), custom_call_target="tpu_custom_call" | custom-call | flops 700000000 | bytes 4000000 | tf_op jit(solution)/shard_map/mid_forward/pallas_call | solution.py:178
  66.8 14.9 %all-to-all-start = ((bf16[4,144,256]{2,1,0:T(8,128)(2,1)}), bf16[4,144,256]{2,1,0:T(8,128)(2,1)S(1)}, u32[]{:S(2)}, u32[]{:S(2)}) async-start(bf16[4,144,256]{2,1,0:T(8,128)(2,1)} %bitcast.8), calls=%async_computation | async-start | bytes 589824 | tf_op jit(solution)/shard_map/all_to_all | solution.py:544
  81.7 7.7 %full_stats.1 = (bf16[384,1024]{1,0:T(8,128)(2,1)}, f32[24,384]{1,0:T(8,128)}, f32[24,384]{1,0:T(8,128)}) custom-call(bf16[384,1024]{1,0:T(8,128)(2,1)} %bitcast.31, bf16[384,1024]{1,0:T(8,128)(2,1)} %bitcast.38, bf16[144,1024]{1,0:T(8,128)(2,1)} %get-tuple-element.64.refs_2_, bf16[1024,1024]{1,0:T(8,128)(2,1)} %w_ref.1, bf16[384,1024]{1,0:T(8,128)(2,1)} %bitcast.29, ...), custom_call_target="tpu_custom_call" | custom-call | flops 2000000000 | bytes 8000000 | tf_op jit(solution)/shard_map/full_stats/pallas_call | solution.py:294
  89.4 3.4 %collective-permute-start.9 = (f32[24,384]{1,0:T(8,128)}, f32[24,384]{1,0:T(8,128)S(1)}, u32[]{:S(2)}, u32[]{:S(2)}) collective-permute-start(f32[24,384]{1,0:T(8,128)} %get-tuple-element.65.refs_15_), channel_id=1, source_target_pairs={{0,2},{1,3},{2,4},{3,5},{4,6},{5,7},{6,8},{7,9},{8,10},{9,11},{10,... | collective-permute-start | bytes 110600 | tf_op jit(solution)/shard_map/ppermute | solution.py:523
  95.4 2.3 %collective-permute-done.10.refs_19_ = f32[24,384]{1,0:T(8,128)S(1)} collective-permute-done((f32[24,384]{1,0:T(8,128)}, f32[24,384]{1,0:T(8,128)S(1)}, u32[]{:S(2)}, u32[]{:S(2)}) %collective-permute-start.10) | collective-permute-done | bytes 36896 | tf_op jit(solution)/shard_map/ppermute | solution.py:523
  98.7 4.8 %next_stats.1.refs_14_ = f32[24,384]{1,0:T(8,128)} custom-call(s32[1]{0:T(128)} %bitcast.flag.refs_0_, bf16[384,1024]{1,0:T(8,128)(2,1)} %bitcast.32, bf16[384,1024]{1,0:T(8,128)(2,1)} %get-tuple-element.73.refs_2_, bf16[384,1024]{1,0:T(8,128)(2,1)} %collective-permute-done.5.refs_6_.refs_3_.refs_4_.refs_5_, ...), custom_call_target="tpu_custom_call" | custom-call | flops 1000000000 | bytes 6000000 | tf_op jit(solution)/shard_map/next_stats/pallas_call | solution.py:313
  105.8 4.3 %collective-permute-start.12 = (f32[48,384]{1,0:T(8,128)S(1)}, f32[48,384]{1,0:T(8,128)S(1)}, u32[]{:S(2)}, u32[]{:S(2)}) collective-permute-start(f32[48,384]{1,0:T(8,128)S(1)} %get-tuple-element.104), channel_id=1, source_target_pairs={{0,1},{1,2},{2,3},{3,4},{4,5},{5,6},{6,7},{7,8},{8,9},{9,10},{10,1... | collective-permute-start | bytes 221192 | tf_op jit(solution)/shard_map/ppermute | solution.py:523
  111.9 14.9 %full_grads.1 = (bf16[384,1024]{1,0:T(8,128)(2,1)}, bf16[384,1024]{1,0:T(8,128)(2,1)}, f32[384,1024]{1,0:T(8,128)}, bf16[384,1024]{1,0:T(8,128)(2,1)}, bf16[384,...) custom-call(s32[1]{0:T(128)} %bitcast.flag.refs_0_, ...), custom_call_target="tpu_custom_call" | custom-call | flops 8000000000 | bytes 14000000 | tf_op jit(solution)/shard_map/full_grads/pallas_call | solution.py:384
  128.2 3.9 %collective-permute-done.14.refs_3_ = f32[8,1024]{1,0:T(8,128)S(1)} collective-permute-done((f32[8,1024]{1,0:T(8,128)}, f32[8,1024]{1,0:T(8,128)S(1)}, u32[]{:S(2)}, u32[]{:S(2)}) %collective-permute-start.14) | collective-permute-done | bytes 32800 | tf_op jit(solution)/shard_map/ppermute | solution.py:523
  135.8 7.3 %collective-permute-done.15.refs_14_ = bf16[144,1024]{1,0:T(8,128)(2,1)S(1)} collective-permute-done((bf16[144,1024]{1,0:T(8,128)(2,1)S(1)}, bf16[144,1024]{1,0:T(8,128)(2,1)S(1)}, u32[]{:S(2)}, u32[]{:S(2)}) %collective-permute-start.15) | collective-permute-done | bytes 294944 | tf_op jit(solution)/shard_map/ppermute | solution.py:523
  143.1 10.4 %all-to-all-start.1 = ((bf16[4,144,1024]{2,1,0:T(8,128)(2,1)}), bf16[4,144,1024]{2,1,0:T(8,128)(2,1)S(1)}, u32[]{:S(2)}, u32[]{:S(2)}) async-start(bf16[4,144,1024]{2,1,0:T(8,128)(2,1)} %bitcast.34), calls=%async_computation.1 | async-start | bytes 2359296 | tf_op jit(solution)/shard_map/all_to_all | solution.py:544
  154.7 9.2 %all-to-all-done.1 = bf16[4,144,1024]{2,1,0:T(8,128)(2,1)S(1)} async-done(((bf16[4,144,1024]{2,1,0:T(8,128)(2,1)}), bf16[4,144,1024]{2,1,0:T(8,128)(2,1)S(1)}, u32[]{:S(2)}, u32[]{:S(2)}) %all-to-all-start.1) | async-done | bytes 1179680 | tf_op jit(solution)/shard_map/all_to_all | solution.py:544
  165.3 8.0 %all-to-all-start.2 = ((bf16[16,16,1024]{2,1,0:T(8,128)(2,1)}), bf16[16,16,1024]{2,1,0:T(8,128)(2,1)S(1)}, u32[]{:S(2)}, u32[]{:S(2)}) async-start(bf16[16,16,1024]{2,1,0:T(8,128)(2,1)} %bitcast.17), calls=%async_computation.2 | async-start | bytes 1048576 | tf_op jit(solution)/shard_map/all_to_all | solution.py:544
  177.7 7.7 %all-to-all-done.2 = bf16[16,16,1024]{2,1,0:T(8,128)(2,1)S(1)} async-done(((bf16[16,16,1024]{2,1,0:T(8,128)(2,1)}), bf16[16,16,1024]{2,1,0:T(8,128)(2,1)S(1)}, u32[]{:S(2)}, u32[]{:S(2)}) %all-to-all-start.2) | async-done | bytes 524320 | tf_op jit(solution)/shard_map/all_to_all | solution.py:544
  187.4 4.0 %collective-permute-start.20 = (bf16[384,1024]{1,0:T(8,128)(2,1)S(1)}, bf16[384,1024]{1,0:T(8,128)(2,1)}, u32[]{:S(2)}, u32[]{:S(2)}) collective-permute-start(bf16[384,1024]{1,0:T(8,128)(2,1)S(1)} %fusion.2), channel_id=1, source_target_pairs={{0,2},{1,3},{2,4},{3,5},{4,6},{5,7},{6,8},{7,9},{8,10},{9,11},{10,... | collective-permute-start | bytes 2359304 | tf_op jit(solution)/shard_map/ppermute | solution.py:523
  192.1 22.8 %all-to-all-start.3 = ((f32[4,16,1024]{2,1,0:T(8,128)}), f32[4,16,1024]{2,1,0:T(8,128)S(1)}, u32[]{:S(2)}, u32[]{:S(2)}) async-start(f32[4,16,1024]{2,1,0:T(8,128)} %bitcast.21), calls=%async_computation.3 | async-start | bytes 524288 | tf_op jit(solution)/shard_map/all_to_all | solution.py:544
  214.9 8.1 %mid_backward.1 = (bf16[128,1024]{1,0:T(8,128)(2,1)}, bf16[128,1024]{1,0:T(8,128)(2,1)}, bf16[128,1024]{1,0:T(8,128)(2,1)}) custom-call(s32[1]{0:T(128)} %bitcast.flag.refs_0_, bf16[288,1024]{1,0:T(8,128)(2,1)} %copy-done.9, bf16[288,1024]{1,0:T(8,128)(2,1)} %copy-done.13, bf16[384,1024]{1,0:T(8,128)(2,1)} %collective-permute-done.2.refs_4_.refs_5_.refs_3_, ...), custom_call_target="tpu_custom_call" | custom-call | flops 3000000000 | bytes 6000000 | tf_op jit(solution)/shard_map/mid_backward/pallas_call | solution.py:508
  223.7 2.4 %fusion.3 = bf16[1,384,1024]{2,1,0:T(8,128)(2,1)} fusion(bf16[384,1024]{1,0:T(8,128)(2,1)S(1)} %collective-permute-done.19, f32[384,1024]{1,0:T(8,128)S(1)} %copy-done.10, bf16[384,1024]{1,0:T(8,128)(2,1)} %collective-permute-done.20, pred[]{:T(512)S(6)} %eq.6), kind=kLoop, calls=%fused_computation.8 | loop fusion | flops 2359296 | bytes 3932161 | tf_op jit(solution)/shard_map/broadcast_in_dim | solution.py:607
  (104 shorter events, 38.0 us)
Async XLA Ops:
  0.6 24.5 %collective-permute-start = (bf16[384,1024]{1,0:T(8,128)(2,1)}, bf16[384,1024]{1,0:T(8,128)(2,1)S(1)}, u32[]{:S(2)}, u32[]{:S(2)}) collective-permute-start(bf16[384,1024]{1,0:T(8,128)(2,1)} %bitcast.27), channel_id=1, source_target_pairs={{2,0},{3,1},{4,2},{5,3},{6,4},{7,5},{8,6},{9,7},{10,8},{11,9},{12,... | collective-permute-start | bytes 2359304 | tf_op jit(solution)/shard_map/ppermute | solution.py:523
  7.2 18.4 %collective-permute-start.2 = (bf16[384,1024]{1,0:T(8,128)(2,1)}, bf16[384,1024]{1,0:T(8,128)(2,1)}, u32[]{:S(2)}, u32[]{:S(2)}) collective-permute-start(bf16[384,1024]{1,0:T(8,128)(2,1)} %get-tuple-element.55), channel_id=1, source_target_pairs={{0,1},{1,0},{2,3},{3,2},{4,5},{5,4},{6,7},{7,6},{8,9},{9,8},{10,11... | collective-permute-start | bytes 2359304 | tf_op jit(solution)/shard_map/ppermute | solution.py:528
  9.3 15.8 %collective-permute-start.1 = (bf16[288,1024]{1,0:T(8,128)(2,1)}, bf16[288,1024]{1,0:T(8,128)(2,1)S(1)}, u32[]{:S(2)}, u32[]{:S(2)}) collective-permute-start(bf16[288,1024]{1,0:T(8,128)(2,1)} %get-tuple-element.54.refs_7_.refs_6_), channel_id=1, source_target_pairs={{0,2},{1,3},{2,4},{3,5},{4,6},{5,7},{6,8},{7,9},{8,10},{9,11},{10,... | collective-permute-start | bytes 1769480 | tf_op jit(solution)/shard_map/ppermute | solution.py:523
  25.1 12.7 %collective-permute-start.4 = (bf16[288,1024]{1,0:T(8,128)(2,1)S(1)}, bf16[288,1024]{1,0:T(8,128)(2,1)S(1)}, u32[]{:S(2)}, u32[]{:S(2)}) collective-permute-start(bf16[288,1024]{1,0:T(8,128)(2,1)S(1)} %collective-permute-done.1.refs_3_.refs_2_), channel_id=1, source_target_pairs={{0,1},{1,0},{2,3},{3,2},{4,5},{5,4},{6,7},{7,6},{8,9},{9,8},{10,11... | collective-permute-start | bytes 1769480 | tf_op jit(solution)/shard_map/ppermute | solution.py:528
  25.6 13.6 %collective-permute-start.3 = (bf16[288,1024]{1,0:T(8,128)(2,1)S(1)}, bf16[288,1024]{1,0:T(8,128)(2,1)S(1)}, u32[]{:S(2)}, u32[]{:S(2)}) collective-permute-start(bf16[288,1024]{1,0:T(8,128)(2,1)S(1)} %collective-permute-done.1.refs_3_.refs_2_), channel_id=1, source_target_pairs={{0,2},{1,3},{2,4},{3,5},{4,6},{5,7},{6,8},{7,9},{8,10},{9,11},{10,... | collective-permute-start | bytes 1769480 | tf_op jit(solution)/shard_map/ppermute | solution.py:523
  29.7 26.9 %collective-permute-start.6 = (bf16[528,1024]{1,0:T(8,128)(2,1)}, bf16[528,1024]{1,0:T(8,128)(2,1)S(1)}, u32[]{:S(2)}, u32[]{:S(2)}) collective-permute-start(bf16[528,1024]{1,0:T(8,128)(2,1)} %get-tuple-element.61.refs_6_.refs_8_.refs_7_.refs_10_), channel_id=1, source_target_pairs={{2,0},{3,1},{4,2},{5,3},{6,4},{7,5},{8,6},{9,7},{10,8},{11,9},{12,... | collective-permute-start | bytes 3244040 | tf_op jit(solution)/shard_map/ppermute | solution.py:523
  40.0 16.6 %collective-permute-start.5 = (bf16[384,1024]{1,0:T(8,128)(2,1)S(1)}, bf16[384,1024]{1,0:T(8,128)(2,1)}, u32[]{:S(2)}, u32[]{:S(2)}) collective-permute-start(bf16[384,1024]{1,0:T(8,128)(2,1)S(1)} %pad_maximum_fusion), channel_id=1, source_target_pairs={{0,1},{1,0},{2,3},{3,2},{4,5},{5,4},{6,7},{7,6},{8,9},{9,8},{10,11... | collective-permute-start | bytes 2359304 | tf_op jit(solution)/shard_map/ppermute | solution.py:528
  56.7 41.0 %collective-permute-start.7 = (bf16[528,1024]{1,0:T(8,128)(2,1)S(1)}, bf16[528,1024]{1,0:T(8,128)(2,1)S(1)}, u32[]{:S(2)}, u32[]{:S(2)}) collective-permute-start(bf16[528,1024]{1,0:T(8,128)(2,1)S(1)} %broadcast_select_fusion), channel_id=1, source_target_pairs={{0,1},{1,0},{2,3},{3,2},{4,5},{5,4},{6,7},{7,6},{8,9},{9,8},{10,11... | collective-permute-start | bytes 3244040 | tf_op jit(solution)/shard_map/ppermute | solution.py:528
  57.7 24.0 %collective-permute-start.8 = (bf16[144,1024]{1,0:T(8,128)(2,1)S(1)}, bf16[144,1024]{1,0:T(8,128)(2,1)S(1)}, u32[]{:S(2)}, u32[]{:S(2)}) collective-permute-start(bf16[144,1024]{1,0:T(8,128)(2,1)S(1)} %slice.27), channel_id=1, source_target_pairs={{2,0},{3,1},{4,2},{5,3},{6,4},{7,5},{8,6},{9,7},{10,8},{11,9},{12,... | collective-permute-start | bytes 884744 | tf_op jit(solution)/shard_map/ppermute | solution.py:523
  66.8 28.6 %all-to-all-start = ((bf16[4,144,256]{2,1,0:T(8,128)(2,1)}), bf16[4,144,256]{2,1,0:T(8,128)(2,1)S(1)}, u32[]{:S(2)}, u32[]{:S(2)}) async-start(bf16[4,144,256]{2,1,0:T(8,128)(2,1)} %bitcast.8), calls=%async_computation | async-start | bytes 589824 | tf_op jit(solution)/shard_map/all_to_all | solution.py:544
  89.4 6.0 %collective-permute-start.9 = (f32[24,384]{1,0:T(8,128)}, f32[24,384]{1,0:T(8,128)S(1)}, u32[]{:S(2)}, u32[]{:S(2)}) collective-permute-start(f32[24,384]{1,0:T(8,128)} %get-tuple-element.65.refs_15_), channel_id=1, source_target_pairs={{0,2},{1,3},{2,4},{3,5},{4,6},{5,7},{6,8},{7,9},{8,10},{9,11},{10,... | collective-permute-start | bytes 110600 | tf_op jit(solution)/shard_map/ppermute | solution.py:523
  95.1 15.0 %collective-permute-start.11 = (bf16[144,1024]{1,0:T(8,128)(2,1)S(1)}, bf16[144,1024]{1,0:T(8,128)(2,1)}, u32[]{:S(2)}, u32[]{:S(2)}) collective-permute-start(bf16[144,1024]{1,0:T(8,128)(2,1)S(1)} %broadcast_select_fusion.3), channel_id=1, source_target_pairs={{0,1},{1,0},{2,3},{3,2},{4,5},{5,4},{6,7},{7,6},{8,9},{9,8},{10,11... | collective-permute-start | bytes 884744 | tf_op jit(solution)/shard_map/ppermute | solution.py:528
  104.4 5.7 %collective-permute-start.13 = (f32[48,384]{1,0:T(8,128)S(1)}, f32[48,384]{1,0:T(8,128)S(1)}, u32[]{:S(2)}, u32[]{:S(2)}) collective-permute-start(f32[48,384]{1,0:T(8,128)S(1)} %get-tuple-element.103), channel_id=1, source_target_pairs={{1,0},{2,1},{3,2},{4,3},{5,4},{6,5},{7,6},{8,7},{9,8},{10,9},{11,1... | collective-permute-start | bytes 221192 | tf_op jit(solution)/shard_map/ppermute | solution.py:523
  105.8 5.5 %collective-permute-start.12 = (f32[48,384]{1,0:T(8,128)S(1)}, f32[48,384]{1,0:T(8,128)S(1)}, u32[]{:S(2)}, u32[]{:S(2)}) collective-permute-start(f32[48,384]{1,0:T(8,128)S(1)} %get-tuple-element.104), channel_id=1, source_target_pairs={{0,1},{1,2},{2,3},{3,4},{4,5},{5,6},{6,7},{7,8},{8,9},{9,10},{10,1... | collective-permute-start | bytes 221192 | tf_op jit(solution)/shard_map/ppermute | solution.py:523
  126.9 5.2 %collective-permute-start.14 = (f32[8,1024]{1,0:T(8,128)}, f32[8,1024]{1,0:T(8,128)S(1)}, u32[]{:S(2)}, u32[]{:S(2)}) collective-permute-start(f32[8,1024]{1,0:T(8,128)} %get-tuple-element.78), channel_id=1, source_target_pairs={{1,0},{2,1},{3,2},{4,3},{5,4},{6,5},{7,6},{8,7},{9,8},{10,9},{11,1... | collective-permute-start | bytes 98312 | tf_op jit(solution)/shard_map/ppermute | solution.py:523
  134.3 8.7 %collective-permute-start.15 = (bf16[144,1024]{1,0:T(8,128)(2,1)S(1)}, bf16[144,1024]{1,0:T(8,128)(2,1)S(1)}, u32[]{:S(2)}, u32[]{:S(2)}) collective-permute-start(bf16[144,1024]{1,0:T(8,128)(2,1)S(1)} %mid_cotangent.1.refs_12_), channel_id=1, source_target_pairs={{2,0},{3,1},{4,2},{5,3},{6,4},{7,5},{8,6},{9,7},{10,8},{11,9},{12,... | collective-permute-start | bytes 884744 | tf_op jit(solution)/shard_map/ppermute | solution.py:523
  143.1 20.8 %all-to-all-start.1 = ((bf16[4,144,1024]{2,1,0:T(8,128)(2,1)}), bf16[4,144,1024]{2,1,0:T(8,128)(2,1)S(1)}, u32[]{:S(2)}, u32[]{:S(2)}) async-start(bf16[4,144,1024]{2,1,0:T(8,128)(2,1)} %bitcast.34), calls=%async_computation.1 | async-start | bytes 2359296 | tf_op jit(solution)/shard_map/all_to_all | solution.py:544
  153.5 11.8 %collective-permute-start.17 = (bf16[144,1024]{1,0:T(8,128)(2,1)S(1)}, bf16[144,1024]{1,0:T(8,128)(2,1)S(1)}, u32[]{:S(2)}, u32[]{:S(2)}) collective-permute-start(bf16[144,1024]{1,0:T(8,128)(2,1)S(1)} %collective-permute-done.15.refs_14_), channel_id=1, source_target_pairs={{2,0},{3,1},{4,2},{5,3},{6,4},{7,5},{8,6},{9,7},{10,8},{11,9},{12,... | collective-permute-start | bytes 884744 | tf_op jit(solution)/shard_map/ppermute | solution.py:523
  165.3 20.0 %all-to-all-start.2 = ((bf16[16,16,1024]{2,1,0:T(8,128)(2,1)}), bf16[16,16,1024]{2,1,0:T(8,128)(2,1)S(1)}, u32[]{:S(2)}, u32[]{:S(2)}) async-start(bf16[16,16,1024]{2,1,0:T(8,128)(2,1)} %bitcast.17), calls=%async_computation.2 | async-start | bytes 1048576 | tf_op jit(solution)/shard_map/all_to_all | solution.py:544
  173.3 13.8 %collective-permute-start.19 = (bf16[384,1024]{1,0:T(8,128)(2,1)}, bf16[384,1024]{1,0:T(8,128)(2,1)S(1)}, u32[]{:S(2)}, u32[]{:S(2)}) collective-permute-start(bf16[384,1024]{1,0:T(8,128)(2,1)} %get-tuple-element.93), channel_id=1, source_target_pairs={{0,1},{1,0},{2,3},{3,2},{4,5},{5,4},{6,7},{7,6},{8,9},{9,8},{10,11... | collective-permute-start | bytes 2359304 | tf_op jit(solution)/shard_map/ppermute | solution.py:528
  175.4 39.5 %collective-permute-start.16 = (bf16[144,1024]{1,0:T(8,128)(2,1)}, bf16[144,1024]{1,0:T(8,128)(2,1)}, u32[]{:S(2)}, u32[]{:S(2)}) collective-permute-start(bf16[144,1024]{1,0:T(8,128)(2,1)} %broadcast_select_fusion.2), channel_id=1, source_target_pairs={{0,1},{1,0},{2,3},{3,2},{4,5},{5,4},{6,7},{7,6},{8,9},{9,8},{10,11... | collective-permute-start | bytes 884744 | tf_op jit(solution)/shard_map/ppermute | solution.py:528
  176.4 38.6 %collective-permute-start.18 = (bf16[144,1024]{1,0:T(8,128)(2,1)}, bf16[144,1024]{1,0:T(8,128)(2,1)}, u32[]{:S(2)}, u32[]{:S(2)}) collective-permute-start(bf16[144,1024]{1,0:T(8,128)(2,1)} %broadcast_select_fusion.1), channel_id=1, source_target_pairs={{0,1},{1,0},{2,3},{3,2},{4,5},{5,4},{6,7},{7,6},{8,9},{9,8},{10,11... | collective-permute-start | bytes 884744 | tf_op jit(solution)/shard_map/ppermute | solution.py:528
  187.4 36.3 %collective-permute-start.20 = (bf16[384,1024]{1,0:T(8,128)(2,1)S(1)}, bf16[384,1024]{1,0:T(8,128)(2,1)}, u32[]{:S(2)}, u32[]{:S(2)}) collective-permute-start(bf16[384,1024]{1,0:T(8,128)(2,1)S(1)} %fusion.2), channel_id=1, source_target_pairs={{0,2},{1,3},{2,4},{3,5},{4,6},{5,7},{6,8},{7,9},{8,10},{9,11},{10,... | collective-permute-start | bytes 2359304 | tf_op jit(solution)/shard_map/ppermute | solution.py:523
  192.1 31.0 %all-to-all-start.3 = ((f32[4,16,1024]{2,1,0:T(8,128)}), f32[4,16,1024]{2,1,0:T(8,128)S(1)}, u32[]{:S(2)}, u32[]{:S(2)}) async-start(f32[4,16,1024]{2,1,0:T(8,128)} %bitcast.21), calls=%async_computation.3 | async-start | bytes 524288 | tf_op jit(solution)/shard_map/all_to_all | solution.py:544
  (26 other events, 350.4 us)

commit v9 on v8

--- a/solution.py
+++ b/solution.py
@@ -565,13 +565,11 @@
 
     pays = (kv4, kv2, got_a, got_b, got_c, own_kv)
     mid_ext, attended, mid_stat = mid_forward(flag, q_m, pays)
-    parts = jnp.concatenate([mid_ext[:, n * 256 : (n + 1) * 256] for n in range(4)], axis=0)
-    left = exchange(parts, "ctx", X_GROUPS)
     qm2 = cq2[F:]
     qm4, mid_ext = together(shift(qm2, -2), mid_ext)
     values, s0, s2 = full_stats(k_f, v_base[0], mid_ext, w_link, q_f, qf2, late_cq, cq2)
     up2, down2 = shift(s2, 2), shift(s0, -2)
-    left, cq1, up2, down2 = together(left, cq1, up2, down2)
+    cq1, up2, down2 = together(cq1, up2, down2)
     s1 = next_stats(flag, k_f, values, got_c_late, got_a, late_cq, cq1)
     up1 = shift(jnp.concatenate([s1, s2], axis=0), 1)
     down1 = shift(jnp.concatenate([s0, s1], axis=0), -1)
@@ -585,20 +583,22 @@
 
     next_tail = shift(tail, -1)
     cot_m = mid_cotangent(sums, next_tail, w_link, attended, mid_stat)
-    cot_m, dq1 = together(cot_m, dq1)
+    cot_m, dq1, mid_ext = together(cot_m, dq1, mid_ext)
+    parts = jnp.concatenate([mid_ext[:, n * 256 : (n + 1) * 256] for n in range(4)], axis=0)
+    left = exchange(parts, "ctx", X_GROUPS)
     near = swap(dq1, "ctx", 1)
     g2, sum_ext = together(shift(cot_m, -2), sum_ext)
     right = exchange(sum_ext, "ctx", X_GROUPS)
     term = dot_tn(left, right).astype(BF16)
     g1 = swap(jnp.where(upper, cot_m, g2), "ctx", 1)
-    term, g4 = together(term, shift(g2, -2))
+    term, g4, near = together(term, shift(g2, -2), near)
     total = jnp.sum(exchange(term, "ctx", YZ_GROUPS).astype(F32).reshape(16, 16, WIDTH), axis=0)
-    near, total = together(near, total)
+    g2_late, g4 = together(g2, g4)
+    total, g3 = together(total, swap(jnp.where(upper, g2_late, g4), "ctx", 1))
+    every = exchange(jnp.concatenate([total] * 4, axis=0), "dp", None)
+    near, every = together(near, every)
     passed = jnp.where(upper, dq2.astype(F32), dq2.astype(F32) + near.astype(F32)).astype(BF16)
     far = shift(passed, 2)
-    g2_late, g4 = together(g2, g4)
-    g3 = swap(jnp.where(upper, g2_late, g4), "ctx", 1)
-    every = exchange(jnp.concatenate([total] * 4, axis=0), "dp", None)
     factor = float(lax.axis_size("dp") * lax.axis_size("ctx") * F) ** (-0.5)
     grad_link = jnp.sum(every.reshape(4, 16, WIDTH), axis=0) * factor
     dq_m, dk_m, dv_m = mid_backward(flag, pays, (late_cq, cq1, cq2, qm3, qm4), (cot_m, g1, g2, g3, g4))

time: 230 us -> 244 us (1.061)
  the two profiles are of different devices: /device:TPU:1 before, /device:TPU:4 now
where the time goes in v9:
time: 244 us; the launch traced here: 243 us
  waiting for transfers between devices  100 us (41%)
  starting transfers between devices  78.7 us (32%)
  Pallas kernels  46.7 us (19%)
  other arithmetic  9.27 us (4%)
  local copies, waits for them, and re-layouts  5.54 us (2%)
    ppermute x13, waiting for transfers between devices, shift(): lax.ppermute(value, 'ctx', [(n, n + steps) for n in range(first, last)])  61.3 us
    ppermute x13, starting transfers between devices, shift(): lax.ppermute(value, 'ctx', [(n, n + steps) for n in range(first, last)])  45.5 us
    all_to_all x4, waiting for transfers between devices, exchange(): lax.all_to_all(value, axis, 0, 0, axis_index_groups=groups, tiled=True)  23.1 us
    all_to_all x4, starting transfers between devices, exchange(): lax.all_to_all(value, axis, 0, 0, axis_index_groups=groups, tiled=True)  20.6 us
    ppermute x8, waiting for transfers between devices, swap(): return lax.ppermute(value, axis, [(n, n ^ bit) for n in range(count)])  16 us
    pallas_call x1, Pallas kernels, full_grads(): call(grads_body, 'full_grads', 8000000000, 14000000, in_specs=[FLAG, head...  14.9 us
    ppermute x8, starting transfers between devices, swap(): return lax.ppermute(value, axis, [(n, n ^ bit) for n in range(count)])  12.6 us
    pallas_call x1, Pallas kernels, mid_backward(): call(mid_bwd_body, 'mid_backward', 3000000000, 6000000, in_specs=[FLAG] +...  7.99 us
  transfers between devices with their start and end apart: 25, of which 16 were waited for; matrix products, arithmetic and copies ran while one was open for 4% of the time, Pallas kernels for 13%

profile of v9, /device:TPU:4, one launch (start us, length us, event | category | flops | bytes accessed | tf_op | source)
XLA Modules:
  0.0 243.1 jit_solution(1792039403538409918)
XLA Ops:
  0.6 7.7 %collective-permute-start = (bf16[384,1024]{1,0:T(8,128)(2,1)}, bf16[384,1024]{1,0:T(8,128)(2,1)S(1)}, u32[]{:S(2)}, u32[]{:S(2)}) collective-permute-start(bf16[384,1024]{1,0:T(8,128)(2,1)} %bitcast.31), channel_id=1, source_target_pairs={{2,0},{3,1},{4,2},{5,3},{6,4},{7,5},{8,6},{9,7},{10,8},{11,9},{12,... | collective-permute-start | bytes 2359304 | tf_op jit(solution)/shard_map/ppermute | solution.py:523
  17.1 16.9 %collective-permute-done.1.refs_3_.refs_2_ = bf16[288,1024]{1,0:T(8,128)(2,1)} collective-permute-done((bf16[288,1024]{1,0:T(8,128)(2,1)}, bf16[288,1024]{1,0:T(8,128)(2,1)}, u32[]{:S(2)}, u32[]{:S(2)}) %collective-permute-start.1) | collective-permute-done | bytes 589856 | tf_op jit(solution)/shard_map/ppermute | solution.py:523
  36.4 6.2 %collective-permute-start.6 = (bf16[528,1024]{1,0:T(8,128)(2,1)}, bf16[528,1024]{1,0:T(8,128)(2,1)S(1)}, u32[]{:S(2)}, u32[]{:S(2)}) collective-permute-start(bf16[528,1024]{1,0:T(8,128)(2,1)} %get-tuple-element.64.refs_6_.refs_8_.refs_7_.refs_10_), channel_id=1, source_target_pairs={{2,0},{3,1},{4,2},{5,3},{6,4},{7,5},{8,6},{9,7},{10,8},{11,9},{12,... | collective-permute-start | bytes 3244040 | tf_op jit(solution)/shard_map/ppermute | solution.py:523
  42.6 5.3 %collective-permute-done.4.refs_5_.refs_4_ = bf16[288,1024]{1,0:T(8,128)(2,1)} collective-permute-done((bf16[288,1024]{1,0:T(8,128)(2,1)}, bf16[288,1024]{1,0:T(8,128)(2,1)}, u32[]{:S(2)}, u32[]{:S(2)}) %collective-permute-start.4) | collective-permute-done | bytes 589856 | tf_op jit(solution)/shard_map/ppermute | solution.py:528
  54.4 9.6 %collective-permute-done.6.refs_7_.refs_9_.refs_12_ = bf16[528,1024]{1,0:T(8,128)(2,1)S(1)} collective-permute-done((bf16[528,1024]{1,0:T(8,128)(2,1)}, bf16[528,1024]{1,0:T(8,128)(2,1)S(1)}, u32[]{:S(2)}, u32[]{:S(2)}) %collective-permute-start.6) | collective-permute-done | bytes 1081376 | tf_op jit(solution)/shard_map/ppermute | solution.py:523
  64.0 6.3 %collective-permute-done.5.refs_6_.refs_3_.refs_4_.refs_5_ = bf16[384,1024]{1,0:T(8,128)(2,1)} collective-permute-done((bf16[384,1024]{1,0:T(8,128)(2,1)S(1)}, bf16[384,1024]{1,0:T(8,128)(2,1)}, u32[]{:S(2)}, u32[]{:S(2)}) %collective-permute-start.5) | collective-permute-done | bytes 786464 | tf_op jit(solution)/shard_map/ppermute | solution.py:528
  74.7 6.1 %mid_forward.1 = (bf16[144,1024]{1,0:T(8,128)(2,1)}, f32[128,1024]{1,0:T(8,128)}, f32[8,1024]{1,0:T(8,128)}) custom-call(s32[1]{0:T(128)} %bitcast.flag.refs_0_, bf16[128,1024]{1,0:T(8,128)(2,1)} %bitcast.39, bf16[288,1024]{1,0:T(8,128)(2,1)} %copy-done.9, bf16[288,1024]{1,0:T(8,128)(2,1)} %collective-permute-done.1.refs_3_.refs_2_, ...), custom_call_target="tpu_custom_call" | custom-call | flops 700000000 | bytes 4000000 | tf_op jit(solution)/shard_map/mid_forward/pallas_call | solution.py:178
  81.6 7.7 %full_stats.1 = (bf16[384,1024]{1,0:T(8,128)(2,1)}, f32[24,384]{1,0:T(8,128)}, f32[24,384]{1,0:T(8,128)}) custom-call(bf16[384,1024]{1,0:T(8,128)(2,1)} %bitcast.35, bf16[384,1024]{1,0:T(8,128)(2,1)} %bitcast.40, bf16[144,1024]{1,0:T(8,128)(2,1)} %get-tuple-element.86.refs_2_, bf16[1024,1024]{1,0:T(8,128)(2,1)} %w_ref.1, bf16[384,1024]{1,0:T(8,128)(2,1)} %bitcast.33, ...), custom_call_target="tpu_custom_call" | custom-call | flops 2000000000 | bytes 8000000 | tf_op jit(solution)/shard_map/full_stats/pallas_call | solution.py:294
  92.5 4.8 %collective-permute-start.10 = (f32[24,384]{1,0:T(8,128)}, f32[24,384]{1,0:T(8,128)S(1)}, u32[]{:S(2)}, u32[]{:S(2)}) collective-permute-start(f32[24,384]{1,0:T(8,128)} %get-tuple-element.69.refs_13_), channel_id=1, source_target_pairs={{2,0},{3,1},{4,2},{5,3},{6,4},{7,5},{8,6},{9,7},{10,8},{11,9},{12,... | collective-permute-start | bytes 110600 | tf_op jit(solution)/shard_map/ppermute | solution.py:523
  100.6 4.8 %next_stats.1.refs_14_ = f32[24,384]{1,0:T(8,128)} custom-call(s32[1]{0:T(128)} %bitcast.flag.refs_0_, bf16[384,1024]{1,0:T(8,128)(2,1)} %bitcast.36, bf16[384,1024]{1,0:T(8,128)(2,1)} %get-tuple-element.76.refs_2_, bf16[384,1024]{1,0:T(8,128)(2,1)} %collective-permute-done.5.refs_6_.refs_3_.refs_4_.refs_5_, ...), custom_call_target="tpu_custom_call" | custom-call | flops 1000000000 | bytes 6000000 | tf_op jit(solution)/shard_map/next_stats/pallas_call | solution.py:313
  106.2 5.9 %collective-permute-start.13 = (f32[48,384]{1,0:T(8,128)S(1)}, f32[48,384]{1,0:T(8,128)S(1)}, u32[]{:S(2)}, u32[]{:S(2)}) collective-permute-start(f32[48,384]{1,0:T(8,128)S(1)} %get-tuple-element.109), channel_id=1, source_target_pairs={{1,0},{2,1},{3,2},{4,3},{5,4},{6,5},{7,6},{8,7},{9,8},{10,9},{11,1... | collective-permute-start | bytes 221192 | tf_op jit(solution)/shard_map/ppermute | solution.py:523
  114.4 7.1 %collective-permute-done.12.refs_16_ = f32[48,384]{1,0:T(8,128)S(1)} collective-permute-done((f32[48,384]{1,0:T(8,128)S(1)}, f32[48,384]{1,0:T(8,128)S(1)}, u32[]{:S(2)}, u32[]{:S(2)}) %collective-permute-start.12) | collective-permute-done | bytes 73760 | tf_op jit(solution)/shard_map/ppermute | solution.py:523
  122.2 14.9 %full_grads.1 = (bf16[384,1024]{1,0:T(8,128)(2,1)}, bf16[384,1024]{1,0:T(8,128)(2,1)}, f32[384,1024]{1,0:T(8,128)}, bf16[384,1024]{1,0:T(8,128)(2,1)}, bf16[384,...) custom-call(s32[1]{0:T(128)} %bitcast.flag.refs_0_, ...), custom_call_target="tpu_custom_call" | custom-call | flops 8000000000 | bytes 14000000 | tf_op jit(solution)/shard_map/full_grads/pallas_call | solution.py:384
  148.1 4.8 %all-to-all-start = ((bf16[4,144,256]{2,1,0:T(8,128)(2,1)}), bf16[4,144,256]{2,1,0:T(8,128)(2,1)S(1)}, u32[]{:S(2)}, u32[]{:S(2)}) async-start(bf16[4,144,256]{2,1,0:T(8,128)(2,1)} %bitcast.10), calls=%async_computation | async-start | bytes 589824 | tf_op jit(solution)/shard_map/all_to_all | solution.py:544
  157.9 7.0 %all-to-all-start.1 = ((bf16[4,144,1024]{2,1,0:T(8,128)(2,1)}), bf16[4,144,1024]{2,1,0:T(8,128)(2,1)S(1)}, u32[]{:S(2)}, u32[]{:S(2)}) async-start(bf16[4,144,1024]{2,1,0:T(8,128)(2,1)} %bitcast.11), calls=%async_computation.1 | async-start | bytes 2359296 | tf_op jit(solution)/shard_map/all_to_all | solution.py:544
  164.9 4.8 %collective-permute-start.18 = (bf16[384,1024]{1,0:T(8,128)(2,1)}, bf16[384,1024]{1,0:T(8,128)(2,1)S(1)}, u32[]{:S(2)}, u32[]{:S(2)}) collective-permute-start(bf16[384,1024]{1,0:T(8,128)(2,1)} %get-tuple-element.88), channel_id=1, source_target_pairs={{0,1},{1,0},{2,3},{3,2},{4,5},{5,4},{6,7},{7,6},{8,9},{9,8},{10,11... | collective-permute-start | bytes 2359304 | tf_op jit(solution)/shard_map/ppermute | solution.py:528
  174.9 6.5 %collective-permute-done.17.refs_16_ = bf16[144,1024]{1,0:T(8,128)(2,1)S(1)} collective-permute-done((bf16[144,1024]{1,0:T(8,128)(2,1)S(1)}, bf16[144,1024]{1,0:T(8,128)(2,1)S(1)}, u32[]{:S(2)}, u32[]{:S(2)}) %collective-permute-start.17) | collective-permute-done | bytes 294944 | tf_op jit(solution)/shard_map/ppermute | solution.py:523
  181.5 4.4 %collective-permute-done.18 = bf16[384,1024]{1,0:T(8,128)(2,1)S(1)} collective-permute-done((bf16[384,1024]{1,0:T(8,128)(2,1)}, bf16[384,1024]{1,0:T(8,128)(2,1)S(1)}, u32[]{:S(2)}, u32[]{:S(2)}) %collective-permute-start.18) | collective-permute-done | bytes 786464 | tf_op jit(solution)/shard_map/ppermute | solution.py:528
  185.9 4.3 %all-to-all-start.2 = ((bf16[16,16,1024]{2,1,0:T(8,128)(2,1)}), bf16[16,16,1024]{2,1,0:T(8,128)(2,1)S(1)}, u32[]{:S(2)}, u32[]{:S(2)}) async-start(bf16[16,16,1024]{2,1,0:T(8,128)(2,1)} %bitcast.13), calls=%async_computation.2 | async-start | bytes 1048576 | tf_op jit(solution)/shard_map/all_to_all | solution.py:544
  192.2 11.0 %all-to-all-done.2 = bf16[16,16,1024]{2,1,0:T(8,128)(2,1)S(1)} async-done(((bf16[16,16,1024]{2,1,0:T(8,128)(2,1)}), bf16[16,16,1024]{2,1,0:T(8,128)(2,1)S(1)}, u32[]{:S(2)}, u32[]{:S(2)}) %all-to-all-start.2) | async-done | bytes 524320 | tf_op jit(solution)/shard_map/all_to_all | solution.py:544
  204.0 4.5 %all-to-all-start.3 = ((f32[4,16,1024]{2,1,0:T(8,128)}), f32[4,16,1024]{2,1,0:T(8,128)S(1)}, u32[]{:S(2)}, u32[]{:S(2)}) async-start(f32[4,16,1024]{2,1,0:T(8,128)} %bitcast.17), calls=%async_computation.3 | async-start | bytes 524288 | tf_op jit(solution)/shard_map/all_to_all | solution.py:544
  208.6 7.9 %all-to-all-done.3 = f32[4,16,1024]{2,1,0:T(8,128)S(1)} async-done(((f32[4,16,1024]{2,1,0:T(8,128)}), f32[4,16,1024]{2,1,0:T(8,128)S(1)}, u32[]{:S(2)}, u32[]{:S(2)}) %all-to-all-start.3) | async-done | bytes 262176 | tf_op jit(solution)/shard_map/all_to_all | solution.py:544
  221.0 8.0 %mid_backward.1 = (bf16[128,1024]{1,0:T(8,128)(2,1)}, bf16[128,1024]{1,0:T(8,128)(2,1)}, bf16[128,1024]{1,0:T(8,128)(2,1)}) custom-call(s32[1]{0:T(128)} %bitcast.flag.refs_0_, bf16[288,1024]{1,0:T(8,128)(2,1)} %copy-done.9, bf16[288,1024]{1,0:T(8,128)(2,1)} %collective-permute-done.1.refs_3_.refs_2_, ...), custom_call_target="tpu_custom_call" | custom-call | flops 3000000000 | bytes 6000000 | tf_op jit(solution)/shard_map/mid_backward/pallas_call | solution.py:508
  229.7 11.0 %collective-permute-done.20 = bf16[384,1024]{1,0:T(8,128)(2,1)} collective-permute-done((bf16[384,1024]{1,0:T(8,128)(2,1)}, bf16[384,1024]{1,0:T(8,128)(2,1)}, u32[]{:S(2)}, u32[]{:S(2)}) %collective-permute-start.20) | collective-permute-done | bytes 786464 | tf_op jit(solution)/shard_map/ppermute | solution.py:523
  (102 shorter events, 64.5 us)
Async XLA Ops:
  0.6 33.8 %collective-permute-start = (bf16[384,1024]{1,0:T(8,128)(2,1)}, bf16[384,1024]{1,0:T(8,128)(2,1)S(1)}, u32[]{:S(2)}, u32[]{:S(2)}) collective-permute-start(bf16[384,1024]{1,0:T(8,128)(2,1)} %bitcast.31), channel_id=1, source_target_pairs={{2,0},{3,1},{4,2},{5,3},{6,4},{7,5},{8,6},{9,7},{10,8},{11,9},{12,... | collective-permute-start | bytes 2359304 | tf_op jit(solution)/shard_map/ppermute | solution.py:523
  13.6 20.9 %collective-permute-start.2 = (bf16[384,1024]{1,0:T(8,128)(2,1)}, bf16[384,1024]{1,0:T(8,128)(2,1)}, u32[]{:S(2)}, u32[]{:S(2)}) collective-permute-start(bf16[384,1024]{1,0:T(8,128)(2,1)} %get-tuple-element.58), channel_id=1, source_target_pairs={{0,1},{1,0},{2,3},{3,2},{4,5},{5,4},{6,7},{7,6},{8,9},{9,8},{10,11... | collective-permute-start | bytes 2359304 | tf_op jit(solution)/shard_map/ppermute | solution.py:528
  15.2 18.8 %collective-permute-start.1 = (bf16[288,1024]{1,0:T(8,128)(2,1)}, bf16[288,1024]{1,0:T(8,128)(2,1)}, u32[]{:S(2)}, u32[]{:S(2)}) collective-permute-start(bf16[288,1024]{1,0:T(8,128)(2,1)} %get-tuple-element.57.refs_7_.refs_6_), channel_id=1, source_target_pairs={{0,2},{1,3},{2,4},{3,5},{4,6},{5,7},{6,8},{7,9},{8,10},{9,11},{10,... | collective-permute-start | bytes 1769480 | tf_op jit(solution)/shard_map/ppermute | solution.py:523
  34.0 13.9 %collective-permute-start.4 = (bf16[288,1024]{1,0:T(8,128)(2,1)}, bf16[288,1024]{1,0:T(8,128)(2,1)}, u32[]{:S(2)}, u32[]{:S(2)}) collective-permute-start(bf16[288,1024]{1,0:T(8,128)(2,1)} %collective-permute-done.1.refs_3_.refs_2_), channel_id=1, source_target_pairs={{0,1},{1,0},{2,3},{3,2},{4,5},{5,4},{6,7},{7,6},{8,9},{9,8},{10,11... | collective-permute-start | bytes 1769480 | tf_op jit(solution)/shard_map/ppermute | solution.py:528
  34.5 17.5 %collective-permute-start.3 = (bf16[288,1024]{1,0:T(8,128)(2,1)}, bf16[288,1024]{1,0:T(8,128)(2,1)S(1)}, u32[]{:S(2)}, u32[]{:S(2)}) collective-permute-start(bf16[288,1024]{1,0:T(8,128)(2,1)} %collective-permute-done.1.refs_3_.refs_2_), channel_id=1, source_target_pairs={{0,2},{1,3},{2,4},{3,5},{4,6},{5,7},{6,8},{7,9},{8,10},{9,11},{10,... | collective-permute-start | bytes 1769480 | tf_op jit(solution)/shard_map/ppermute | solution.py:523
  36.4 27.5 %collective-permute-start.6 = (bf16[528,1024]{1,0:T(8,128)(2,1)}, bf16[528,1024]{1,0:T(8,128)(2,1)S(1)}, u32[]{:S(2)}, u32[]{:S(2)}) collective-permute-start(bf16[528,1024]{1,0:T(8,128)(2,1)} %get-tuple-element.64.refs_6_.refs_8_.refs_7_.refs_10_), channel_id=1, source_target_pairs={{2,0},{3,1},{4,2},{5,3},{6,4},{7,5},{8,6},{9,7},{10,8},{11,9},{12,... | collective-permute-start | bytes 3244040 | tf_op jit(solution)/shard_map/ppermute | solution.py:523
  52.8 17.5 %collective-permute-start.5 = (bf16[384,1024]{1,0:T(8,128)(2,1)S(1)}, bf16[384,1024]{1,0:T(8,128)(2,1)}, u32[]{:S(2)}, u32[]{:S(2)}) collective-permute-start(bf16[384,1024]{1,0:T(8,128)(2,1)S(1)} %pad_maximum_fusion), channel_id=1, source_target_pairs={{0,1},{1,0},{2,3},{3,2},{4,5},{5,4},{6,7},{7,6},{8,9},{9,8},{10,11... | collective-permute-start | bytes 2359304 | tf_op jit(solution)/shard_map/ppermute | solution.py:528
  70.4 29.1 %collective-permute-start.7 = (bf16[528,1024]{1,0:T(8,128)(2,1)S(1)}, bf16[528,1024]{1,0:T(8,128)(2,1)S(1)}, u32[]{:S(2)}, u32[]{:S(2)}) collective-permute-start(bf16[528,1024]{1,0:T(8,128)(2,1)S(1)} %broadcast_select_fusion), channel_id=1, source_target_pairs={{0,1},{1,0},{2,3},{3,2},{4,5},{5,4},{6,7},{7,6},{8,9},{9,8},{10,11... | collective-permute-start | bytes 3244040 | tf_op jit(solution)/shard_map/ppermute | solution.py:528
  72.8 8.8 %collective-permute-start.8 = (bf16[144,1024]{1,0:T(8,128)(2,1)}, bf16[144,1024]{1,0:T(8,128)(2,1)S(1)}, u32[]{:S(2)}, u32[]{:S(2)}) collective-permute-start(bf16[144,1024]{1,0:T(8,128)(2,1)} %slice.23), channel_id=1, source_target_pairs={{2,0},{3,1},{4,2},{5,3},{6,4},{7,5},{8,6},{9,7},{10,8},{11,9},{12,... | collective-permute-start | bytes 884744 | tf_op jit(solution)/shard_map/ppermute | solution.py:523
  89.4 10.2 %collective-permute-start.9 = (f32[24,384]{1,0:T(8,128)}, f32[24,384]{1,0:T(8,128)S(1)}, u32[]{:S(2)}, u32[]{:S(2)}) collective-permute-start(f32[24,384]{1,0:T(8,128)} %get-tuple-element.68.refs_15_), channel_id=1, source_target_pairs={{0,2},{1,3},{2,4},{3,5},{4,6},{5,7},{6,8},{7,9},{8,10},{9,11},{10,... | collective-permute-start | bytes 110600 | tf_op jit(solution)/shard_map/ppermute | solution.py:523
  92.5 7.0 %collective-permute-start.10 = (f32[24,384]{1,0:T(8,128)}, f32[24,384]{1,0:T(8,128)S(1)}, u32[]{:S(2)}, u32[]{:S(2)}) collective-permute-start(f32[24,384]{1,0:T(8,128)} %get-tuple-element.69.refs_13_), channel_id=1, source_target_pairs={{2,0},{3,1},{4,2},{5,3},{6,4},{7,5},{8,6},{9,7},{10,8},{11,9},{12,... | collective-permute-start | bytes 110600 | tf_op jit(solution)/shard_map/ppermute | solution.py:523
  99.0 15.4 %collective-permute-start.11 = (bf16[144,1024]{1,0:T(8,128)(2,1)}, bf16[144,1024]{1,0:T(8,128)(2,1)S(1)}, u32[]{:S(2)}, u32[]{:S(2)}) collective-permute-start(bf16[144,1024]{1,0:T(8,128)(2,1)} %broadcast_select_fusion.3), channel_id=1, source_target_pairs={{0,1},{1,0},{2,3},{3,2},{4,5},{5,4},{6,7},{7,6},{8,9},{9,8},{10,11... | collective-permute-start | bytes 884744 | tf_op jit(solution)/shard_map/ppermute | solution.py:528
  106.2 8.2 %collective-permute-start.13 = (f32[48,384]{1,0:T(8,128)S(1)}, f32[48,384]{1,0:T(8,128)S(1)}, u32[]{:S(2)}, u32[]{:S(2)}) collective-permute-start(f32[48,384]{1,0:T(8,128)S(1)} %get-tuple-element.109), channel_id=1, source_target_pairs={{1,0},{2,1},{3,2},{4,3},{5,4},{6,5},{7,6},{8,7},{9,8},{10,9},{11,1... | collective-permute-start | bytes 221192 | tf_op jit(solution)/shard_map/ppermute | solution.py:523
  112.2 9.4 %collective-permute-start.12 = (f32[48,384]{1,0:T(8,128)S(1)}, f32[48,384]{1,0:T(8,128)S(1)}, u32[]{:S(2)}, u32[]{:S(2)}) collective-permute-start(f32[48,384]{1,0:T(8,128)S(1)} %get-tuple-element.110), channel_id=1, source_target_pairs={{0,1},{1,2},{2,3},{3,4},{4,5},{5,6},{6,7},{7,8},{8,9},{9,10},{10,1... | collective-permute-start | bytes 221192 | tf_op jit(solution)/shard_map/ppermute | solution.py:523
  145.4 8.6 %collective-permute-start.15 = (bf16[144,1024]{1,0:T(8,128)(2,1)S(1)}, bf16[144,1024]{1,0:T(8,128)(2,1)S(1)}, u32[]{:S(2)}, u32[]{:S(2)}) collective-permute-start(bf16[144,1024]{1,0:T(8,128)(2,1)S(1)} %mid_cotangent.1.refs_12_), channel_id=1, source_target_pairs={{2,0},{3,1},{4,2},{5,3},{6,4},{7,5},{8,6},{9,7},{10,8},{11,9},{12,... | collective-permute-start | bytes 884744 | tf_op jit(solution)/shard_map/ppermute | solution.py:523
  148.1 9.8 %all-to-all-start = ((bf16[4,144,256]{2,1,0:T(8,128)(2,1)}), bf16[4,144,256]{2,1,0:T(8,128)(2,1)S(1)}, u32[]{:S(2)}, u32[]{:S(2)}) async-start(bf16[4,144,256]{2,1,0:T(8,128)(2,1)} %bitcast.10), calls=%async_computation | async-start | bytes 589824 | tf_op jit(solution)/shard_map/all_to_all | solution.py:544
  157.9 15.7 %all-to-all-start.1 = ((bf16[4,144,1024]{2,1,0:T(8,128)(2,1)}), bf16[4,144,1024]{2,1,0:T(8,128)(2,1)S(1)}, u32[]{:S(2)}, u32[]{:S(2)}) async-start(bf16[4,144,1024]{2,1,0:T(8,128)(2,1)} %bitcast.11), calls=%async_computation.1 | async-start | bytes 2359296 | tf_op jit(solution)/shard_map/all_to_all | solution.py:544
  164.9 20.9 %collective-permute-start.18 = (bf16[384,1024]{1,0:T(8,128)(2,1)}, bf16[384,1024]{1,0:T(8,128)(2,1)S(1)}, u32[]{:S(2)}, u32[]{:S(2)}) collective-permute-start(bf16[384,1024]{1,0:T(8,128)(2,1)} %get-tuple-element.88), channel_id=1, source_target_pairs={{0,1},{1,0},{2,3},{3,2},{4,5},{5,4},{6,7},{7,6},{8,9},{9,8},{10,11... | collective-permute-start | bytes 2359304 | tf_op jit(solution)/shard_map/ppermute | solution.py:528
  169.7 11.8 %collective-permute-start.17 = (bf16[144,1024]{1,0:T(8,128)(2,1)S(1)}, bf16[144,1024]{1,0:T(8,128)(2,1)S(1)}, u32[]{:S(2)}, u32[]{:S(2)}) collective-permute-start(bf16[144,1024]{1,0:T(8,128)(2,1)S(1)} %collective-permute-done.15.refs_14_), channel_id=1, source_target_pairs={{2,0},{3,1},{4,2},{5,3},{6,4},{7,5},{8,6},{9,7},{10,8},{11,9},{12,... | collective-permute-start | bytes 884744 | tf_op jit(solution)/shard_map/ppermute | solution.py:523
  185.9 17.3 %all-to-all-start.2 = ((bf16[16,16,1024]{2,1,0:T(8,128)(2,1)}), bf16[16,16,1024]{2,1,0:T(8,128)(2,1)S(1)}, u32[]{:S(2)}, u32[]{:S(2)}) async-start(bf16[16,16,1024]{2,1,0:T(8,128)(2,1)} %bitcast.13), calls=%async_computation.2 | async-start | bytes 1048576 | tf_op jit(solution)/shard_map/all_to_all | solution.py:544
  190.2 13.1 %collective-permute-start.19 = (bf16[144,1024]{1,0:T(8,128)(2,1)S(1)}, bf16[144,1024]{1,0:T(8,128)(2,1)}, u32[]{:S(2)}, u32[]{:S(2)}) collective-permute-start(bf16[144,1024]{1,0:T(8,128)(2,1)S(1)} %broadcast_select_fusion.1), channel_id=1, source_target_pairs={{0,1},{1,0},{2,3},{3,2},{4,5},{5,4},{6,7},{7,6},{8,9},{9,8},{10,11... | collective-permute-start | bytes 884744 | tf_op jit(solution)/shard_map/ppermute | solution.py:528
  204.0 12.5 %all-to-all-start.3 = ((f32[4,16,1024]{2,1,0:T(8,128)}), f32[4,16,1024]{2,1,0:T(8,128)S(1)}, u32[]{:S(2)}, u32[]{:S(2)}) async-start(f32[4,16,1024]{2,1,0:T(8,128)} %bitcast.17), calls=%async_computation.3 | async-start | bytes 524288 | tf_op jit(solution)/shard_map/all_to_all | solution.py:544
  208.5 11.8 %collective-permute-start.16 = (bf16[144,1024]{1,0:T(8,128)(2,1)S(1)}, bf16[144,1024]{1,0:T(8,128)(2,1)S(1)}, u32[]{:S(2)}, u32[]{:S(2)}) collective-permute-start(bf16[144,1024]{1,0:T(8,128)(2,1)S(1)} %broadcast_select_fusion.2), channel_id=1, source_target_pairs={{0,1},{1,0},{2,3},{3,2},{4,5},{5,4},{6,7},{7,6},{8,9},{9,8},{10,11... | collective-permute-start | bytes 884744 | tf_op jit(solution)/shard_map/ppermute | solution.py:528
  217.7 23.1 %collective-permute-start.20 = (bf16[384,1024]{1,0:T(8,128)(2,1)}, bf16[384,1024]{1,0:T(8,128)(2,1)}, u32[]{:S(2)}, u32[]{:S(2)}) collective-permute-start(bf16[384,1024]{1,0:T(8,128)(2,1)} %fusion.2), channel_id=1, source_target_pairs={{0,2},{1,3},{2,4},{3,5},{4,6},{5,7},{6,8},{7,9},{8,10},{9,11},{10,... | collective-permute-start | bytes 2359304 | tf_op jit(solution)/shard_map/ppermute | solution.py:523
  (25 other events, 433.9 us)

commit v10 on v8

--- a/solution.py
+++ b/solution.py
@@ -591,17 +591,18 @@
     right = exchange(sum_ext, "ctx", X_GROUPS)
     term = dot_tn(left, right).astype(BF16)
     g1 = swap(jnp.where(upper, cot_m, g2), "ctx", 1)
-    term, g4 = together(term, shift(g2, -2))
+    term, g4, near = together(term, shift(g2, -2), near)
     total = jnp.sum(exchange(term, "ctx", YZ_GROUPS).astype(F32).reshape(16, 16, WIDTH), axis=0)
     near, total = together(near, total)
     passed = jnp.where(upper, dq2.astype(F32), dq2.astype(F32) + near.astype(F32)).astype(BF16)
     far = shift(passed, 2)
     g2_late, g4 = together(g2, g4)
     g3 = swap(jnp.where(upper, g2_late, g4), "ctx", 1)
+    dq_m, dk_m, dv_m = mid_backward(flag, pays, (late_cq, cq1, cq2, qm3, qm4), (cot_m, g1, g2, g3, g4))
+    dq_m, total = together(dq_m, total)
     every = exchange(jnp.concatenate([total] * 4, axis=0), "dp", None)
     factor = float(lax.axis_size("dp") * lax.axis_size("ctx") * F) ** (-0.5)
     grad_link = jnp.sum(every.reshape(4, 16, WIDTH), axis=0) * factor
-    dq_m, dk_m, dv_m = mid_backward(flag, pays, (late_cq, cq1, cq2, qm3, qm4), (cot_m, g1, g2, g3, g4))
 
     dq_f = (dq0 + far.astype(F32) + jnp.where(upper, near.astype(F32), 0.0)).astype(BF16)
     return (dq_m[None], dk_m[None], dv_m[None], dq_f[None], dk_f[None], dv_f[None], grad_link)

time: 230 us -> 230 us (level); the launches traced: 226 us -> 229 us
  blocking collectives: 0 us -> 29.3 us
  starting transfers between devices: 94.8 us -> 70.9 us
    all_to_all x0 -> x1, blocking collectives: none -> 29.3 us  [exchange(): lax.all_to_all(value, axis, 0, 0, axis_index_groups=groups, tiled=True)]
    all_to_all x4 -> x3, starting transfers between devices: 56.1 us -> 33.3 us  [exchange(): lax.all_to_all(value, axis, 0, 0, axis_index_groups=groups, tiled=True)]
    all_to_all x4 -> x3, waiting for transfers between devices: 16.8 us -> 17.4 us  [exchange(): lax.all_to_all(value, axis, 0, 0, axis_index_groups=groups, tiled=True)]
  transfers between devices with their start and end apart: 25 -> 24, of which waited for: 12 -> 11; matrix products, arithmetic and copies ran while one was open for 4% -> 4% of each run, Pallas kernels for 14% -> 13%
where the time goes in v10:
time: 230 us; the launch traced here: 229 us
  starting transfers between devices  70.9 us (31%)
  waiting for transfers between devices  66.6 us (29%)
  Pallas kernels  46.8 us (20%)
  blocking collectives  29.3 us (13%)
  other arithmetic  7.72 us (3%)
  local copies, waits for them, and re-layouts  5.21 us (2%)
    ppermute x13, waiting for transfers between devices, shift(): lax.ppermute(value, 'ctx', [(n, n + steps) for n in range(first, last)])  42.1 us
    all_to_all x3, starting transfers between devices, exchange(): lax.all_to_all(value, axis, 0, 0, axis_index_groups=groups, tiled=True)  33.3 us
    all_to_all x1, blocking collectives, exchange(): lax.all_to_all(value, axis, 0, 0, axis_index_groups=groups, tiled=True)  29.3 us
    ppermute x13, starting transfers between devices, shift(): lax.ppermute(value, 'ctx', [(n, n + steps) for n in range(first, last)])  29.3 us
    all_to_all x3, waiting for transfers between devices, exchange(): lax.all_to_all(value, axis, 0, 0, axis_index_groups=groups, tiled=True)  17.4 us
    pallas_call x1, Pallas kernels, full_grads(): call(grads_body, 'full_grads', 8000000000, 14000000, in_specs=[FLAG, head...  14.9 us
    ppermute x8, starting transfers between devices, swap(): return lax.ppermute(value, axis, [(n, n ^ bit) for n in range(count)])  8.33 us
    pallas_call x1, Pallas kernels, mid_backward(): call(mid_bwd_body, 'mid_backward', 3000000000, 6000000, in_specs=[FLAG] +...  8.11 us
  transfers between devices with their start and end apart: 24, of which 11 were waited for; matrix products, arithmetic and copies ran while one was open for 4% of the time, Pallas kernels for 13%

profile of v10, /device:TPU:1, one launch (start us, length us, event | category | flops | bytes accessed | tf_op | source)
XLA Modules:
  0.0 229.1 jit_solution(14199026919163645074)
XLA Ops:
  3.2 4.0 %pack.1 = (bf16[288,1024]{1,0:T(8,128)(2,1)}, bf16[528,1024]{1,0:T(8,128)(2,1)}, bf16[384,1024]{1,0:T(8,128)(2,1)}) custom-call(s32[1]{0:T(128)} %bitcast.flag.refs_0_, bf16[128,1024]{1,0:T(8,128)(2,1)} %bitcast.37, bf16[128,1024]{1,0:T(8,128)(2,1)} %bitcast.42, bf16[128,1024]{1,0:T(8,128)(2,1)} %bitcast.43, bf16[16,256]{1,0:T(8,128)(2,1)} %broadcast_in_dim.27.ids, ...), custom_call_target="tpu_custom_call" | custom-call | tf_op jit(solution)/shard_map/pack/pallas_call | solution.py:118
  9.3 4.2 %collective-permute-start.1 = (bf16[288,1024]{1,0:T(8,128)(2,1)}, bf16[288,1024]{1,0:T(8,128)(2,1)S(1)}, u32[]{:S(2)}, u32[]{:S(2)}) collective-permute-start(bf16[288,1024]{1,0:T(8,128)(2,1)} %get-tuple-element.57.refs_7_.refs_6_), channel_id=1, source_target_pairs={{0,2},{1,3},{2,4},{3,5},{4,6},{5,7},{6,8},{7,9},{8,10},{9,11},{10,... | collective-permute-start | bytes 1769480 | tf_op jit(solution)/shard_map/ppermute | solution.py:523
  13.5 11.6 %collective-permute-done.1.refs_3_.refs_2_ = bf16[288,1024]{1,0:T(8,128)(2,1)S(1)} collective-permute-done((bf16[288,1024]{1,0:T(8,128)(2,1)}, bf16[288,1024]{1,0:T(8,128)(2,1)S(1)}, u32[]{:S(2)}, u32[]{:S(2)}) %collective-permute-start.1) | collective-permute-done | bytes 589856 | tf_op jit(solution)/shard_map/ppermute | solution.py:523
  25.6 4.1 %collective-permute-start.3 = (bf16[288,1024]{1,0:T(8,128)(2,1)S(1)}, bf16[288,1024]{1,0:T(8,128)(2,1)S(1)}, u32[]{:S(2)}, u32[]{:S(2)}) collective-permute-start(bf16[288,1024]{1,0:T(8,128)(2,1)S(1)} %collective-permute-done.1.refs_3_.refs_2_), channel_id=1, source_target_pairs={{0,2},{1,3},{2,4},{3,5},{4,6},{5,7},{6,8},{7,9},{8,10},{9,11},{10,... | collective-permute-start | bytes 1769480 | tf_op jit(solution)/shard_map/ppermute | solution.py:523
  31.2 6.7 %collective-permute-done.4.refs_5_.refs_4_ = bf16[288,1024]{1,0:T(8,128)(2,1)S(1)} collective-permute-done((bf16[288,1024]{1,0:T(8,128)(2,1)S(1)}, bf16[288,1024]{1,0:T(8,128)(2,1)S(1)}, u32[]{:S(2)}, u32[]{:S(2)}) %collective-permute-start.4) | collective-permute-done | bytes 589856 | tf_op jit(solution)/shard_map/ppermute | solution.py:528
  42.2 14.4 %collective-permute-done.6.refs_7_.refs_9_.refs_12_ = bf16[528,1024]{1,0:T(8,128)(2,1)S(1)} collective-permute-done((bf16[528,1024]{1,0:T(8,128)(2,1)}, bf16[528,1024]{1,0:T(8,128)(2,1)S(1)}, u32[]{:S(2)}, u32[]{:S(2)}) %collective-permute-start.6) | collective-permute-done | bytes 1081376 | tf_op jit(solution)/shard_map/ppermute | solution.py:523
  59.0 6.0 %mid_forward.1 = (bf16[144,1024]{1,0:T(8,128)(2,1)}, f32[128,1024]{1,0:T(8,128)}, f32[8,1024]{1,0:T(8,128)}) custom-call(s32[1]{0:T(128)} %bitcast.flag.refs_0_, bf16[128,1024]{1,0:T(8,128)(2,1)} %bitcast.38, bf16[288,1024]{1,0:T(8,128)(2,1)} %copy-done.9, bf16[288,1024]{1,0:T(8,128)(2,1)} %copy-done.13, ...), custom_call_target="tpu_custom_call" | custom-call | flops 700000000 | bytes 4000000 | tf_op jit(solution)/shard_map/mid_forward/pallas_call | solution.py:178
  66.8 14.9 %all-to-all-start = ((bf16[4,144,256]{2,1,0:T(8,128)(2,1)}), bf16[4,144,256]{2,1,0:T(8,128)(2,1)S(1)}, u32[]{:S(2)}, u32[]{:S(2)}) async-start(bf16[4,144,256]{2,1,0:T(8,128)(2,1)} %bitcast.8), calls=%async_computation | async-start | bytes 589824 | tf_op jit(solution)/shard_map/all_to_all | solution.py:544
  81.7 7.7 %full_stats.1 = (bf16[384,1024]{1,0:T(8,128)(2,1)}, f32[24,384]{1,0:T(8,128)}, f32[24,384]{1,0:T(8,128)}) custom-call(bf16[384,1024]{1,0:T(8,128)(2,1)} %bitcast.31, bf16[384,1024]{1,0:T(8,128)(2,1)} %bitcast.39, bf16[144,1024]{1,0:T(8,128)(2,1)} %get-tuple-element.67.refs_2_, bf16[1024,1024]{1,0:T(8,128)(2,1)} %w_ref.1, bf16[384,1024]{1,0:T(8,128)(2,1)} %bitcast.29, ...), custom_call_target="tpu_custom_call" | custom-call | flops 2000000000 | bytes 8000000 | tf_op jit(solution)/shard_map/full_stats/pallas_call | solution.py:294
  89.4 3.3 %collective-permute-start.9 = (f32[24,384]{1,0:T(8,128)}, f32[24,384]{1,0:T(8,128)S(1)}, u32[]{:S(2)}, u32[]{:S(2)}) collective-permute-start(f32[24,384]{1,0:T(8,128)} %get-tuple-element.68.refs_15_), channel_id=1, source_target_pairs={{0,2},{1,3},{2,4},{3,5},{4,6},{5,7},{6,8},{7,9},{8,10},{9,11},{10,... | collective-permute-start | bytes 110600 | tf_op jit(solution)/shard_map/ppermute | solution.py:523
  95.4 2.3 %collective-permute-done.10.refs_19_ = f32[24,384]{1,0:T(8,128)S(1)} collective-permute-done((f32[24,384]{1,0:T(8,128)}, f32[24,384]{1,0:T(8,128)S(1)}, u32[]{:S(2)}, u32[]{:S(2)}) %collective-permute-start.10) | collective-permute-done | bytes 36896 | tf_op jit(solution)/shard_map/ppermute | solution.py:523
  98.7 4.8 %next_stats.1.refs_14_ = f32[24,384]{1,0:T(8,128)} custom-call(s32[1]{0:T(128)} %bitcast.flag.refs_0_, bf16[384,1024]{1,0:T(8,128)(2,1)} %bitcast.32, bf16[384,1024]{1,0:T(8,128)(2,1)} %get-tuple-element.76.refs_2_, bf16[384,1024]{1,0:T(8,128)(2,1)} %collective-permute-done.5.refs_6_.refs_3_.refs_4_.refs_5_, ...), custom_call_target="tpu_custom_call" | custom-call | flops 1000000000 | bytes 6000000 | tf_op jit(solution)/shard_map/next_stats/pallas_call | solution.py:313
  105.8 4.3 %collective-permute-start.12 = (f32[48,384]{1,0:T(8,128)S(1)}, f32[48,384]{1,0:T(8,128)S(1)}, u32[]{:S(2)}, u32[]{:S(2)}) collective-permute-start(f32[48,384]{1,0:T(8,128)S(1)} %get-tuple-element.110), channel_id=1, source_target_pairs={{0,1},{1,2},{2,3},{3,4},{4,5},{5,6},{6,7},{7,8},{8,9},{9,10},{10,1... | collective-permute-start | bytes 221192 | tf_op jit(solution)/shard_map/ppermute | solution.py:523
  111.9 14.9 %full_grads.1 = (bf16[384,1024]{1,0:T(8,128)(2,1)}, bf16[384,1024]{1,0:T(8,128)(2,1)}, f32[384,1024]{1,0:T(8,128)}, bf16[384,1024]{1,0:T(8,128)(2,1)}, bf16[384,...) custom-call(s32[1]{0:T(128)} %bitcast.flag.refs_0_, ...), custom_call_target="tpu_custom_call" | custom-call | flops 8000000000 | bytes 14000000 | tf_op jit(solution)/shard_map/full_grads/pallas_call | solution.py:384
  128.1 3.9 %collective-permute-done.14.refs_3_ = f32[8,1024]{1,0:T(8,128)S(1)} collective-permute-done((f32[8,1024]{1,0:T(8,128)}, f32[8,1024]{1,0:T(8,128)S(1)}, u32[]{:S(2)}, u32[]{:S(2)}) %collective-permute-start.14) | collective-permute-done | bytes 32800 | tf_op jit(solution)/shard_map/ppermute | solution.py:523
  135.7 7.3 %collective-permute-done.15.refs_14_ = bf16[144,1024]{1,0:T(8,128)(2,1)S(1)} collective-permute-done((bf16[144,1024]{1,0:T(8,128)(2,1)S(1)}, bf16[144,1024]{1,0:T(8,128)(2,1)S(1)}, u32[]{:S(2)}, u32[]{:S(2)}) %collective-permute-start.15) | collective-permute-done | bytes 294944 | tf_op jit(solution)/shard_map/ppermute | solution.py:523
  143.1 10.3 %all-to-all-start.1 = ((bf16[4,144,1024]{2,1,0:T(8,128)(2,1)}), bf16[4,144,1024]{2,1,0:T(8,128)(2,1)S(1)}, u32[]{:S(2)}, u32[]{:S(2)}) async-start(bf16[4,144,1024]{2,1,0:T(8,128)(2,1)} %bitcast.34), calls=%async_computation.1 | async-start | bytes 2359296 | tf_op jit(solution)/shard_map/all_to_all | solution.py:544
  156.1 7.8 %all-to-all-done.1 = bf16[4,144,1024]{2,1,0:T(8,128)(2,1)S(1)} async-done(((bf16[4,144,1024]{2,1,0:T(8,128)(2,1)}), bf16[4,144,1024]{2,1,0:T(8,128)(2,1)S(1)}, u32[]{:S(2)}, u32[]{:S(2)}) %all-to-all-start.1) | async-done | bytes 1179680 | tf_op jit(solution)/shard_map/all_to_all | solution.py:544
  165.3 8.0 %all-to-all-start.2 = ((bf16[16,16,1024]{2,1,0:T(8,128)(2,1)}), bf16[16,16,1024]{2,1,0:T(8,128)(2,1)S(1)}, u32[]{:S(2)}, u32[]{:S(2)}) async-start(bf16[16,16,1024]{2,1,0:T(8,128)(2,1)} %bitcast.14), calls=%async_computation.2 | async-start | bytes 1048576 | tf_op jit(solution)/shard_map/all_to_all | solution.py:544
  175.7 9.6 %all-to-all-done.2 = bf16[16,16,1024]{2,1,0:T(8,128)(2,1)S(1)} async-done(((bf16[16,16,1024]{2,1,0:T(8,128)(2,1)}), bf16[16,16,1024]{2,1,0:T(8,128)(2,1)S(1)}, u32[]{:S(2)}, u32[]{:S(2)}) %all-to-all-start.2) | async-done | bytes 524320 | tf_op jit(solution)/shard_map/all_to_all | solution.py:544
  185.7 2.8 %collective-permute-start.20 = (bf16[384,1024]{1,0:T(8,128)(2,1)S(1)}, bf16[384,1024]{1,0:T(8,128)(2,1)}, u32[]{:S(2)}, u32[]{:S(2)}) collective-permute-start(bf16[384,1024]{1,0:T(8,128)(2,1)S(1)} %fusion.2), channel_id=1, source_target_pairs={{0,2},{1,3},{2,4},{3,5},{4,6},{5,7},{6,8},{7,9},{8,10},{9,11},{10,... | collective-permute-start | bytes 2359304 | tf_op jit(solution)/shard_map/ppermute | solution.py:523
  188.5 8.1 %mid_backward.1 = (bf16[128,1024]{1,0:T(8,128)(2,1)}, bf16[128,1024]{1,0:T(8,128)(2,1)}, bf16[128,1024]{1,0:T(8,128)(2,1)}) custom-call(s32[1]{0:T(128)} %bitcast.flag.refs_0_, bf16[288,1024]{1,0:T(8,128)(2,1)} %copy-done.9, bf16[288,1024]{1,0:T(8,128)(2,1)} %copy-done.13, bf16[384,1024]{1,0:T(8,128)(2,1)} %collective-permute-done.2.refs_4_.refs_5_.refs_3_, ...), custom_call_target="tpu_custom_call" | custom-call | flops 3000000000 | bytes 6000000 | tf_op jit(solution)/shard_map/mid_backward/pallas_call | solution.py:508
  196.7 29.3 %all_to_all.42 = f32[4,16,1024]{2,1,0:T(8,128)S(1)} all-to-all(f32[4,16,1024]{2,1,0:T(8,128)S(1)} %bitcast.36), channel_id=1, replica_groups=mesh['dp'=4,'ctx'=64] {'dp'}, dimensions={0} | all-to-all | bytes 524288 | tf_op jit(solution)/shard_map/all_to_all | solution.py:544
  226.7 2.4 %fusion.3 = bf16[1,384,1024]{2,1,0:T(8,128)(2,1)} fusion(bf16[384,1024]{1,0:T(8,128)(2,1)S(1)} %collective-permute-done.18, f32[384,1024]{1,0:T(8,128)S(1)} %copy-done.10, bf16[384,1024]{1,0:T(8,128)(2,1)} %collective-permute-done.20, pred[]{:T(512)S(6)} %eq.6), kind=kLoop, calls=%fused_computation.8 | loop fusion | flops 2359296 | bytes 3932161 | tf_op jit(solution)/shard_map/broadcast_in_dim | solution.py:608
  (103 shorter events, 35.0 us)
Async XLA Ops:
  0.6 24.5 %collective-permute-start = (bf16[384,1024]{1,0:T(8,128)(2,1)}, bf16[384,1024]{1,0:T(8,128)(2,1)S(1)}, u32[]{:S(2)}, u32[]{:S(2)}) collective-permute-start(bf16[384,1024]{1,0:T(8,128)(2,1)} %bitcast.27), channel_id=1, source_target_pairs={{2,0},{3,1},{4,2},{5,3},{6,4},{7,5},{8,6},{9,7},{10,8},{11,9},{12,... | collective-permute-start | bytes 2359304 | tf_op jit(solution)/shard_map/ppermute | solution.py:523
  7.2 18.4 %collective-permute-start.2 = (bf16[384,1024]{1,0:T(8,128)(2,1)}, bf16[384,1024]{1,0:T(8,128)(2,1)}, u32[]{:S(2)}, u32[]{:S(2)}) collective-permute-start(bf16[384,1024]{1,0:T(8,128)(2,1)} %get-tuple-element.58), channel_id=1, source_target_pairs={{0,1},{1,0},{2,3},{3,2},{4,5},{5,4},{6,7},{7,6},{8,9},{9,8},{10,11... | collective-permute-start | bytes 2359304 | tf_op jit(solution)/shard_map/ppermute | solution.py:528
  9.3 15.8 %collective-permute-start.1 = (bf16[288,1024]{1,0:T(8,128)(2,1)}, bf16[288,1024]{1,0:T(8,128)(2,1)S(1)}, u32[]{:S(2)}, u32[]{:S(2)}) collective-permute-start(bf16[288,1024]{1,0:T(8,128)(2,1)} %get-tuple-element.57.refs_7_.refs_6_), channel_id=1, source_target_pairs={{0,2},{1,3},{2,4},{3,5},{4,6},{5,7},{6,8},{7,9},{8,10},{9,11},{10,... | collective-permute-start | bytes 1769480 | tf_op jit(solution)/shard_map/ppermute | solution.py:523
  25.1 12.7 %collective-permute-start.4 = (bf16[288,1024]{1,0:T(8,128)(2,1)S(1)}, bf16[288,1024]{1,0:T(8,128)(2,1)S(1)}, u32[]{:S(2)}, u32[]{:S(2)}) collective-permute-start(bf16[288,1024]{1,0:T(8,128)(2,1)S(1)} %collective-permute-done.1.refs_3_.refs_2_), channel_id=1, source_target_pairs={{0,1},{1,0},{2,3},{3,2},{4,5},{5,4},{6,7},{7,6},{8,9},{9,8},{10,11... | collective-permute-start | bytes 1769480 | tf_op jit(solution)/shard_map/ppermute | solution.py:528
  25.6 13.6 %collective-permute-start.3 = (bf16[288,1024]{1,0:T(8,128)(2,1)S(1)}, bf16[288,1024]{1,0:T(8,128)(2,1)S(1)}, u32[]{:S(2)}, u32[]{:S(2)}) collective-permute-start(bf16[288,1024]{1,0:T(8,128)(2,1)S(1)} %collective-permute-done.1.refs_3_.refs_2_), channel_id=1, source_target_pairs={{0,2},{1,3},{2,4},{3,5},{4,6},{5,7},{6,8},{7,9},{8,10},{9,11},{10,... | collective-permute-start | bytes 1769480 | tf_op jit(solution)/shard_map/ppermute | solution.py:523
  29.7 26.9 %collective-permute-start.6 = (bf16[528,1024]{1,0:T(8,128)(2,1)}, bf16[528,1024]{1,0:T(8,128)(2,1)S(1)}, u32[]{:S(2)}, u32[]{:S(2)}) collective-permute-start(bf16[528,1024]{1,0:T(8,128)(2,1)} %get-tuple-element.64.refs_6_.refs_8_.refs_7_.refs_10_), channel_id=1, source_target_pairs={{2,0},{3,1},{4,2},{5,3},{6,4},{7,5},{8,6},{9,7},{10,8},{11,9},{12,... | collective-permute-start | bytes 3244040 | tf_op jit(solution)/shard_map/ppermute | solution.py:523
  40.0 16.6 %collective-permute-start.5 = (bf16[384,1024]{1,0:T(8,128)(2,1)S(1)}, bf16[384,1024]{1,0:T(8,128)(2,1)}, u32[]{:S(2)}, u32[]{:S(2)}) collective-permute-start(bf16[384,1024]{1,0:T(8,128)(2,1)S(1)} %pad_maximum_fusion), channel_id=1, source_target_pairs={{0,1},{1,0},{2,3},{3,2},{4,5},{5,4},{6,7},{7,6},{8,9},{9,8},{10,11... | collective-permute-start | bytes 2359304 | tf_op jit(solution)/shard_map/ppermute | solution.py:528
  56.7 41.0 %collective-permute-start.7 = (bf16[528,1024]{1,0:T(8,128)(2,1)S(1)}, bf16[528,1024]{1,0:T(8,128)(2,1)S(1)}, u32[]{:S(2)}, u32[]{:S(2)}) collective-permute-start(bf16[528,1024]{1,0:T(8,128)(2,1)S(1)} %broadcast_select_fusion), channel_id=1, source_target_pairs={{0,1},{1,0},{2,3},{3,2},{4,5},{5,4},{6,7},{7,6},{8,9},{9,8},{10,11... | collective-permute-start | bytes 3244040 | tf_op jit(solution)/shard_map/ppermute | solution.py:528
  57.7 24.0 %collective-permute-start.8 = (bf16[144,1024]{1,0:T(8,128)(2,1)S(1)}, bf16[144,1024]{1,0:T(8,128)(2,1)S(1)}, u32[]{:S(2)}, u32[]{:S(2)}) collective-permute-start(bf16[144,1024]{1,0:T(8,128)(2,1)S(1)} %slice.27), channel_id=1, source_target_pairs={{2,0},{3,1},{4,2},{5,3},{6,4},{7,5},{8,6},{9,7},{10,8},{11,9},{12,... | collective-permute-start | bytes 884744 | tf_op jit(solution)/shard_map/ppermute | solution.py:523
  66.8 28.6 %all-to-all-start = ((bf16[4,144,256]{2,1,0:T(8,128)(2,1)}), bf16[4,144,256]{2,1,0:T(8,128)(2,1)S(1)}, u32[]{:S(2)}, u32[]{:S(2)}) async-start(bf16[4,144,256]{2,1,0:T(8,128)(2,1)} %bitcast.8), calls=%async_computation | async-start | bytes 589824 | tf_op jit(solution)/shard_map/all_to_all | solution.py:544
  89.4 6.0 %collective-permute-start.9 = (f32[24,384]{1,0:T(8,128)}, f32[24,384]{1,0:T(8,128)S(1)}, u32[]{:S(2)}, u32[]{:S(2)}) collective-permute-start(f32[24,384]{1,0:T(8,128)} %get-tuple-element.68.refs_15_), channel_id=1, source_target_pairs={{0,2},{1,3},{2,4},{3,5},{4,6},{5,7},{6,8},{7,9},{8,10},{9,11},{10,... | collective-permute-start | bytes 110600 | tf_op jit(solution)/shard_map/ppermute | solution.py:523
  92.8 4.9 %collective-permute-start.10 = (f32[24,384]{1,0:T(8,128)}, f32[24,384]{1,0:T(8,128)S(1)}, u32[]{:S(2)}, u32[]{:S(2)}) collective-permute-start(f32[24,384]{1,0:T(8,128)} %get-tuple-element.69.refs_13_), channel_id=1, source_target_pairs={{2,0},{3,1},{4,2},{5,3},{6,4},{7,5},{8,6},{9,7},{10,8},{11,9},{12,... | collective-permute-start | bytes 110600 | tf_op jit(solution)/shard_map/ppermute | solution.py:523
  95.1 15.0 %collective-permute-start.11 = (bf16[144,1024]{1,0:T(8,128)(2,1)S(1)}, bf16[144,1024]{1,0:T(8,128)(2,1)}, u32[]{:S(2)}, u32[]{:S(2)}) collective-permute-start(bf16[144,1024]{1,0:T(8,128)(2,1)S(1)} %broadcast_select_fusion.3), channel_id=1, source_target_pairs={{0,1},{1,0},{2,3},{3,2},{4,5},{5,4},{6,7},{7,6},{8,9},{9,8},{10,11... | collective-permute-start | bytes 884744 | tf_op jit(solution)/shard_map/ppermute | solution.py:528
  104.4 5.7 %collective-permute-start.13 = (f32[48,384]{1,0:T(8,128)S(1)}, f32[48,384]{1,0:T(8,128)S(1)}, u32[]{:S(2)}, u32[]{:S(2)}) collective-permute-start(f32[48,384]{1,0:T(8,128)S(1)} %get-tuple-element.109), channel_id=1, source_target_pairs={{1,0},{2,1},{3,2},{4,3},{5,4},{6,5},{7,6},{8,7},{9,8},{10,9},{11,1... | collective-permute-start | bytes 221192 | tf_op jit(solution)/shard_map/ppermute | solution.py:523
  105.8 5.5 %collective-permute-start.12 = (f32[48,384]{1,0:T(8,128)S(1)}, f32[48,384]{1,0:T(8,128)S(1)}, u32[]{:S(2)}, u32[]{:S(2)}) collective-permute-start(f32[48,384]{1,0:T(8,128)S(1)} %get-tuple-element.110), channel_id=1, source_target_pairs={{0,1},{1,2},{2,3},{3,4},{4,5},{5,6},{6,7},{7,8},{8,9},{9,10},{10,1... | collective-permute-start | bytes 221192 | tf_op jit(solution)/shard_map/ppermute | solution.py:523
  126.8 5.2 %collective-permute-start.14 = (f32[8,1024]{1,0:T(8,128)}, f32[8,1024]{1,0:T(8,128)S(1)}, u32[]{:S(2)}, u32[]{:S(2)}) collective-permute-start(f32[8,1024]{1,0:T(8,128)} %get-tuple-element.81), channel_id=1, source_target_pairs={{1,0},{2,1},{3,2},{4,3},{5,4},{6,5},{7,6},{8,7},{9,8},{10,9},{11,1... | collective-permute-start | bytes 98312 | tf_op jit(solution)/shard_map/ppermute | solution.py:523
  134.3 8.8 %collective-permute-start.15 = (bf16[144,1024]{1,0:T(8,128)(2,1)S(1)}, bf16[144,1024]{1,0:T(8,128)(2,1)S(1)}, u32[]{:S(2)}, u32[]{:S(2)}) collective-permute-start(bf16[144,1024]{1,0:T(8,128)(2,1)S(1)} %mid_cotangent.1.refs_12_), channel_id=1, source_target_pairs={{2,0},{3,1},{4,2},{5,3},{6,4},{7,5},{8,6},{9,7},{10,8},{11,9},{12,... | collective-permute-start | bytes 884744 | tf_op jit(solution)/shard_map/ppermute | solution.py:523
  143.1 20.8 %all-to-all-start.1 = ((bf16[4,144,1024]{2,1,0:T(8,128)(2,1)}), bf16[4,144,1024]{2,1,0:T(8,128)(2,1)S(1)}, u32[]{:S(2)}, u32[]{:S(2)}) async-start(bf16[4,144,1024]{2,1,0:T(8,128)(2,1)} %bitcast.34), calls=%async_computation.1 | async-start | bytes 2359296 | tf_op jit(solution)/shard_map/all_to_all | solution.py:544
  153.4 11.8 %collective-permute-start.18 = (bf16[384,1024]{1,0:T(8,128)(2,1)}, bf16[384,1024]{1,0:T(8,128)(2,1)S(1)}, u32[]{:S(2)}, u32[]{:S(2)}) collective-permute-start(bf16[384,1024]{1,0:T(8,128)(2,1)} %get-tuple-element.88), channel_id=1, source_target_pairs={{0,1},{1,0},{2,3},{3,2},{4,5},{5,4},{6,7},{7,6},{8,9},{9,8},{10,11... | collective-permute-start | bytes 2359304 | tf_op jit(solution)/shard_map/ppermute | solution.py:528
  154.8 10.4 %collective-permute-start.17 = (bf16[144,1024]{1,0:T(8,128)(2,1)S(1)}, bf16[144,1024]{1,0:T(8,128)(2,1)S(1)}, u32[]{:S(2)}, u32[]{:S(2)}) collective-permute-start(bf16[144,1024]{1,0:T(8,128)(2,1)S(1)} %collective-permute-done.15.refs_14_), channel_id=1, source_target_pairs={{2,0},{3,1},{4,2},{5,3},{6,4},{7,5},{8,6},{9,7},{10,8},{11,9},{12,... | collective-permute-start | bytes 884744 | tf_op jit(solution)/shard_map/ppermute | solution.py:523
  165.3 20.0 %all-to-all-start.2 = ((bf16[16,16,1024]{2,1,0:T(8,128)(2,1)}), bf16[16,16,1024]{2,1,0:T(8,128)(2,1)S(1)}, u32[]{:S(2)}, u32[]{:S(2)}) async-start(bf16[16,16,1024]{2,1,0:T(8,128)(2,1)} %bitcast.14), calls=%async_computation.2 | async-start | bytes 1048576 | tf_op jit(solution)/shard_map/all_to_all | solution.py:544
  174.1 14.4 %collective-permute-start.16 = (bf16[144,1024]{1,0:T(8,128)(2,1)}, bf16[144,1024]{1,0:T(8,128)(2,1)}, u32[]{:S(2)}, u32[]{:S(2)}) collective-permute-start(bf16[144,1024]{1,0:T(8,128)(2,1)} %broadcast_select_fusion.2), channel_id=1, source_target_pairs={{0,1},{1,0},{2,3},{3,2},{4,5},{5,4},{6,7},{7,6},{8,9},{9,8},{10,11... | collective-permute-start | bytes 884744 | tf_op jit(solution)/shard_map/ppermute | solution.py:528
  175.5 13.0 %collective-permute-start.19 = (bf16[144,1024]{1,0:T(8,128)(2,1)S(1)}, bf16[144,1024]{1,0:T(8,128)(2,1)}, u32[]{:S(2)}, u32[]{:S(2)}) collective-permute-start(bf16[144,1024]{1,0:T(8,128)(2,1)S(1)} %broadcast_select_fusion.1), channel_id=1, source_target_pairs={{0,1},{1,0},{2,3},{3,2},{4,5},{5,4},{6,7},{7,6},{8,9},{9,8},{10,11... | collective-permute-start | bytes 884744 | tf_op jit(solution)/shard_map/ppermute | solution.py:528
  185.7 41.0 %collective-permute-start.20 = (bf16[384,1024]{1,0:T(8,128)(2,1)S(1)}, bf16[384,1024]{1,0:T(8,128)(2,1)}, u32[]{:S(2)}, u32[]{:S(2)}) collective-permute-start(bf16[384,1024]{1,0:T(8,128)(2,1)S(1)} %fusion.2), channel_id=1, source_target_pairs={{0,2},{1,3},{2,4},{3,5},{4,6},{5,7},{6,8},{7,9},{8,10},{9,11},{10,... | collective-permute-start | bytes 2359304 | tf_op jit(solution)/shard_map/ppermute | solution.py:523
  (25 other events, 371.5 us)
